TPU v7x, 32 devices: a whole 2x2x4 slice. The times are simulated.
32 devices in a mesh: groups: 2 (over x), ctx: 4 (over y, core), head: 4 (over z).
Axes of the slice: x: 2, y: 2, z: 4, core: 2. Of those that a mesh axis runs over, the one named last changes fastest.
Arguments:
- hidden: bfloat16 [2, 2048, 4096], P(None, ('groups', 'ctx'), 'head'), parts along dimension 1, may hold values from -40 to 40
- strand_bases: int32 [2048], P(('groups', 'ctx')), parts along dimension 0, may hold values from 0 to 3
- variant_sites: int32 [256], P('groups'), parts along dimension 0, may hold values from 0 to 1023, as said below
- base_shift: int32 [256], P('groups'), parts along dimension 0, may hold values from 1 to 3
- base_embed: bfloat16 [4, 4096], replicated, may hold values from -6 to 6
- query_weight: bfloat16 [4096, 2048], P(None, 'head')
- key_weight: bfloat16 [4096, 2048], P(None, 'head')
- value_weight: bfloat16 [4096, 2048], P(None, 'head'), may hold values from -0.09375 to 0.09375
- out_weight: bfloat16 [2048, 4096], P('head'), may hold values from -4 to 4
Outputs:
- mixed: bfloat16 [2048, 4096], P(('groups', 'ctx'), 'head'), parts along dimension 0
There are 2 independent parts, one for each index of `groups`. A program takes and returns all parts, laid end to end along the dimension named above; an argument that names none is the same for every part. Nothing has to cross between parts.
Inputs may be any that keep to these rules, and one draw needn't show every extreme that they name: `variant_sites`: distinct positions; each aligned block of 256 positions holds at most 64 of them, and some block holds exactly that many.
All inputs are finite; a program needn't handle non-finite values.
Results may differ from a plain program's by a relative error of at most 0.019.
Values may be sent and summed in bfloat16 or wider, within the bound.
No kernel may reach another device: no remote copies, remote signals or barrier semaphores. Data moves between devices by JAX's collectives and lax.ppermute only.
A program may use at most 128 MiB of HBM per device.

v0:
```python
import math

import jax
import jax.numpy as jnp
from jax import lax
from jax.sharding import PartitionSpec as P

HEAD_DIM = 128
VAR_DEV = 32


ROPE_BASE = 10000.0
NEG_FILL = -1e30


def rotate(values, positions):
    half_dim = values.shape[-1] // 2
    freq_table = jnp.power(
        ROPE_BASE, -jnp.arange(half_dim, dtype=jnp.float32) * 2.0 / values.shape[-1]
    )
    angle_grid = positions[:, None] * freq_table[None, :]
    cos_part = jnp.cos(angle_grid)[:, None, :]
    sin_part = jnp.sin(angle_grid)[:, None, :]
    lower_half = values[..., :half_dim]
    upper_half = values[..., half_dim:]
    return jnp.concatenate(
        [
            lower_half * cos_part - upper_half * sin_part,
            upper_half * cos_part + lower_half * sin_part,
        ],
        axis=-1,
    )


def project_all(inputs, query_weight, key_weight, value_weight, positions):
    n_rows = inputs.shape[0]
    heads_here = query_weight.shape[1] // HEAD_DIM

    def rotated(weight):
        product = jnp.dot(inputs, weight, preferred_element_type=jnp.float32)
        return (
            rotate(product.reshape(n_rows, heads_here, HEAD_DIM), positions)
            .reshape(n_rows, -1)
            .astype(jnp.bfloat16)
        )

    values_out = jnp.dot(inputs, value_weight, preferred_element_type=jnp.float32).astype(
        jnp.bfloat16
    )
    return (rotated(query_weight), rotated(key_weight), values_out)


def shards(
    hidden,
    strand_bases,
    variant_sites,
    base_shift,
    base_embed,
    query_weight,
    key_weight,
    value_weight,
    out_weight,
):
    row_count = hidden.shape[1]
    shard_total = lax.axis_size("ctx")
    window_rows = row_count * shard_total
    my_block = lax.axis_index("ctx")
    my_start = my_block * row_count
    slot_cap = 2 * VAR_DEV
    head_width = query_weight.shape[1]
    heads_here = head_width // HEAD_DIM
    score_scale = 1.0 / math.sqrt(HEAD_DIM)
    gathered = lax.all_gather(hidden, "head", axis=2, tiled=True)
    row_iota = jnp.arange(row_count, dtype=jnp.int32)
    query_pos = my_start + row_iota
    plus_pos = query_pos.astype(jnp.float32)
    minus_pos = (window_rows - 1 - query_pos).astype(jnp.float32)
    variant_count = variant_sites.shape[0]
    variant_iota = jnp.arange(variant_count, dtype=jnp.int32)
    variant_block = variant_sites // row_count
    same_block = (variant_block[:, None] == variant_block[None, :]) & (
        variant_iota[None, :] < variant_iota[:, None]
    )
    variant_rank = jnp.sum(same_block.astype(jnp.int32), axis=1)
    is_mine = variant_block == my_block
    slot_iota = jnp.arange(slot_cap, dtype=jnp.int32)
    slot_match = (variant_rank[:, None] == slot_iota[None, :]) & is_mine[:, None]
    row_match = ((variant_sites - my_start)[:, None] == row_iota[None, :]) & is_mine[:, None]
    selector_f = lax.dot_general(
        slot_match.astype(jnp.bfloat16),
        row_match.astype(jnp.bfloat16),
        (((0,), (0,)), ((), ())),
        preferred_element_type=jnp.float32,
    )
    selector = selector_f.astype(jnp.bfloat16)
    has_row = jnp.sum(selector_f, axis=0) > 0.5
    old_base = jnp.sum(jnp.where(row_match, strand_bases[None, :], 0), axis=1)
    new_base = jnp.mod(old_base + base_shift, 4)
    slot_old = jnp.sum(jnp.where(slot_match, old_base[:, None], 0), axis=0)
    slot_new = jnp.sum(jnp.where(slot_match, new_base[:, None], 0), axis=0)
    slot_pos = jnp.sum(jnp.where(slot_match, variant_sites[:, None], 0), axis=0)
    slot_live = jnp.sum(slot_match.astype(jnp.int32), axis=0) > 0
    embed_table = base_embed.astype(jnp.float32)
    code_iota = jnp.arange(4, dtype=jnp.int32)

    def embed_diff(new_codes, old_codes):
        onehot = (new_codes[:, None] == code_iota[None, :]).astype(jnp.float32) - (
            old_codes[:, None] == code_iota[None, :]
        ).astype(jnp.float32)
        onehot = jnp.where(slot_live[:, None], onehot, 0.0)
        return jnp.dot(onehot, embed_table, precision=lax.Precision.HIGHEST)

    def picked_rows(full_rows):
        return lax.dot_general(
            selector, full_rows, (((1,), (0,)), ((), ())), preferred_element_type=jnp.float32
        )

    mutant_rows_plus = (picked_rows(gathered[0]) + embed_diff(slot_new, slot_old)).astype(
        jnp.bfloat16
    )
    mutant_rows_minus = (picked_rows(gathered[1]) + embed_diff(3 - slot_new, 3 - slot_old)).astype(
        jnp.bfloat16
    )
    slot_plus_pos = slot_pos.astype(jnp.float32)
    slot_minus_pos = (window_rows - 1 - slot_pos).astype(jnp.float32)

    def spread(slot_rows, full_rows):
        placed = lax.dot_general(
            selector, slot_rows, (((0,), (0,)), ((), ())), preferred_element_type=jnp.float32
        )
        return jnp.where(has_row[:, None], placed.astype(jnp.bfloat16), full_rows)

    ref_plus = project_all(gathered[0], query_weight, key_weight, value_weight, plus_pos)
    ref_minus = project_all(gathered[1], query_weight, key_weight, value_weight, minus_pos)

    def strand_update(running, query_part, key_part, value_part, key_pos, forward):
        run_max, run_sum, run_vec = running
        scores = (
            jnp.einsum("sqhd,kshd->shqk", query_part, key_part, preferred_element_type=jnp.float32)
            * score_scale
        )
        if forward:
            allowed = key_pos[None, :] <= query_pos[:, None]
        else:
            allowed = key_pos[None, :] >= query_pos[:, None]
        masked = jnp.where(allowed, scores, NEG_FILL)
        new_max = jnp.maximum(run_max, jnp.max(masked, axis=-1))
        rescale = jnp.exp(run_max - new_max)
        weights = jnp.where(allowed, jnp.exp(scores - new_max[..., None]), 0.0)
        new_sum = rescale * run_sum + jnp.sum(weights, axis=-1)
        new_vec = rescale[..., None] * run_vec + jnp.einsum(
            "shqk,kshd->shqd",
            weights.astype(jnp.bfloat16),
            value_part,
            preferred_element_type=jnp.float32,
        )
        return (new_max, new_sum, new_vec)

    def make_fold(query_heads):

        def fold_rows(running, cache_rows, row_start):
            row_span = cache_rows.shape[0]
            per_block = math.gcd(row_span // row_count, max(1, 1024 // row_count))
            block_rows = per_block * row_count

            def block_step(block_index, carried):
                first_row = block_index * block_rows
                cache_block = lax.dynamic_slice_in_dim(cache_rows, first_row, block_rows, 0)
                cache_heads = cache_block.reshape(block_rows, 4, 2, heads_here, HEAD_DIM)
                key_pos = first_row + jnp.arange(block_rows, dtype=jnp.int32)
                plus_part = tuple((member[:2] for member in carried))
                minus_part = tuple((member[2:] for member in carried))
                plus_live = first_row <= my_start + row_count - 1
                minus_live = first_row + block_rows - 1 >= my_start
                plus_next = lax.cond(
                    plus_live,
                    lambda: strand_update(
                        plus_part,
                        query_heads[:2],
                        cache_heads[:, :2, 0],
                        cache_heads[:, :2, 1],
                        key_pos,
                        True,
                    ),
                    lambda: plus_part,
                )
                minus_next = lax.cond(
                    minus_live,
                    lambda: strand_update(
                        minus_part,
                        query_heads[2:],
                        cache_heads[:, 2:, 0],
                        cache_heads[:, 2:, 1],
                        key_pos,
                        False,
                    ),
                    lambda: minus_part,
                )
                return tuple(
                    (
                        jnp.concatenate([plus_item, minus_item], axis=0)
                        for plus_item, minus_item in zip(plus_next, minus_next)
                    )
                )

            return lax.fori_loop(0, row_span // block_rows, block_step, running)

        return fold_rows

    initial = (
        jnp.full((4, heads_here, row_count), NEG_FILL, jnp.float32),
        jnp.zeros((4, heads_here, row_count), jnp.float32),
        jnp.zeros((4, heads_here, row_count, HEAD_DIM), jnp.float32),
    )
    slot_plus = project_all(mutant_rows_plus, query_weight, key_weight, value_weight, slot_plus_pos)
    slot_minus = project_all(
        mutant_rows_minus, query_weight, key_weight, value_weight, slot_minus_pos
    )
    all_queries = jnp.stack(
        [
            ref_plus[0],
            spread(slot_plus[0], ref_plus[0]),
            ref_minus[0],
            spread(slot_minus[0], ref_minus[0]),
        ],
        axis=0,
    ).reshape(4, row_count, heads_here, HEAD_DIM)
    fold_rows = make_fold(all_queries)
    cache_ref = jnp.stack(
        [
            jnp.stack([ref_plus[1], ref_plus[2]], axis=1),
            jnp.stack([ref_minus[1], ref_minus[2]], axis=1),
        ],
        axis=1,
    )
    packet = jnp.stack(
        [
            jnp.stack([slot_plus[1], slot_plus[2]], axis=1),
            jnp.stack([slot_minus[1], slot_minus[2]], axis=1),
        ],
        axis=1,
    )
    shard_start = jnp.int32(0)
    ref_piece = lax.all_gather(cache_ref[None], "ctx", axis=0, tiled=True)
    packet_piece = lax.all_gather(packet[None], "ctx", axis=0, tiled=True)
    shard_count = ref_piece.shape[0]
    row_span = shard_count * row_count
    in_range = (variant_block >= shard_start) & (variant_block < shard_start + shard_count)
    slot_index = variant_block * slot_cap + variant_rank
    slot_hits = (
        (slot_index[:, None] == jnp.arange(shard_count * slot_cap, dtype=jnp.int32)[None, :])
        & in_range[:, None]
    ).astype(jnp.bfloat16)
    row_hits = (
        (variant_sites[:, None] == jnp.arange(row_span, dtype=jnp.int32)[None, :])
        & in_range[:, None]
    ).astype(jnp.bfloat16)
    placing = lax.dot_general(
        row_hits, slot_hits, (((0,), (0,)), ((), ())), preferred_element_type=jnp.float32
    )
    has_key = jnp.sum(placing, axis=1) > 0.5
    flat_packet = packet_piece.reshape(shard_count * slot_cap, 4 * head_width)
    moved = (
        jnp.dot(placing.astype(jnp.bfloat16), flat_packet, preferred_element_type=jnp.float32)
        .astype(jnp.bfloat16)
        .reshape(row_span, 2, 2, head_width)
    )
    flat_ref = ref_piece.reshape(row_span, 2, 2, head_width)
    mutant = jnp.where(has_key[:, None, None, None], moved, flat_ref)
    full_piece = jnp.stack([flat_ref[:, 0], mutant[:, 0], flat_ref[:, 1], mutant[:, 1]], axis=1)
    final = fold_rows(initial, full_piece, shard_start * row_count)
    attended = final[2] / final[1][..., None]
    combined = 0.5 * (attended[0] - attended[1] + (attended[2] - attended[3]))
    combined = combined.transpose(1, 0, 2).reshape(row_count, head_width).astype(jnp.bfloat16)
    summed = lax.psum_scatter(
        lax.dot_general(
            out_weight, combined, (((0,), (1,)), ((), ())), preferred_element_type=jnp.float32
        ).astype(jnp.bfloat16),
        "head",
        scatter_dimension=0,
        tiled=True,
    ).astype(jnp.float32)
    return summed.T.astype(jnp.bfloat16)


def solution(mesh):
    return jax.shard_map(
        shards,
        mesh=mesh,
        in_specs=(
            P(None, ("groups", "ctx"), "head"),
            P(("groups", "ctx")),
            P("groups"),
            P("groups"),
            P(),
            P(None, "head"),
            P(None, "head"),
            P(None, "head"),
            P("head", None),
        ),
        out_specs=P(("groups", "ctx"), "head"),
        check_vma=False,
    )
```

profile of v0, /device:TPU:0, one launch (start us, length us, event | category | flops | bytes accessed | tf_op | source)
XLA Modules:
  0.0 278.7 jit_solution(1111753587806421746)
XLA Ops:
  6.5 0.7 all-gather.6.cloned.1.call-update
  7.3 6.5 %copy.67 = bf16[512,4096]{1,0:T(8,128)(2,1)} copy(bf16[512,4096]{0,1:T(8,128)(2,1)} %bitcast.148) | data formatting | bytes 8388608 | tf_op jit(solution)/shard_map/dot_general | solution.py:40
  13.8 6.4 %copy.66 = bf16[512,4096]{1,0:T(8,128)(2,1)} copy(bf16[512,4096]{0,1:T(8,128)(2,1)} %bitcast.149) | data formatting | bytes 8388608 | tf_op jit(solution)/shard_map/dot_general | solution.py:40
  23.3 69.1 %all-gather.6.cloned.1.call-done = bf16[2,256,4096]{2,1,0:T(8,128)(2,1)} async-done(((bf16[2,256,1024]{2,1,0:T(8,128)(2,1)}), bf16[2,256,4096]{2,1,0:T(8,128)(2,1)}) %all-gather.6.cloned.1.call-update) | async-done | bytes 4194320 | tf_op jit(solution)/shard_map/all_gather | solution.py:73
  92.4 2.2 fusion.30
  94.7 3.2 %fusion.126 = f32[64,512]{1,0:T(8,128)S(1)} fusion(bf16[64,4096]{1,0:T(8,128)(2,1)S(1)} %fusion.30, bf16[4096,512]{1,0:T(8,128)(2,1)} %param.19), kind=kOutput, calls=%fused_computation.210 | convolution fusion | flops 268435456 | bytes 4849664 | tf_op jit(solution)/shard_map/dot_general | solution.py:40
  97.9 0.8 fusion.124
  98.7 0.8 fusion.68
  100.7 0.8 fusion.67
  101.5 0.8 copy-done.2
  102.3 0.8 fusion.125
  103.2 0.8 fusion.123
  105.2 0.7 pad_maximum_fusion.7
  106.2 4.3 %fusion.38 = f32[256,4,128]{0,2,1:T(8,128)S(1)} fusion(bf16[4,128,4096]{2,1,0:T(8,128)(2,1)} %bitcast.154, bf16[2,256,4096]{2,1,0:T(8,128)(2,1)} %all-gather.6.cloned.1.call-done), kind=kOutput, calls=%fused_computation.53 | convolution fusion | flops 1073741824 | bytes 6815744 | tf_op jit(solution)/shard_map/dot_general | solution.py:40
  110.4 1.1 copy-done.11
  111.6 1.3 fusion.40
  113.0 0.9 copy-done.12
  113.9 1.3 fusion.31
  115.2 1.3 fusion.33
  117.0 4.2 %fusion.59 = bf16[256,1,512]{2,0,1:T(8,128)(2,1)S(1)} fusion(bf16[4096,512]{1,0:T(8,128)(2,1)} %param.20, bf16[2,256,4096]{2,1,0:T(8,128)(2,1)} %all-gather.6.cloned.1.call-done), kind=kOutput, calls=%fused_computation.72 | convolution fusion | flops 1073872896 | bytes 6553600 | tf_op jit(solution)/shard_map/dot_general | solution.py:47
  121.3 1.0 copy-done.9
  122.3 1.2 fusion.62
  123.6 1.1 pad_maximum_fusion.2
  126.9 1.1 pad_maximum_fusion.1
  128.0 1.5 copy.53
  129.4 3.5 %convolution_convert_fusion.1 = bf16[1024,2048]{1,0:T(8,128)(2,1)} fusion(bf16[256,2048]{0,1:T(8,128)(2,1)S(1)} %bitcast.151, bf16[1024,256]{0,1:T(8,128)(2,1)S(1)} %get-tuple-element.230), kind=kOutput, calls=%fused_computation.44 | convolution fusion | flops 1075838976 | bytes 5767168 | tf_op jit(solution)/shard_map/dot_general | solution.py:264
  132.9 6.4 %copy.54 = bf16[1024,2048]{0,1:T(8,128)(2,1)} copy(bf16[1024,2048]{1,0:T(8,128)(2,1)} %convolution_convert_fusion.1) | data formatting | bytes 8388608 | tf_op jit(solution)/shard_map/convert_element_type | solution.py:265
  139.4 6.2 %copy.55 = bf16[1024,2,2,512]{3,0,2,1:T(8,128)(2,1)} copy(bf16[1024,2,2,512]{0,3,2,1:T(8,128)(2,1)} %bitcast.150) | data formatting | bytes 8388608 | tf_op jit(solution)/shard_map/reshape | solution.py:266
  145.6 12.3 %all-gather.8.cloned.1.call-done = bf16[1024,2,2,512]{3,0,2,1:T(8,128)(2,1)} async-done(((bf16[256,2,2,512]{3,0,2,1:T(8,128)(2,1)}), bf16[1024,2,2,512]{3,0,2,1:T(8,128)(2,1)}) %all-gather.8.cloned.1.call-update) | async-done | bytes 4194320 | tf_op jit(solution)/shard_map/all_gather | solution.py:244
  157.9 3.9 %broadcast_select_fusion = bf16[1024,2,2,512]{3,0,2,1:T(8,128)(2,1)S(1)} fusion(bf16[1024,2,2,512]{3,0,2,1:T(8,128)(2,1)} %copy.55, bf16[1024,2,2,512]{3,0,2,1:T(8,128)(2,1)} %all-gather.8.cloned.1.call-done, pred[1024]{0:T(1024)(128)(4,1)S(1)} %broadcast_compare_fusion.2), kind=kLoop, calls=%fused_computation.43 | loop fusion | flops 2097152 | bytes 12583936 | tf_op jit(solution)/shard_map/jit(_where)/select_n | solution.py:269
  162.1 1.9 copy-done.4
  164.3 3.9 %pad_maximum_fusion = bf16[1024,4,2,512]{3,0,2,1:T(8,128)(2,1)} fusion(bf16[1024,1,2,512]{3,0,2,1:T(8,128)(2,1)S(1)} %get-tuple-element.187, bf16[1024,1,2,512]{3,0,2,1:T(8,128)(2,1)S(1)} %get-tuple-element.185, bf16[1024,1,2,512]{3,0,2,1:T(8,128)(2,1)S(1)} %get-tuple-element.186, bf16[1024,1,2,512]{3,0,2,1:T(8,128)(2,1)S(1)} %get-tuple-element.184), kind=kLoop, calls=%fused_computation.36 | loop fusion | flops 12582912 | bytes 16777216 | tf_op jit(solution)/shard_map/stack | solution.py:270
  168.2 12.7 %reshape.408 = bf16[1024,4,2,4,128]{4,3,0,2,1:T(4,128)(2,1)} reshape(bf16[1024,4,2,512]{3,0,2,1:T(8,128)(2,1)} %pad_maximum_fusion) | data formatting | bytes 16777216 | tf_op jit(solution)/shard_map/while/body/eval_jaxpr/reshape | solution.py:169
  180.8 21.3 %conditional.3 = (f32[2,4,256]{2,1,0:T(4,128)S(1)}, f32[2,4,256,128]{2,3,1,0:T(8,128)S(1)}) conditional(s32[]{:T(128)} %convert_element_type.229, (f32[2,4,256]{2,1,0:T(4,128)S(1)}, f32[2,4,256,128]{3,2,1,0:T(8,128)S(1)}) %tuple.31, (s32[1024]{0:T(1024)S(1)}, s32[256]{0:T(256)S(1)}, bf16[4,256,4,128]{1,3,2,0:T(8,128)(2,1)S(1)}, ...), branch_computations={%region_12.13_spmd, %region_13.16_spmd} | conditional | flops 1097601024 | bytes 52548624 | solution.py:187
  181.0 8.7 %copy.59 = bf16[1024,4,2,4,128]{4,0,3,1,2:T(8,128)(2,1)} copy(bf16[1024,4,2,4,128]{4,3,0,2,1:T(4,128)(2,1)} %get-tuple-element.160) | data formatting | bytes 16777216 | tf_op jit(solution)/shard_map
  189.7 3.7 %select_reduce_fusion.1 = (f32[2,4,256]{2,1,0:T(4,128)S(1)}, f32[2,4,256,1024]{3,2,1,0:T(8,128)S(1)}) fusion(pred[256,1024]{1,0:T(8,128)(4,1)S(1)} %broadcast_compare_fusion.1, bf16[4,256,4,128]{1,3,2,0:T(8,128)(2,1)S(1)} %get-tuple-element.159, bf16[1024,4,2,4,128]{4,0,3,1,2:T(8,128)(2,1)} %copy.59), kind=kOutput, calls=%fused_computation.19 | convolution fusion | flops 543160320 | bytes 11804672 | tf_op jit(solution)/shard_map/while/body/eval_jaxpr/cond/branch_1_fun/sqhd,kshd->shqk/dot_general | solution.py:139
  193.4 2.6 fusion.15
  196.0 4.6 %fusion.23 = f32[2,4,256,128]{3,2,1,0:T(8,128)} fusion(bf16[1024,4,2,4,128]{4,0,3,1,2:T(8,128)(2,1)} %copy.59, f32[2,4,256,1024]{3,2,1,0:T(8,128)S(1)} %get-tuple-element.183, f32[2,4,256]{2,1,0:T(4,128)S(1)} %max.7, pred[256,1024]{1,0:T(8,128)(4,1)S(1)} %broadcast_compare_fusion.1, f32[2,4,256,128]{3,2,1,0:T(8,128)S(1)} %get-tuple-element.113, ...), kind=kOutput, calls=%fused_computation.30 | convolution fusion | flops 545783808 | bytes 12861440 | tf_op jit(solution)/shard_map/while/body/eval_jaxpr/cond/branch_1_fun/shqk,kshd->shqd/dot_general | solution.py:151
  200.6 1.6 copy.65
  202.2 21.1 %conditional.2 = (f32[2,4,256]{2,1,0:T(4,128)S(1)}, f32[2,4,256,128]{2,3,1,0:T(8,128)S(1)}) conditional(s32[]{:T(128)} %convert_element_type.199, (f32[2,4,256]{2,1,0:T(4,128)S(1)}, f32[2,4,256,128]{3,2,1,0:T(8,128)S(1)}) %tuple.31, (s32[1024]{0:T(1024)S(1)}, s32[256]{0:T(256)S(1)}, bf16[4,256,4,128]{1,3,2,0:T(8,128)(2,1)S(1)}, ...), branch_computations={%region_8.9_spmd, %region_9.12_spmd} | conditional | flops 1097601024 | bytes 52548624 | solution.py:175
  202.4 8.7 %copy.57 = bf16[1024,4,2,4,128]{4,0,3,1,2:T(8,128)(2,1)} copy(bf16[1024,4,2,4,128]{4,3,0,2,1:T(4,128)(2,1)} %get-tuple-element.153) | data formatting | bytes 16777216 | tf_op jit(solution)/shard_map
  211.1 3.7 %select_reduce_fusion = (f32[2,4,256]{2,1,0:T(4,128)S(1)}, f32[2,4,256,1024]{3,2,1,0:T(8,128)S(1)}) fusion(pred[256,1024]{1,0:T(8,128)(4,1)S(1)} %broadcast_compare_fusion, bf16[4,256,4,128]{1,3,2,0:T(8,128)(2,1)S(1)} %get-tuple-element.152, bf16[1024,4,2,4,128]{4,0,3,1,2:T(8,128)(2,1)} %copy.57), kind=kOutput, calls=%fused_computation.1 | convolution fusion | flops 543160320 | bytes 11804672 | tf_op jit(solution)/shard_map/while/body/eval_jaxpr/cond/branch_1_fun/sqhd,kshd->shqk/dot_general | solution.py:139
  214.8 2.3 fusion.1
  217.1 4.6 %fusion.9 = f32[2,4,256,128]{3,2,1,0:T(8,128)} fusion(bf16[1024,4,2,4,128]{4,0,3,1,2:T(8,128)(2,1)} %copy.57, f32[2,4,256,1024]{3,2,1,0:T(8,128)S(1)} %get-tuple-element.181, f32[2,4,256]{2,1,0:T(4,128)S(1)} %max.6, pred[256,1024]{1,0:T(8,128)(4,1)S(1)} %broadcast_compare_fusion, f32[2,4,256,128]{3,2,1,0:T(8,128)S(1)} %get-tuple-element.106, ...), kind=kOutput, calls=%fused_computation.12 | convolution fusion | flops 545783808 | bytes 12861440 | tf_op jit(solution)/shard_map/while/body/eval_jaxpr/cond/branch_1_fun/shqk,kshd->shqd/dot_general | solution.py:151
  221.7 1.6 copy.63
  223.7 1.8 copy-done.10
  225.5 2.6 fusion.28
  228.1 44.0 %reduce-scatter.2.cloned.1.call-done = bf16[1024,256]{0,1:T(8,128)(2,1)} async-done(((bf16[4096,256]{0,1:T(8,128)(2,1)}), bf16[1024,256]{0,1:T(8,128)(2,1)}) %reduce-scatter.2.cloned.1.call-update) | async-done | bytes 524304 | tf_op jit(solution)/shard_map/reduce_scatter | solution.py:275
  (103 shorter events, 9.6 us)
Async XLA Ops:
  6.5 15.5 %copy-start = (bf16[4,4096]{1,0:T(4,128)(2,1)S(1)}, bf16[4,4096]{1,0:T(4,128)(2,1)}, u32[]{:S(2)}) copy-start(bf16[4,4096]{1,0:T(4,128)(2,1)} %param.17) | copy-start | bytes 98308
  6.5 85.9 %all-gather.6.cloned.1.call-start = ((), (), s32[]{:S(2)}) async-start(), calls=%async_computation.1 | async-start | bytes 5242880 | tf_op jit(solution)/shard_map/all_gather | solution.py:73
  7.3 120.7 %all-gather.10.cloned.1.call-start = ((), (), s32[]{:S(2)}) async-start(), calls=%async_computation.4 | async-start | bytes 1310720 | tf_op jit(solution)/shard_map/all_gather | solution.py:245
  13.8 6.5 %copy-start.15 = (s32[128]{0:T(128)S(1)}, s32[128]{0:T(128)}, u32[]{:S(2)}) copy-start(s32[128]{0:T(128)} %param.15) | copy-start | bytes 1540
  13.8 6.7 %copy-start.14 = (s32[256]{0:T(256)S(1)}, s32[256]{0:T(256)}, u32[]{:S(2)}) copy-start(s32[256]{0:T(256)} %param.14) | copy-start | bytes 3076
  13.8 6.9 %copy-start.16 = (s32[128]{0:T(128)S(1)}, s32[128]{0:T(128)}, u32[]{:S(2)}) copy-start(s32[128]{0:T(128)} %param.16) | copy-start | bytes 1540
  92.4 5.4 %copy-start.3 = (bf16[4096,512]{1,0:T(8,128)(2,1)S(1)}, bf16[4096,512]{1,0:T(8,128)(2,1)}, u32[]{:S(2)}) copy-start(bf16[4096,512]{1,0:T(8,128)(2,1)} %param.18) | copy-start | bytes 12582916
  94.7 4.1 %copy-start.5 = (bf16[4096,512]{1,0:T(8,128)(2,1)S(1)}, bf16[4096,512]{1,0:T(8,128)(2,1)}, u32[]{:S(2)}) copy-start(bf16[4096,512]{1,0:T(8,128)(2,1)} %param.20) | copy-start | bytes 12582916
  97.9 2.3 copy-start.7
  100.1 2.2 copy-start.2
  105.9 52.0 %all-gather.8.cloned.1.call-start = ((), (), s32[]{:S(2)}) async-start(), calls=%async_computation.3 | async-start | bytes 5242880 | tf_op jit(solution)/shard_map/all_gather | solution.py:244
  106.2 4.3 %copy-start.8 = (bf16[2,256,4096]{2,1,0:T(8,128)(2,1)S(1)}, bf16[2,256,4096]{2,1,0:T(8,128)(2,1)}, u32[]{:S(2)}) copy-start(bf16[2,256,4096]{2,1,0:T(8,128)(2,1)} %all-gather.6.cloned.1.call-done) | copy-start | bytes 12582916
  106.2 5.4 %copy-start.11 = (bf16[512,4096]{1,0:T(8,128)(2,1)S(1)}, bf16[512,4096]{1,0:T(8,128)(2,1)}, u32[]{:S(2)}) copy-start(bf16[512,4096]{1,0:T(8,128)(2,1)} %copy.66) | copy-start | bytes 12582916
  111.6 2.3 copy-start.12
  116.9 4.3 %copy-start.6 = (bf16[4096,512]{1,0:T(8,128)(2,1)S(1)}, bf16[4096,512]{1,0:T(8,128)(2,1)}, u32[]{:S(2)}) copy-start(bf16[4096,512]{1,0:T(8,128)(2,1)} %param.20) | copy-start | bytes 12582916
  117.0 5.4 %copy-start.9 = (bf16[2,256,4096]{2,1,0:T(8,128)(2,1)S(1)}, bf16[2,256,4096]{2,1,0:T(8,128)(2,1)}, u32[]{:S(2)}) copy-start(bf16[2,256,4096]{2,1,0:T(8,128)(2,1)} %all-gather.6.cloned.1.call-done) | copy-start | bytes 12582916
  124.8 147.4 %reduce-scatter.2.cloned.1.call-start = ((), (), s32[]{:S(2)}) async-start(), calls=%async_computation.2 | async-start | bytes 2621440 | tf_op jit(solution)/shard_map/reduce_scatter | solution.py:275
  161.8 2.2 copy-start.4
  168.2 12.7 %copy-start.13 = (bf16[4,256,4,128]{1,3,2,0:T(8,128)(2,1)S(1)}, bf16[4,256,4,128]{1,3,2,0:T(8,128)(2,1)}, u32[]{:S(2)}) copy-start(bf16[4,256,4,128]{1,3,2,0:T(8,128)(2,1)} %pad_maximum_fusion.1) | copy-start | bytes 3145732
  223.3 2.2 copy-start.10
  223.7 48.5 %copy-start.1 = (bf16[4,4096]{1,0:T(4,128)(2,1)S(1)}, bf16[4,4096]{1,0:T(4,128)(2,1)}, u32[]{:S(2)}) copy-start(bf16[4,4096]{1,0:T(4,128)(2,1)} %param.17) | copy-start | bytes 98308
Sparse Core Ops, SparseCore 0:
  8.9 83.4 all-gather.5
  106.0 15.2 all-gather.9
  124.9 32.9 all-gather.7
  228.2 43.8 reduce-scatter.1
where the time goes:
time: 280 us; the launch traced here: 279 us
  waiting for transfers between devices  126 us (45%)
  local copies, waits for them, and re-layouts  70.1 us (25%)
  matrix products  48.7 us (17%)
  other arithmetic  19.3 us (7%)
  between operations  13.8 us (5%)
    all_gather x1, waiting for transfers between devices, shards(): gathered = lax.all_gather(hidden, 'head', axis=2, tiled=True)  69.1 us
    reduce_scatter x1, waiting for transfers between devices, shards(): lax.psum_scatter(lax.dot_general(out_weight, combined, (((0,), (1,)), (()...  44 us
    another operation x2, local copies, waits for them, and re-layouts  17.4 us
    dot_general x8, matrix products, rotated(): product = jnp.dot(inputs, weight, preferred_element_type=jnp.float32)  13.7 us
    dot_general x2, local copies, waits for them, and re-layouts, rotated(): product = jnp.dot(inputs, weight, preferred_element_type=jnp.float32)  12.9 us
    reshape x1, local copies, waits for them, and re-layouts, block_step(): cache_heads = cache_block.reshape(block_rows, 4, 2, heads_here, HEAD_DIM)  12.7 us
    all_gather x1, waiting for transfers between devices, shards(): ref_piece = lax.all_gather(cache_ref[None], 'ctx', axis=0, tiled=True)  12.3 us
    dot_general x2, matrix products, strand_update(): jnp.einsum('shqk,kshd->shqd', weights.astype(jnp.bfloat16), value_part, p...  9.16 us
  transfers between devices with their start and end apart: 4, of which 3 were waited for; matrix products, arithmetic and copies ran while one was open for 19% of the time, Pallas kernels for 0%

commit v1 on v0

v1 whole, which is shorter than its diff:
```python
import functools
import math

import jax
import jax.numpy as jnp
from jax import lax
from jax.experimental import pallas as pl
from jax.experimental.pallas import tpu as pltpu
from jax.sharding import PartitionSpec as P

HEAD_DIM = 128
BASES = 4
BASE_PAD = 16
ROPE_BASE = 10000.0
NEG_FILL = -1e30
VMEM_LIMIT = 40 * 1024 * 1024
F32 = jnp.float32
BF16 = jnp.bfloat16


def params():
    return pltpu.CompilerParams(vmem_limit_bytes=VMEM_LIMIT)


def rope_tables(positions):
    half = HEAD_DIM // 2
    freq = jnp.power(ROPE_BASE, -jnp.arange(half, dtype=F32) * 2.0 / HEAD_DIM)
    angle = positions[:, None] * freq[None, :]
    cos, sin = jnp.cos(angle), jnp.sin(angle)
    return jnp.concatenate([cos, cos], axis=1), jnp.concatenate([-sin, sin], axis=1)


def turned(value, cos, sin):
    return value * cos + pltpu.roll(value, HEAD_DIM // 2, axis=1) * sin


def mixed_rows(codes, table):
    total = codes[:, 0:1] * table[0:1, :]
    for base in range(1, BASES):
        total = total + codes[:, base : base + 1] * table[base : base + 1, :]
    return total


def embed_kernel(embed_ref, wq_ref, wk_ref, wv_ref, out_ref):
    width = wq_ref.shape[1]

    @pl.when(pl.program_id(0) == 0)
    def _():
        out_ref[...] = jnp.zeros_like(out_ref)

    for index, weight in enumerate((wq_ref, wk_ref, wv_ref)):
        out_ref[:, index * width : (index + 1) * width] += jnp.dot(
            embed_ref[...], weight[...], preferred_element_type=F32
        )


def embed_project(embed, wq, wk, wv):
    depth, width = wq.shape
    tile = min(512, depth)
    weight_spec = pl.BlockSpec((tile, width), lambda i: (i, 0))
    return pl.pallas_call(
        embed_kernel,
        grid=(depth // tile,),
        in_specs=[pl.BlockSpec((BASE_PAD, tile), lambda i: (0, i))] + [weight_spec] * 3,
        out_specs=pl.BlockSpec((BASE_PAD, 3 * width), lambda i: (0, 0)),
        out_shape=jax.ShapeDtypeStruct((BASE_PAD, 3 * width), F32),
        compiler_params=params(),
        cost_estimate=pl.CostEstimate(
            flops=2 * BASE_PAD * depth * 3 * width,
            bytes_accessed=3 * depth * width * 2,
            transcendentals=0,
        ),
        name="embed_project",
    )(embed, wq, wk, wv)


def project_kernel(
    x_ref, wq_ref, wk_ref, wv_ref, ew_ref, codes_ref, cos_ref, sin_ref, q_ref, qm_ref, kv_ref, acc
):
    width = wq_ref.shape[1]
    step = pl.program_id(0)

    @pl.when(step == 0)
    def _():
        acc[...] = jnp.zeros_like(acc)

    rows = x_ref[...]
    for index, weight in enumerate((wq_ref, wk_ref, wv_ref)):
        acc[:, index * width : (index + 1) * width] += jnp.dot(
            rows, weight[...], preferred_element_type=F32
        )

    @pl.when(step == pl.num_programs(0) - 1)
    def _():
        cos, sin, codes = cos_ref[...], sin_ref[...], codes_ref[...]
        for start in range(0, width, HEAD_DIM):
            cols = slice(start, start + HEAD_DIM)
            query = acc[:, cols]
            change = mixed_rows(codes, ew_ref[0:BASES, cols])
            q_ref[:, cols] = turned(query, cos, sin).astype(BF16)
            qm_ref[:, cols] = turned(query + change, cos, sin).astype(BF16)
            kv_ref[:, cols] = turned(
                acc[:, width + start : width + start + HEAD_DIM], cos, sin
            ).astype(BF16)
        kv_ref[:, width:] = acc[:, 2 * width :].astype(BF16)


def project(x, wq, wk, wv, ew, codes, cos, sin, slabs):
    rows, depth = x.shape
    width = wq.shape[1]
    tile = depth // slabs
    weight_spec = pl.BlockSpec((tile, width), lambda i: (i, 0))

    def whole(shape):
        return pl.BlockSpec(shape, lambda i: (0, 0))

    return pl.pallas_call(
        project_kernel,
        grid=(slabs,),
        in_specs=[pl.BlockSpec((rows, tile), lambda i: (0, i))]
        + [weight_spec] * 3
        + [whole(item.shape) for item in (ew, codes, cos, sin)],
        out_specs=[whole((rows, width)), whole((rows, width)), whole((rows, 2 * width))],
        out_shape=[
            jax.ShapeDtypeStruct((rows, width), BF16),
            jax.ShapeDtypeStruct((rows, width), BF16),
            jax.ShapeDtypeStruct((rows, 2 * width), BF16),
        ],
        scratch_shapes=[pltpu.VMEM((rows, 3 * width), F32)],
        compiler_params=params(),
        cost_estimate=pl.CostEstimate(
            flops=2 * rows * depth * 3 * width,
            bytes_accessed=3 * depth * width * 2 + rows * depth * 2,
            transcendentals=0,
        ),
        name="project",
    )(x, wq, wk, wv, ew, codes, cos, sin)


def attend_kernel(forward, block_count, has_before, *refs):
    (ids_ref, q_ref, qm_ref, ew_ref), refs = refs[:4], refs[4:]
    kv_refs, refs = refs[:block_count], refs[block_count:]
    code_refs, refs = refs[:block_count], refs[block_count:]
    cos_ref, sin_ref = refs[:2]
    refs = refs[2:]
    before_ref = None
    if has_before:
        before_ref, refs = refs[0], refs[1:]
    out_ref, top, total, acc = refs
    rows, width = q_ref.shape
    heads = width // HEAD_DIM
    scale = math.log2(math.e) / math.sqrt(HEAD_DIM)
    my_id = ids_ref[0]

    def block(index):
        kv_ref, code_ref = kv_refs[index], code_refs[index]
        first = pl.multiple_of(ids_ref[index] * rows, rows)
        cos = cos_ref[pl.ds(first, rows), :]
        sin = sin_ref[pl.ds(first, rows), :]
        codes = code_ref[...]
        if index == 0:
            key_at = lax.broadcasted_iota(jnp.int32, (rows, rows), 0)
            query_at = lax.broadcasted_iota(jnp.int32, (rows, rows), 1)
            seen = key_at <= query_at if forward else key_at >= query_at
        for head in range(heads):
            cols = slice(head * HEAD_DIM, (head + 1) * HEAD_DIM)
            key_cols = slice(width + cols.start, width + cols.stop)
            value_cols = slice(2 * width + cols.start, 2 * width + cols.stop)
            key, value = kv_ref[:, cols], kv_ref[:, key_cols]
            key_change = turned(mixed_rows(codes, ew_ref[0:BASES, key_cols]), cos, sin)
            value_change = mixed_rows(codes, ew_ref[0:BASES, value_cols])
            mutant_key = (key.astype(F32) + key_change).astype(BF16)
            mutant_value = (value.astype(F32) + value_change).astype(BF16)
            for kind, (query, keys, values) in enumerate(
                ((q_ref[:, cols], key, value), (qm_ref[:, cols], mutant_key, mutant_value))
            ):
                unit = 2 * head + kind
                area = slice(unit * HEAD_DIM, (unit + 1) * HEAD_DIM)
                scores = lax.dot_general(
                    keys, query, (((1,), (1,)), ((), ())), preferred_element_type=F32
                )
                if index == 0:
                    scores = jnp.where(seen, scores, NEG_FILL)
                peak = jnp.max(scores, axis=0, keepdims=True)
                if index:
                    old_peak = top[unit : unit + 1, :]
                    peak = jnp.maximum(old_peak, peak)
                    fade = jnp.exp2((old_peak - peak) * scale)
                weights = jnp.exp2((scores - peak) * scale)
                if index == 0:
                    weights = jnp.where(seen, weights, 0.0)
                weight_sum = jnp.sum(weights, axis=0, keepdims=True)
                product = lax.dot_general(
                    values,
                    weights.astype(BF16),
                    (((0,), (0,)), ((), ())),
                    preferred_element_type=F32,
                )
                if index:
                    weight_sum = total[unit : unit + 1, :] * fade + weight_sum
                    product = acc[area, :] * fade + product
                top[unit : unit + 1, :] = peak
                total[unit : unit + 1, :] = weight_sum
                acc[area, :] = product

    for index in range(block_count):
        if index == 0:
            block(0)
        else:
            other = ids_ref[index]
            pl.when(other < my_id if forward else other > my_id)(functools.partial(block, index))

    for head in range(heads):
        cols = slice(head * HEAD_DIM, (head + 1) * HEAD_DIM)
        parts = []
        for unit in (2 * head, 2 * head + 1):
            area = slice(unit * HEAD_DIM, (unit + 1) * HEAD_DIM)
            parts.append(acc[area, :] / total[unit : unit + 1, :])
        difference = (parts[0] - parts[1]).T
        if has_before:
            out_ref[:, cols] = (0.5 * (before_ref[:, cols] + difference)).astype(BF16)
        else:
            out_ref[:, cols] = difference


def attend(forward, ids, q, qm, ew, kv_blocks, code_blocks, cos, sin, before=None):
    rows, width = q.shape
    units = 2 * (width // HEAD_DIM)
    vmem = pl.BlockSpec(memory_space=pltpu.VMEM)
    operands = [q, qm, ew, *kv_blocks, *code_blocks, cos, sin]
    if before is not None:
        operands.append(before)
    count = len(kv_blocks)
    return pl.pallas_call(
        functools.partial(attend_kernel, forward, count, before is not None),
        in_specs=[pl.BlockSpec(memory_space=pltpu.SMEM)] + [vmem] * len(operands),
        out_specs=vmem,
        out_shape=jax.ShapeDtypeStruct((rows, width), F32 if before is None else BF16),
        scratch_shapes=[
            pltpu.VMEM((max(units, 8), rows), F32),
            pltpu.VMEM((max(units, 8), rows), F32),
            pltpu.VMEM((units * HEAD_DIM, rows), F32),
        ],
        compiler_params=params(),
        cost_estimate=pl.CostEstimate(
            flops=8 * rows * rows * count * width,
            bytes_accessed=count * rows * width * 4,
            transcendentals=2 * rows * rows * count * (width // HEAD_DIM),
        ),
        name="attend_forward" if forward else "attend_reverse",
    )(ids, *operands)


def out_kernel(rows_ref, weight_ref, out_ref):
    out_ref[0] = jnp.dot(
        rows_ref[...], weight_ref[...], preferred_element_type=F32
    ).astype(BF16)


def out_project(combined, wo, slabs):
    rows, width = combined.shape
    tile = wo.shape[1] // slabs
    return pl.pallas_call(
        out_kernel,
        grid=(slabs,),
        in_specs=[
            pl.BlockSpec((rows, width), lambda i: (0, 0)),
            pl.BlockSpec((width, tile), lambda i: (0, i)),
        ],
        out_specs=pl.BlockSpec((1, rows, tile), lambda i: (i, 0, 0)),
        out_shape=jax.ShapeDtypeStruct((slabs, rows, tile), BF16),
        compiler_params=params(),
        cost_estimate=pl.CostEstimate(
            flops=2 * rows * width * wo.shape[1],
            bytes_accessed=width * wo.shape[1] * 2 + rows * wo.shape[1] * 2,
            transcendentals=0,
        ),
        name="out_project",
    )(combined, wo)


def shards(
    hidden,
    strand_bases,
    variant_sites,
    base_shift,
    base_embed,
    query_weight,
    key_weight,
    value_weight,
    out_weight,
):
    rows = hidden.shape[1]
    ctx = lax.axis_size("ctx")
    slabs = lax.axis_size("head")
    me = lax.axis_index("ctx")
    window = rows * ctx
    cores = 2 if ctx % 2 == 0 else 1

    def ctx_gather(block):
        held = [block]
        for shift in range(1, ctx // cores):
            pairs = [(i, (i + cores * shift) % ctx) for i in range(ctx)]
            held.append(lax.ppermute(block, "ctx", pairs))
        if cores == 2:
            pairs = [(i, i ^ 1) for i in range(ctx)]
            held = held + [lax.ppermute(item, "ctx", pairs) for item in held]
        return held

    near = [(me - cores * shift) % ctx for shift in range(ctx // cores)]
    if cores == 2:
        near = near + [item ^ 1 for item in near]
    ids = jnp.stack(near).astype(jnp.int32)

    gathered = [
        lax.all_gather(hidden[strand], "head", axis=1, tiled=True) for strand in range(2)
    ]

    base_blocks = ctx_gather(strand_bases)
    embed = jnp.zeros((BASE_PAD, base_embed.shape[1]), BF16).at[:BASES].set(base_embed)
    ew_plus = embed_project(embed, query_weight, key_weight, value_weight)
    ew_minus = ew_plus.at[:BASES].set(ew_plus[:BASES][::-1])

    row_iota = jnp.arange(rows, dtype=jnp.int32)
    code_iota = jnp.arange(BASES, dtype=jnp.int32)
    code_blocks = []
    for bases, owner in zip(base_blocks, near):
        match = (owner * rows + row_iota)[:, None] == variant_sites[None, :]
        changed = jnp.any(match, axis=1)
        shift = jnp.sum(jnp.where(match, base_shift[None, :], 0), axis=1)
        fresh = jnp.mod(bases + shift, BASES)
        codes = (fresh[:, None] == code_iota[None, :]).astype(F32) - (
            bases[:, None] == code_iota[None, :]
        ).astype(F32)
        code_blocks.append(jnp.where(changed[:, None], codes, 0.0))

    positions = jnp.arange(window, dtype=jnp.int32)
    tables = [
        rope_tables(positions.astype(F32)),
        rope_tables((window - 1 - positions).astype(F32)),
    ]
    before = None
    for strand in range(2):
        cos, sin = tables[strand]
        ew = ew_plus if strand == 0 else ew_minus
        own_cos = lax.dynamic_slice_in_dim(cos, me * rows, rows, 0)
        own_sin = lax.dynamic_slice_in_dim(sin, me * rows, rows, 0)
        q, qm, kv = project(
            gathered[strand],
            query_weight,
            key_weight,
            value_weight,
            ew,
            code_blocks[0],
            own_cos,
            own_sin,
            slabs,
        )
        kv_blocks = ctx_gather(kv)
        before = attend(
            strand == 0, ids, q, qm, ew, kv_blocks, code_blocks, cos, sin, before
        )
    partial = out_project(before, out_weight, slabs)
    return lax.psum_scatter(partial, "head", scatter_dimension=0, tiled=True)[0]


def solution(mesh):
    return jax.shard_map(
        shards,
        mesh=mesh,
        in_specs=(
            P(None, ("groups", "ctx"), "head"),
            P(("groups", "ctx")),
            P("groups"),
            P("groups"),
            P(),
            P(None, "head"),
            P(None, "head"),
            P(None, "head"),
            P("head", None),
        ),
        out_specs=P(("groups", "ctx"), "head"),
        check_vma=False,
    )
```

time: 280 us -> 195 us (0.70)
  local copies, waits for them, and re-layouts: 70.1 us -> 17.8 us
  matrix products: 48.7 us -> 0 us
  Pallas kernels: 0 us -> 33 us
  other arithmetic: 19.3 us -> 6.3 us
  waiting for transfers between devices: 126 us -> 117 us
  starting transfers between devices: 0.53 us -> 7.05 us
    dot_general x26 -> x0, matrix products: 48.7 us -> none  [the longest x8 13.7 us: rotated(): product = jnp.dot(inputs, weight, preferred_element_type=jnp.float32)]
    all_gather x3 -> x2, waiting for transfers between devices: 81.4 us -> 48.2 us  [shards(): lax.all_gather(hidden[strand], 'head', axis=1, tiled=True)]
    pallas_call x0 -> x6, Pallas kernels: none -> 33 us  [the longest x2 14.4 us: attend(): pl.pallas_call(functools.partial(attend_kernel, forward, count, before is...]
    ppermute x0 -> x9, waiting for transfers between devices: none -> 26.8 us  [the longest x3 23.8 us: ctx_gather(): held.append(lax.ppermute(block, 'ctx', pairs))]
    reshape x6 -> x0, local copies, waits for them, and re-layouts: 19.1 us -> none  [the longest x1 12.7 us: block_step(): cache_heads = cache_block.reshape(block_rows, 4, 2, heads_here, HEAD_DIM)]
    another operation x2 -> x0, local copies, waits for them, and re-layouts: 17.4 us -> none
    dot_general x2 -> x0, local copies, waits for them, and re-layouts: 12.9 us -> none  [rotated(): product = jnp.dot(inputs, weight, preferred_element_type=jnp.float32)]
    another operation x12 -> x1, other arithmetic: 7.68 us -> 0.08 us  [shards(): ids = jnp.stack(near).astype(jnp.int32)]
  transfers between devices with their start and end apart: 4 -> 12, of which waited for: 3 -> 7; matrix products, arithmetic and copies ran while one was open for 19% -> 4% of each run, Pallas kernels for 0% -> 6%
where the time goes in v1:
time: 195 us
  waiting for transfers between devices  117 us (60%)
  Pallas kernels  33 us (17%)
  local copies, waits for them, and re-layouts  17.8 us (9%)
  between operations  13.4 us (7%)
  starting transfers between devices  7.05 us (4%)
  other arithmetic  6.3 us (3%)
    all_gather x2, waiting for transfers between devices, shards(): lax.all_gather(hidden[strand], 'head', axis=1, tiled=True)  48.2 us
    reduce_scatter x1, waiting for transfers between devices, shards(): return lax.psum_scatter(partial, 'head', scatter_dimension=0, tiled=True)[0]  42 us
    ppermute x3, waiting for transfers between devices, ctx_gather(): held.append(lax.ppermute(block, 'ctx', pairs))  23.8 us
    unnamed x30, local copies, waits for them, and re-layouts  14.4 us
    pallas_call x2, Pallas kernels, attend(): pl.pallas_call(functools.partial(attend_kernel, forward, count, before is...  14.4 us
    pallas_call x2, Pallas kernels, project(): pl.pallas_call(project_kernel, grid=(slabs,), in_specs=[pl.BlockSpec((row...  12.9 us
    ppermute x3, starting transfers between devices, ctx_gather(): held.append(lax.ppermute(block, 'ctx', pairs))  6.31 us
  transfers between devices with their start and end apart: 12, of which 7 were waited for; matrix products, arithmetic and copies ran while one was open for 4% of the time, Pallas kernels for 6%

profile of v1, /device:TPU:0, one launch (start us, length us, event | category | flops | bytes accessed | tf_op | source)
XLA Modules:
  0.0 194.7 jit_solution(15087030482883139943)
XLA Ops:
  6.5 2.2 %fusion.14 = (bf16[1,256,1024]{2,1,0:T(8,128)(2,1)}, bf16[1,256,1024]{2,1,0:T(8,128)(2,1)}) fusion(bf16[2,256,1024]{2,1,0:T(8,128)(2,1)} %param.13), kind=kLoop, calls=%fused_computation.71 | loop fusion | bytes 2097152 | tf_op jit(solution)/shard_map/slice | solution.py:316
  8.8 0.0 all-gather.7.cloned.1.call-update
  8.8 0.0 all-gather.5.cloned.1.call-start
  8.9 3.0 %collective-permute-start.3 = (s32[256]{0:T(256)}, s32[256]{0:T(256)S(1)}, u32[]{:S(2)}, u32[]{:S(2)}) collective-permute-start(s32[256]{0:T(256)} %param.14), channel_id=1, source_target_pairs={{0,8},{4,12},{8,0},{12,4},{1,9},{5,13},{9,1},{13,5},{2,10},{6,14},... | collective-permute-start | bytes 3080 | tf_op jit(solution)/shard_map/ppermute | solution.py:304
  11.9 0.0 all-gather.5.cloned.1.call-update
  11.9 0.0 reduce-scatter.2.cloned.1.call-start
  12.1 0.8 scatter.6.embed_ref
  12.9 0.0 copy-start
  12.9 0.0 copy-start.3
  12.9 3.7 %multiply_sine_fusion = (f32[1024,64]{1,0:T(8,128)S(1)}, f32[1024,64]{1,0:T(8,128)S(1)}, f32[1024,64]{1,0:T(8,128)S(1)}, f32[1024,64]{1,0:T(8,128)S(1)}, f32[1024,64]{1,0:T(8,128)S(1)}, /*index=5*/f32[1024,64]{1,0:T(8,128)S(1)}) fusion(f32[1024]{0:T(1024)S(1)} %iota_convert_fusion, f32[64]{0:T(128)S(1)} %multiply_power_fusion, f32[1024]{0:T(1024)S(1)} %subtract_convert_fusion), kind=kLoop, calls=%fused_computation | loop fusion | flops 262144 | bytes 1581312 | tf_op jit(solution)/shard_map/sin | solution.py:29
  16.6 0.1 pad_add_fusion.refs_0_
  16.7 0.1 fusion.6
  16.8 0.1 fusion.8
  17.0 0.4 compare_reduce_fusion
  17.4 0.4 fusion.5
  17.8 0.3 pad_maximum_fusion.2
  18.2 0.2 subtract_select_fusion.3.codes_ref.refs_8_
  18.4 0.0 copy-start.6
  18.4 2.4 %copy-done.6 = bf16[4096,512]{1,0:T(8,128)(2,1)S(1)} copy-done((bf16[4096,512]{1,0:T(8,128)(2,1)S(1)}, bf16[4096,512]{1,0:T(8,128)(2,1)}, u32[]{:S(2)}) %copy-start.6) | copy-done | bytes 4194328
  20.8 2.6 %embed_project.1.ew_ref.refs_3_ = f32[16,1536]{1,0:T(8,128)S(1)} custom-call(bf16[16,4096]{1,0:T(8,128)(2,1)S(1)} %scatter.6.embed_ref, bf16[4096,512]{1,0:T(8,128)(2,1)S(1)} %copy-done, bf16[4096,512]{1,0:T(8,128)(2,1)S(1)} %copy-done.3, bf16[4096,512]{1,0:T(8,128)(2,1)S(1)} %copy-done.6), custom_call_target="tpu_custom_call" | custom-call | flops 201326592 | bytes 12582912 | tf_op jit(solution)/shard_map/embed_project/pallas_call | solution.py:61
  23.4 0.3 rev.3
  23.7 0.6 collective-permute-start.5
  24.3 33.3 %all-gather.7.cloned.1.call-done = bf16[1,256,4096]{2,1,0:T(8,128)(2,1)} async-done(((bf16[1,256,1024]{2,1,0:T(8,128)(2,1)}), bf16[1,256,4096]{2,1,0:T(8,128)(2,1)}) %all-gather.7.cloned.1.call-update) | async-done | bytes 2097168 | tf_op jit(solution)/shard_map/all_gather | solution.py:316
  57.6 2.2 %copy-done.1 = bf16[4096,512]{1,0:T(8,128)(2,1)S(1)} copy-done((bf16[4096,512]{1,0:T(8,128)(2,1)S(1)}, bf16[4096,512]{1,0:T(8,128)(2,1)}, u32[]{:S(2)}) %copy-start.1) | copy-done | bytes 4194328
  59.8 2.2 %copy-done.4 = bf16[4096,512]{1,0:T(8,128)(2,1)S(1)} copy-done((bf16[4096,512]{1,0:T(8,128)(2,1)S(1)}, bf16[4096,512]{1,0:T(8,128)(2,1)}, u32[]{:S(2)}) %copy-start.4) | copy-done | bytes 4194328
  62.0 1.6 copy-done.9
  63.5 6.5 %project.3 = (bf16[256,512]{1,0:T(8,128)(2,1)S(1)}, bf16[256,512]{1,0:T(8,128)(2,1)S(1)}, bf16[256,1024]{1,0:T(8,128)(2,1)S(1)}) custom-call(bf16[256,4096]{1,0:T(8,128)(2,1)S(1)} %bitcast.8, bf16[4096,512]{1,0:T(8,128)(2,1)S(1)} %copy-done.1, bf16[4096,512]{1,0:T(8,128)(2,1)S(1)} %copy-done.4, bf16[4096,512]{1,0:T(8,128)(2,1)} %wv_ref.5, ...), custom_call_target="tpu_custom_call" | custom-call | flops 3221225472 | bytes 14680064 | tf_op jit(solution)/shard_map/project/pallas_call | solution.py:117
  70.0 1.6 collective-permute-start.6
  71.6 0.2 subtract_select_fusion.1.refs_10_
  71.8 0.1 collective-permute-start.7
  71.9 11.8 %collective-permute-done.6.refs_5_ = bf16[256,1024]{1,0:T(8,128)(2,1)S(1)} collective-permute-done((bf16[256,1024]{1,0:T(8,128)(2,1)S(1)}, bf16[256,1024]{1,0:T(8,128)(2,1)S(1)}, u32[]{:S(2)}, u32[]{:S(2)}) %collective-permute-start.6) | collective-permute-done | bytes 524320 | tf_op jit(solution)/shard_map/ppermute | solution.py:304
  83.7 0.2 subtract_select_fusion.2.refs_9_
  83.9 0.2 subtract_select_fusion.refs_11_
  84.0 1.5 collective-permute-done.8.refs_7_
  85.6 3.3 %attend_forward.1.refs_14_ = f32[256,512]{1,0:T(8,128)S(1)} custom-call(s32[4]{0:T(128)S(1)} %pad_add_fusion.refs_0_, bf16[256,512]{1,0:T(8,128)(2,1)S(1)} %get-tuple-element.38.refs_1_, bf16[256,512]{1,0:T(8,128)(2,1)S(1)} %get-tuple-element.39.refs_2_, f32[16,1536]{1,0:T(8,128)S(1)} %embed_project.1.ew_ref.refs_3_, ...), custom_call_target="tpu_custom_call" | custom-call | flops 1073741824 | bytes 2097152 | tf_op jit(solution)/shard_map/attend_forward/pallas_call | solution.py:234
  88.9 14.9 %all-gather.5.cloned.1.call-done = bf16[1,256,4096]{2,1,0:T(8,128)(2,1)} async-done(((bf16[1,256,1024]{2,1,0:T(8,128)(2,1)}), bf16[1,256,4096]{2,1,0:T(8,128)(2,1)}) %all-gather.5.cloned.1.call-update) | async-done | bytes 2097168 | tf_op jit(solution)/shard_map/all_gather | solution.py:316
  103.8 2.2 %copy-done.2 = bf16[4096,512]{1,0:T(8,128)(2,1)S(1)} copy-done((bf16[4096,512]{1,0:T(8,128)(2,1)S(1)}, bf16[4096,512]{1,0:T(8,128)(2,1)}, u32[]{:S(2)}) %copy-start.2) | copy-done | bytes 4194328
  106.0 2.2 %copy-done.5 = bf16[4096,512]{1,0:T(8,128)(2,1)S(1)} copy-done((bf16[4096,512]{1,0:T(8,128)(2,1)S(1)}, bf16[4096,512]{1,0:T(8,128)(2,1)}, u32[]{:S(2)}) %copy-start.5) | copy-done | bytes 4194328
  108.2 1.6 copy-done.8
  109.8 6.4 %project.2 = (bf16[256,512]{1,0:T(8,128)(2,1)S(1)}, bf16[256,512]{1,0:T(8,128)(2,1)S(1)}, bf16[256,1024]{1,0:T(8,128)(2,1)S(1)}) custom-call(bf16[256,4096]{1,0:T(8,128)(2,1)S(1)} %bitcast.7, bf16[4096,512]{1,0:T(8,128)(2,1)S(1)} %copy-done.2, bf16[4096,512]{1,0:T(8,128)(2,1)S(1)} %copy-done.5, bf16[4096,512]{1,0:T(8,128)(2,1)} %wv_ref.5, ...), custom_call_target="tpu_custom_call" | custom-call | flops 3221225472 | bytes 14680064 | tf_op jit(solution)/shard_map/project/pallas_call | solution.py:117
  116.2 1.7 collective-permute-start
  117.9 12.0 %collective-permute-done.refs_5_ = bf16[256,1024]{1,0:T(8,128)(2,1)S(1)} collective-permute-done((bf16[256,1024]{1,0:T(8,128)(2,1)S(1)}, bf16[256,1024]{1,0:T(8,128)(2,1)S(1)}, u32[]{:S(2)}, u32[]{:S(2)}) %collective-permute-start) | collective-permute-done | bytes 524320 | tf_op jit(solution)/shard_map/ppermute | solution.py:304
  129.9 0.3 pad_maximum_fusion
  130.3 1.5 collective-permute-done.2.refs_7_
  131.8 11.0 %attend_reverse.1.rows_ref = bf16[256,512]{1,0:T(8,128)(2,1)S(1)} custom-call(s32[4]{0:T(128)S(1)} %pad_add_fusion.refs_0_, bf16[256,512]{1,0:T(8,128)(2,1)S(1)} %get-tuple-element.35.refs_1_, bf16[256,512]{1,0:T(8,128)(2,1)S(1)} %get-tuple-element.36.refs_2_, f32[16,1536]{1,0:T(8,128)S(1)} %constant_dynamic-update-slice_fusion.ew_ref.refs_3_, ...), custom_call_target="tpu_custom_call" | custom-call | flops 1073741824 | bytes 2097152 | tf_op jit(solution)/shard_map/attend_reverse/pallas_call | solution.py:234
  142.9 3.2 %out_project.1 = bf16[4,256,1024]{2,1,0:T(8,128)(2,1)} custom-call(bf16[256,512]{1,0:T(8,128)(2,1)S(1)} %attend_reverse.1.rows_ref, bf16[512,4096]{1,0:T(8,128)(2,1)S(1)} %copy-done.7), custom_call_target="tpu_custom_call" | custom-call | flops 1073741824 | bytes 6291456 | tf_op jit(solution)/shard_map/out_project/pallas_call | solution.py:263
  146.1 0.0 reduce-scatter.2.cloned.1.call-update
  146.1 42.0 %reduce-scatter.2.cloned.1.call-done = bf16[1,256,1024]{2,1,0:T(8,128)(2,1)} async-done(((bf16[4,256,1024]{2,1,0:T(8,128)(2,1)}), bf16[1,256,1024]{2,1,0:T(8,128)(2,1)}) %reduce-scatter.2.cloned.1.call-update) | async-done | bytes 524304 | tf_op jit(solution)/shard_map/reduce_scatter | solution.py:364
  (41 shorter events, 0.2 us)
Async XLA Ops:
  6.5 51.0 %all-gather.7.cloned.1.call-start = ((), (), s32[]{:S(2)}) async-start(), calls=%async_computation.3 | async-start | bytes 2621440 | tf_op jit(solution)/shard_map/all_gather | solution.py:316
  8.8 8.2 %copy-start.13 = (s32[128]{0:T(128)S(1)}, s32[128]{0:T(128)}, u32[]{:S(2)}) copy-start(s32[128]{0:T(128)} %param.15) | copy-start | bytes 1540
  8.8 8.6 %copy-start.14 = (s32[128]{0:T(128)S(1)}, s32[128]{0:T(128)}, u32[]{:S(2)}) copy-start(s32[128]{0:T(128)} %param.16) | copy-start | bytes 1540
  8.8 95.0 %all-gather.5.cloned.1.call-start = ((), (), s32[]{:S(2)}) async-start(), calls=%async_computation.2 | async-start | bytes 2621440 | tf_op jit(solution)/shard_map/all_gather | solution.py:316
  8.9 14.8 %collective-permute-start.3 = (s32[256]{0:T(256)}, s32[256]{0:T(256)S(1)}, u32[]{:S(2)}, u32[]{:S(2)}) collective-permute-start(s32[256]{0:T(256)} %param.14), channel_id=1, source_target_pairs={{0,8},{4,12},{8,0},{12,4},{1,9},{5,13},{9,1},{13,5},{2,10},{6,14},... | collective-permute-start | bytes 3080 | tf_op jit(solution)/shard_map/ppermute | solution.py:304
  11.9 59.7 %collective-permute-start.4 = (s32[256]{0:T(256)}, s32[256]{0:T(256)S(1)}, u32[]{:S(2)}, u32[]{:S(2)}) collective-permute-start(s32[256]{0:T(256)} %param.14), channel_id=1, source_target_pairs={{0,4},{4,0},{8,12},{12,8},{1,5},{5,1},{9,13},{13,9},{2,6},{6,2},{1... | collective-permute-start | bytes 3080 | tf_op jit(solution)/shard_map/ppermute | solution.py:307
  11.9 176.2 %reduce-scatter.2.cloned.1.call-start = ((), (), s32[]{:S(2)}) async-start(), calls=%async_computation.1 | async-start | bytes 2621440 | tf_op jit(solution)/shard_map/reduce_scatter | solution.py:364
  12.8 5.3 %copy-start.12 = (s32[256]{0:T(256)S(1)}, s32[256]{0:T(256)}, u32[]{:S(2)}) copy-start(s32[256]{0:T(256)} %param.14) | copy-start | bytes 3076
  12.9 5.5 %copy-start = (bf16[4096,512]{1,0:T(8,128)(2,1)S(1)}, bf16[4096,512]{1,0:T(8,128)(2,1)}, u32[]{:S(2)}) copy-start(bf16[4096,512]{1,0:T(8,128)(2,1)} %wq_ref.5) | copy-start | bytes 12582916
  12.9 5.5 %copy-start.3 = (bf16[4096,512]{1,0:T(8,128)(2,1)S(1)}, bf16[4096,512]{1,0:T(8,128)(2,1)}, u32[]{:S(2)}) copy-start(bf16[4096,512]{1,0:T(8,128)(2,1)} %wk_ref.5) | copy-start | bytes 12582916
  16.6 6.7 %copy-start.10 = (f32[1024,64]{1,0:T(8,128)}, f32[1024,64]{1,0:T(8,128)S(1)}, u32[]{:S(2)}) copy-start(f32[1024,64]{1,0:T(8,128)S(1)} %get-tuple-element.59) | copy-start | bytes 786436
  18.4 2.4 %copy-start.6 = (bf16[4096,512]{1,0:T(8,128)(2,1)S(1)}, bf16[4096,512]{1,0:T(8,128)(2,1)}, u32[]{:S(2)}) copy-start(bf16[4096,512]{1,0:T(8,128)(2,1)} %wv_ref.5) | copy-start | bytes 12582916
  23.7 60.1 %collective-permute-start.5 = (s32[256]{0:T(256)S(1)}, s32[256]{0:T(256)S(1)}, u32[]{:S(2)}, u32[]{:S(2)}) collective-permute-start(s32[256]{0:T(256)S(1)} %collective-permute-done.3), channel_id=1, source_target_pairs={{0,4},{4,0},{8,12},{12,8},{1,5},{5,1},{9,13},{13,9},{2,6},{6,2},{1... | collective-permute-start | bytes 3080 | tf_op jit(solution)/shard_map/ppermute | solution.py:307
  57.6 2.2 %copy-start.1 = (bf16[4096,512]{1,0:T(8,128)(2,1)S(1)}, bf16[4096,512]{1,0:T(8,128)(2,1)}, u32[]{:S(2)}) copy-start(bf16[4096,512]{1,0:T(8,128)(2,1)} %wq_ref.5) | copy-start | bytes 12582916
  59.8 2.2 %copy-start.4 = (bf16[4096,512]{1,0:T(8,128)(2,1)S(1)}, bf16[4096,512]{1,0:T(8,128)(2,1)}, u32[]{:S(2)}) copy-start(bf16[4096,512]{1,0:T(8,128)(2,1)} %wk_ref.5) | copy-start | bytes 12582916
  62.0 1.6 copy-start.9
  70.0 13.6 %collective-permute-start.6 = (bf16[256,1024]{1,0:T(8,128)(2,1)S(1)}, bf16[256,1024]{1,0:T(8,128)(2,1)S(1)}, u32[]{:S(2)}, u32[]{:S(2)}) collective-permute-start(bf16[256,1024]{1,0:T(8,128)(2,1)S(1)} %get-tuple-element.40.refs_4_), channel_id=1, source_target_pairs={{0,8},{4,12},{8,0},{12,4},{1,9},{5,13},{9,1},{13,5},{2,10},{6,14},... | collective-permute-start | bytes 1572872 | tf_op jit(solution)/shard_map/ppermute | solution.py:304
  71.8 12.3 %collective-permute-start.7 = (bf16[256,1024]{1,0:T(8,128)(2,1)S(1)}, bf16[256,1024]{1,0:T(8,128)(2,1)S(1)}, u32[]{:S(2)}, u32[]{:S(2)}) collective-permute-start(bf16[256,1024]{1,0:T(8,128)(2,1)S(1)} %get-tuple-element.40.refs_4_), channel_id=1, source_target_pairs={{0,4},{4,0},{8,12},{12,8},{1,5},{5,1},{9,13},{13,9},{2,6},{6,2},{1... | collective-permute-start | bytes 1572872 | tf_op jit(solution)/shard_map/ppermute | solution.py:307
  83.7 1.9 collective-permute-start.8
  103.8 2.2 %copy-start.2 = (bf16[4096,512]{1,0:T(8,128)(2,1)S(1)}, bf16[4096,512]{1,0:T(8,128)(2,1)}, u32[]{:S(2)}) copy-start(bf16[4096,512]{1,0:T(8,128)(2,1)} %wq_ref.5) | copy-start | bytes 12582916
  106.0 2.2 %copy-start.5 = (bf16[4096,512]{1,0:T(8,128)(2,1)S(1)}, bf16[4096,512]{1,0:T(8,128)(2,1)}, u32[]{:S(2)}) copy-start(bf16[4096,512]{1,0:T(8,128)(2,1)} %wk_ref.5) | copy-start | bytes 12582916
  108.2 1.6 copy-start.8
  109.8 20.1 %copy-start.11 = (f32[1024,64]{1,0:T(8,128)S(1)}, f32[1024,64]{1,0:T(8,128)}, u32[]{:S(2)}) copy-start(f32[1024,64]{1,0:T(8,128)} %copy-done.10) | copy-start | bytes 786436
  116.2 26.7 %copy-start.7 = (bf16[512,4096]{1,0:T(8,128)(2,1)S(1)}, bf16[512,4096]{1,0:T(8,128)(2,1)}, u32[]{:S(2)}) copy-start(bf16[512,4096]{1,0:T(8,128)(2,1)} %weight_ref.1) | copy-start | bytes 12582916
  116.2 13.7 %collective-permute-start = (bf16[256,1024]{1,0:T(8,128)(2,1)S(1)}, bf16[256,1024]{1,0:T(8,128)(2,1)S(1)}, u32[]{:S(2)}, u32[]{:S(2)}) collective-permute-start(bf16[256,1024]{1,0:T(8,128)(2,1)S(1)} %get-tuple-element.37.refs_4_), channel_id=1, source_target_pairs={{0,8},{4,12},{8,0},{12,4},{1,9},{5,13},{9,1},{13,5},{2,10},{6,14},... | collective-permute-start | bytes 1572872 | tf_op jit(solution)/shard_map/ppermute | solution.py:304
  117.9 12.3 %collective-permute-start.1 = (bf16[256,1024]{1,0:T(8,128)(2,1)S(1)}, bf16[256,1024]{1,0:T(8,128)(2,1)S(1)}, u32[]{:S(2)}, u32[]{:S(2)}) collective-permute-start(bf16[256,1024]{1,0:T(8,128)(2,1)S(1)} %get-tuple-element.37.refs_4_), channel_id=1, source_target_pairs={{0,4},{4,0},{8,12},{12,8},{1,5},{5,1},{9,13},{13,9},{2,6},{6,2},{1... | collective-permute-start | bytes 1572872 | tf_op jit(solution)/shard_map/ppermute | solution.py:307
  129.9 1.9 collective-permute-start.2
Sparse Core Ops, SparseCore 0:
  8.9 48.6 all-gather.6
  59.1 44.6 all-gather.4
  146.2 41.8 reduce-scatter.1

commit v2 on v1

--- a/solution.py
+++ b/solution.py
@@ -13,7 +13,7 @@
 BASE_PAD = 16
 ROPE_BASE = 10000.0
 NEG_FILL = -1e30
-VMEM_LIMIT = 40 * 1024 * 1024
+VMEM_LIMIT = 56 * 1024 * 1024
 F32 = jnp.float32
 BF16 = jnp.bfloat16
 
@@ -74,67 +74,88 @@
     )(embed, wq, wk, wv)
 
 
-def project_kernel(
-    x_ref, wq_ref, wk_ref, wv_ref, ew_ref, codes_ref, cos_ref, sin_ref, q_ref, qm_ref, kv_ref, acc
-):
-    width = wq_ref.shape[1]
-    step = pl.program_id(0)
-
-    @pl.when(step == 0)
-    def _():
-        acc[...] = jnp.zeros_like(acc)
-
-    rows = x_ref[...]
+def slab_kernel(has_total, last, slab_ref, x_ref, wq_ref, wk_ref, wv_ref, *refs):
+    del slab_ref
+    if has_total:
+        total_refs, refs = refs[:3], refs[3:]
+    if last:
+        (ewq_ref, ewk_ref, ewv_ref, codes_ref, cos_ref, sin_ref), refs = refs[:6], refs[6:]
+        q_ref, qm_ref, kv_ref = refs
+    rows = x_ref[...].reshape(x_ref.shape[-2:])
+    sums = []
     for index, weight in enumerate((wq_ref, wk_ref, wv_ref)):
-        acc[:, index * width : (index + 1) * width] += jnp.dot(
-            rows, weight[...], preferred_element_type=F32
-        )
-
-    @pl.when(step == pl.num_programs(0) - 1)
-    def _():
-        cos, sin, codes = cos_ref[...], sin_ref[...], codes_ref[...]
-        for start in range(0, width, HEAD_DIM):
-            cols = slice(start, start + HEAD_DIM)
-            query = acc[:, cols]
-            change = mixed_rows(codes, ew_ref[0:BASES, cols])
-            q_ref[:, cols] = turned(query, cos, sin).astype(BF16)
-            qm_ref[:, cols] = turned(query + change, cos, sin).astype(BF16)
-            kv_ref[:, cols] = turned(
-                acc[:, width + start : width + start + HEAD_DIM], cos, sin
-            ).astype(BF16)
-        kv_ref[:, width:] = acc[:, 2 * width :].astype(BF16)
-
-
-def project(x, wq, wk, wv, ew, codes, cos, sin, slabs):
-    rows, depth = x.shape
-    width = wq.shape[1]
-    tile = depth // slabs
-    weight_spec = pl.BlockSpec((tile, width), lambda i: (i, 0))
-
-    def whole(shape):
-        return pl.BlockSpec(shape, lambda i: (0, 0))
-
-    return pl.pallas_call(
-        project_kernel,
-        grid=(slabs,),
-        in_specs=[pl.BlockSpec((rows, tile), lambda i: (0, i))]
-        + [weight_spec] * 3
-        + [whole(item.shape) for item in (ew, codes, cos, sin)],
-        out_specs=[whole((rows, width)), whole((rows, width)), whole((rows, 2 * width))],
-        out_shape=[
+        item = jnp.dot(rows, weight[...], preferred_element_type=F32)
+        if has_total:
+            item = total_refs[index][...] + item
+        sums.append(item)
+    if not last:
+        for index in range(3):
+            refs[index][...] = sums[index]
+        return
+    cos, sin, codes = cos_ref[...], sin_ref[...], codes_ref[...]
+    for start in range(0, wq_ref.shape[1], HEAD_DIM):
+        cols = slice(start, start + HEAD_DIM)
+        query, key = sums[0][:, cols], sums[1][:, cols]
+        change = mixed_rows(codes, ewq_ref[0:BASES, cols])
+        q_ref[:, cols] = turned(query, cos, sin).astype(BF16)
+        qm_ref[:, cols] = turned(query + change, cos, sin).astype(BF16)
+        kv_ref[0, :, cols] = turned(key, cos, sin).astype(BF16)
+    kv_ref[1] = sums[2].astype(BF16)
+
+
+def project_slab(slab, x, strand, weights, total=None, finish=None):
+    rows, tile = x.shape[-2:]
+    width = weights[0].shape[1]
+    cols = min(2 * HEAD_DIM, width)
+    if x.ndim == 3:
+        x_spec = pl.BlockSpec((1, rows, tile), lambda j, slab: (strand, 0, 0))
+    else:
+        x_spec = pl.BlockSpec((rows, tile), lambda j, slab: (0, 0))
+    in_specs = [x_spec] + [pl.BlockSpec((tile, cols), lambda j, slab: (slab[0], j))] * 3
+    operands = [x, *weights]
+    sum_spec = pl.BlockSpec((rows, cols), lambda j, slab: (0, j))
+    aliases = {}
+    if total is not None:
+        in_specs += [sum_spec] * 3
+        operands += total
+        if finish is None:
+            aliases = {5 + index: index for index in range(3)}
+    if finish is None:
+        out_specs = [sum_spec] * 3
+        out_shape = [jax.ShapeDtypeStruct((rows, width), F32)] * 3
+    else:
+        ew, codes, cos, sin = finish
+        steps = width // cols
+        in_specs += [
+            pl.BlockSpec((BASE_PAD, cols), lambda j, slab: (0, j)),
+            pl.BlockSpec((BASE_PAD, cols), lambda j, slab: (0, j + steps)),
+            pl.BlockSpec((BASE_PAD, cols), lambda j, slab: (0, j + 2 * steps)),
+        ] + [pl.BlockSpec(item.shape, lambda j, slab: (0, 0)) for item in (codes, cos, sin)]
+        operands += [ew, ew, ew, codes, cos, sin]
+        out_specs = [sum_spec, sum_spec, pl.BlockSpec((2, rows, cols), lambda j, slab: (0, 0, j))]
+        out_shape = [
             jax.ShapeDtypeStruct((rows, width), BF16),
             jax.ShapeDtypeStruct((rows, width), BF16),
-            jax.ShapeDtypeStruct((rows, 2 * width), BF16),
-        ],
-        scratch_shapes=[pltpu.VMEM((rows, 3 * width), F32)],
+            jax.ShapeDtypeStruct((2, rows, width), BF16),
+        ]
+    return pl.pallas_call(
+        functools.partial(slab_kernel, total is not None, finish is not None),
+        grid_spec=pltpu.PrefetchScalarGridSpec(
+            num_scalar_prefetch=1,
+            grid=(width // cols,),
+            in_specs=in_specs,
+            out_specs=out_specs,
+        ),
+        out_shape=out_shape,
+        input_output_aliases=aliases,
         compiler_params=params(),
         cost_estimate=pl.CostEstimate(
-            flops=2 * rows * depth * 3 * width,
-            bytes_accessed=3 * depth * width * 2 + rows * depth * 2,
+            flops=6 * rows * tile * width,
+            bytes_accessed=6 * tile * width + 2 * rows * tile + 12 * rows * width,
             transcendentals=0,
         ),
-        name="project",
-    )(x, wq, wk, wv, ew, codes, cos, sin)
+        name="project_slab" if finish is None else "project_finish",
+    )(slab, *operands)
 
 
 def attend_kernel(forward, block_count, has_before, *refs):
@@ -166,7 +187,7 @@
             cols = slice(head * HEAD_DIM, (head + 1) * HEAD_DIM)
             key_cols = slice(width + cols.start, width + cols.stop)
             value_cols = slice(2 * width + cols.start, 2 * width + cols.stop)
-            key, value = kv_ref[:, cols], kv_ref[:, key_cols]
+            key, value = kv_ref[0, :, cols], kv_ref[1, :, cols]
             key_change = turned(mixed_rows(codes, ew_ref[0:BASES, key_cols]), cos, sin)
             value_change = mixed_rows(codes, ew_ref[0:BASES, value_cols])
             mutant_key = (key.astype(F32) + key_change).astype(BF16)
@@ -312,9 +333,9 @@
         near = near + [item ^ 1 for item in near]
     ids = jnp.stack(near).astype(jnp.int32)
 
-    gathered = [
-        lax.all_gather(hidden[strand], "head", axis=1, tiled=True) for strand in range(2)
-    ]
+    ring = [(i, (i + 1) % slabs) for i in range(slabs)]
+    head = lax.axis_index("head")
+    weights = (query_weight, key_weight, value_weight)
 
     base_blocks = ctx_gather(strand_bases)
     embed = jnp.zeros((BASE_PAD, base_embed.shape[1]), BF16).at[:BASES].set(base_embed)
@@ -340,22 +361,27 @@
         rope_tables((window - 1 - positions).astype(F32)),
     ]
     before = None
+    ring_free = None
     for strand in range(2):
         cos, sin = tables[strand]
         ew = ew_plus if strand == 0 else ew_minus
         own_cos = lax.dynamic_slice_in_dim(cos, me * rows, rows, 0)
         own_sin = lax.dynamic_slice_in_dim(sin, me * rows, rows, 0)
-        q, qm, kv = project(
-            gathered[strand],
-            query_weight,
-            key_weight,
-            value_weight,
-            ew,
-            code_blocks[0],
-            own_cos,
-            own_sin,
-            slabs,
-        )
+        finish = (ew, code_blocks[0], own_cos, own_sin)
+        moving = hidden[strand]
+        if ring_free is not None:
+            moving, ring_free = lax.optimization_barrier((moving, ring_free))
+        total, here = None, hidden
+        for step in range(slabs):
+            slab = ((head - step) % slabs).astype(jnp.int32)[None]
+            if step < slabs - 1:
+                moving = lax.ppermute(moving, "head", ring)
+            total = project_slab(
+                slab, here, strand, weights, total, finish if step == slabs - 1 else None
+            )
+            here = moving
+        ring_free = moving
+        q, qm, kv = total
         kv_blocks = ctx_gather(kv)
         before = attend(
             strand == 0, ids, q, qm, ew, kv_blocks, code_blocks, cos, sin, before

time: 195 us -> 201 us (1.031)
  Pallas kernels: 33 us -> 65.2 us
  waiting for transfers between devices: 117 us -> 89.5 us
  local copies, waits for them, and re-layouts: 17.8 us -> 5.8 us
  other arithmetic: 6.3 us -> 12.9 us
  starting transfers between devices: 7.05 us -> 13.3 us
    all_gather x2 -> x0, waiting for transfers between devices: 48.2 us -> none  [shards(): lax.all_gather(hidden[strand], 'head', axis=1, tiled=True)]
    ppermute x0 -> x6, waiting for transfers between devices: none -> 21.9 us  [shards(): moving = lax.ppermute(moving, 'head', ring)]
    pallas_call x2 -> x8, Pallas kernels: 12.9 us -> 33 us  [project_slab(): pl.pallas_call(functools.partial(slab_kernel, total is not None, finish i...]
    unnamed x30 -> x34, local copies, waits for them, and re-layouts: 14.4 us -> 2.58 us
    pallas_call x1, Pallas kernels: 2.57 us -> 8.26 us  [embed_project(): pl.pallas_call(embed_kernel, grid=(depth // tile,), in_specs=[pl.BlockSpe...]
    pallas_call x2, Pallas kernels: 14.4 us -> 18.9 us  [attend(): pl.pallas_call(functools.partial(attend_kernel, forward, count, before is...]
    ppermute x3, starting transfers between devices: 6.31 us -> 10.1 us  [ctx_gather(): held.append(lax.ppermute(block, 'ctx', pairs))]
    ppermute x0 -> x6, starting transfers between devices: none -> 3.13 us  [shards(): moving = lax.ppermute(moving, 'head', ring)]
  transfers between devices with their start and end apart: 12 -> 16, of which waited for: 7 -> 9; matrix products, arithmetic and copies ran while one was open for 4% -> 8% of each run, Pallas kernels for 6% -> 21%
where the time goes in v2:
time: 201 us; the launch traced here: 200 us
  waiting for transfers between devices  89.5 us (45%)
  Pallas kernels  65.2 us (32%)
  between operations  13.6 us (7%)
  starting transfers between devices  13.3 us (7%)
  other arithmetic  12.9 us (6%)
  local copies, waits for them, and re-layouts  5.8 us (3%)
    reduce_scatter x1, waiting for transfers between devices, shards(): return lax.psum_scatter(partial, 'head', scatter_dimension=0, tiled=True)[0]  44.2 us
    pallas_call x8, Pallas kernels, project_slab(): pl.pallas_call(functools.partial(slab_kernel, total is not None, finish i...  33 us
    ppermute x3, waiting for transfers between devices, ctx_gather(): held.append(lax.ppermute(block, 'ctx', pairs))  22.7 us
    ppermute x6, waiting for transfers between devices, shards(): moving = lax.ppermute(moving, 'head', ring)  21.9 us
    pallas_call x2, Pallas kernels, attend(): pl.pallas_call(functools.partial(attend_kernel, forward, count, before is...  18.9 us
    ppermute x3, starting transfers between devices, ctx_gather(): held.append(lax.ppermute(block, 'ctx', pairs))  10.1 us
    pallas_call x1, Pallas kernels, embed_project(): pl.pallas_call(embed_kernel, grid=(depth // tile,), in_specs=[pl.BlockSpe...  8.26 us
    pallas_call x1, Pallas kernels, out_project(): pl.pallas_call(out_kernel, grid=(slabs,), in_specs=[pl.BlockSpec((rows, w...  5.03 us
  transfers between devices with their start and end apart: 16, of which 9 were waited for; matrix products, arithmetic and copies ran while one was open for 8% of the time, Pallas kernels for 21%

profile of v2, /device:TPU:0, one launch (start us, length us, event | category | flops | bytes accessed | tf_op | source)
XLA Modules:
  0.0 200.2 jit_solution(1749099256574217987)
XLA Ops:
  6.5 3.0 %collective-permute-start.9 = (s32[256]{0:T(256)}, s32[256]{0:T(256)S(1)}, u32[]{:S(2)}, u32[]{:S(2)}) collective-permute-start(s32[256]{0:T(256)} %param.14), channel_id=1, source_target_pairs={{0,8},{4,12},{8,0},{12,4},{1,9},{5,13},{9,1},{13,5},{2,10},{6,14},... | collective-permute-start | bytes 3080 | tf_op jit(solution)/shard_map/ppermute | solution.py:325
  9.5 2.2 %slice_bitcast_fusion = (bf16[256,1024]{1,0:T(8,128)(2,1)}, bf16[256,1024]{1,0:T(8,128)(2,1)}) fusion(bf16[2,256,1024]{2,1,0:T(8,128)(2,1)} %x_ref.3), kind=kLoop, calls=%fused_computation.4 | loop fusion | bytes 2097152 | tf_op jit(solution)/shard_map/squeeze | solution.py:371
  11.8 1.6 collective-permute-start
  13.4 0.7 pad_add_fusion.refs_0_
  14.1 3.7 %multiply_sine_fusion = (f32[1024,64]{1,0:T(8,128)S(1)}, f32[1024,64]{1,0:T(8,128)S(1)}, f32[1024,64]{1,0:T(8,128)S(1)}, f32[1024,64]{1,0:T(8,128)S(1)}, f32[1024,64]{1,0:T(8,128)S(1)}, /*index=5*/f32[1024,64]{1,0:T(8,128)S(1)}) fusion(f32[1024]{0:T(1024)S(1)} %iota_convert_fusion, f32[64]{0:T(128)S(1)} %multiply_power_fusion, f32[1024]{0:T(1024)S(1)} %subtract_convert_fusion), kind=kLoop, calls=%fused_computation | loop fusion | flops 262144 | bytes 1581312 | tf_op jit(solution)/shard_map/sin | solution.py:29
  17.8 0.9 fusion.6
  18.7 9.6 %collective-permute-done.x_ref = bf16[256,1024]{1,0:T(8,128)(2,1)} collective-permute-done((bf16[256,1024]{1,0:T(8,128)(2,1)}, bf16[256,1024]{1,0:T(8,128)(2,1)}, u32[]{:S(2)}, u32[]{:S(2)}) %collective-permute-start) | collective-permute-done | bytes 524320 | tf_op jit(solution)/shard_map/ppermute | solution.py:378
  28.3 3.8 %project_slab.9 = (f32[256,512]{1,0:T(8,128)}, f32[256,512]{1,0:T(8,128)}, f32[256,512]{1,0:T(8,128)}) custom-call(s32[1]{0:T(128)} %bitcast.9.slab_ref, bf16[2,256,1024]{2,1,0:T(8,128)(2,1)} %x_ref.3, bf16[4096,512]{1,0:T(8,128)(2,1)} %wq_ref.17, bf16[4096,512]{1,0:T(8,128)(2,1)} %wk_ref.17, bf16[4096,512]{1,0:T(8,128)(2,1)} %wv_ref.17), custom_call_target="tpu_custom_call" | custom-call | flops 805306368 | bytes 5242880 | tf_op jit(solution)/shard_map/project_slab/pallas_call | solution.py:141
  32.0 0.7 scatter.6.embed_ref
  32.7 8.3 %embed_project.1.refs_3_.refs_4_.refs_5_ = f32[16,1536]{1,0:T(8,128)} custom-call(bf16[16,4096]{1,0:T(8,128)(2,1)} %scatter.6.embed_ref, bf16[4096,512]{1,0:T(8,128)(2,1)} %wq_ref.17, bf16[4096,512]{1,0:T(8,128)(2,1)} %wk_ref.17, bf16[4096,512]{1,0:T(8,128)(2,1)} %wv_ref.17), custom_call_target="tpu_custom_call" | custom-call | flops 201326592 | bytes 12582912 | tf_op jit(solution)/shard_map/embed_project/pallas_call | solution.py:61
  41.0 0.8 fusion.8
  41.8 0.4 compare_reduce_fusion
  42.2 0.4 fusion.5
  42.6 1.3 pad_maximum_fusion.2
  43.9 0.1 collective-permute-done.1.x_ref
  44.0 1.3 collective-permute-start.2
  45.3 3.7 %project_slab.6 = (f32[256,512]{1,0:T(8,128)}, f32[256,512]{1,0:T(8,128)}, f32[256,512]{1,0:T(8,128)}) custom-call(s32[1]{0:T(128)} %bitcast.9.slab_ref, bf16[2,256,1024]{2,1,0:T(8,128)(2,1)} %x_ref.3, bf16[4096,512]{1,0:T(8,128)(2,1)} %wq_ref.17, bf16[4096,512]{1,0:T(8,128)(2,1)} %wk_ref.17, bf16[4096,512]{1,0:T(8,128)(2,1)} %wv_ref.17), custom_call_target="tpu_custom_call" | custom-call | flops 805306368 | bytes 5242880 | tf_op jit(solution)/shard_map/project_slab/pallas_call | solution.py:141
  49.0 0.8 subtract_select_fusion.3.refs_6_.refs_8_
  49.8 0.3 rev.3
  50.3 9.4 %collective-permute-done.2.x_ref = bf16[256,1024]{1,0:T(8,128)(2,1)S(1)} collective-permute-done((bf16[256,1024]{1,0:T(8,128)(2,1)}, bf16[256,1024]{1,0:T(8,128)(2,1)S(1)}, u32[]{:S(2)}, u32[]{:S(2)}) %collective-permute-start.2) | collective-permute-done | bytes 524320 | tf_op jit(solution)/shard_map/ppermute | solution.py:378
  59.7 4.3 %project_slab.10 = (f32[256,512]{1,0:T(8,128)}, f32[256,512]{1,0:T(8,128)}, f32[256,512]{1,0:T(8,128)}) custom-call(s32[1]{0:T(128)} %bitcast.8.slab_ref, bf16[256,1024]{1,0:T(8,128)(2,1)} %collective-permute-done.x_ref, bf16[4096,512]{1,0:T(8,128)(2,1)} %wq_ref.17, ...), custom_call_target="tpu_custom_call", output_to_operand_aliasing={{0}: (5, {}), {1}: (6, {}), {2}: (7, {})} | custom-call | flops 805306368 | bytes 5242880 | tf_op jit(solution)/shard_map/project_slab/pallas_call | solution.py:141
  63.9 4.1 %project_slab.11 = (f32[256,512]{1,0:T(8,128)}, f32[256,512]{1,0:T(8,128)}, f32[256,512]{1,0:T(8,128)}) custom-call(s32[1]{0:T(128)} %bitcast.7.slab_ref, bf16[256,1024]{1,0:T(8,128)(2,1)} %collective-permute-done.1.x_ref, bf16[4096,512]{1,0:T(8,128)(2,1)} %wq_ref.17, ...), custom_call_target="tpu_custom_call", output_to_operand_aliasing={{0}: (5, {}), {1}: (6, {}), {2}: (7, {})} | custom-call | flops 805306368 | bytes 5242880 | tf_op jit(solution)/shard_map/project_slab/pallas_call | solution.py:141
  68.1 4.4 %project_finish.3 = (bf16[256,512]{1,0:T(8,128)(2,1)}, bf16[256,512]{1,0:T(8,128)(2,1)}, bf16[2,256,512]{2,1,0:T(8,128)(2,1)}) custom-call(s32[1]{0:T(128)} %bitcast.4.slab_ref, bf16[256,1024]{1,0:T(8,128)(2,1)} %copy-done.2, bf16[4096,512]{1,0:T(8,128)(2,1)} %wq_ref.17, bf16[4096,512]{1,0:T(8,128)(2,1)} %wk_ref.17, bf16[4096,512]{1,0:T(8,128)(2,1)} %wv_ref.17, ...), custom_call_target="tpu_custom_call" | custom-call | flops 805306368 | bytes 5242880 | tf_op jit(solution)/shard_map/project_finish/pallas_call | solution.py:141
  72.5 0.7 collective-permute-start.12
  73.2 0.8 subtract_select_fusion.2.refs_9_
  74.0 0.2 collective-permute-done.3.x_ref
  74.2 0.3 collective-permute-start.4
  74.5 0.8 subtract_select_fusion.1.refs_10_
  75.3 10.2 %collective-permute-done.12.refs_5_ = bf16[2,256,512]{2,1,0:T(8,128)(2,1)S(1)} collective-permute-done((bf16[2,256,512]{2,1,0:T(8,128)(2,1)}, bf16[2,256,512]{2,1,0:T(8,128)(2,1)S(1)}, u32[]{:S(2)}, u32[]{:S(2)}) %collective-permute-start.12) | collective-permute-done | bytes 524320 | tf_op jit(solution)/shard_map/ppermute | solution.py:325
  85.5 2.7 %collective-permute-done.4.x_ref = bf16[256,1024]{1,0:T(8,128)(2,1)S(1)} collective-permute-done((bf16[256,1024]{1,0:T(8,128)(2,1)S(1)}, bf16[256,1024]{1,0:T(8,128)(2,1)S(1)}, u32[]{:S(2)}, u32[]{:S(2)}) %collective-permute-start.4) | collective-permute-done | bytes 524320 | tf_op jit(solution)/shard_map/ppermute | solution.py:378
  88.3 0.8 subtract_select_fusion.refs_11_
  89.1 4.1 %project_slab.7 = (f32[256,512]{1,0:T(8,128)}, f32[256,512]{1,0:T(8,128)}, f32[256,512]{1,0:T(8,128)}) custom-call(s32[1]{0:T(128)} %bitcast.8.slab_ref, bf16[256,1024]{1,0:T(8,128)(2,1)} %copy-done.3, bf16[4096,512]{1,0:T(8,128)(2,1)} %wq_ref.17, bf16[4096,512]{1,0:T(8,128)(2,1)} %wk_ref.17, ...), custom_call_target="tpu_custom_call", output_to_operand_aliasing={{0}: (5, {}), {1}: (6, {}), {2}: (7, {})} | custom-call | flops 805306368 | bytes 5242880 | tf_op jit(solution)/shard_map/project_slab/pallas_call | solution.py:141
  93.2 4.1 %project_slab.8 = (f32[256,512]{1,0:T(8,128)}, f32[256,512]{1,0:T(8,128)}, f32[256,512]{1,0:T(8,128)}) custom-call(s32[1]{0:T(128)} %bitcast.7.slab_ref, bf16[256,1024]{1,0:T(8,128)(2,1)} %copy-done.5, bf16[4096,512]{1,0:T(8,128)(2,1)} %wq_ref.17, bf16[4096,512]{1,0:T(8,128)(2,1)} %wk_ref.17, ...), custom_call_target="tpu_custom_call", output_to_operand_aliasing={{0}: (5, {}), {1}: (6, {}), {2}: (7, {})} | custom-call | flops 805306368 | bytes 5242880 | tf_op jit(solution)/shard_map/project_slab/pallas_call | solution.py:141
  97.4 0.8 copy-done.6
  98.1 0.2 copy-done.8
  98.3 5.6 %attend_forward.1.refs_14_ = f32[256,512]{1,0:T(8,128)} custom-call(s32[4]{0:T(128)} %pad_add_fusion.refs_0_, bf16[256,512]{1,0:T(8,128)(2,1)} %get-tuple-element.76.refs_1_, bf16[256,512]{1,0:T(8,128)(2,1)} %get-tuple-element.77.refs_2_, f32[16,1536]{1,0:T(8,128)} %embed_project.1.refs_3_.refs_4_.refs_5_, bf16[2,256,512]{2,1,0:T(8,128)(2,1)} %get-tuple-element.78.refs_4_, ...), custom_call_target="tpu_custom_call" | custom-call | flops 1073741824 | bytes 2097152 | tf_op jit(solution)/shard_map/attend_forward/pallas_call | solution.py:255
  104.0 0.6 copy-done.1
  104.6 0.2 copy-done.7
  104.7 4.4 %project_finish.2 = (bf16[256,512]{1,0:T(8,128)(2,1)}, bf16[256,512]{1,0:T(8,128)(2,1)}, bf16[2,256,512]{2,1,0:T(8,128)(2,1)}) custom-call(s32[1]{0:T(128)} %bitcast.4.slab_ref, bf16[256,1024]{1,0:T(8,128)(2,1)} %copy-done.7, bf16[4096,512]{1,0:T(8,128)(2,1)} %wq_ref.17, bf16[4096,512]{1,0:T(8,128)(2,1)} %wk_ref.17, bf16[4096,512]{1,0:T(8,128)(2,1)} %wv_ref.17, ...), custom_call_target="tpu_custom_call" | custom-call | flops 805306368 | bytes 5242880 | tf_op jit(solution)/shard_map/project_finish/pallas_call | solution.py:141
  109.2 6.4 %collective-permute-start.6 = (bf16[2,256,512]{2,1,0:T(8,128)(2,1)}, bf16[2,256,512]{2,1,0:T(8,128)(2,1)S(1)}, u32[]{:S(2)}, u32[]{:S(2)}) collective-permute-start(bf16[2,256,512]{2,1,0:T(8,128)(2,1)} %get-tuple-element.66.refs_4_), channel_id=1, source_target_pairs={{0,8},{4,12},{8,0},{12,4},{1,9},{5,13},{9,1},{13,5},{2,10},{6,14},... | collective-permute-start | bytes 1572872 | tf_op jit(solution)/shard_map/ppermute | solution.py:325
  115.6 12.5 %collective-permute-done.6.refs_5_ = bf16[2,256,512]{2,1,0:T(8,128)(2,1)S(1)} collective-permute-done((bf16[2,256,512]{2,1,0:T(8,128)(2,1)}, bf16[2,256,512]{2,1,0:T(8,128)(2,1)S(1)}, u32[]{:S(2)}, u32[]{:S(2)}) %collective-permute-start.6) | collective-permute-done | bytes 524320 | tf_op jit(solution)/shard_map/ppermute | solution.py:325
  128.1 1.3 pad_maximum_fusion
  129.4 0.6 collective-permute-done.8.refs_7_
  130.0 0.2 copy-done.11
  130.2 0.6 copy-done.12
  130.8 13.3 %attend_reverse.1.rows_ref = bf16[256,512]{1,0:T(8,128)(2,1)} custom-call(s32[4]{0:T(128)} %pad_add_fusion.refs_0_, bf16[256,512]{1,0:T(8,128)(2,1)} %get-tuple-element.64.refs_1_, bf16[256,512]{1,0:T(8,128)(2,1)} %get-tuple-element.65.refs_2_, f32[16,1536]{1,0:T(8,128)} %copy-done.1, bf16[2,256,512]{2,1,0:T(8,128)(2,1)} %get-tuple-element.66.refs_4_, ...), custom_call_target="tpu_custom_call" | custom-call | flops 1073741824 | bytes 2097152 | tf_op jit(solution)/shard_map/attend_reverse/pallas_call | solution.py:255
  144.1 5.0 %out_project.1 = bf16[4,256,1024]{2,1,0:T(8,128)(2,1)} custom-call(bf16[256,512]{1,0:T(8,128)(2,1)} %attend_reverse.1.rows_ref, bf16[512,4096]{1,0:T(8,128)(2,1)} %weight_ref.1), custom_call_target="tpu_custom_call" | custom-call | flops 1073741824 | bytes 6291456 | tf_op jit(solution)/shard_map/out_project/pallas_call | solution.py:284
  149.1 44.2 %reduce-scatter.2.cloned.1.call-done = bf16[1,256,1024]{2,1,0:T(8,128)(2,1)} async-done(((bf16[4,256,1024]{2,1,0:T(8,128)(2,1)}), bf16[1,256,1024]{2,1,0:T(8,128)(2,1)}) %reduce-scatter.2.cloned.1.call-update) | async-done | bytes 524304 | tf_op jit(solution)/shard_map/reduce_scatter | solution.py:390
  (58 shorter events, 0.3 us)
Async XLA Ops:
  6.5 186.8 %reduce-scatter.2.cloned.1.call-start = ((), (), s32[]{:S(2)}) async-start(), calls=%async_computation.1 | async-start | bytes 2621440 | tf_op jit(solution)/shard_map/reduce_scatter | solution.py:390
  6.5 43.6 %collective-permute-start.9 = (s32[256]{0:T(256)}, s32[256]{0:T(256)S(1)}, u32[]{:S(2)}, u32[]{:S(2)}) collective-permute-start(s32[256]{0:T(256)} %param.14), channel_id=1, source_target_pairs={{0,8},{4,12},{8,0},{12,4},{1,9},{5,13},{9,1},{13,5},{2,10},{6,14},... | collective-permute-start | bytes 3080 | tf_op jit(solution)/shard_map/ppermute | solution.py:325
  9.5 64.9 %collective-permute-start.10 = (s32[256]{0:T(256)}, s32[256]{0:T(256)S(1)}, u32[]{:S(2)}, u32[]{:S(2)}) collective-permute-start(s32[256]{0:T(256)} %param.14), channel_id=1, source_target_pairs={{0,4},{4,0},{8,12},{12,8},{1,5},{5,1},{9,13},{13,9},{2,6},{6,2},{1... | collective-permute-start | bytes 3080 | tf_op jit(solution)/shard_map/ppermute | solution.py:328
  11.8 16.5 %collective-permute-start = (bf16[256,1024]{1,0:T(8,128)(2,1)}, bf16[256,1024]{1,0:T(8,128)(2,1)}, u32[]{:S(2)}, u32[]{:S(2)}) collective-permute-start(bf16[256,1024]{1,0:T(8,128)(2,1)} %get-tuple-element.87), channel_id=1, source_target_pairs={{0,1},{1,2},{2,3},{3,0},{4,5},{5,6},{6,7},{7,4},{8,9},{9,10},{10,1... | collective-permute-start | bytes 1572872 | tf_op jit(solution)/shard_map/ppermute | solution.py:378
  28.3 15.7 %collective-permute-start.1 = (bf16[256,1024]{1,0:T(8,128)(2,1)}, bf16[256,1024]{1,0:T(8,128)(2,1)}, u32[]{:S(2)}, u32[]{:S(2)}) collective-permute-start(bf16[256,1024]{1,0:T(8,128)(2,1)} %collective-permute-done.x_ref), channel_id=1, source_target_pairs={{0,1},{1,2},{2,3},{3,0},{4,5},{5,6},{6,7},{7,4},{8,9},{9,10},{10,1... | collective-permute-start | bytes 1572872 | tf_op jit(solution)/shard_map/ppermute | solution.py:378
  28.3 3.8 %copy-start.13 = (bf16[4,4096]{1,0:T(4,128)(2,1)S(1)}, bf16[4,4096]{1,0:T(4,128)(2,1)}, u32[]{:S(2)}) copy-start(bf16[4,4096]{1,0:T(4,128)(2,1)} %param.17) | copy-start | bytes 98308
  32.7 9.1 %copy-start.15 = (s32[128]{0:T(128)S(1)}, s32[128]{0:T(128)}, u32[]{:S(2)}) copy-start(s32[128]{0:T(128)} %param.15) | copy-start | bytes 1540
  32.7 9.5 %copy-start.16 = (s32[128]{0:T(128)S(1)}, s32[128]{0:T(128)}, u32[]{:S(2)}) copy-start(s32[128]{0:T(128)} %param.16) | copy-start | bytes 1540
  43.9 5.1 %copy-start.14 = (s32[256]{0:T(256)S(1)}, s32[256]{0:T(256)}, u32[]{:S(2)}) copy-start(s32[256]{0:T(256)} %param.14) | copy-start | bytes 3076
  43.9 5.9 %slice-start = ((f32[16,1536]{1,0:T(8,128)}), f32[4,1536]{1,0:T(4,128)S(1)}, s32[]{:S(2)}) async-start(f32[16,1536]{1,0:T(8,128)} %embed_project.1.refs_3_.refs_4_.refs_5_), calls=%async_computation.2 | async-start | bytes 49152 | tf_op jit(solution)/shard_map/slice | solution.py:343
  43.9 15.7 %copy-start.9 = (bf16[256,1024]{1,0:T(8,128)(2,1)S(1)}, bf16[256,1024]{1,0:T(8,128)(2,1)}, u32[]{:S(2)}) copy-start(bf16[256,1024]{1,0:T(8,128)(2,1)} %get-tuple-element.54) | copy-start | bytes 1572868
  44.0 15.6 %collective-permute-start.2 = (bf16[256,1024]{1,0:T(8,128)(2,1)}, bf16[256,1024]{1,0:T(8,128)(2,1)S(1)}, u32[]{:S(2)}, u32[]{:S(2)}) collective-permute-start(bf16[256,1024]{1,0:T(8,128)(2,1)} %collective-permute-done.1.x_ref), channel_id=1, source_target_pairs={{0,1},{1,2},{2,3},{3,0},{4,5},{5,6},{6,7},{7,4},{8,9},{9,10},{10,1... | collective-permute-start | bytes 1572872 | tf_op jit(solution)/shard_map/ppermute | solution.py:378
  50.2 35.3 %collective-permute-start.11 = (s32[256]{0:T(256)S(1)}, s32[256]{0:T(256)S(1)}, u32[]{:S(2)}, u32[]{:S(2)}) collective-permute-start(s32[256]{0:T(256)S(1)} %collective-permute-done.9), channel_id=1, source_target_pairs={{0,4},{4,0},{8,12},{12,8},{1,5},{5,1},{9,13},{13,9},{2,6},{6,2},{1... | collective-permute-start | bytes 3080 | tf_op jit(solution)/shard_map/ppermute | solution.py:328
  59.6 4.3 %copy-start.2 = (bf16[256,1024]{1,0:T(8,128)(2,1)}, bf16[256,1024]{1,0:T(8,128)(2,1)S(1)}, u32[]{:S(2)}) copy-start(bf16[256,1024]{1,0:T(8,128)(2,1)S(1)} %collective-permute-done.2.x_ref) | copy-start | bytes 1572868
  59.6 14.5 %collective-permute-start.3 = (bf16[256,1024]{1,0:T(8,128)(2,1)S(1)}, bf16[256,1024]{1,0:T(8,128)(2,1)S(1)}, u32[]{:S(2)}, u32[]{:S(2)}) collective-permute-start(bf16[256,1024]{1,0:T(8,128)(2,1)S(1)} %copy-done.9), channel_id=1, source_target_pairs={{0,1},{1,2},{2,3},{3,0},{4,5},{5,6},{6,7},{7,4},{8,9},{9,10},{10,1... | collective-permute-start | bytes 1572872 | tf_op jit(solution)/shard_map/ppermute | solution.py:378
  72.5 13.0 %collective-permute-start.12 = (bf16[2,256,512]{2,1,0:T(8,128)(2,1)}, bf16[2,256,512]{2,1,0:T(8,128)(2,1)S(1)}, u32[]{:S(2)}, u32[]{:S(2)}) collective-permute-start(bf16[2,256,512]{2,1,0:T(8,128)(2,1)} %get-tuple-element.78.refs_4_), channel_id=1, source_target_pairs={{0,8},{4,12},{8,0},{12,4},{1,9},{5,13},{9,1},{13,5},{2,10},{6,14},... | collective-permute-start | bytes 1572872 | tf_op jit(solution)/shard_map/ppermute | solution.py:325
  74.2 14.9 %copy-start.3 = (bf16[256,1024]{1,0:T(8,128)(2,1)}, bf16[256,1024]{1,0:T(8,128)(2,1)S(1)}, u32[]{:S(2)}) copy-start(bf16[256,1024]{1,0:T(8,128)(2,1)S(1)} %collective-permute-done.3.x_ref) | copy-start | bytes 1572868
  74.2 14.1 %collective-permute-start.4 = (bf16[256,1024]{1,0:T(8,128)(2,1)S(1)}, bf16[256,1024]{1,0:T(8,128)(2,1)S(1)}, u32[]{:S(2)}, u32[]{:S(2)}) collective-permute-start(bf16[256,1024]{1,0:T(8,128)(2,1)S(1)} %collective-permute-done.3.x_ref), channel_id=1, source_target_pairs={{0,1},{1,2},{2,3},{3,0},{4,5},{5,6},{6,7},{7,4},{8,9},{9,10},{10,1... | collective-permute-start | bytes 1572872 | tf_op jit(solution)/shard_map/ppermute | solution.py:378
  75.3 22.1 %collective-permute-start.13 = (bf16[2,256,512]{2,1,0:T(8,128)(2,1)}, bf16[2,256,512]{2,1,0:T(8,128)(2,1)S(1)}, u32[]{:S(2)}, u32[]{:S(2)}) collective-permute-start(bf16[2,256,512]{2,1,0:T(8,128)(2,1)} %get-tuple-element.78.refs_4_), channel_id=1, source_target_pairs={{0,4},{4,0},{8,12},{12,8},{1,5},{5,1},{9,13},{13,9},{2,6},{6,2},{1... | collective-permute-start | bytes 1572872 | tf_op jit(solution)/shard_map/ppermute | solution.py:328
  85.5 7.7 %copy-start.4 = (bf16[2,256,512]{2,1,0:T(8,128)(2,1)}, bf16[2,256,512]{2,1,0:T(8,128)(2,1)S(1)}, u32[]{:S(2)}) copy-start(bf16[2,256,512]{2,1,0:T(8,128)(2,1)S(1)} %collective-permute-done.12.refs_5_) | copy-start | bytes 1572868
  85.5 11.9 %collective-permute-start.14 = (bf16[2,256,512]{2,1,0:T(8,128)(2,1)S(1)}, bf16[2,256,512]{2,1,0:T(8,128)(2,1)S(1)}, u32[]{:S(2)}, u32[]{:S(2)}) collective-permute-start(bf16[2,256,512]{2,1,0:T(8,128)(2,1)S(1)} %collective-permute-done.12.refs_5_), channel_id=1, source_target_pairs={{0,4},{4,0},{8,12},{12,8},{1,5},{5,1},{9,13},{13,9},{2,6},{6,2},{1... | collective-permute-start | bytes 1572872 | tf_op jit(solution)/shard_map/ppermute | solution.py:328
  88.3 4.9 %copy-start.5 = (bf16[256,1024]{1,0:T(8,128)(2,1)}, bf16[256,1024]{1,0:T(8,128)(2,1)S(1)}, u32[]{:S(2)}) copy-start(bf16[256,1024]{1,0:T(8,128)(2,1)S(1)} %collective-permute-done.4.x_ref) | copy-start | bytes 1572868
  88.3 15.7 %collective-permute-start.5 = (bf16[256,1024]{1,0:T(8,128)(2,1)S(1)}, bf16[256,1024]{1,0:T(8,128)(2,1)S(1)}, u32[]{:S(2)}, u32[]{:S(2)}) collective-permute-start(bf16[256,1024]{1,0:T(8,128)(2,1)S(1)} %collective-permute-done.4.x_ref), channel_id=1, source_target_pairs={{0,1},{1,2},{2,3},{3,0},{4,5},{5,6},{6,7},{7,4},{8,9},{9,10},{10,1... | collective-permute-start | bytes 1572872 | tf_op jit(solution)/shard_map/ppermute | solution.py:378
  97.3 6.6 %copy-start = (f32[16,1536]{1,0:T(8,128)S(1)}, f32[16,1536]{1,0:T(8,128)}, u32[]{:S(2)}) copy-start(f32[16,1536]{1,0:T(8,128)} %embed_project.1.refs_3_.refs_4_.refs_5_) | copy-start | bytes 294916
  97.4 0.8 copy-start.6
  97.4 1.0 copy-start.8
  103.9 0.6 copy-start.1
  103.9 0.8 copy-start.7
  109.2 18.9 %collective-permute-start.6 = (bf16[2,256,512]{2,1,0:T(8,128)(2,1)}, bf16[2,256,512]{2,1,0:T(8,128)(2,1)S(1)}, u32[]{:S(2)}, u32[]{:S(2)}) collective-permute-start(bf16[2,256,512]{2,1,0:T(8,128)(2,1)} %get-tuple-element.66.refs_4_), channel_id=1, source_target_pairs={{0,8},{4,12},{8,0},{12,4},{1,9},{5,13},{9,1},{13,5},{2,10},{6,14},... | collective-permute-start | bytes 1572872 | tf_op jit(solution)/shard_map/ppermute | solution.py:325
  115.6 13.8 %collective-permute-start.7 = (bf16[2,256,512]{2,1,0:T(8,128)(2,1)}, bf16[2,256,512]{2,1,0:T(8,128)(2,1)S(1)}, u32[]{:S(2)}, u32[]{:S(2)}) collective-permute-start(bf16[2,256,512]{2,1,0:T(8,128)(2,1)} %get-tuple-element.66.refs_4_), channel_id=1, source_target_pairs={{0,4},{4,0},{8,12},{12,8},{1,5},{5,1},{9,13},{13,9},{2,6},{6,2},{1... | collective-permute-start | bytes 1572872 | tf_op jit(solution)/shard_map/ppermute | solution.py:328
  128.1 1.9 copy-start.10
  128.1 1.9 collective-permute-start.8
  129.4 0.8 copy-start.11
  130.0 0.8 copy-start.12
Sparse Core Ops, SparseCore 0:
  149.2 44.0 reduce-scatter.1

commit v3 on v1

v3 whole, which is shorter than its diff:
```python
import functools
import math

import jax
import jax.numpy as jnp
from jax import lax
from jax.experimental import pallas as pl
from jax.experimental.pallas import tpu as pltpu
from jax.sharding import PartitionSpec as P

HEAD_DIM = 128
BASES = 4
CODES = 16
SUM_CODE = 8
ROPE_BASE = 10000.0
NEG_FILL = -1e30
COST_CUT = 64
SCORE_SCALE = math.log2(math.e) / math.sqrt(HEAD_DIM)
VMEM_LIMIT = 56 * 1024 * 1024
F32 = jnp.float32
BF16 = jnp.bfloat16


def params():
    return pltpu.CompilerParams(vmem_limit_bytes=VMEM_LIMIT)


def cost(flops, moved, exps=0):
    return pl.CostEstimate(
        flops=flops // COST_CUT, bytes_accessed=moved // COST_CUT, transcendentals=exps // COST_CUT
    )


def dot(left, right):
    return jnp.dot(left, right, preferred_element_type=F32)


def rope_tables(positions):
    half = HEAD_DIM // 2
    freq = jnp.power(ROPE_BASE, -jnp.arange(half, dtype=F32) * 2.0 / HEAD_DIM)
    angle = positions[:, None] * freq[None, :]
    cos, sin = jnp.cos(angle), jnp.sin(angle)
    return jnp.concatenate([cos, cos], axis=1), jnp.concatenate([-sin, sin], axis=1)


def swapped(value):
    return pltpu.roll(value, HEAD_DIM // 2, axis=1)


def turned(value, cos, sin):
    return value * cos + swapped(value) * sin


def code_table(rows):
    high = rows.astype(BF16)
    low = (rows - high.astype(F32)).astype(BF16)
    at = lax.broadcasted_iota(jnp.int32, rows.shape, 0)
    return jnp.where(at < BASES, high.astype(F32), low.astype(F32)).astype(BF16)


def read_rows(refs):
    parts = [ref[...].reshape(ref.shape[-2:]) for ref in refs]
    return parts[0] if len(parts) == 1 else jnp.concatenate(parts, axis=0)


def x_spec(x, strand):
    if x.ndim == 3:
        return pl.BlockSpec((1, *x.shape[1:]), lambda j, s: (strand, 0, 0))
    return pl.BlockSpec(x.shape, lambda j, s: (0, 0))


def slab_kernel(slab_parts, with_embed, has_total, scalars, *refs):
    del scalars
    sums = [None] * (6 if with_embed else 3)

    def add(index, item):
        sums[index] = item if sums[index] is None else sums[index] + item

    for parts in slab_parts:
        x_refs, refs = refs[:parts], refs[parts:]
        weights, refs = refs[:3], refs[3:]
        rows = read_rows(x_refs)
        if with_embed:
            embed, refs = refs[0][...], refs[1:]
        for index, weight in enumerate(weights):
            add(index, dot(rows, weight[...]))
            if with_embed:
                add(3 + index, dot(embed, weight[...]))
    if has_total:
        for index in range(len(sums)):
            sums[index] = refs[index][...] + sums[index]
        refs = refs[len(sums) :]
    for ref, item in zip(refs, sums):
        ref[...] = item


def slab_sums(slabs, scalars, strand, weights, embed=None, total=None):
    width = weights[0].shape[1]
    cols = min(2 * HEAD_DIM, width)
    tile = slabs[0][0].shape[-1]
    rows = sum(x.shape[-2] for x in slabs[0])
    in_specs, operands = [], []
    for index, parts in enumerate(slabs):
        in_specs += [x_spec(x, strand) for x in parts]
        in_specs += [pl.BlockSpec((tile, cols), lambda j, s, index=index: (s[index], j))] * 3
        operands += [*parts, *weights]
        if embed is not None:
            in_specs.append(pl.BlockSpec((CODES, tile), lambda j, s, index=index: (0, s[index])))
            operands.append(embed)
    heights = [rows] * 3 + ([CODES] * 3 if embed is not None else [])
    sum_specs = [pl.BlockSpec((height, cols), lambda j, s: (0, j)) for height in heights]
    aliases = {}
    if total is not None:
        aliases = {1 + len(operands) + index: index for index in range(len(heights))}
        in_specs += sum_specs
        operands += total
    return pl.pallas_call(
        functools.partial(
            slab_kernel, [len(parts) for parts in slabs], embed is not None, total is not None
        ),
        grid_spec=pltpu.PrefetchScalarGridSpec(
            num_scalar_prefetch=1,
            grid=(width // cols,),
            in_specs=in_specs,
            out_specs=sum_specs,
        ),
        out_shape=[jax.ShapeDtypeStruct((height, width), F32) for height in heights],
        input_output_aliases=aliases,
        compiler_params=params(),
        cost_estimate=cost(
            6 * rows * tile * width * len(slabs), 6 * tile * width * len(slabs) + 20 * rows * width
        ),
        name="slab_sums",
    )(scalars, *operands)


def finish_kv_kernel(parts, with_embed, scalars, *refs):
    del scalars
    x_refs, refs = refs[:parts], refs[parts:]
    (wk_ref, wv_ref, ksum_ref, vsum_ref, cos_ref, sin_ref), refs = refs[:6], refs[6:]
    if with_embed:
        (embed_ref, ek_ref, ev_ref), refs = refs[:3], refs[3:]
    kv_ref = refs[0]
    rows = read_rows(x_refs)
    cos, sin = cos_ref[...], sin_ref[...]
    key = ksum_ref[...] + dot(rows, wk_ref[...])
    for start in range(0, key.shape[1], HEAD_DIM):
        cols = slice(start, start + HEAD_DIM)
        kv_ref[0, :, cols] = turned(key[:, cols], cos, sin).astype(BF16)
    kv_ref[1] = (vsum_ref[...] + dot(rows, wv_ref[...])).astype(BF16)
    if with_embed:
        _, table_ref, swapped_ref, ev_out = refs
        embed = embed_ref[...]
        ek = ek_ref[...] + dot(embed, wk_ref[...])
        table_ref[...] = code_table(ek)
        for start in range(0, key.shape[1], HEAD_DIM):
            cols = slice(start, start + HEAD_DIM)
            swapped_ref[:, cols] = code_table(swapped(ek[:, cols]))
        ev_out[...] = ev_ref[...] + dot(embed, wv_ref[...])


def finish_kv(part, cols, x_parts, scalars, wk, wv, ksum, vsum, cos, sin, embed_parts):
    tile = x_parts[0].shape[-1]
    rows = ksum.shape[0]

    def at(height):
        return pl.BlockSpec((height, cols), lambda j, s: (0, part))

    weight_spec = pl.BlockSpec((tile, cols), lambda j, s: (s[0], part))
    table_spec = pl.BlockSpec((rows, HEAD_DIM), lambda j, s: (s[1], 0))
    in_specs = [x_spec(x, 0) for x in x_parts]
    in_specs += [weight_spec, weight_spec, at(rows), at(rows), table_spec, table_spec]
    operands = [*x_parts, wk, wv, ksum, vsum, cos, sin]
    out_specs = [pl.BlockSpec((2, rows, cols), lambda j, s: (0, 0, 0))]
    out_shape = [jax.ShapeDtypeStruct((2, rows, cols), BF16)]
    if embed_parts is not None:
        in_specs += [
            pl.BlockSpec((CODES, tile), lambda j, s: (0, s[0])),
            at(CODES),
            at(CODES),
        ]
        operands += embed_parts
        out_specs += [pl.BlockSpec((CODES, cols), lambda j, s: (0, 0))] * 3
        out_shape += [jax.ShapeDtypeStruct((CODES, cols), kind) for kind in (BF16, BF16, F32)]
    return pl.pallas_call(
        functools.partial(finish_kv_kernel, len(x_parts), embed_parts is not None),
        grid_spec=pltpu.PrefetchScalarGridSpec(
            num_scalar_prefetch=1,
            grid=(1,),
            in_specs=in_specs,
            out_specs=out_specs,
        ),
        out_shape=out_shape,
        compiler_params=params(),
        cost_estimate=cost(4 * rows * tile * cols, 4 * tile * cols + 14 * rows * cols),
        name="finish_kv",
    )(scalars, *operands)


def finish_q_kernel(parts, with_embed, scalars, *refs):
    del scalars
    x_refs, refs = refs[:parts], refs[parts:]
    (wq_ref, qsum_ref, cos_ref, sin_ref, codes_ref, eq_ref), refs = refs[:6], refs[6:]
    eq = eq_ref[...]
    if with_embed:
        embed_ref, q_ref, qm_ref, eq_out = refs
        eq = eq + dot(embed_ref[...], wq_ref[...])
        eq_out[...] = eq
    else:
        q_ref, qm_ref = refs
    cos, sin = cos_ref[...] * SCORE_SCALE, sin_ref[...] * SCORE_SCALE
    query = qsum_ref[...] + dot(read_rows(x_refs), wq_ref[...])
    mutant = query + dot(codes_ref[0], code_table(eq))
    for start in range(0, query.shape[1], HEAD_DIM):
        cols = slice(start, start + HEAD_DIM)
        q_ref[:, cols] = turned(query[:, cols], cos, sin).astype(BF16)
        qm_ref[:, cols] = turned(mutant[:, cols], cos, sin).astype(BF16)


def finish_q(cols, x_parts, scalars, wq, qsum, cos, sin, codes, eq, embed):
    tile = x_parts[0].shape[-1]
    rows, width = qsum.shape

    def at(height):
        return pl.BlockSpec((height, cols), lambda j, s: (0, j))

    table_spec = pl.BlockSpec((rows, HEAD_DIM), lambda j, s: (s[1], 0))
    in_specs = [x_spec(x, 0) for x in x_parts]
    in_specs += [
        pl.BlockSpec((tile, cols), lambda j, s: (s[0], j)),
        at(rows),
        table_spec,
        table_spec,
        pl.BlockSpec((1, rows, CODES), lambda j, s: (0, 0, 0)),
        at(CODES),
    ]
    operands = [*x_parts, wq, qsum, cos, sin, codes, eq]
    out_specs = [at(rows), at(rows)]
    out_shape = [jax.ShapeDtypeStruct((rows, width), BF16)] * 2
    if embed is not None:
        in_specs.append(pl.BlockSpec((CODES, tile), lambda j, s: (0, s[0])))
        operands.append(embed)
        out_specs.append(at(CODES))
        out_shape.append(jax.ShapeDtypeStruct((CODES, width), F32))
    return pl.pallas_call(
        functools.partial(finish_q_kernel, len(x_parts), embed is not None),
        grid_spec=pltpu.PrefetchScalarGridSpec(
            num_scalar_prefetch=1,
            grid=(width // cols,),
            in_specs=in_specs,
            out_specs=out_specs,
        ),
        out_shape=out_shape,
        compiler_params=params(),
        cost_estimate=cost(2 * rows * tile * width, 2 * tile * width + 8 * rows * width),
        name="finish_q",
    )(scalars, *operands)


def attend_kernel(forward, block_count, has_before, *refs):
    (ids_ref, q_ref, qm_ref, table_ref, swapped_ref, ev_ref), refs = refs[:6], refs[6:]
    (codes_ref, codes_t_ref, cos_ref, sin_ref), refs = refs[:4], refs[4:]
    kv_refs, refs = refs[:block_count], refs[block_count:]
    before_ref = None
    if has_before:
        before_ref, refs = refs[0], refs[1:]
    out_ref, top, acc = refs
    rows, cols_here = q_ref.shape
    heads = cols_here // HEAD_DIM
    tall = HEAD_DIM + CODES
    my_id = ids_ref[0]

    def block(index):
        kv_ref = kv_refs[index]
        first = pl.multiple_of(ids_ref[index] * rows, rows)
        cos = cos_ref[pl.ds(first, rows), :]
        sin = sin_ref[pl.ds(first, rows), :]
        codes, codes_t = codes_ref[index], codes_t_ref[index]
        change = dot(codes, table_ref[...])
        change_swapped = dot(codes, swapped_ref[...])
        if index == 0:
            key_at = lax.broadcasted_iota(jnp.int32, (rows, rows), 0)
            query_at = lax.broadcasted_iota(jnp.int32, (rows, rows), 1)
            seen = key_at <= query_at if forward else key_at >= query_at
        for head in range(heads):
            cols = slice(head * HEAD_DIM, (head + 1) * HEAD_DIM)
            key = kv_ref[0, :, cols]
            mutant_key = (
                key.astype(F32) + change[:, cols] * cos + change_swapped[:, cols] * sin
            ).astype(BF16)
            values_t = jnp.concatenate([kv_ref[1, :, cols].T, codes_t], axis=0)
            for kind, (query, keys) in enumerate(
                ((q_ref[:, cols], key), (qm_ref[:, cols], mutant_key))
            ):
                unit = 2 * head + kind
                area = slice(unit * tall, (unit + 1) * tall)
                scores = lax.dot_general(
                    keys, query, (((1,), (1,)), ((), ())), preferred_element_type=F32
                )
                if index == 0:
                    scores = jnp.where(seen, scores, NEG_FILL)
                peak = jnp.max(scores, axis=0, keepdims=True)
                if index:
                    old_peak = top[unit : unit + 1, :]
                    peak = jnp.maximum(old_peak, peak)
                    fade = jnp.exp2(old_peak - peak)
                weights = jnp.exp2(scores - peak).astype(BF16)
                product = dot(values_t, weights)
                if index:
                    product = acc[area, :] * fade + product
                top[unit : unit + 1, :] = peak
                acc[area, :] = product

    for index in range(block_count):
        if index == 0:
            block(0)
        else:
            other = ids_ref[index]
            pl.when(other < my_id if forward else other > my_id)(functools.partial(block, index))

    code_at = lax.broadcasted_iota(jnp.int32, (CODES, HEAD_DIM), 0)
    for head in range(heads):
        cols = slice(head * HEAD_DIM, (head + 1) * HEAD_DIM)
        ev = jnp.where(code_at < BASES, ev_ref[:, cols], 0.0)
        parts = []
        for kind in range(2):
            start = (2 * head + kind) * tall
            value = acc[start : start + HEAD_DIM, :]
            tail = acc[start + HEAD_DIM : start + tall, :]
            if kind:
                value = value + lax.dot_general(
                    ev,
                    tail,
                    (((0,), (0,)), ((), ())),
                    precision=lax.Precision.HIGHEST,
                    preferred_element_type=F32,
                )
            parts.append(value / tail[SUM_CODE : SUM_CODE + 1, :])
        difference = (parts[0] - parts[1]).T
        if has_before:
            out_ref[:, cols] = (0.5 * (before_ref[:, cols] + difference)).astype(BF16)
        else:
            out_ref[:, cols] = difference


def attend(forward, part, cols, ids, q, qm, tables, codes, codes_t, cos, sin, kv_blocks, before):
    rows = q.shape[0]
    heads = cols // HEAD_DIM
    vmem = pl.BlockSpec(memory_space=pltpu.VMEM)
    row_spec = pl.BlockSpec((rows, cols), lambda j: (0, part))

    def whole(item):
        return pl.BlockSpec(item.shape, lambda j: (0,) * item.ndim)

    operands = [*tables, codes, codes_t, cos, sin, *kv_blocks]
    if before is not None:
        operands.append(before)
    count = len(kv_blocks)
    return pl.pallas_call(
        functools.partial(attend_kernel, forward, count, before is not None),
        grid=(1,),
        in_specs=[pl.BlockSpec(memory_space=pltpu.SMEM), row_spec, row_spec]
        + [whole(item) for item in operands],
        out_specs=pl.BlockSpec((rows, cols), lambda j: (0, 0)),
        out_shape=jax.ShapeDtypeStruct((rows, cols), F32 if before is None else BF16),
        scratch_shapes=[
            pltpu.VMEM((max(2 * heads, 8), rows), F32),
            pltpu.VMEM((2 * heads * (HEAD_DIM + CODES), rows), F32),
        ],
        compiler_params=params(),
        cost_estimate=cost(
            8 * rows * rows * count * cols,
            4 * count * rows * cols,
            2 * rows * rows * count * heads,
        ),
        name="attend_forward" if forward else "attend_reverse",
    )(ids, q, qm, *operands)


def out_kernel(has_before, scalars, rows_ref, weight_ref, *refs):
    del scalars
    if has_before:
        before_ref, out_ref, acc = refs
    else:
        out_ref, acc = refs
    step = pl.program_id(0)

    @pl.when(step == 0)
    def _():
        acc[...] = before_ref[...] if has_before else jnp.zeros_like(acc)

    acc[...] += dot(rows_ref[0], weight_ref[0])

    @pl.when(step == pl.num_programs(0) - 1)
    def _():
        out_ref[...] = acc[...].astype(out_ref.dtype)


def out_project(part, gathered, weight, slots, last, before):
    slabs, rows, cols = gathered.shape
    width = weight.shape[2]
    whole = pl.BlockSpec((rows, width), lambda i, s: (0, 0))
    in_specs = [
        pl.BlockSpec((1, rows, cols), lambda i, s: (i, 0, 0)),
        pl.BlockSpec((1, cols, width), lambda i, s: (s[i], part, 0)),
    ]
    operands = [gathered, weight]
    if before is not None:
        in_specs.append(whole)
        operands.append(before)
    return pl.pallas_call(
        functools.partial(out_kernel, before is not None),
        grid_spec=pltpu.PrefetchScalarGridSpec(
            num_scalar_prefetch=1,
            grid=(slabs,),
            in_specs=in_specs,
            out_specs=whole,
            scratch_shapes=[pltpu.VMEM((rows, width), F32)],
        ),
        out_shape=jax.ShapeDtypeStruct((rows, width), BF16 if last else F32),
        compiler_params=params(),
        cost_estimate=cost(2 * slabs * rows * cols * width, 2 * slabs * cols * width),
        name="out_project",
    )(slots, *operands)


def shards(
    hidden,
    strand_bases,
    variant_sites,
    base_shift,
    base_embed,
    query_weight,
    key_weight,
    value_weight,
    out_weight,
):
    rows, tile = hidden.shape[1:]
    ctx = lax.axis_size("ctx")
    slabs = lax.axis_size("head")
    me = lax.axis_index("ctx")
    head = lax.axis_index("head")
    window = rows * ctx
    width = query_weight.shape[1]
    cores = 2 if ctx % 2 == 0 else 1
    chains = 2 if rows % 32 == 0 else 1
    parts = 2 if width % (2 * HEAD_DIM) == 0 else 1
    cols = width // parts
    weights = (query_weight, key_weight, value_weight)
    my_row = me.astype(jnp.int32)
    ring = [(i, (i + 1) % slabs) for i in range(slabs)]
    slab_at = [((head - step) % slabs).astype(jnp.int32) for step in range(slabs)]

    def tie(items, *first):
        return lax.optimization_barrier((items, first))[0]

    def ctx_far(block):
        return [
            lax.ppermute(block, "ctx", [(i, (i + cores * shift) % ctx) for i in range(ctx)])
            for shift in range(1, ctx // cores)
        ]

    def ctx_swap(blocks):
        if cores == 1:
            return []
        return [lax.ppermute(item, "ctx", [(i, i ^ 1) for i in range(ctx)]) for item in blocks]

    def hop(blocks):
        return [lax.ppermute(block, "head", ring) for block in blocks]

    near = [(me - cores * shift) % ctx for shift in range(ctx // cores)]
    if cores == 2:
        near = near + [item ^ 1 for item in near]
    ids = jnp.stack(near).astype(jnp.int32)

    span = rows // chains

    def own_chains(source, strand):
        return [source[strand, chain * span : (chain + 1) * span] for chain in range(chains)]

    moving = hop(own_chains(hidden, 0))

    bases = [strand_bases] + ctx_far(strand_bases)
    bases = jnp.stack(bases + ctx_swap(bases))
    positions = ids[:, None] * rows + jnp.arange(rows, dtype=jnp.int32)[None, :]
    match = positions[:, :, None] == variant_sites[None, None, :]
    shifts = jnp.sum(jnp.where(match, base_shift[None, None, :], 0), axis=2)
    fresh = jnp.mod(bases + shifts, BASES)
    code_iota = jnp.arange(CODES, dtype=jnp.int32)

    def code_arrays(forward):
        want = code_iota % BASES
        want = want if forward else BASES - 1 - want

        def fill(old, new, want, at):
            codes = (new == want).astype(F32) - (old == want).astype(F32)
            codes = jnp.where(at < 2 * BASES, codes, (at == SUM_CODE).astype(F32))
            return codes.astype(BF16)

        return (
            fill(bases[:, :, None], fresh[:, :, None], want, code_iota),
            fill(bases[:, None, :], fresh[:, None, :], want[:, None], code_iota[:, None]),
        )

    embed = jnp.concatenate(
        [base_embed, base_embed, jnp.zeros((CODES - 2 * BASES, base_embed.shape[1]), BF16)]
    )
    window_iota = jnp.arange(window, dtype=jnp.int32)
    rope = [
        rope_tables(window_iota.astype(F32)),
        rope_tables((window - 1 - window_iota).astype(F32)),
    ]

    lanes = lax.axis_size("groups") * ctx
    piece_rows = width // lanes
    lane = lax.axis_index("groups") * ctx + me
    piece = lax.dynamic_slice_in_dim(tie(out_weight, rope, bases, moving), lane * piece_rows, piece_rows, 0)
    pieces = []
    for shift in range(slabs):
        target = (head + shift) % slabs
        item = lax.dynamic_slice_in_dim(piece, target * tile, tile, 1)
        if shift:
            item = lax.ppermute(
                item, "head", [(i, (i + shift) % slabs) for i in range(slabs)]
            )
        pieces.append(item)
    pieces = jnp.stack(pieces)
    out_slabs = lax.all_gather(pieces, ("groups", "ctx"), axis=1, tiled=True)
    out_slots = jnp.stack([(head - i) % slabs for i in range(slabs)]).astype(jnp.int32)

    code_sets = [code_arrays(True), code_arrays(False)]

    def add_slabs(strand, steps, total):
        return slab_sums(
            [[hidden] if step == 0 else arrived[strand][step - 1] for step in steps],
            jnp.stack([slab_at[step] for step in steps]),
            strand,
            weights,
            embed if strand == 0 else None,
            total,
        )

    def run_ring(strand, moving, early):
        total, waiting = None, [0]
        for step in range(1, slabs):
            arrived[strand].append(moving)
            if step < slabs - 1:
                if strand == 0 and early and step > 1:
                    early[0] = (early[0], total)
                first = early.pop(0) if early else None
                moving = hop([tie(block, first) for block in moving])
                waiting.append(step)
                total = add_slabs(strand, waiting, total)
                waiting = []
        if waiting:
            total = add_slabs(strand, waiting, total)
        return total

    def finish(strand, last, total, eq):
        first = strand == 0
        cos, sin = rope[strand]
        scalars = jnp.stack([slab_at[-1], my_row])
        own, far, made = [], [], []
        for part in range(parts):
            out = finish_kv(
                part,
                cols,
                last,
                scalars,
                key_weight,
                value_weight,
                total[1],
                total[2],
                cos,
                sin,
                [embed, total[4], total[5]] if first else None,
            )
            own.append(out[0])
            far.append(ctx_far(out[0]) if first else None)
            made.append(out[1:])
        out = finish_q(
            cols,
            last,
            scalars,
            query_weight,
            total[0],
            cos,
            sin,
            code_sets[strand][0],
            total[3] if first else eq,
            embed if first else None,
        )
        return own, far, made, out

    def spread_out(own, far):
        local = [own] + far
        return local + ctx_swap(local)

    def attend_all(strand, blocks, query, tables, before, ids):
        return [
            attend(
                strand == 0,
                part,
                cols,
                ids,
                query[0],
                query[1],
                tables[part],
                *code_sets[strand],
                *rope[strand],
                blocks[part],
                before[part],
            )
            for part in range(parts)
        ]

    arrived = [[], []]
    total = run_ring(0, moving, [None, (code_sets, pieces)])
    last = arrived[0][-1]
    cut = own_chains(tie(hidden, arrived[0][max(0, slabs - 3)]), 1)
    moving = hop([tie(block, item, total) for block, item in zip(cut, last)])
    own, far, tables, query = finish(0, last, total, None)
    eq = query[2]
    total = run_ring(1, moving, [(own, query)])
    blocks = [spread_out(item, item_far) for item, item_far in zip(own, far)]
    last = tie(arrived[1][-1], blocks)
    own_then, _, _, query_then = finish(1, last, total, eq)
    ids_then = tie(ids, own_then, query_then, out_slabs)
    before = attend_all(0, blocks, query, tables, [None] * parts, ids_then)
    far = [ctx_far(item) for item in own_then]
    blocks = []
    for part in range(parts):
        arriving = tie(far[part], before[: part + 1])
        blocks.append(spread_out(own_then[part], arriving))
    combined = attend_all(1, blocks, query_then, tables, before, ids)
    result = None
    for part in range(parts):
        gathered = lax.all_gather(combined[part], "head", axis=0, tiled=False)
        result = out_project(part, gathered, out_slabs, out_slots, part == parts - 1, result)
    return result


def solution(mesh):
    return jax.shard_map(
        shards,
        mesh=mesh,
        in_specs=(
            P(None, ("groups", "ctx"), "head"),
            P(("groups", "ctx")),
            P("groups"),
            P("groups"),
            P(),
            P(None, "head"),
            P(None, "head"),
            P(None, "head"),
            P("head", None),
        ),
        out_specs=P(("groups", "ctx"), "head"),
        check_vma=False,
    )
```

time: 195 us -> 211 us (1.082)
  waiting for transfers between devices: 117 us -> 41.4 us
  Pallas kernels: 33 us -> 79.5 us
  blocking collectives: 0 us -> 33.7 us
  starting transfers between devices: 7.05 us -> 23 us
  local copies, waits for them, and re-layouts: 17.8 us -> 6.37 us
  other arithmetic: 6.3 us -> 12.8 us
    all_gather x2 -> x1, waiting for transfers between devices: 48.2 us -> 0.02 us  [shards(): out_slabs = lax.all_gather(pieces, ('groups', 'ctx'), axis=1, tiled=True)]
    reduce_scatter x1 -> x0, waiting for transfers between devices: 42 us -> none  [shards(): return lax.psum_scatter(partial, 'head', scatter_dimension=0, tiled=True)[0]]
    pallas_call x4 -> x12, Pallas kernels: 18.7 us -> 54.1 us  [the longest x4 21.9 us: slab_sums(): pl.pallas_call(functools.partial(slab_kernel, [len(parts) for parts in sl...]
    all_gather x0 -> x2, blocking collectives: none -> 33.7 us  [shards(): gathered = lax.all_gather(combined[part], 'head', axis=0, tiled=False)]
    ppermute x9 -> x30, starting transfers between devices: 6.97 us -> 23 us  [the longest x12 8.66 us: hop(): return [lax.ppermute(block, 'head', ring) for block in blocks]]
    ppermute x9 -> x30, waiting for transfers between devices: 26.8 us -> 41.4 us  [the longest x12 30 us: hop(): return [lax.ppermute(block, 'head', ring) for block in blocks]]
    pallas_call x2 -> x4, Pallas kernels: 14.4 us -> 25.4 us  [attend(): pl.pallas_call(functools.partial(attend_kernel, forward, count, before is...]
    unnamed x30 -> x66, local copies, waits for them, and re-layouts: 14.4 us -> 3.65 us
  transfers between devices with their start and end apart: 12 -> 31, of which waited for: 7 -> 10; matrix products, arithmetic and copies ran while one was open for 4% -> 6% of each run, Pallas kernels for 6% -> 29%
where the time goes in v3:
time: 211 us
  Pallas kernels  79.5 us (38%)
  waiting for transfers between devices  41.4 us (20%)
  blocking collectives  33.7 us (16%)
  starting transfers between devices  23 us (11%)
  between operations  13.9 us (7%)
  other arithmetic  12.8 us (6%)
  local copies, waits for them, and re-layouts  6.37 us (3%)
    all_gather x2, blocking collectives, shards(): gathered = lax.all_gather(combined[part], 'head', axis=0, tiled=False)  33.7 us
    ppermute x12, waiting for transfers between devices, hop(): return [lax.ppermute(block, 'head', ring) for block in blocks]  30 us
    pallas_call x4, Pallas kernels, attend(): pl.pallas_call(functools.partial(attend_kernel, forward, count, before is...  25.4 us
    pallas_call x4, Pallas kernels, slab_sums(): pl.pallas_call(functools.partial(slab_kernel, [len(parts) for parts in sl...  21.9 us
    pallas_call x4, Pallas kernels, finish_kv(): pl.pallas_call(functools.partial(finish_kv_kernel, len(x_parts), embed_pa...  14.1 us
    ppermute x3, waiting for transfers between devices, shards(): lax.ppermute(item, 'head', [(i, (i + shift) % slabs) for i in range(slabs)])  10.2 us
    pallas_call x2, Pallas kernels, out_project(): pl.pallas_call(functools.partial(out_kernel, before is not None), grid_sp...  10.1 us
    ppermute x12, starting transfers between devices, hop(): return [lax.ppermute(block, 'head', ring) for block in blocks]  8.66 us
  transfers between devices with their start and end apart: 31, of which 10 were waited for; matrix products, arithmetic and copies ran while one was open for 6% of the time, Pallas kernels for 29%

profile of v3, /device:TPU:0, one launch (start us, length us, event | category | flops | bytes accessed | tf_op | source)
XLA Modules:
  0.0 210.7 jit_solution(9807231452362592592)
XLA Ops:
  6.5 3.0 %collective-permute-start.4 = (s32[256]{0:T(256)}, s32[256]{0:T(256)S(1)}, u32[]{:S(2)}, u32[]{:S(2)}) collective-permute-start(s32[256]{0:T(256)} %param.10), channel_id=1, source_target_pairs={{0,8},{4,12},{8,0},{12,4},{1,9},{5,13},{9,1},{13,5},{2,10},{6,14},... | collective-permute-start | bytes 3080 | tf_op jit(solution)/shard_map/ppermute | solution.py:459
  9.5 1.1 slice_bitcast_fusion.2
  10.6 1.6 collective-permute-start.2
  12.2 1.6 collective-permute-start
  14.5 3.7 %fusion.1 = (f32[1024,64]{1,0:T(8,128)S(1)}, f32[1024,64]{1,0:T(8,128)S(1)}, f32[1024,64]{1,0:T(8,128)S(1)}, f32[1024,64]{1,0:T(8,128)S(1)}, f32[1024,64]{1,0:T(8,128)S(1)}, /*index=5*/f32[1024,64]{1,0:T(8,128)S(1)}) fusion(f32[64]{0:T(128)S(1)} %multiply_power_fusion, f32[1024]{0:T(1024)S(1)} %subtract_convert_fusion, f32[1024]{0:T(1024)S(1)} %iota_convert_fusion), kind=kLoop, calls=%fused_computation.17 | loop fusion | flops 262144 | bytes 1581312 | tf_op jit(solution)/shard_map/neg | solution.py:43
  18.2 1.3 pad_maximum_fusion
  19.6 1.3 pad_maximum_fusion.2
  21.5 1.1 collective-permute-done.6
  22.6 4.2 %collective-permute-done.refs_5_ = bf16[128,1024]{1,0:T(8,128)(2,1)S(1)} collective-permute-done((bf16[128,1024]{1,0:T(8,128)(2,1)S(1)}, bf16[128,1024]{1,0:T(8,128)(2,1)S(1)}, u32[]{:S(2)}, u32[]{:S(2)}) %collective-permute-start) | collective-permute-done | bytes 262176 | tf_op jit(solution)/shard_map/ppermute | solution.py:469
  26.8 1.5 dynamic-slice_bitcast_fusion
  28.4 1.8 collective-permute-start.9
  30.2 1.0 collective-permute-start.7
  31.2 3.0 %collective-permute-done.9 = bf16[64,1024]{1,0:T(8,128)(2,1)S(1)} collective-permute-done((bf16[64,1024]{1,0:T(8,128)(2,1)S(1)}, bf16[64,1024]{1,0:T(8,128)(2,1)S(1)}, u32[]{:S(2)}, u32[]{:S(2)}) %collective-permute-start.9) | collective-permute-done | bytes 131104 | tf_op jit(solution)/shard_map/ppermute | solution.py:523
  34.2 7.3 %collective-permute-done.8 = bf16[64,1024]{1,0:T(8,128)(2,1)S(1)} collective-permute-done((bf16[64,1024]{1,0:T(8,128)(2,1)S(1)}, bf16[64,1024]{1,0:T(8,128)(2,1)S(1)}, u32[]{:S(2)}, u32[]{:S(2)}) %collective-permute-start.8) | collective-permute-done | bytes 131104 | tf_op jit(solution)/shard_map/ppermute | solution.py:523
  41.4 0.9 pad_maximum_fusion.4
  43.0 0.7 maximum_maximum_fusion.refs_4_.refs_10_.refs_5_.refs_8_
  44.3 2.5 %collective-permute-start.1 = (bf16[128,1024]{1,0:T(8,128)(2,1)S(1)}, bf16[128,1024]{1,0:T(8,128)(2,1)S(1)}, u32[]{:S(2)}, u32[]{:S(2)}) collective-permute-start(bf16[128,1024]{1,0:T(8,128)(2,1)S(1)} %collective-permute-done.refs_5_), channel_id=1, source_target_pairs={{0,1},{1,2},{2,3},{3,0},{4,5},{5,6},{6,7},{7,4},{8,9},{9,10},{10,1... | collective-permute-start | bytes 786440 | tf_op jit(solution)/shard_map/ppermute | solution.py:469
  47.5 1.2 select_convert_fusion
  48.7 7.0 %slab_sums.4 = (f32[256,512]{1,0:T(8,128)}, f32[256,512]{1,0:T(8,128)}, f32[256,512]{1,0:T(8,128)}, f32[16,512]{1,0:T(8,128)}, f32[16,512]{1,0:T(8,128)}, /*index=5*/f32[16,512]{1,0:T(8,128)}) custom-call(s32[2]{0:T(128)} %pad_add_fusion.4.scalars, bf16[2,256,1024]{2,1,0:T(8,128)(2,1)} %refs_0_.3, bf16[4096,512]{1,0:T(8,128)(2,1)} %refs_2_.17, ...), custom_call_target="tpu_custom_call" | custom-call | flops 25165824 | bytes 139264 | tf_op jit(solution)/shard_map/slab_sums/pallas_call | solution.py:117
  55.7 3.0 %collective-permute-done.1.refs_0_ = bf16[128,1024]{1,0:T(8,128)(2,1)S(1)} collective-permute-done((bf16[128,1024]{1,0:T(8,128)(2,1)S(1)}, bf16[128,1024]{1,0:T(8,128)(2,1)S(1)}, u32[]{:S(2)}, u32[]{:S(2)}) %collective-permute-start.1) | collective-permute-done | bytes 262176 | tf_op jit(solution)/shard_map/ppermute | solution.py:469
  58.7 1.2 collective-permute-start.12
  59.9 4.7 %slab_sums.5 = (f32[256,512]{1,0:T(8,128)}, f32[256,512]{1,0:T(8,128)}, f32[256,512]{1,0:T(8,128)}, f32[16,512]{1,0:T(8,128)}, f32[16,512]{1,0:T(8,128)}, /*index=5*/f32[16,512]{1,0:T(8,128)}) custom-call(s32[1]{0:T(128)} %bitcast.2.scalars, ...), custom_call_target="tpu_custom_call", output_to_operand_aliasing={{0}: (7, {}), {1}: (8, {}), {2}: (9, {}), {3}: (10, {}), {4... | custom-call | flops 12582912 | bytes 90112 | tf_op jit(solution)/shard_map/slab_sums/pallas_call | solution.py:117
  64.7 5.1 %collective-permute-done.10.refs_0_ = bf16[128,1024]{1,0:T(8,128)(2,1)S(1)} collective-permute-done((bf16[128,1024]{1,0:T(8,128)(2,1)S(1)}, bf16[128,1024]{1,0:T(8,128)(2,1)S(1)}, u32[]{:S(2)}, u32[]{:S(2)}) %collective-permute-start.10) | collective-permute-done | bytes 262176 | tf_op jit(solution)/shard_map/ppermute | solution.py:469
  69.7 5.6 %collective-permute-done.12.refs_1_ = bf16[128,1024]{1,0:T(8,128)(2,1)S(1)} collective-permute-done((bf16[128,1024]{1,0:T(8,128)(2,1)S(1)}, bf16[128,1024]{1,0:T(8,128)(2,1)S(1)}, u32[]{:S(2)}, u32[]{:S(2)}) %collective-permute-start.12) | collective-permute-done | bytes 262176 | tf_op jit(solution)/shard_map/ppermute | solution.py:469
  76.0 3.7 %finish_kv.4 = (bf16[2,256,256]{2,1,0:T(8,128)(2,1)}, bf16[16,256]{1,0:T(8,128)(2,1)}, bf16[16,256]{1,0:T(8,128)(2,1)}, f32[16,256]{1,0:T(8,128)}) custom-call(s32[2]{0:T(128)} %pad_add_fusion.3.scalars, bf16[128,1024]{1,0:T(8,128)(2,1)} %copy-done.1, bf16[128,1024]{1,0:T(8,128)(2,1)} %copy-done.2, bf16[4096,512]{1,0:T(8,128)(2,1)} %refs_2_.19, ...), custom_call_target="tpu_custom_call" | custom-call | flops 4194304 | bytes 30720 | tf_op jit(solution)/shard_map/finish_kv/pallas_call | solution.py:185
  80.3 3.6 %finish_kv.5 = (bf16[2,256,256]{2,1,0:T(8,128)(2,1)}, bf16[16,256]{1,0:T(8,128)(2,1)}, bf16[16,256]{1,0:T(8,128)(2,1)}, f32[16,256]{1,0:T(8,128)}) custom-call(s32[2]{0:T(128)} %pad_add_fusion.3.scalars, bf16[128,1024]{1,0:T(8,128)(2,1)} %copy-done.1, bf16[128,1024]{1,0:T(8,128)(2,1)} %copy-done.2, bf16[4096,512]{1,0:T(8,128)(2,1)} %refs_2_.19, ...), custom_call_target="tpu_custom_call" | custom-call | flops 4194304 | bytes 30720 | tf_op jit(solution)/shard_map/finish_kv/pallas_call | solution.py:185
  83.9 1.5 collective-permute-start.21
  85.4 4.0 %finish_q.2 = (bf16[256,512]{1,0:T(8,128)(2,1)}, bf16[256,512]{1,0:T(8,128)(2,1)}, f32[16,512]{1,0:T(8,128)}) custom-call(s32[2]{0:T(128)} %pad_add_fusion.3.scalars, bf16[128,1024]{1,0:T(8,128)(2,1)} %copy-done.1, bf16[128,1024]{1,0:T(8,128)(2,1)} %copy-done.2, bf16[4096,512]{1,0:T(8,128)(2,1)} %refs_2_.17, f32[256,512]{1,0:T(8,128)} %get-tuple-element.58.refs_3_, ...), custom_call_target="tpu_custom_call" | custom-call | flops 4194304 | bytes 32768 | tf_op jit(solution)/shard_map/finish_q/pallas_call | solution.py:245
  90.8 6.9 %collective-permute-done.13.refs_0_ = bf16[128,1024]{1,0:T(8,128)(2,1)S(1)} collective-permute-done((bf16[128,1024]{1,0:T(8,128)(2,1)S(1)}, bf16[128,1024]{1,0:T(8,128)(2,1)S(1)}, u32[]{:S(2)}, u32[]{:S(2)}) %collective-permute-start.13) | collective-permute-done | bytes 262176 | tf_op jit(solution)/shard_map/ppermute | solution.py:469
  97.6 2.8 %collective-permute-done.16.refs_1_ = bf16[128,1024]{1,0:T(8,128)(2,1)S(1)} collective-permute-done((bf16[128,1024]{1,0:T(8,128)(2,1)S(1)}, bf16[128,1024]{1,0:T(8,128)(2,1)S(1)}, u32[]{:S(2)}, u32[]{:S(2)}) %collective-permute-start.16) | collective-permute-done | bytes 262176 | tf_op jit(solution)/shard_map/ppermute | solution.py:469
  101.0 6.1 %slab_sums.6 = (f32[256,512]{1,0:T(8,128)}, f32[256,512]{1,0:T(8,128)}, f32[256,512]{1,0:T(8,128)}) custom-call(s32[2]{0:T(128)} %pad_add_fusion.4.scalars, bf16[2,256,1024]{2,1,0:T(8,128)(2,1)} %refs_0_.3, bf16[4096,512]{1,0:T(8,128)(2,1)} %refs_2_.17, bf16[4096,512]{1,0:T(8,128)(2,1)} %refs_2_.19, bf16[4096,512]{1,0:T(8,128)(2,1)} %refs_3_.15, ...), custom_call_target="tpu_custom_call" | custom-call | flops 25165824 | bytes 139264 | tf_op jit(solution)/shard_map/slab_sums/pallas_call | solution.py:117
  107.2 4.1 %slab_sums.7 = (f32[256,512]{1,0:T(8,128)}, f32[256,512]{1,0:T(8,128)}, f32[256,512]{1,0:T(8,128)}) custom-call(s32[1]{0:T(128)} %bitcast.2.scalars, bf16[128,1024]{1,0:T(8,128)(2,1)} %copy-done.13, bf16[128,1024]{1,0:T(8,128)(2,1)} %copy-done.14, bf16[4096,512]{1,0:T(8,128)(2,1)} %refs_2_.17, ...), custom_call_target="tpu_custom_call", output_to_operand_aliasing={{0}: (6, {}), {1}: (7, {}), {2}: (8, {})} | custom-call | flops 12582912 | bytes 90112 | tf_op jit(solution)/shard_map/slab_sums/pallas_call | solution.py:117
  111.3 2.4 %collective-permute-done.17.refs_1_ = bf16[128,1024]{1,0:T(8,128)(2,1)S(1)} collective-permute-done((bf16[128,1024]{1,0:T(8,128)(2,1)S(1)}, bf16[128,1024]{1,0:T(8,128)(2,1)S(1)}, u32[]{:S(2)}, u32[]{:S(2)}) %collective-permute-start.17) | collective-permute-done | bytes 262176 | tf_op jit(solution)/shard_map/ppermute | solution.py:469
  113.8 0.7 copy-done.4
  114.5 3.4 %finish_kv.6.refs_10_ = bf16[2,256,256]{2,1,0:T(8,128)(2,1)} custom-call(s32[2]{0:T(128)} %pad_add_fusion.3.scalars, bf16[128,1024]{1,0:T(8,128)(2,1)} %copy-done.3, bf16[128,1024]{1,0:T(8,128)(2,1)} %copy-done.4, bf16[4096,512]{1,0:T(8,128)(2,1)} %refs_2_.19, bf16[4096,512]{1,0:T(8,128)(2,1)} %refs_3_.15, f32[256,512]{1,0:T(8,128)} %get-tuple-element.85.refs_4_, ...), custom_call_target="tpu_custom_call" | custom-call | flops 4194304 | bytes 30720 | tf_op jit(solution)/shard_map/finish_kv/pallas_call | solution.py:185
  118.5 3.5 %finish_kv.7.refs_10_ = bf16[2,256,256]{2,1,0:T(8,128)(2,1)} custom-call(s32[2]{0:T(128)} %pad_add_fusion.3.scalars, bf16[128,1024]{1,0:T(8,128)(2,1)} %copy-done.3, bf16[128,1024]{1,0:T(8,128)(2,1)} %copy-done.4, bf16[4096,512]{1,0:T(8,128)(2,1)} %refs_2_.19, bf16[4096,512]{1,0:T(8,128)(2,1)} %refs_3_.15, f32[256,512]{1,0:T(8,128)} %get-tuple-element.85.refs_4_, ...), custom_call_target="tpu_custom_call" | custom-call | flops 4194304 | bytes 30720 | tf_op jit(solution)/shard_map/finish_kv/pallas_call | solution.py:185
  122.0 1.4 collective-permute-start.27
  123.4 3.9 %finish_q.3 = (bf16[256,512]{1,0:T(8,128)(2,1)}, bf16[256,512]{1,0:T(8,128)(2,1)}) custom-call(s32[2]{0:T(128)} %pad_add_fusion.3.scalars, bf16[128,1024]{1,0:T(8,128)(2,1)} %copy-done.3, bf16[128,1024]{1,0:T(8,128)(2,1)} %copy-done.4, bf16[4096,512]{1,0:T(8,128)(2,1)} %refs_2_.17, f32[256,512]{1,0:T(8,128)} %get-tuple-element.79.refs_3_, ...), custom_call_target="tpu_custom_call" | custom-call | flops 4194304 | bytes 32768 | tf_op jit(solution)/shard_map/finish_q/pallas_call | solution.py:245
  127.4 4.3 %attend_forward.2.refs_14_ = f32[256,256]{1,0:T(8,128)} custom-call(s32[4]{0:T(128)} %get-tuple-element.87.refs_0_, bf16[256,512]{1,0:T(8,128)(2,1)} %get-tuple-element.68.refs_1_, bf16[256,512]{1,0:T(8,128)(2,1)} %get-tuple-element.69.refs_2_, bf16[16,256]{1,0:T(8,128)(2,1)} %get-tuple-element.88.refs_3_, bf16[16,256]{1,0:T(8,128)(2,1)} %get-tuple-element.89.refs_4_, ...), custom_call_target="tpu_custom_call" | custom-call | flops 8388608 | bytes 16384 | tf_op jit(solution)/shard_map/attend_forward/pallas_call | solution.py:359
  131.7 4.3 %attend_forward.3.refs_14_ = f32[256,256]{1,0:T(8,128)} custom-call(s32[4]{0:T(128)} %get-tuple-element.87.refs_0_, bf16[256,512]{1,0:T(8,128)(2,1)} %get-tuple-element.68.refs_1_, bf16[256,512]{1,0:T(8,128)(2,1)} %get-tuple-element.69.refs_2_, bf16[16,256]{1,0:T(8,128)(2,1)} %get-tuple-element.82.refs_3_, bf16[16,256]{1,0:T(8,128)(2,1)} %get-tuple-element.83.refs_4_, ...), custom_call_target="tpu_custom_call" | custom-call | flops 8388608 | bytes 16384 | tf_op jit(solution)/shard_map/attend_forward/pallas_call | solution.py:359
  136.0 3.2 %collective-permute-start.26 = (bf16[2,256,256]{2,1,0:T(8,128)(2,1)S(1)}, bf16[2,256,256]{2,1,0:T(8,128)(2,1)S(1)}, u32[]{:S(2)}, u32[]{:S(2)}) collective-permute-start(bf16[2,256,256]{2,1,0:T(8,128)(2,1)S(1)} %collective-permute-done.24.refs_11_), channel_id=1, source_target_pairs={{0,4},{4,0},{8,12},{12,8},{1,5},{5,1},{9,13},{13,9},{2,6},{6,2},{1... | collective-permute-start | bytes 786440 | tf_op jit(solution)/shard_map/ppermute | solution.py:466
  141.8 8.5 %attend_reverse.2 = bf16[256,256]{1,0:T(8,128)(2,1)} custom-call(s32[4]{0:T(128)} %get-tuple-element.87.refs_0_, bf16[256,512]{1,0:T(8,128)(2,1)} %get-tuple-element.80.refs_1_, bf16[256,512]{1,0:T(8,128)(2,1)} %get-tuple-element.81.refs_2_, bf16[16,256]{1,0:T(8,128)(2,1)} %get-tuple-element.82.refs_3_, bf16[16,256]{1,0:T(8,128)(2,1)} %get-tuple-element.83.refs_4_, ...), custom_call_target="tpu_custom_call" | custom-call | flops 8388608 | bytes 16384 | tf_op jit(solution)/shard_map/attend_reverse/pallas_call | solution.py:359
  150.3 17.0 %all-gather = bf16[1024,256]{1,0:T(8,128)(2,1)} all-gather(bf16[256,256]{1,0:T(8,128)(2,1)} %attend_reverse.2), channel_id=2, replica_groups=mesh['groups'=2,'ctx'=4,'head'=4] {'head'}, dimensions={0}, use_global_device_ids=true | all-gather | bytes 655360 | tf_op jit(solution)/shard_map/all_gather | solution.py:638
  168.0 0.7 copy-done.27
  168.7 8.3 %attend_reverse.3 = bf16[256,256]{1,0:T(8,128)(2,1)} custom-call(s32[4]{0:T(128)} %get-tuple-element.87.refs_0_, bf16[256,512]{1,0:T(8,128)(2,1)} %get-tuple-element.80.refs_1_, bf16[256,512]{1,0:T(8,128)(2,1)} %get-tuple-element.81.refs_2_, bf16[16,256]{1,0:T(8,128)(2,1)} %get-tuple-element.88.refs_3_, bf16[16,256]{1,0:T(8,128)(2,1)} %get-tuple-element.89.refs_4_, ...), custom_call_target="tpu_custom_call" | custom-call | flops 8388608 | bytes 16384 | tf_op jit(solution)/shard_map/attend_reverse/pallas_call | solution.py:359
  177.0 16.7 %all-gather.1 = bf16[1024,256]{1,0:T(8,128)(2,1)} all-gather(bf16[256,256]{1,0:T(8,128)(2,1)} %attend_reverse.3), channel_id=3, replica_groups=mesh['groups'=2,'ctx'=4,'head'=4] {'head'}, dimensions={0}, use_global_device_ids=true | all-gather | bytes 655360 | tf_op jit(solution)/shard_map/all_gather | solution.py:638
  193.7 5.0 %out_project.2.refs_0_ = f32[256,1024]{1,0:T(8,128)} custom-call(s32[4]{0:T(128)} %pad_add_fusion.1.scalars, bf16[4,256,256]{2,1,0:T(8,128)(2,1)} %bitcast.29, bf16[4,512,1024]{2,1,0:T(8,128)(2,1)} %all-gather.4.cloned.1.call-done.weight_ref), custom_call_target="tpu_custom_call" | custom-call | flops 8388608 | bytes 32768 | tf_op jit(solution)/shard_map/out_project/pallas_call | solution.py:411
  198.7 5.1 %out_project.3 = bf16[256,1024]{1,0:T(8,128)(2,1)} custom-call(s32[4]{0:T(128)} %pad_add_fusion.1.scalars, bf16[4,256,256]{2,1,0:T(8,128)(2,1)} %bitcast.28, bf16[4,512,1024]{2,1,0:T(8,128)(2,1)} %all-gather.4.cloned.1.call-done.weight_ref, f32[256,1024]{1,0:T(8,128)} %out_project.2.refs_0_), custom_call_target="tpu_custom_call" | custom-call | flops 8388608 | bytes 32768 | tf_op jit(solution)/shard_map/out_project/pallas_call | solution.py:411
  (123 shorter events, 10.3 us)
Async XLA Ops:
  6.5 120.9 %all-gather.4.cloned.1.call-start = ((), (), s32[]{:S(2)}) async-start(), calls=%async_computation | async-start | bytes 4718592 | tf_op jit(solution)/shard_map/all_gather | solution.py:528
  6.5 14.8 %collective-permute-start.4 = (s32[256]{0:T(256)}, s32[256]{0:T(256)S(1)}, u32[]{:S(2)}, u32[]{:S(2)}) collective-permute-start(s32[256]{0:T(256)} %param.10), channel_id=1, source_target_pairs={{0,8},{4,12},{8,0},{12,4},{1,9},{5,13},{9,1},{13,5},{2,10},{6,14},... | collective-permute-start | bytes 3080 | tf_op jit(solution)/shard_map/ppermute | solution.py:459
  9.5 11.9 %collective-permute-start.5 = (s32[256]{0:T(256)}, s32[256]{0:T(256)S(1)}, u32[]{:S(2)}, u32[]{:S(2)}) collective-permute-start(s32[256]{0:T(256)} %param.10), channel_id=1, source_target_pairs={{0,4},{4,0},{8,12},{12,8},{1,5},{5,1},{9,13},{13,9},{2,6},{6,2},{1... | collective-permute-start | bytes 3080 | tf_op jit(solution)/shard_map/ppermute | solution.py:466
  10.6 12.0 %collective-permute-start.2 = (bf16[128,1024]{1,0:T(8,128)(2,1)S(1)}, bf16[128,1024]{1,0:T(8,128)(2,1)S(1)}, u32[]{:S(2)}, u32[]{:S(2)}) collective-permute-start(bf16[128,1024]{1,0:T(8,128)(2,1)S(1)} %get-tuple-element.101), channel_id=1, source_target_pairs={{0,1},{1,2},{2,3},{3,0},{4,5},{5,6},{6,7},{7,4},{8,9},{9,10},{10,1... | collective-permute-start | bytes 786440 | tf_op jit(solution)/shard_map/ppermute | solution.py:469
  12.2 14.6 %collective-permute-start = (bf16[128,1024]{1,0:T(8,128)(2,1)S(1)}, bf16[128,1024]{1,0:T(8,128)(2,1)S(1)}, u32[]{:S(2)}, u32[]{:S(2)}) collective-permute-start(bf16[128,1024]{1,0:T(8,128)(2,1)S(1)} %get-tuple-element.102), channel_id=1, source_target_pairs={{0,1},{1,2},{2,3},{3,0},{4,5},{5,6},{6,7},{7,4},{8,9},{9,10},{10,1... | collective-permute-start | bytes 786440 | tf_op jit(solution)/shard_map/ppermute | solution.py:469
  14.5 6.4 %copy-start.32 = (s32[128]{0:T(128)S(1)}, s32[128]{0:T(128)}, u32[]{:S(2)}) copy-start(s32[128]{0:T(128)} %param.11) | copy-start | bytes 1540
  14.5 8.1 %copy-start.30 = (s32[256]{0:T(256)S(1)}, s32[256]{0:T(256)}, u32[]{:S(2)}) copy-start(s32[256]{0:T(256)} %param.10) | copy-start | bytes 3076
  18.2 24.8 %copy-start.29 = (bf16[4,4096]{1,0:T(4,128)(2,1)S(1)}, bf16[4,4096]{1,0:T(4,128)(2,1)}, u32[]{:S(2)}) copy-start(bf16[4,4096]{1,0:T(4,128)(2,1)} %param.13) | copy-start | bytes 98308
  21.3 1.2 collective-permute-start.6
  22.6 26.1 %copy-start.7 = (bf16[128,1024]{1,0:T(8,128)(2,1)}, bf16[128,1024]{1,0:T(8,128)(2,1)S(1)}, u32[]{:S(2)}) copy-start(bf16[128,1024]{1,0:T(8,128)(2,1)S(1)} %collective-permute-done.2.refs_6_) | copy-start | bytes 786436
  26.8 21.9 %copy-start.8 = (bf16[128,1024]{1,0:T(8,128)(2,1)}, bf16[128,1024]{1,0:T(8,128)(2,1)S(1)}, u32[]{:S(2)}) copy-start(bf16[128,1024]{1,0:T(8,128)(2,1)S(1)} %collective-permute-done.refs_5_) | copy-start | bytes 786436
  28.4 5.8 %collective-permute-start.9 = (bf16[64,1024]{1,0:T(8,128)(2,1)S(1)}, bf16[64,1024]{1,0:T(8,128)(2,1)S(1)}, u32[]{:S(2)}, u32[]{:S(2)}) collective-permute-start(bf16[64,1024]{1,0:T(8,128)(2,1)S(1)} %get-tuple-element.96), channel_id=1, source_target_pairs={{0,3},{1,0},{2,1},{3,2},{4,7},{5,4},{6,5},{7,6},{8,11},{9,8},{10,9... | collective-permute-start | bytes 393224 | tf_op jit(solution)/shard_map/ppermute | solution.py:523
  30.2 11.2 %collective-permute-start.8 = (bf16[64,1024]{1,0:T(8,128)(2,1)S(1)}, bf16[64,1024]{1,0:T(8,128)(2,1)S(1)}, u32[]{:S(2)}, u32[]{:S(2)}) collective-permute-start(bf16[64,1024]{1,0:T(8,128)(2,1)S(1)} %get-tuple-element.97), channel_id=1, source_target_pairs={{0,2},{1,3},{2,0},{3,1},{4,6},{5,7},{6,4},{7,5},{8,10},{9,11},{10,... | collective-permute-start | bytes 393224 | tf_op jit(solution)/shard_map/ppermute | solution.py:523
  30.2 11.2 %collective-permute-start.7 = (bf16[64,1024]{1,0:T(8,128)(2,1)S(1)}, bf16[64,1024]{1,0:T(8,128)(2,1)S(1)}, u32[]{:S(2)}, u32[]{:S(2)}) collective-permute-start(bf16[64,1024]{1,0:T(8,128)(2,1)S(1)} %get-tuple-element.98), channel_id=1, source_target_pairs={{0,1},{1,2},{2,3},{3,0},{4,5},{5,6},{6,7},{7,4},{8,9},{9,10},{10,1... | collective-permute-start | bytes 393224 | tf_op jit(solution)/shard_map/ppermute | solution.py:523
  43.8 14.9 %collective-permute-start.3 = (bf16[128,1024]{1,0:T(8,128)(2,1)S(1)}, bf16[128,1024]{1,0:T(8,128)(2,1)S(1)}, u32[]{:S(2)}, u32[]{:S(2)}) collective-permute-start(bf16[128,1024]{1,0:T(8,128)(2,1)S(1)} %collective-permute-done.2.refs_6_), channel_id=1, source_target_pairs={{0,1},{1,2},{2,3},{3,0},{4,5},{5,6},{6,7},{7,4},{8,9},{9,10},{10,1... | collective-permute-start | bytes 786440 | tf_op jit(solution)/shard_map/ppermute | solution.py:469
  44.3 14.3 %collective-permute-start.1 = (bf16[128,1024]{1,0:T(8,128)(2,1)S(1)}, bf16[128,1024]{1,0:T(8,128)(2,1)S(1)}, u32[]{:S(2)}, u32[]{:S(2)}) collective-permute-start(bf16[128,1024]{1,0:T(8,128)(2,1)S(1)} %collective-permute-done.refs_5_), channel_id=1, source_target_pairs={{0,1},{1,2},{2,3},{3,0},{4,5},{5,6},{6,7},{7,4},{8,9},{9,10},{10,1... | collective-permute-start | bytes 786440 | tf_op jit(solution)/shard_map/ppermute | solution.py:469
  58.7 11.0 %collective-permute-start.10 = (bf16[128,1024]{1,0:T(8,128)(2,1)S(1)}, bf16[128,1024]{1,0:T(8,128)(2,1)S(1)}, u32[]{:S(2)}, u32[]{:S(2)}) collective-permute-start(bf16[128,1024]{1,0:T(8,128)(2,1)S(1)} %collective-permute-done.1.refs_0_), channel_id=1, source_target_pairs={{0,1},{1,2},{2,3},{3,0},{4,5},{5,6},{6,7},{7,4},{8,9},{9,10},{10,1... | collective-permute-start | bytes 786440 | tf_op jit(solution)/shard_map/ppermute | solution.py:469
  58.7 16.6 %collective-permute-start.12 = (bf16[128,1024]{1,0:T(8,128)(2,1)S(1)}, bf16[128,1024]{1,0:T(8,128)(2,1)S(1)}, u32[]{:S(2)}, u32[]{:S(2)}) collective-permute-start(bf16[128,1024]{1,0:T(8,128)(2,1)S(1)} %collective-permute-done.3.refs_1_), channel_id=1, source_target_pairs={{0,1},{1,2},{2,3},{3,0},{4,5},{5,6},{6,7},{7,4},{8,9},{9,10},{10,1... | collective-permute-start | bytes 786440 | tf_op jit(solution)/shard_map/ppermute | solution.py:469
  69.7 19.7 %collective-permute-start.11 = (bf16[128,1024]{1,0:T(8,128)(2,1)S(1)}, bf16[128,1024]{1,0:T(8,128)(2,1)S(1)}, u32[]{:S(2)}, u32[]{:S(2)}) collective-permute-start(bf16[128,1024]{1,0:T(8,128)(2,1)S(1)} %get-tuple-element.64), channel_id=1, source_target_pairs={{0,1},{1,2},{2,3},{3,0},{4,5},{5,6},{6,7},{7,4},{8,9},{9,10},{10,1... | collective-permute-start | bytes 786440 | tf_op jit(solution)/shard_map/ppermute | solution.py:469
  75.3 14.1 %collective-permute-start.15 = (bf16[128,1024]{1,0:T(8,128)(2,1)S(1)}, bf16[128,1024]{1,0:T(8,128)(2,1)S(1)}, u32[]{:S(2)}, u32[]{:S(2)}) collective-permute-start(bf16[128,1024]{1,0:T(8,128)(2,1)S(1)} %get-tuple-element.72), channel_id=1, source_target_pairs={{0,1},{1,2},{2,3},{3,0},{4,5},{5,6},{6,7},{7,4},{8,9},{9,10},{10,1... | collective-permute-start | bytes 786440 | tf_op jit(solution)/shard_map/ppermute | solution.py:469
  79.7 10.4 %collective-permute-start.18 = (bf16[2,256,256]{2,1,0:T(8,128)(2,1)}, bf16[2,256,256]{2,1,0:T(8,128)(2,1)S(1)}, u32[]{:S(2)}, u32[]{:S(2)}) collective-permute-start(bf16[2,256,256]{2,1,0:T(8,128)(2,1)} %get-tuple-element.66.refs_10_), channel_id=1, source_target_pairs={{0,8},{4,12},{8,0},{12,4},{1,9},{5,13},{9,1},{13,5},{2,10},{6,14},... | collective-permute-start | bytes 786440 | tf_op jit(solution)/shard_map/ppermute | solution.py:459
  83.9 6.8 %collective-permute-start.21 = (bf16[2,256,256]{2,1,0:T(8,128)(2,1)}, bf16[2,256,256]{2,1,0:T(8,128)(2,1)S(1)}, u32[]{:S(2)}, u32[]{:S(2)}) collective-permute-start(bf16[2,256,256]{2,1,0:T(8,128)(2,1)} %get-tuple-element.67.refs_10_), channel_id=1, source_target_pairs={{0,8},{4,12},{8,0},{12,4},{1,9},{5,13},{9,1},{13,5},{2,10},{6,14},... | collective-permute-start | bytes 786440 | tf_op jit(solution)/shard_map/ppermute | solution.py:459
  89.4 11.6 %copy-start.9 = (bf16[128,1024]{1,0:T(8,128)(2,1)}, bf16[128,1024]{1,0:T(8,128)(2,1)S(1)}, u32[]{:S(2)}) copy-start(bf16[128,1024]{1,0:T(8,128)(2,1)S(1)} %collective-permute-done.11.refs_4_) | copy-start | bytes 786436
  89.4 8.2 %collective-permute-start.13 = (bf16[128,1024]{1,0:T(8,128)(2,1)S(1)}, bf16[128,1024]{1,0:T(8,128)(2,1)S(1)}, u32[]{:S(2)}, u32[]{:S(2)}) collective-permute-start(bf16[128,1024]{1,0:T(8,128)(2,1)S(1)} %collective-permute-done.11.refs_4_), channel_id=1, source_target_pairs={{0,1},{1,2},{2,3},{3,0},{4,5},{5,6},{6,7},{7,4},{8,9},{9,10},{10,1... | collective-permute-start | bytes 786440 | tf_op jit(solution)/shard_map/ppermute | solution.py:469
  89.5 11.5 %copy-start.10 = (bf16[128,1024]{1,0:T(8,128)(2,1)}, bf16[128,1024]{1,0:T(8,128)(2,1)S(1)}, u32[]{:S(2)}) copy-start(bf16[128,1024]{1,0:T(8,128)(2,1)S(1)} %collective-permute-done.15.refs_5_) | copy-start | bytes 786436
  89.5 10.9 %collective-permute-start.16 = (bf16[128,1024]{1,0:T(8,128)(2,1)S(1)}, bf16[128,1024]{1,0:T(8,128)(2,1)S(1)}, u32[]{:S(2)}, u32[]{:S(2)}) collective-permute-start(bf16[128,1024]{1,0:T(8,128)(2,1)S(1)} %collective-permute-done.15.refs_5_), channel_id=1, source_target_pairs={{0,1},{1,2},{2,3},{3,0},{4,5},{5,6},{6,7},{7,4},{8,9},{9,10},{10,1... | collective-permute-start | bytes 786440 | tf_op jit(solution)/shard_map/ppermute | solution.py:469
  90.1 10.4 %collective-permute-start.19 = (bf16[2,256,256]{2,1,0:T(8,128)(2,1)S(1)}, bf16[2,256,256]{2,1,0:T(8,128)(2,1)S(1)}, u32[]{:S(2)}, u32[]{:S(2)}) collective-permute-start(bf16[2,256,256]{2,1,0:T(8,128)(2,1)S(1)} %copy-done.16), channel_id=1, source_target_pairs={{0,4},{4,0},{8,12},{12,8},{1,5},{5,1},{9,13},{13,9},{2,6},{6,2},{1... | collective-permute-start | bytes 786440 | tf_op jit(solution)/shard_map/ppermute | solution.py:466
  90.1 17.0 %copy-start.17 = (bf16[2,256,256]{2,1,0:T(8,128)(2,1)}, bf16[2,256,256]{2,1,0:T(8,128)(2,1)S(1)}, u32[]{:S(2)}) copy-start(bf16[2,256,256]{2,1,0:T(8,128)(2,1)S(1)} %collective-permute-done.18.refs_11_) | copy-start | bytes 786436
  90.1 21.1 %collective-permute-start.22 = (bf16[2,256,256]{2,1,0:T(8,128)(2,1)S(1)}, bf16[2,256,256]{2,1,0:T(8,128)(2,1)S(1)}, u32[]{:S(2)}, u32[]{:S(2)}) collective-permute-start(bf16[2,256,256]{2,1,0:T(8,128)(2,1)S(1)} %copy-done.15), channel_id=1, source_target_pairs={{0,4},{4,0},{8,12},{12,8},{1,5},{5,1},{9,13},{13,9},{2,6},{6,2},{1... | collective-permute-start | bytes 786440 | tf_op jit(solution)/shard_map/ppermute | solution.py:466
  90.7 16.4 %copy-start.18 = (bf16[2,256,256]{2,1,0:T(8,128)(2,1)}, bf16[2,256,256]{2,1,0:T(8,128)(2,1)S(1)}, u32[]{:S(2)}) copy-start(bf16[2,256,256]{2,1,0:T(8,128)(2,1)S(1)} %collective-permute-done.21.refs_11_) | copy-start | bytes 786436
  90.7 20.6 %collective-permute-start.20 = (bf16[2,256,256]{2,1,0:T(8,128)(2,1)S(1)}, bf16[2,256,256]{2,1,0:T(8,128)(2,1)S(1)}, u32[]{:S(2)}, u32[]{:S(2)}) collective-permute-start(bf16[2,256,256]{2,1,0:T(8,128)(2,1)S(1)} %collective-permute-done.18.refs_11_), channel_id=1, source_target_pairs={{0,4},{4,0},{8,12},{12,8},{1,5},{5,1},{9,13},{13,9},{2,6},{6,2},{1... | collective-permute-start | bytes 786440 | tf_op jit(solution)/shard_map/ppermute | solution.py:466
  97.6 9.5 %copy-start.13 = (bf16[128,1024]{1,0:T(8,128)(2,1)}, bf16[128,1024]{1,0:T(8,128)(2,1)S(1)}, u32[]{:S(2)}) copy-start(bf16[128,1024]{1,0:T(8,128)(2,1)S(1)} %collective-permute-done.13.refs_0_) | copy-start | bytes 786436
  97.6 13.7 %collective-permute-start.23 = (bf16[2,256,256]{2,1,0:T(8,128)(2,1)S(1)}, bf16[2,256,256]{2,1,0:T(8,128)(2,1)S(1)}, u32[]{:S(2)}, u32[]{:S(2)}) collective-permute-start(bf16[2,256,256]{2,1,0:T(8,128)(2,1)S(1)} %collective-permute-done.21.refs_11_), channel_id=1, source_target_pairs={{0,4},{4,0},{8,12},{12,8},{1,5},{5,1},{9,13},{13,9},{2,6},{6,2},{1... | collective-permute-start | bytes 786440 | tf_op jit(solution)/shard_map/ppermute | solution.py:466
  100.4 6.7 %copy-start.14 = (bf16[128,1024]{1,0:T(8,128)(2,1)}, bf16[128,1024]{1,0:T(8,128)(2,1)S(1)}, u32[]{:S(2)}) copy-start(bf16[128,1024]{1,0:T(8,128)(2,1)S(1)} %collective-permute-done.16.refs_1_) | copy-start | bytes 786436
  100.4 10.9 %collective-permute-start.14 = (bf16[128,1024]{1,0:T(8,128)(2,1)S(1)}, bf16[128,1024]{1,0:T(8,128)(2,1)S(1)}, u32[]{:S(2)}, u32[]{:S(2)}) collective-permute-start(bf16[128,1024]{1,0:T(8,128)(2,1)S(1)} %collective-permute-done.13.refs_0_), channel_id=1, source_target_pairs={{0,1},{1,2},{2,3},{3,0},{4,5},{5,6},{6,7},{7,4},{8,9},{9,10},{10,1... | collective-permute-start | bytes 786440 | tf_op jit(solution)/shard_map/ppermute | solution.py:469
  100.5 6.7 %copy-start.20 = (bf16[2,256,256]{2,1,0:T(8,128)(2,1)}, bf16[2,256,256]{2,1,0:T(8,128)(2,1)S(1)}, u32[]{:S(2)}) copy-start(bf16[2,256,256]{2,1,0:T(8,128)(2,1)S(1)} %collective-permute-done.19.refs_12_) | copy-start | bytes 786436
  100.5 13.3 %collective-permute-start.17 = (bf16[128,1024]{1,0:T(8,128)(2,1)S(1)}, bf16[128,1024]{1,0:T(8,128)(2,1)S(1)}, u32[]{:S(2)}, u32[]{:S(2)}) collective-permute-start(bf16[128,1024]{1,0:T(8,128)(2,1)S(1)} %collective-permute-done.16.refs_1_), channel_id=1, source_target_pairs={{0,1},{1,2},{2,3},{3,0},{4,5},{5,6},{6,7},{7,4},{8,9},{9,10},{10,1... | collective-permute-start | bytes 786440 | tf_op jit(solution)/shard_map/ppermute | solution.py:469
  111.3 16.1 %copy-start.19 = (bf16[2,256,256]{2,1,0:T(8,128)(2,1)}, bf16[2,256,256]{2,1,0:T(8,128)(2,1)S(1)}, u32[]{:S(2)}) copy-start(bf16[2,256,256]{2,1,0:T(8,128)(2,1)S(1)} %collective-permute-done.22.refs_12_) | copy-start | bytes 786436
  111.3 16.1 %copy-start.23 = (bf16[2,256,256]{2,1,0:T(8,128)(2,1)}, bf16[2,256,256]{2,1,0:T(8,128)(2,1)S(1)}, u32[]{:S(2)}) copy-start(bf16[2,256,256]{2,1,0:T(8,128)(2,1)S(1)} %collective-permute-done.20.refs_13_) | copy-start | bytes 786436
  111.3 16.1 %copy-start.21 = (bf16[2,256,256]{2,1,0:T(8,128)(2,1)}, bf16[2,256,256]{2,1,0:T(8,128)(2,1)S(1)}, u32[]{:S(2)}) copy-start(bf16[2,256,256]{2,1,0:T(8,128)(2,1)S(1)} %collective-permute-done.23.refs_13_) | copy-start | bytes 786436
  117.9 18.1 %collective-permute-start.24 = (bf16[2,256,256]{2,1,0:T(8,128)(2,1)}, bf16[2,256,256]{2,1,0:T(8,128)(2,1)S(1)}, u32[]{:S(2)}, u32[]{:S(2)}) collective-permute-start(bf16[2,256,256]{2,1,0:T(8,128)(2,1)} %finish_kv.6.refs_10_), channel_id=1, source_target_pairs={{0,8},{4,12},{8,0},{12,4},{1,9},{5,13},{9,1},{13,5},{2,10},{6,14},... | collective-permute-start | bytes 786440 | tf_op jit(solution)/shard_map/ppermute | solution.py:459
  122.0 17.3 %collective-permute-start.27 = (bf16[2,256,256]{2,1,0:T(8,128)(2,1)}, bf16[2,256,256]{2,1,0:T(8,128)(2,1)S(1)}, u32[]{:S(2)}, u32[]{:S(2)}) collective-permute-start(bf16[2,256,256]{2,1,0:T(8,128)(2,1)} %finish_kv.7.refs_10_), channel_id=1, source_target_pairs={{0,8},{4,12},{8,0},{12,4},{1,9},{5,13},{9,1},{13,5},{2,10},{6,14},... | collective-permute-start | bytes 786440 | tf_op jit(solution)/shard_map/ppermute | solution.py:459
  123.4 16.9 %collective-permute-start.25 = (bf16[2,256,256]{2,1,0:T(8,128)(2,1)S(1)}, bf16[2,256,256]{2,1,0:T(8,128)(2,1)S(1)}, u32[]{:S(2)}, u32[]{:S(2)}) collective-permute-start(bf16[2,256,256]{2,1,0:T(8,128)(2,1)S(1)} %copy-done.6), channel_id=1, source_target_pairs={{0,4},{4,0},{8,12},{12,8},{1,5},{5,1},{9,13},{13,9},{2,6},{6,2},{1... | collective-permute-start | bytes 786440 | tf_op jit(solution)/shard_map/ppermute | solution.py:466
  127.4 11.8 %copy-start.5 = (bf16[2,256,256]{2,1,0:T(8,128)(2,1)S(1)}, bf16[2,256,256]{2,1,0:T(8,128)(2,1)}, u32[]{:S(2)}) copy-start(bf16[2,256,256]{2,1,0:T(8,128)(2,1)} %finish_kv.7.refs_10_) | copy-start | bytes 786436
  136.0 4.4 %collective-permute-start.26 = (bf16[2,256,256]{2,1,0:T(8,128)(2,1)S(1)}, bf16[2,256,256]{2,1,0:T(8,128)(2,1)S(1)}, u32[]{:S(2)}, u32[]{:S(2)}) collective-permute-start(bf16[2,256,256]{2,1,0:T(8,128)(2,1)S(1)} %collective-permute-done.24.refs_11_), channel_id=1, source_target_pairs={{0,4},{4,0},{8,12},{12,8},{1,5},{5,1},{9,13},{13,9},{2,6},{6,2},{1... | collective-permute-start | bytes 786440 | tf_op jit(solution)/shard_map/ppermute | solution.py:466
  139.2 28.0 %collective-permute-start.28 = (bf16[2,256,256]{2,1,0:T(8,128)(2,1)S(1)}, bf16[2,256,256]{2,1,0:T(8,128)(2,1)S(1)}, u32[]{:S(2)}, u32[]{:S(2)}) collective-permute-start(bf16[2,256,256]{2,1,0:T(8,128)(2,1)S(1)} %copy-done.5), channel_id=1, source_target_pairs={{0,4},{4,0},{8,12},{12,8},{1,5},{5,1},{9,13},{13,9},{2,6},{6,2},{1... | collective-permute-start | bytes 786440 | tf_op jit(solution)/shard_map/ppermute | solution.py:466
  139.3 28.0 %copy-start.22 = (bf16[2,256,256]{2,1,0:T(8,128)(2,1)}, bf16[2,256,256]{2,1,0:T(8,128)(2,1)S(1)}, u32[]{:S(2)}) copy-start(bf16[2,256,256]{2,1,0:T(8,128)(2,1)S(1)} %collective-permute-done.27.refs_11_) | copy-start | bytes 786436
  139.3 27.9 %collective-permute-start.29 = (bf16[2,256,256]{2,1,0:T(8,128)(2,1)S(1)}, bf16[2,256,256]{2,1,0:T(8,128)(2,1)S(1)}, u32[]{:S(2)}, u32[]{:S(2)}) collective-permute-start(bf16[2,256,256]{2,1,0:T(8,128)(2,1)S(1)} %collective-permute-done.27.refs_11_), channel_id=1, source_target_pairs={{0,4},{4,0},{8,12},{12,8},{1,5},{5,1},{9,13},{13,9},{2,6},{6,2},{1... | collective-permute-start | bytes 786440 | tf_op jit(solution)/shard_map/ppermute | solution.py:466
  (16 other events, 48.9 us)
Sparse Core Ops, SparseCore 0:
  42.4 35.8 all-gather.3

commit v4 on v3

--- a/solution.py
+++ b/solution.py
@@ -16,7 +16,7 @@
 NEG_FILL = -1e30
 COST_CUT = 64
 SCORE_SCALE = math.log2(math.e) / math.sqrt(HEAD_DIM)
-VMEM_LIMIT = 56 * 1024 * 1024
+VMEM_LIMIT = 24 * 1024 * 1024
 F32 = jnp.float32
 BF16 = jnp.bfloat16
 
@@ -257,7 +257,7 @@
     )(scalars, *operands)
 
 
-def attend_kernel(forward, block_count, has_before, *refs):
+def attend_kernel(forward, block_count, has_before, q_start, table_start, before_start, *refs):
     (ids_ref, q_ref, qm_ref, table_ref, swapped_ref, ev_ref), refs = refs[:6], refs[6:]
     (codes_ref, codes_t_ref, cos_ref, sin_ref), refs = refs[:4], refs[4:]
     kv_refs, refs = refs[:block_count], refs[block_count:]
@@ -265,7 +265,7 @@
     if has_before:
         before_ref, refs = refs[0], refs[1:]
     out_ref, top, acc = refs
-    rows, cols_here = q_ref.shape
+    rows, cols_here = out_ref.shape
     heads = cols_here // HEAD_DIM
     tall = HEAD_DIM + CODES
     my_id = ids_ref[0]
@@ -276,40 +276,43 @@
         cos = cos_ref[pl.ds(first, rows), :]
         sin = sin_ref[pl.ds(first, rows), :]
         codes, codes_t = codes_ref[index], codes_t_ref[index]
-        change = dot(codes, table_ref[...])
-        change_swapped = dot(codes, swapped_ref[...])
+        here = slice(table_start, table_start + cols_here)
+        change = dot(codes, table_ref[:, here])
+        change_swapped = dot(codes, swapped_ref[:, here])
         if index == 0:
             key_at = lax.broadcasted_iota(jnp.int32, (rows, rows), 0)
             query_at = lax.broadcasted_iota(jnp.int32, (rows, rows), 1)
             seen = key_at <= query_at if forward else key_at >= query_at
+        scores, values = [], []
         for head in range(heads):
             cols = slice(head * HEAD_DIM, (head + 1) * HEAD_DIM)
+            q_cols = slice(q_start + cols.start, q_start + cols.stop)
             key = kv_ref[0, :, cols]
             mutant_key = (
                 key.astype(F32) + change[:, cols] * cos + change_swapped[:, cols] * sin
             ).astype(BF16)
-            values_t = jnp.concatenate([kv_ref[1, :, cols].T, codes_t], axis=0)
-            for kind, (query, keys) in enumerate(
-                ((q_ref[:, cols], key), (qm_ref[:, cols], mutant_key))
-            ):
-                unit = 2 * head + kind
-                area = slice(unit * tall, (unit + 1) * tall)
-                scores = lax.dot_general(
-                    keys, query, (((1,), (1,)), ((), ())), preferred_element_type=F32
+            values.append(jnp.concatenate([kv_ref[1, :, cols].T, codes_t], axis=0))
+            for query, keys in ((q_ref[:, q_cols], key), (qm_ref[:, q_cols], mutant_key)):
+                scores.append(
+                    lax.dot_general(
+                        keys, query, (((1,), (1,)), ((), ())), preferred_element_type=F32
+                    )
                 )
-                if index == 0:
-                    scores = jnp.where(seen, scores, NEG_FILL)
-                peak = jnp.max(scores, axis=0, keepdims=True)
-                if index:
-                    old_peak = top[unit : unit + 1, :]
-                    peak = jnp.maximum(old_peak, peak)
-                    fade = jnp.exp2(old_peak - peak)
-                weights = jnp.exp2(scores - peak).astype(BF16)
-                product = dot(values_t, weights)
-                if index:
-                    product = acc[area, :] * fade + product
-                top[unit : unit + 1, :] = peak
-                acc[area, :] = product
+        fades, weights = [], []
+        for unit, score in enumerate(scores):
+            if index == 0:
+                score = jnp.where(seen, score, NEG_FILL)
+            peak = jnp.max(score, axis=0, keepdims=True)
+            if index:
+                old_peak = top[unit : unit + 1, :]
+                peak = jnp.maximum(old_peak, peak)
+                fades.append(jnp.exp2(old_peak - peak))
+            top[unit : unit + 1, :] = peak
+            weights.append(jnp.exp2(score - peak).astype(BF16))
+        for unit, weight in enumerate(weights):
+            area = slice(unit * tall, (unit + 1) * tall)
+            product = dot(values[unit // 2], weight)
+            acc[area, :] = acc[area, :] * fades[unit] + product if index else product
 
     for index in range(block_count):
         if index == 0:
@@ -321,7 +324,8 @@
     code_at = lax.broadcasted_iota(jnp.int32, (CODES, HEAD_DIM), 0)
     for head in range(heads):
         cols = slice(head * HEAD_DIM, (head + 1) * HEAD_DIM)
-        ev = jnp.where(code_at < BASES, ev_ref[:, cols], 0.0)
+        table_cols = slice(table_start + cols.start, table_start + cols.stop)
+        ev = jnp.where(code_at < BASES, ev_ref[:, table_cols], 0.0)
         parts = []
         for kind in range(2):
             start = (2 * head + kind) * tall
@@ -338,30 +342,26 @@
             parts.append(value / tail[SUM_CODE : SUM_CODE + 1, :])
         difference = (parts[0] - parts[1]).T
         if has_before:
-            out_ref[:, cols] = (0.5 * (before_ref[:, cols] + difference)).astype(BF16)
+            earlier = before_ref[:, before_start + cols.start : before_start + cols.stop]
+            out_ref[:, cols] = (0.5 * (earlier + difference)).astype(BF16)
         else:
             out_ref[:, cols] = difference
 
 
-def attend(forward, part, cols, ids, q, qm, tables, codes, codes_t, cos, sin, kv_blocks, before):
+def attend(forward, start, cols, ids, q, qm, tables, codes, codes_t, cos, sin, kv_blocks, before):
     rows = q.shape[0]
     heads = cols // HEAD_DIM
     vmem = pl.BlockSpec(memory_space=pltpu.VMEM)
-    row_spec = pl.BlockSpec((rows, cols), lambda j: (0, part))
-
-    def whole(item):
-        return pl.BlockSpec(item.shape, lambda j: (0,) * item.ndim)
-
-    operands = [*tables, codes, codes_t, cos, sin, *kv_blocks]
+    operands = [q, qm, *tables, codes, codes_t, cos, sin, *kv_blocks]
     if before is not None:
         operands.append(before)
     count = len(kv_blocks)
     return pl.pallas_call(
-        functools.partial(attend_kernel, forward, count, before is not None),
-        grid=(1,),
-        in_specs=[pl.BlockSpec(memory_space=pltpu.SMEM), row_spec, row_spec]
-        + [whole(item) for item in operands],
-        out_specs=pl.BlockSpec((rows, cols), lambda j: (0, 0)),
+        functools.partial(
+            attend_kernel, forward, count, before is not None, start, start, start
+        ),
+        in_specs=[pl.BlockSpec(memory_space=pltpu.SMEM)] + [vmem] * len(operands),
+        out_specs=vmem,
         out_shape=jax.ShapeDtypeStruct((rows, cols), F32 if before is None else BF16),
         scratch_shapes=[
             pltpu.VMEM((max(2 * heads, 8), rows), F32),
@@ -374,54 +374,56 @@
             2 * rows * rows * count * heads,
         ),
         name="attend_forward" if forward else "attend_reverse",
-    )(ids, q, qm, *operands)
-
-
-def out_kernel(has_before, scalars, rows_ref, weight_ref, *refs):
-    del scalars
+    )(ids, *operands)
+
+
+def out_kernel(slabs, has_before, *refs):
+    row_refs, weight_ref, refs = refs[:slabs], refs[slabs], refs[slabs + 1 :]
     if has_before:
         before_ref, out_ref, acc = refs
     else:
         out_ref, acc = refs
     step = pl.program_id(0)
-
-    @pl.when(step == 0)
-    def _():
-        acc[...] = before_ref[...] if has_before else jnp.zeros_like(acc)
-
-    acc[...] += dot(rows_ref[0], weight_ref[0])
-
-    @pl.when(step == pl.num_programs(0) - 1)
-    def _():
-        out_ref[...] = acc[...].astype(out_ref.dtype)
-
-
-def out_project(part, gathered, weight, slots, last, before):
-    slabs, rows, cols = gathered.shape
+    for index in range(slabs):
+
+        @pl.when(step == index)
+        def _(index=index):
+            item = dot(row_refs[index][...], weight_ref[0])
+            if index:
+                item = acc[...] + item
+            elif has_before:
+                item = before_ref[...] + item
+            if index < slabs - 1:
+                acc[...] = item
+            else:
+                out_ref[...] = item.astype(out_ref.dtype)
+
+
+def out_project(part, slab_rows, weight, last, before):
+    slabs = len(slab_rows)
+    rows, cols = slab_rows[0].shape
     width = weight.shape[2]
-    whole = pl.BlockSpec((rows, width), lambda i, s: (0, 0))
-    in_specs = [
-        pl.BlockSpec((1, rows, cols), lambda i, s: (i, 0, 0)),
-        pl.BlockSpec((1, cols, width), lambda i, s: (s[i], part, 0)),
-    ]
-    operands = [gathered, weight]
+
+    def whole(item):
+        return pl.BlockSpec(item.shape, lambda i: (0, 0))
+
+    in_specs = [whole(item) for item in slab_rows]
+    in_specs.append(pl.BlockSpec((1, cols, width), lambda i: (i, part, 0)))
+    operands = [*slab_rows, weight]
     if before is not None:
-        in_specs.append(whole)
+        in_specs.append(whole(before))
         operands.append(before)
     return pl.pallas_call(
-        functools.partial(out_kernel, before is not None),
-        grid_spec=pltpu.PrefetchScalarGridSpec(
-            num_scalar_prefetch=1,
-            grid=(slabs,),
-            in_specs=in_specs,
-            out_specs=whole,
-            scratch_shapes=[pltpu.VMEM((rows, width), F32)],
-        ),
+        functools.partial(out_kernel, slabs, before is not None),
+        grid=(slabs,),
+        in_specs=in_specs,
+        out_specs=pl.BlockSpec((rows, width), lambda i: (0, 0)),
         out_shape=jax.ShapeDtypeStruct((rows, width), BF16 if last else F32),
+        scratch_shapes=[pltpu.VMEM((rows, width), F32)],
         compiler_params=params(),
         cost_estimate=cost(2 * slabs * rows * cols * width, 2 * slabs * cols * width),
         name="out_project",
-    )(slots, *operands)
+    )(*operands)
 
 
 def shards(
@@ -511,23 +513,6 @@
         rope_tables((window - 1 - window_iota).astype(F32)),
     ]
 
-    lanes = lax.axis_size("groups") * ctx
-    piece_rows = width // lanes
-    lane = lax.axis_index("groups") * ctx + me
-    piece = lax.dynamic_slice_in_dim(tie(out_weight, rope, bases, moving), lane * piece_rows, piece_rows, 0)
-    pieces = []
-    for shift in range(slabs):
-        target = (head + shift) % slabs
-        item = lax.dynamic_slice_in_dim(piece, target * tile, tile, 1)
-        if shift:
-            item = lax.ppermute(
-                item, "head", [(i, (i + shift) % slabs) for i in range(slabs)]
-            )
-        pieces.append(item)
-    pieces = jnp.stack(pieces)
-    out_slabs = lax.all_gather(pieces, ("groups", "ctx"), axis=1, tiled=True)
-    out_slots = jnp.stack([(head - i) % slabs for i in range(slabs)]).astype(jnp.int32)
-
     code_sets = [code_arrays(True), code_arrays(False)]
 
     def add_slabs(strand, steps, total):
@@ -542,27 +527,26 @@
 
     def run_ring(strand, moving, early):
         total, waiting = None, [0]
+        partial.clear()
         for step in range(1, slabs):
             arrived[strand].append(moving)
             if step < slabs - 1:
-                if strand == 0 and early and step > 1:
-                    early[0] = (early[0], total)
-                first = early.pop(0) if early else None
+                first = (early.pop(0) if early else None, total)
                 moving = hop([tie(block, first) for block in moving])
                 waiting.append(step)
                 total = add_slabs(strand, waiting, total)
+                partial.append(total)
                 waiting = []
         if waiting:
             total = add_slabs(strand, waiting, total)
         return total
 
-    def finish(strand, last, total, eq):
+    def finish(strand, last, total, eq, cols):
         first = strand == 0
         cos, sin = rope[strand]
         scalars = jnp.stack([slab_at[-1], my_row])
-        own, far, made = [], [], []
-        for part in range(parts):
-            out = finish_kv(
+        made = [
+            finish_kv(
                 part,
                 cols,
                 last,
@@ -575,11 +559,10 @@
                 sin,
                 [embed, total[4], total[5]] if first else None,
             )
-            own.append(out[0])
-            far.append(ctx_far(out[0]) if first else None)
-            made.append(out[1:])
-        out = finish_q(
-            cols,
+            for part in range(width // cols)
+        ]
+        query = finish_q(
+            min(2 * HEAD_DIM, width),
             last,
             scalars,
             query_weight,
@@ -590,53 +573,70 @@
             total[3] if first else eq,
             embed if first else None,
         )
-        return own, far, made, out
+        return made, query
 
     def spread_out(own, far):
         local = [own] + far
         return local + ctx_swap(local)
 
-    def attend_all(strand, blocks, query, tables, before, ids):
-        return [
-            attend(
-                strand == 0,
-                part,
-                cols,
-                ids,
-                query[0],
-                query[1],
-                tables[part],
-                *code_sets[strand],
-                *rope[strand],
-                blocks[part],
-                before[part],
-            )
-            for part in range(parts)
-        ]
-
-    arrived = [[], []]
-    total = run_ring(0, moving, [None, (code_sets, pieces)])
+    def attend_part(strand, part, cols, blocks, query, tables, before, ids):
+        return attend(
+            strand == 0,
+            part * cols,
+            cols,
+            ids,
+            query[0],
+            query[1],
+            tables,
+            *code_sets[strand],
+            *rope[strand],
+            blocks,
+            before,
+        )
+
+    arrived, partial = [[], []], []
+    cut = own_chains(tie(hidden, moving), 1)
+    total = run_ring(0, moving, [None, (code_sets, cut)])
     last = arrived[0][-1]
-    cut = own_chains(tie(hidden, arrived[0][max(0, slabs - 3)]), 1)
     moving = hop([tie(block, item, total) for block, item in zip(cut, last)])
-    own, far, tables, query = finish(0, last, total, None)
-    eq = query[2]
-    total = run_ring(1, moving, [(own, query)])
-    blocks = [spread_out(item, item_far) for item, item_far in zip(own, far)]
-    last = tie(arrived[1][-1], blocks)
-    own_then, _, _, query_then = finish(1, last, total, eq)
-    ids_then = tie(ids, own_then, query_then, out_slabs)
-    before = attend_all(0, blocks, query, tables, [None] * parts, ids_then)
-    far = [ctx_far(item) for item in own_then]
-    blocks = []
+    made, query = finish(0, last, total, None, width)
+    own, tables, eq = made[0][0], made[0][1:], query[2]
+    far = ctx_far(own)
+
+    total = run_ring(1, moving, [])
+    blocks = spread_out(own, tie(far, partial[:1]))
+    before = attend_part(0, 0, width, blocks, query, tables, None, tie(ids, total))
+    last = tie(arrived[1][-1], before)
+
+    lanes = lax.axis_size("groups") * ctx
+    piece_rows = width // lanes
+    lane = lax.axis_index("groups") * ctx + me
+    piece = lax.dynamic_slice_in_dim(out_weight, lane * piece_rows, piece_rows, 0)
+    pieces = []
+    for shift in range(slabs):
+        target = (head + shift) % slabs
+        pieces.append(lax.dynamic_slice_in_dim(piece, target * tile, tile, 1))
+    pieces = tie(pieces, arrived[1][max(0, slabs - 3)])
+
+    def around(item, shift):
+        return lax.ppermute(item, "head", [(i, (i + shift) % slabs) for i in range(slabs)])
+
+    pieces = [around(tie(item, last), shift) if shift else item for shift, item in enumerate(pieces)]
+
+    made, query_then = finish(1, last, total, eq, cols)
+    own_then = [item[0] for item in made]
+    far_then = [ctx_far(item) for item in own_then]
+    far_then[0] = tie(far_then[0], own_then, query_then)
+    pieces = tie(jnp.stack(pieces), far_then[0])
+    out_slabs = lax.all_gather(pieces, ("groups", "ctx"), axis=1, tiled=True)
+    combined, result = [], None
     for part in range(parts):
-        arriving = tie(far[part], before[: part + 1])
-        blocks.append(spread_out(own_then[part], arriving))
-    combined = attend_all(1, blocks, query_then, tables, before, ids)
-    result = None
-    for part in range(parts):
-        gathered = lax.all_gather(combined[part], "head", axis=0, tiled=False)
-        result = out_project(part, gathered, out_slabs, out_slots, part == parts - 1, result)
+        blocks = spread_out(own_then[part], tie(far_then[part], combined))
+        item = attend_part(1, part, cols, blocks, query_then, tables, before, ids)
+        combined.append(item)
+    for part, item in enumerate(combined):
+        slab_rows = [around(item, shift) if shift else item for shift in range(slabs)]
+        result = out_project(part, slab_rows, out_slabs, part == parts - 1, result)
     return result
 
 

time: 211 us -> 195 us (0.924)
  Pallas kernels: 79.5 us -> 38.3 us
  blocking collectives: 33.7 us -> 0 us
  local copies, waits for them, and re-layouts: 6.37 us -> 34.2 us
  starting transfers between devices: 23 us -> 36.1 us
  waiting for transfers between devices: 41.4 us -> 53.3 us
  other arithmetic: 12.8 us -> 17.4 us
    all_gather x2 -> x0, blocking collectives: 33.7 us -> none  [shards(): gathered = lax.all_gather(combined[part], 'head', axis=0, tiled=False)]
    unnamed x66 -> x116, local copies, waits for them, and re-layouts: 3.65 us -> 30.8 us
    ppermute x3 -> x9, starting transfers between devices: 2.81 us -> 18 us  [around(): lax.ppermute(item, 'head', [(i, (i + shift) % slabs) for i in range(slabs)])]
    pallas_call x4 -> x3, Pallas kernels: 25.4 us -> 10.9 us  [attend(): pl.pallas_call(functools.partial(attend_kernel, forward, count, before is...]
    all_gather x1, waiting for transfers between devices: 0.02 us -> 14 us  [shards(): out_slabs = lax.all_gather(pieces, ('groups', 'ctx'), axis=1, tiled=True)]
    pallas_call x4, Pallas kernels: 21.9 us -> 13.1 us  [slab_sums(): pl.pallas_call(functools.partial(slab_kernel, [len(parts) for parts in sl...]
    ppermute x3 -> x9, waiting for transfers between devices: 10.2 us -> 2.43 us  [around(): lax.ppermute(item, 'head', [(i, (i + shift) % slabs) for i in range(slabs)])]
    pallas_call x4 -> x3, Pallas kernels: 14.1 us -> 6.39 us  [finish_kv(): pl.pallas_call(functools.partial(finish_kv_kernel, len(x_parts), embed_pa...]
  transfers between devices with their start and end apart: 31 -> 34, of which waited for: 10 -> 13; matrix products, arithmetic and copies ran while one was open for 6% -> 11% of each run, Pallas kernels for 29% -> 17%
where the time goes in v4:
time: 195 us; the launch traced here: 193 us
  waiting for transfers between devices  53.3 us (27%)
  Pallas kernels  38.3 us (20%)
  starting transfers between devices  36.1 us (19%)
  local copies, waits for them, and re-layouts  34.2 us (18%)
  other arithmetic  17.4 us (9%)
  between operations  14.1 us (7%)
    ppermute x12, waiting for transfers between devices, hop(): return [lax.ppermute(block, 'head', ring) for block in blocks]  31.9 us
    unnamed x116, local copies, waits for them, and re-layouts  30.8 us
    ppermute x9, starting transfers between devices, around(): lax.ppermute(item, 'head', [(i, (i + shift) % slabs) for i in range(slabs)])  18 us
    all_gather x1, waiting for transfers between devices, shards(): out_slabs = lax.all_gather(pieces, ('groups', 'ctx'), axis=1, tiled=True)  14 us
    pallas_call x4, Pallas kernels, slab_sums(): pl.pallas_call(functools.partial(slab_kernel, [len(parts) for parts in sl...  13.1 us
    pallas_call x3, Pallas kernels, attend(): pl.pallas_call(functools.partial(attend_kernel, forward, count, before is...  10.9 us
    ppermute x12, starting transfers between devices, hop(): return [lax.ppermute(block, 'head', ring) for block in blocks]  10.3 us
    ppermute x4, starting transfers between devices, ctx_far(): lax.ppermute(block, 'ctx', [(i, (i + cores * shift) % ctx) for i in range...  7.19 us
  transfers between devices with their start and end apart: 34, of which 13 were waited for; matrix products, arithmetic and copies ran while one was open for 11% of the time, Pallas kernels for 17%

profile of v4, /device:TPU:0, one launch (start us, length us, event | category | flops | bytes accessed | tf_op | source)
XLA Modules:
  0.0 193.4 jit_solution(1658116699653972450)
XLA Ops:
  6.5 3.0 %collective-permute-start.3 = (s32[256]{0:T(256)}, s32[256]{0:T(256)S(1)}, u32[]{:S(2)}, u32[]{:S(2)}) collective-permute-start(s32[256]{0:T(256)} %param.10), channel_id=1, source_target_pairs={{0,8},{4,12},{8,0},{12,4},{1,9},{5,13},{9,1},{13,5},{2,10},{6,14},... | collective-permute-start | bytes 3080 | tf_op jit(solution)/shard_map/ppermute | solution.py:461
  10.6 1.6 collective-permute-start
  12.2 1.6 collective-permute-start.1
  21.5 1.3 collective-permute-start.2
  22.8 4.3 %collective-permute-done.1.refs_6_ = bf16[128,1024]{1,0:T(8,128)(2,1)S(1)} collective-permute-done((bf16[128,1024]{1,0:T(8,128)(2,1)S(1)}, bf16[128,1024]{1,0:T(8,128)(2,1)S(1)}, u32[]{:S(2)}, u32[]{:S(2)}) %collective-permute-start.1) | collective-permute-done | bytes 262176 | tf_op jit(solution)/shard_map/ppermute | solution.py:471
  27.8 2.2 %copy-done = bf16[4096,512]{1,0:T(8,128)(2,1)S(1)} copy-done((bf16[4096,512]{1,0:T(8,128)(2,1)S(1)}, bf16[4096,512]{1,0:T(8,128)(2,1)}, u32[]{:S(2)}) %copy-start) | copy-done | bytes 4194328
  30.0 2.2 %copy-done.4 = bf16[4096,512]{1,0:T(8,128)(2,1)S(1)} copy-done((bf16[4096,512]{1,0:T(8,128)(2,1)S(1)}, bf16[4096,512]{1,0:T(8,128)(2,1)}, u32[]{:S(2)}) %copy-start.4) | copy-done | bytes 4194328
  32.2 2.2 %copy-done.8 = bf16[4096,512]{1,0:T(8,128)(2,1)S(1)} copy-done((bf16[4096,512]{1,0:T(8,128)(2,1)S(1)}, bf16[4096,512]{1,0:T(8,128)(2,1)}, u32[]{:S(2)}) %copy-start.8) | copy-done | bytes 4194328
  35.6 4.1 %slab_sums.4 = (f32[256,512]{1,0:T(8,128)S(1)}, f32[256,512]{1,0:T(8,128)S(1)}, f32[256,512]{1,0:T(8,128)S(1)}, f32[16,512]{1,0:T(8,128)S(1)}, f32[16,512]{1,0:T(8,128)S(1)}, /*index=5*/f32[16,512]{1,0:T(8,128)S(1)}) custom-call(s32[2]{0:T(128)S(1)} %pad_add_fusion.3.scalars, bf16[2,256,1024]{2,1,0:T(8,128)(2,1)S(1)} %copy-done.15, ...), custom_call_target="tpu_custom_call" | custom-call | flops 25165824 | bytes 139264 | tf_op jit(solution)/shard_map/slab_sums/pallas_call | solution.py:117
  40.6 1.4 collective-permute-start.10
  42.0 1.6 collective-permute-start.6
  43.6 5.5 %fusion.1 = (f32[1024,64]{1,0:T(8,128)}, f32[1024,64]{1,0:T(8,128)}, f32[1024,64]{1,0:T(8,128)}, f32[1024,64]{1,0:T(8,128)}, f32[1024,64]{1,0:T(8,128)}, /*index=5*/f32[1024,64]{1,0:T(8,128)}) fusion(f32[64]{0:T(128)S(1)} %copy-done.57, f32[1024]{0:T(1024)S(1)} %copy-done.56, f32[1024]{0:T(1024)S(1)} %copy-done.55), kind=kLoop, calls=%fused_computation.17 | loop fusion | flops 262144 | bytes 1581312 | tf_op jit(solution)/shard_map/neg | solution.py:43
  49.2 2.0 %pad_maximum_fusion = (f32[1024,128]{1,0:T(8,128)S(1)}, f32[1024,128]{1,0:T(8,128)S(1)}) fusion(f32[1024,64]{1,0:T(8,128)} %get-tuple-element.123, f32[1024,64]{1,0:T(8,128)} %get-tuple-element.124, f32[1024,64]{1,0:T(8,128)} %get-tuple-element.125), kind=kLoop, calls=%fused_computation.4 | loop fusion | flops 262144 | bytes 1835008 | tf_op jit(solution)/shard_map/concatenate | solution.py:43
  51.2 2.2 %copy-done.1 = bf16[4096,512]{1,0:T(8,128)(2,1)S(1)} copy-done((bf16[4096,512]{1,0:T(8,128)(2,1)S(1)}, bf16[4096,512]{1,0:T(8,128)(2,1)}, u32[]{:S(2)}) %copy-start.1) | copy-done | bytes 4194328
  53.4 2.2 %copy-done.5 = bf16[4096,512]{1,0:T(8,128)(2,1)S(1)} copy-done((bf16[4096,512]{1,0:T(8,128)(2,1)S(1)}, bf16[4096,512]{1,0:T(8,128)(2,1)}, u32[]{:S(2)}) %copy-start.5) | copy-done | bytes 4194328
  55.6 2.2 %copy-done.9 = bf16[4096,512]{1,0:T(8,128)(2,1)S(1)} copy-done((bf16[4096,512]{1,0:T(8,128)(2,1)S(1)}, bf16[4096,512]{1,0:T(8,128)(2,1)}, u32[]{:S(2)}) %copy-start.9) | copy-done | bytes 4194328
  60.0 3.2 %slab_sums.5 = (f32[256,512]{1,0:T(8,128)S(1)}, f32[256,512]{1,0:T(8,128)S(1)}, f32[256,512]{1,0:T(8,128)S(1)}, f32[16,512]{1,0:T(8,128)S(1)}, f32[16,512]{1,0:T(8,128)S(1)}, /*index=5*/f32[16,512]{1,0:T(8,128)S(1)}) custom-call(s32[1]{0:T(128)} %bitcast.16.scalars, ...), custom_call_target="tpu_custom_call", output_to_operand_aliasing={{0}: (7, {}), {1}: (8, {}), {2}: (9, {}), {3}: (10, {}), {4... | custom-call | flops 12582912 | bytes 90112 | tf_op jit(solution)/shard_map/slab_sums/pallas_call | solution.py:117
  63.7 2.2 %finish_kv.3 = (bf16[2,256,512]{2,1,0:T(8,128)(2,1)}, bf16[16,512]{1,0:T(8,128)(2,1)S(1)}, bf16[16,512]{1,0:T(8,128)(2,1)S(1)}, f32[16,512]{1,0:T(8,128)S(1)}) custom-call(s32[2]{0:T(128)S(1)} %pad_add_fusion.2.scalars, bf16[128,1024]{1,0:T(8,128)(2,1)S(1)} %collective-permute-done.6.refs_0_, bf16[128,1024]{1,0:T(8,128)(2,1)S(1)} %collective-permute-done.10.refs_1_, ...), custom_call_target="tpu_custom_call" | custom-call | flops 8388608 | bytes 61440 | tf_op jit(solution)/shard_map/finish_kv/pallas_call | solution.py:185
  66.5 1.9 collective-permute-start.11
  68.5 9.1 %collective-permute-done.11.refs_5_ = bf16[128,1024]{1,0:T(8,128)(2,1)S(1)} collective-permute-done((bf16[128,1024]{1,0:T(8,128)(2,1)S(1)}, bf16[128,1024]{1,0:T(8,128)(2,1)S(1)}, u32[]{:S(2)}, u32[]{:S(2)}) %collective-permute-start.11) | collective-permute-done | bytes 262176 | tf_op jit(solution)/shard_map/ppermute | solution.py:471
  77.6 2.8 %collective-permute-done.8.refs_4_ = bf16[128,1024]{1,0:T(8,128)(2,1)S(1)} collective-permute-done((bf16[128,1024]{1,0:T(8,128)(2,1)S(1)}, bf16[128,1024]{1,0:T(8,128)(2,1)S(1)}, u32[]{:S(2)}, u32[]{:S(2)}) %collective-permute-start.8) | collective-permute-done | bytes 262176 | tf_op jit(solution)/shard_map/ppermute | solution.py:471
  80.4 3.2 %slab_sums.6 = (f32[256,512]{1,0:T(8,128)S(1)}, f32[256,512]{1,0:T(8,128)S(1)}, f32[256,512]{1,0:T(8,128)S(1)}) custom-call(s32[2]{0:T(128)S(1)} %copy-done.52, bf16[2,256,1024]{2,1,0:T(8,128)(2,1)S(1)} %copy-done.16, bf16[4096,512]{1,0:T(8,128)(2,1)S(1)} %copy-done.10, bf16[4096,512]{1,0:T(8,128)(2,1)S(1)} %copy-done.2, bf16[4096,512]{1,0:T(8,128)(2,1)S(1)} %copy-done.6, ...), custom_call_target="tpu_custom_call" | custom-call | flops 25165824 | bytes 139264 | tf_op jit(solution)/shard_map/slab_sums/pallas_call | solution.py:117
  85.2 10.2 %collective-permute-done.13.refs_1_ = bf16[128,1024]{1,0:T(8,128)(2,1)} collective-permute-done((bf16[128,1024]{1,0:T(8,128)(2,1)S(1)}, bf16[128,1024]{1,0:T(8,128)(2,1)}, u32[]{:S(2)}, u32[]{:S(2)}) %collective-permute-start.13) | collective-permute-done | bytes 262176 | tf_op jit(solution)/shard_map/ppermute | solution.py:471
  95.4 5.2 %collective-permute-done.9.refs_0_ = bf16[128,1024]{1,0:T(8,128)(2,1)} collective-permute-done((bf16[128,1024]{1,0:T(8,128)(2,1)S(1)}, bf16[128,1024]{1,0:T(8,128)(2,1)}, u32[]{:S(2)}, u32[]{:S(2)}) %collective-permute-start.9) | collective-permute-done | bytes 262176 | tf_op jit(solution)/shard_map/ppermute | solution.py:471
  100.7 2.0 %pad_maximum_fusion.2 = (f32[1024,128]{1,0:T(8,128)S(1)}, f32[1024,128]{1,0:T(8,128)S(1)}) fusion(f32[1024,64]{1,0:T(8,128)} %get-tuple-element.116, f32[1024,64]{1,0:T(8,128)} %get-tuple-element.117, f32[1024,64]{1,0:T(8,128)} %get-tuple-element.115), kind=kLoop, calls=%fused_computation.6 | loop fusion | flops 262144 | bytes 1835008 | tf_op jit(solution)/shard_map/concatenate | solution.py:43
  102.7 2.9 %copy-done.11 = bf16[4096,512]{1,0:T(8,128)(2,1)S(1)} copy-done((bf16[4096,512]{1,0:T(8,128)(2,1)S(1)}, bf16[4096,512]{1,0:T(8,128)(2,1)}, u32[]{:S(2)}) %copy-start.11) | copy-done | bytes 4194328
  111.0 1.9 finish_q.2
  112.9 2.6 %slab_sums.7 = (f32[256,512]{1,0:T(8,128)S(1)}, f32[256,512]{1,0:T(8,128)S(1)}, f32[256,512]{1,0:T(8,128)S(1)}) custom-call(s32[1]{0:T(128)} %bitcast.16.scalars, bf16[128,1024]{1,0:T(8,128)(2,1)} %collective-permute-done.9.refs_0_, bf16[128,1024]{1,0:T(8,128)(2,1)} %collective-permute-done.13.refs_1_, ...), custom_call_target="tpu_custom_call", output_to_operand_aliasing={{0}: (6, {}), {1}: (7, {}), {2}: (8, {})} | custom-call | flops 12582912 | bytes 90112 | tf_op jit(solution)/shard_map/slab_sums/pallas_call | solution.py:117
  115.6 3.3 %attend_forward.1.refs_14_ = f32[256,512]{1,0:T(8,128)S(1)} custom-call(s32[4]{0:T(128)S(1)} %copy-done.49, bf16[256,512]{1,0:T(8,128)(2,1)S(1)} %get-tuple-element.79.refs_1_, bf16[256,512]{1,0:T(8,128)(2,1)S(1)} %get-tuple-element.80.refs_2_, bf16[16,512]{1,0:T(8,128)(2,1)S(1)} %get-tuple-element.81.refs_3_, bf16[16,512]{1,0:T(8,128)(2,1)S(1)} %copy-done.33, ...), custom_call_target="tpu_custom_call" | custom-call | flops 16777216 | bytes 32768 | tf_op jit(solution)/shard_map/attend_forward/pallas_call | solution.py:359
  118.9 2.1 %finish_kv.5.refs_10_ = bf16[2,256,256]{2,1,0:T(8,128)(2,1)S(1)} custom-call(s32[2]{0:T(128)S(1)} %copy-done.47, bf16[128,1024]{1,0:T(8,128)(2,1)} %collective-permute-done.12.refs_0_, bf16[128,1024]{1,0:T(8,128)(2,1)} %collective-permute-done.14.refs_1_, bf16[4096,512]{1,0:T(8,128)(2,1)S(1)} %copy-done.3, bf16[4096,512]{1,0:T(8,128)(2,1)S(1)} %copy-done.7, ...), custom_call_target="tpu_custom_call" | custom-call | flops 4194304 | bytes 30720 | tf_op jit(solution)/shard_map/finish_kv/pallas_call | solution.py:185
  121.0 3.3 %collective-permute-start.19 = (bf16[2,256,256]{2,1,0:T(8,128)(2,1)S(1)}, bf16[2,256,256]{2,1,0:T(8,128)(2,1)}, u32[]{:S(2)}, u32[]{:S(2)}) collective-permute-start(bf16[2,256,256]{2,1,0:T(8,128)(2,1)S(1)} %finish_kv.5.refs_10_), channel_id=1, source_target_pairs={{0,8},{4,12},{8,0},{12,4},{1,9},{5,13},{9,1},{13,5},{2,10},{6,14},... | collective-permute-start | bytes 786440 | tf_op jit(solution)/shard_map/ppermute | solution.py:461
  124.3 1.4 fusion.3
  126.4 3.9 %collective-permute-start.28 = (bf16[64,1024]{1,0:T(8,128)(2,1)S(1)}, bf16[64,1024]{1,0:T(8,128)(2,1)S(1)}, u32[]{:S(2)}, u32[]{:S(2)}) collective-permute-start(bf16[64,1024]{1,0:T(8,128)(2,1)S(1)} %get-tuple-element.97), channel_id=1, source_target_pairs={{0,2},{1,3},{2,0},{3,1},{4,6},{5,7},{6,4},{7,5},{8,10},{9,11},{10,... | collective-permute-start | bytes 393224 | tf_op jit(solution)/shard_map/ppermute | solution.py:622
  130.3 2.8 %collective-permute-start.29 = (bf16[64,1024]{1,0:T(8,128)(2,1)S(1)}, bf16[64,1024]{1,0:T(8,128)(2,1)S(1)}, u32[]{:S(2)}, u32[]{:S(2)}) collective-permute-start(bf16[64,1024]{1,0:T(8,128)(2,1)S(1)} %get-tuple-element.99), channel_id=1, source_target_pairs={{0,3},{1,0},{2,1},{3,2},{4,7},{5,4},{6,5},{7,6},{8,11},{9,8},{10,9... | collective-permute-start | bytes 393224 | tf_op jit(solution)/shard_map/ppermute | solution.py:622
  133.1 2.1 %finish_kv.4.refs_10_ = bf16[2,256,256]{2,1,0:T(8,128)(2,1)S(1)} custom-call(s32[2]{0:T(128)S(1)} %copy-done.47, bf16[128,1024]{1,0:T(8,128)(2,1)} %collective-permute-done.12.refs_0_, bf16[128,1024]{1,0:T(8,128)(2,1)} %collective-permute-done.14.refs_1_, bf16[4096,512]{1,0:T(8,128)(2,1)S(1)} %copy-done.3, bf16[4096,512]{1,0:T(8,128)(2,1)S(1)} %copy-done.7, ...), custom_call_target="tpu_custom_call" | custom-call | flops 4194304 | bytes 30720 | tf_op jit(solution)/shard_map/finish_kv/pallas_call | solution.py:185
  135.3 2.7 %finish_q.3 = (bf16[256,512]{1,0:T(8,128)(2,1)S(1)}, bf16[256,512]{1,0:T(8,128)(2,1)S(1)}) custom-call(s32[2]{0:T(128)S(1)} %copy-done.48, bf16[128,1024]{1,0:T(8,128)(2,1)} %collective-permute-done.12.refs_0_, bf16[128,1024]{1,0:T(8,128)(2,1)} %collective-permute-done.14.refs_1_, bf16[4096,512]{1,0:T(8,128)(2,1)S(1)} %copy-done.12, ...), custom_call_target="tpu_custom_call" | custom-call | flops 4194304 | bytes 32768 | tf_op jit(solution)/shard_map/finish_q/pallas_call | solution.py:245
  142.2 4.0 %attend_reverse.2.refs_0_ = bf16[256,256]{1,0:T(8,128)(2,1)S(1)} custom-call(s32[4]{0:T(128)S(1)} %copy-done.50, bf16[256,512]{1,0:T(8,128)(2,1)S(1)} %get-tuple-element.89.refs_1_, bf16[256,512]{1,0:T(8,128)(2,1)S(1)} %get-tuple-element.90.refs_2_, bf16[16,512]{1,0:T(8,128)(2,1)S(1)} %get-tuple-element.81.refs_3_, bf16[16,512]{1,0:T(8,128)(2,1)S(1)} %copy-done.34, ...), custom_call_target="tpu_custom_call" | custom-call | flops 8388608 | bytes 16384 | tf_op jit(solution)/shard_map/attend_reverse/pallas_call | solution.py:359
  146.3 2.6 %collective-permute-done.18.refs_11_ = bf16[2,256,256]{2,1,0:T(8,128)(2,1)S(1)} collective-permute-done((bf16[2,256,256]{2,1,0:T(8,128)(2,1)S(1)}, bf16[2,256,256]{2,1,0:T(8,128)(2,1)S(1)}, u32[]{:S(2)}, u32[]{:S(2)}) %collective-permute-start.18) | collective-permute-done | bytes 262176 | tf_op jit(solution)/shard_map/ppermute | solution.py:461
  148.9 3.3 %collective-permute-start.30 = (bf16[256,256]{1,0:T(8,128)(2,1)S(1)}, bf16[256,256]{1,0:T(8,128)(2,1)S(1)}, u32[]{:S(2)}, u32[]{:S(2)}) collective-permute-start(bf16[256,256]{1,0:T(8,128)(2,1)S(1)} %attend_reverse.2.refs_0_), channel_id=1, source_target_pairs={{0,1},{1,2},{2,3},{3,0},{4,5},{5,6},{6,7},{7,4},{8,9},{9,10},{10,1... | collective-permute-start | bytes 393224 | tf_op jit(solution)/shard_map/ppermute | solution.py:622
  152.2 2.9 %collective-permute-start.31 = (bf16[256,256]{1,0:T(8,128)(2,1)S(1)}, bf16[256,256]{1,0:T(8,128)(2,1)S(1)}, u32[]{:S(2)}, u32[]{:S(2)}) collective-permute-start(bf16[256,256]{1,0:T(8,128)(2,1)S(1)} %attend_reverse.2.refs_0_), channel_id=1, source_target_pairs={{0,2},{1,3},{2,0},{3,1},{4,6},{5,7},{6,4},{7,5},{8,10},{9,11},{10,... | collective-permute-start | bytes 393224 | tf_op jit(solution)/shard_map/ppermute | solution.py:622
  155.1 3.6 %attend_reverse.3.refs_0_ = bf16[256,256]{1,0:T(8,128)(2,1)S(1)} custom-call(s32[4]{0:T(128)S(1)} %copy-done.50, bf16[256,512]{1,0:T(8,128)(2,1)S(1)} %get-tuple-element.89.refs_1_, bf16[256,512]{1,0:T(8,128)(2,1)S(1)} %get-tuple-element.90.refs_2_, bf16[16,512]{1,0:T(8,128)(2,1)S(1)} %get-tuple-element.81.refs_3_, bf16[16,512]{1,0:T(8,128)(2,1)S(1)} %copy-done.34, ...), custom_call_target="tpu_custom_call" | custom-call | flops 8388608 | bytes 16384 | tf_op jit(solution)/shard_map/attend_reverse/pallas_call | solution.py:359
  158.7 2.1 %collective-permute-start.24 = (bf16[256,256]{1,0:T(8,128)(2,1)S(1)}, bf16[256,256]{1,0:T(8,128)(2,1)S(1)}, u32[]{:S(2)}, u32[]{:S(2)}) collective-permute-start(bf16[256,256]{1,0:T(8,128)(2,1)S(1)} %attend_reverse.3.refs_0_), channel_id=1, source_target_pairs={{0,1},{1,2},{2,3},{3,0},{4,5},{5,6},{6,7},{7,4},{8,9},{9,10},{10,1... | collective-permute-start | bytes 393224 | tf_op jit(solution)/shard_map/ppermute | solution.py:622
  160.8 2.4 %collective-permute-start.26 = (bf16[256,256]{1,0:T(8,128)(2,1)S(1)}, bf16[256,256]{1,0:T(8,128)(2,1)S(1)}, u32[]{:S(2)}, u32[]{:S(2)}) collective-permute-start(bf16[256,256]{1,0:T(8,128)(2,1)S(1)} %attend_reverse.3.refs_0_), channel_id=1, source_target_pairs={{0,3},{1,0},{2,1},{3,2},{4,7},{5,4},{6,5},{7,6},{8,11},{9,8},{10,9... | collective-permute-start | bytes 393224 | tf_op jit(solution)/shard_map/ppermute | solution.py:622
  163.2 1.3 collective-permute-done.31.refs_2_
  165.2 14.0 %all-gather.2.cloned.1.call-done.refs_4_ = bf16[4,512,1024]{2,1,0:T(8,128)(2,1)} async-done(((bf16[4,64,1024]{2,1,0:T(8,128)(2,1)}), bf16[4,512,1024]{2,1,0:T(8,128)(2,1)}) %all-gather.2.cloned.1.call-update) | async-done | bytes 4194320 | tf_op jit(solution)/shard_map/all_gather | solution.py:631
  179.2 2.2 %copy-done.13 = bf16[4,512,1024]{2,1,0:T(8,128)(2,1)S(1)} copy-done((bf16[4,512,1024]{2,1,0:T(8,128)(2,1)S(1)}, bf16[4,512,1024]{2,1,0:T(8,128)(2,1)}, u32[]{:S(2)}) %copy-start.13) | copy-done | bytes 4194328
  182.3 1.3 out_project.2.refs_5_
  184.5 2.1 %out_project.3 = bf16[256,1024]{1,0:T(8,128)(2,1)} custom-call(bf16[256,256]{1,0:T(8,128)(2,1)S(1)} %attend_reverse.3.refs_0_, bf16[256,256]{1,0:T(8,128)(2,1)S(1)} %collective-permute-done.24.refs_1_, bf16[256,256]{1,0:T(8,128)(2,1)S(1)} %collective-permute-done.25.refs_2_, bf16[256,256]{1,0:T(8,128)(2,1)S(1)} %collective-permute-done.26.refs_3_, ...), custom_call_target="tpu_custom_call" | custom-call | flops 8388608 | bytes 32768 | tf_op jit(solution)/shard_map/out_project/pallas_call | solution.py:416
  (174 shorter events, 29.2 us)
Async XLA Ops:
  6.5 172.7 %all-gather.2.cloned.1.call-start = ((), (), s32[]{:S(2)}) async-start(), calls=%async_computation | async-start | bytes 4718592 | tf_op jit(solution)/shard_map/all_gather | solution.py:631
  6.5 11.7 %collective-permute-start.3 = (s32[256]{0:T(256)}, s32[256]{0:T(256)S(1)}, u32[]{:S(2)}, u32[]{:S(2)}) collective-permute-start(s32[256]{0:T(256)} %param.10), channel_id=1, source_target_pairs={{0,8},{4,12},{8,0},{12,4},{1,9},{5,13},{9,1},{13,5},{2,10},{6,14},... | collective-permute-start | bytes 3080 | tf_op jit(solution)/shard_map/ppermute | solution.py:461
  9.5 8.9 %collective-permute-start.4 = (s32[256]{0:T(256)}, s32[256]{0:T(256)S(1)}, u32[]{:S(2)}, u32[]{:S(2)}) collective-permute-start(s32[256]{0:T(256)} %param.10), channel_id=1, source_target_pairs={{0,4},{4,0},{8,12},{12,8},{1,5},{5,1},{9,13},{13,9},{2,6},{6,2},{1... | collective-permute-start | bytes 3080 | tf_op jit(solution)/shard_map/ppermute | solution.py:468
  10.6 10.9 %collective-permute-start = (bf16[128,1024]{1,0:T(8,128)(2,1)S(1)}, bf16[128,1024]{1,0:T(8,128)(2,1)S(1)}, u32[]{:S(2)}, u32[]{:S(2)}) collective-permute-start(bf16[128,1024]{1,0:T(8,128)(2,1)S(1)} %get-tuple-element.110), channel_id=1, source_target_pairs={{0,1},{1,2},{2,3},{3,0},{4,5},{5,6},{6,7},{7,4},{8,9},{9,10},{10,1... | collective-permute-start | bytes 786440 | tf_op jit(solution)/shard_map/ppermute | solution.py:471
  12.2 14.9 %collective-permute-start.1 = (bf16[128,1024]{1,0:T(8,128)(2,1)S(1)}, bf16[128,1024]{1,0:T(8,128)(2,1)S(1)}, u32[]{:S(2)}, u32[]{:S(2)}) collective-permute-start(bf16[128,1024]{1,0:T(8,128)(2,1)S(1)} %get-tuple-element.109), channel_id=1, source_target_pairs={{0,1},{1,2},{2,3},{3,0},{4,5},{5,6},{6,7},{7,4},{8,9},{9,10},{10,1... | collective-permute-start | bytes 786440 | tf_op jit(solution)/shard_map/ppermute | solution.py:471
  18.3 1.2 collective-permute-start.5
  18.4 21.3 %copy-start.51 = (s32[2]{0:T(128)}, s32[2]{0:T(128)S(1)}, u32[]{:S(2)}) copy-start(s32[2]{0:T(128)S(1)} %pad_add_fusion.3.scalars) | copy-start | bytes 28
  21.5 19.1 %collective-permute-start.2 = (bf16[128,1024]{1,0:T(8,128)(2,1)S(1)}, bf16[128,1024]{1,0:T(8,128)(2,1)}, u32[]{:S(2)}, u32[]{:S(2)}) collective-permute-start(bf16[128,1024]{1,0:T(8,128)(2,1)S(1)} %collective-permute-done.refs_5_), channel_id=1, source_target_pairs={{0,1},{1,2},{2,3},{3,0},{4,5},{5,6},{6,7},{7,4},{8,9},{9,10},{10,1... | collective-permute-start | bytes 786440 | tf_op jit(solution)/shard_map/ppermute | solution.py:471
  27.1 13.5 %collective-permute-start.7 = (bf16[128,1024]{1,0:T(8,128)(2,1)S(1)}, bf16[128,1024]{1,0:T(8,128)(2,1)}, u32[]{:S(2)}, u32[]{:S(2)}) collective-permute-start(bf16[128,1024]{1,0:T(8,128)(2,1)S(1)} %collective-permute-done.1.refs_6_), channel_id=1, source_target_pairs={{0,1},{1,2},{2,3},{3,0},{4,5},{5,6},{6,7},{7,4},{8,9},{9,10},{10,1... | collective-permute-start | bytes 786440 | tf_op jit(solution)/shard_map/ppermute | solution.py:471
  39.8 9.4 %copy-start.35 = (f32[16,512]{1,0:T(8,128)}, f32[16,512]{1,0:T(8,128)S(1)}, u32[]{:S(2)}) copy-start(f32[16,512]{1,0:T(8,128)S(1)} %get-tuple-element.57.refs_9_) | copy-start | bytes 98308
  39.8 9.4 %copy-start.39 = (f32[16,512]{1,0:T(8,128)}, f32[16,512]{1,0:T(8,128)S(1)}, u32[]{:S(2)}) copy-start(f32[16,512]{1,0:T(8,128)S(1)} %get-tuple-element.58.refs_10_) | copy-start | bytes 98308
  39.8 9.4 %copy-start.41 = (f32[16,512]{1,0:T(8,128)}, f32[16,512]{1,0:T(8,128)S(1)}, u32[]{:S(2)}) copy-start(f32[16,512]{1,0:T(8,128)S(1)} %get-tuple-element.59.refs_11_) | copy-start | bytes 98308
  40.6 22.6 %collective-permute-start.10 = (bf16[128,1024]{1,0:T(8,128)(2,1)}, bf16[128,1024]{1,0:T(8,128)(2,1)S(1)}, u32[]{:S(2)}, u32[]{:S(2)}) collective-permute-start(bf16[128,1024]{1,0:T(8,128)(2,1)} %collective-permute-done.7.refs_1_), channel_id=1, source_target_pairs={{0,1},{1,2},{2,3},{3,0},{4,5},{5,6},{6,7},{7,4},{8,9},{9,10},{10,1... | collective-permute-start | bytes 786440 | tf_op jit(solution)/shard_map/ppermute | solution.py:471
  42.0 21.2 %collective-permute-start.6 = (bf16[128,1024]{1,0:T(8,128)(2,1)}, bf16[128,1024]{1,0:T(8,128)(2,1)S(1)}, u32[]{:S(2)}, u32[]{:S(2)}) collective-permute-start(bf16[128,1024]{1,0:T(8,128)(2,1)} %collective-permute-done.2.refs_0_), channel_id=1, source_target_pairs={{0,1},{1,2},{2,3},{3,0},{4,5},{5,6},{6,7},{7,4},{8,9},{9,10},{10,1... | collective-permute-start | bytes 786440 | tf_op jit(solution)/shard_map/ppermute | solution.py:471
  49.2 14.1 %copy-start.46 = (s32[2]{0:T(128)}, s32[2]{0:T(128)S(1)}, u32[]{:S(2)}) copy-start(s32[2]{0:T(128)S(1)} %pad_add_fusion.2.scalars) | copy-start | bytes 28
  63.7 16.7 %copy-start.10 = (bf16[4096,512]{1,0:T(8,128)(2,1)S(1)}, bf16[4096,512]{1,0:T(8,128)(2,1)}, u32[]{:S(2)}) copy-start(bf16[4096,512]{1,0:T(8,128)(2,1)} %refs_2_.15) | copy-start | bytes 12582916
  63.7 16.7 %copy-start.16 = (bf16[2,256,1024]{2,1,0:T(8,128)(2,1)S(1)}, bf16[2,256,1024]{2,1,0:T(8,128)(2,1)}, u32[]{:S(2)}) copy-start(bf16[2,256,1024]{2,1,0:T(8,128)(2,1)} %refs_0_.3) | copy-start | bytes 3145732
  63.7 16.7 %copy-start.52 = (s32[2]{0:T(128)S(1)}, s32[2]{0:T(128)}, u32[]{:S(2)}) copy-start(s32[2]{0:T(128)} %copy-done.51) | copy-start | bytes 28
  65.9 17.7 %copy-start.28 = (f32[16,512]{1,0:T(8,128)}, f32[16,512]{1,0:T(8,128)S(1)}, u32[]{:S(2)}) copy-start(f32[16,512]{1,0:T(8,128)S(1)} %get-tuple-element.83.refs_5_) | copy-start | bytes 98308
  65.9 17.7 %copy-start.32 = (bf16[16,512]{1,0:T(8,128)(2,1)}, bf16[16,512]{1,0:T(8,128)(2,1)S(1)}, u32[]{:S(2)}) copy-start(bf16[16,512]{1,0:T(8,128)(2,1)S(1)} %get-tuple-element.82.refs_4_) | copy-start | bytes 49156
  65.9 18.5 %collective-permute-start.15 = (bf16[2,256,512]{2,1,0:T(8,128)(2,1)}, bf16[2,256,512]{2,1,0:T(8,128)(2,1)}, u32[]{:S(2)}, u32[]{:S(2)}) collective-permute-start(bf16[2,256,512]{2,1,0:T(8,128)(2,1)} %get-tuple-element.84.refs_10_), channel_id=1, source_target_pairs={{0,8},{4,12},{8,0},{12,4},{1,9},{5,13},{9,1},{13,5},{2,10},{6,14},... | collective-permute-start | bytes 1572872 | tf_op jit(solution)/shard_map/ppermute | solution.py:461
  66.5 11.0 %collective-permute-start.11 = (bf16[128,1024]{1,0:T(8,128)(2,1)S(1)}, bf16[128,1024]{1,0:T(8,128)(2,1)S(1)}, u32[]{:S(2)}, u32[]{:S(2)}) collective-permute-start(bf16[128,1024]{1,0:T(8,128)(2,1)S(1)} %copy-done.54), channel_id=1, source_target_pairs={{0,1},{1,2},{2,3},{3,0},{4,5},{5,6},{6,7},{7,4},{8,9},{9,10},{10,1... | collective-permute-start | bytes 786440 | tf_op jit(solution)/shard_map/ppermute | solution.py:471
  68.4 12.0 %collective-permute-start.8 = (bf16[128,1024]{1,0:T(8,128)(2,1)S(1)}, bf16[128,1024]{1,0:T(8,128)(2,1)S(1)}, u32[]{:S(2)}, u32[]{:S(2)}) collective-permute-start(bf16[128,1024]{1,0:T(8,128)(2,1)S(1)} %copy-done.53), channel_id=1, source_target_pairs={{0,1},{1,2},{2,3},{3,0},{4,5},{5,6},{6,7},{7,4},{8,9},{9,10},{10,1... | collective-permute-start | bytes 786440 | tf_op jit(solution)/shard_map/ppermute | solution.py:471
  68.5 47.0 %collective-permute-start.16 = (bf16[2,256,512]{2,1,0:T(8,128)(2,1)}, bf16[2,256,512]{2,1,0:T(8,128)(2,1)}, u32[]{:S(2)}, u32[]{:S(2)}) collective-permute-start(bf16[2,256,512]{2,1,0:T(8,128)(2,1)} %get-tuple-element.84.refs_10_), channel_id=1, source_target_pairs={{0,4},{4,0},{8,12},{12,8},{1,5},{5,1},{9,13},{13,9},{2,6},{6,2},{1... | collective-permute-start | bytes 1572872 | tf_op jit(solution)/shard_map/ppermute | solution.py:468
  84.4 31.1 %collective-permute-start.17 = (bf16[2,256,512]{2,1,0:T(8,128)(2,1)}, bf16[2,256,512]{2,1,0:T(8,128)(2,1)}, u32[]{:S(2)}, u32[]{:S(2)}) collective-permute-start(bf16[2,256,512]{2,1,0:T(8,128)(2,1)} %collective-permute-done.15.refs_11_), channel_id=1, source_target_pairs={{0,4},{4,0},{8,12},{12,8},{1,5},{5,1},{9,13},{13,9},{2,6},{6,2},{1... | collective-permute-start | bytes 1572872 | tf_op jit(solution)/shard_map/ppermute | solution.py:468
  84.4 11.0 %collective-permute-start.13 = (bf16[128,1024]{1,0:T(8,128)(2,1)S(1)}, bf16[128,1024]{1,0:T(8,128)(2,1)}, u32[]{:S(2)}, u32[]{:S(2)}) collective-permute-start(bf16[128,1024]{1,0:T(8,128)(2,1)S(1)} %collective-permute-done.11.refs_5_), channel_id=1, source_target_pairs={{0,1},{1,2},{2,3},{3,0},{4,5},{5,6},{6,7},{7,4},{8,9},{9,10},{10,1... | collective-permute-start | bytes 786440 | tf_op jit(solution)/shard_map/ppermute | solution.py:471
  84.9 15.8 %collective-permute-start.9 = (bf16[128,1024]{1,0:T(8,128)(2,1)S(1)}, bf16[128,1024]{1,0:T(8,128)(2,1)}, u32[]{:S(2)}, u32[]{:S(2)}) collective-permute-start(bf16[128,1024]{1,0:T(8,128)(2,1)S(1)} %collective-permute-done.8.refs_4_), channel_id=1, source_target_pairs={{0,1},{1,2},{2,3},{3,0},{4,5},{5,6},{6,7},{7,4},{8,9},{9,10},{10,1... | collective-permute-start | bytes 786440 | tf_op jit(solution)/shard_map/ppermute | solution.py:471
  100.7 18.2 %collective-permute-start.14 = (bf16[128,1024]{1,0:T(8,128)(2,1)}, bf16[128,1024]{1,0:T(8,128)(2,1)}, u32[]{:S(2)}, u32[]{:S(2)}) collective-permute-start(bf16[128,1024]{1,0:T(8,128)(2,1)} %collective-permute-done.13.refs_1_), channel_id=1, source_target_pairs={{0,1},{1,2},{2,3},{3,0},{4,5},{5,6},{6,7},{7,4},{8,9},{9,10},{10,1... | collective-permute-start | bytes 786440 | tf_op jit(solution)/shard_map/ppermute | solution.py:471
  100.7 18.2 %collective-permute-start.12 = (bf16[128,1024]{1,0:T(8,128)(2,1)}, bf16[128,1024]{1,0:T(8,128)(2,1)}, u32[]{:S(2)}, u32[]{:S(2)}) collective-permute-start(bf16[128,1024]{1,0:T(8,128)(2,1)} %collective-permute-done.9.refs_0_), channel_id=1, source_target_pairs={{0,1},{1,2},{2,3},{3,0},{4,5},{5,6},{6,7},{7,4},{8,9},{9,10},{10,1... | collective-permute-start | bytes 786440 | tf_op jit(solution)/shard_map/ppermute | solution.py:471
  100.7 12.2 %copy-start.3 = (bf16[4096,512]{1,0:T(8,128)(2,1)S(1)}, bf16[4096,512]{1,0:T(8,128)(2,1)}, u32[]{:S(2)}) copy-start(bf16[4096,512]{1,0:T(8,128)(2,1)} %refs_2_.17) | copy-start | bytes 12582916
  100.7 12.2 %copy-start.7 = (bf16[4096,512]{1,0:T(8,128)(2,1)S(1)}, bf16[4096,512]{1,0:T(8,128)(2,1)}, u32[]{:S(2)}) copy-start(bf16[4096,512]{1,0:T(8,128)(2,1)} %refs_3_.13) | copy-start | bytes 12582916
  121.0 19.0 %collective-permute-start.19 = (bf16[2,256,256]{2,1,0:T(8,128)(2,1)S(1)}, bf16[2,256,256]{2,1,0:T(8,128)(2,1)}, u32[]{:S(2)}, u32[]{:S(2)}) collective-permute-start(bf16[2,256,256]{2,1,0:T(8,128)(2,1)S(1)} %finish_kv.5.refs_10_), channel_id=1, source_target_pairs={{0,8},{4,12},{8,0},{12,4},{1,9},{5,13},{9,1},{13,5},{2,10},{6,14},... | collective-permute-start | bytes 786440 | tf_op jit(solution)/shard_map/ppermute | solution.py:461
  125.8 9.5 %copy-start.12 = (bf16[4096,512]{1,0:T(8,128)(2,1)S(1)}, bf16[4096,512]{1,0:T(8,128)(2,1)}, u32[]{:S(2)}) copy-start(bf16[4096,512]{1,0:T(8,128)(2,1)} %refs_2_.15) | copy-start | bytes 12582916
  125.8 9.5 %copy-start.48 = (s32[2]{0:T(128)S(1)}, s32[2]{0:T(128)}, u32[]{:S(2)}) copy-start(s32[2]{0:T(128)} %copy-done.46) | copy-start | bytes 28
  125.8 12.2 %collective-permute-start.27 = (bf16[64,1024]{1,0:T(8,128)(2,1)S(1)}, bf16[64,1024]{1,0:T(8,128)(2,1)S(1)}, u32[]{:S(2)}, u32[]{:S(2)}) collective-permute-start(bf16[64,1024]{1,0:T(8,128)(2,1)S(1)} %get-tuple-element.95), channel_id=1, source_target_pairs={{0,1},{1,2},{2,3},{3,0},{4,5},{5,6},{6,7},{7,4},{8,9},{9,10},{10,1... | collective-permute-start | bytes 393224 | tf_op jit(solution)/shard_map/ppermute | solution.py:622
  126.4 12.7 %collective-permute-start.28 = (bf16[64,1024]{1,0:T(8,128)(2,1)S(1)}, bf16[64,1024]{1,0:T(8,128)(2,1)S(1)}, u32[]{:S(2)}, u32[]{:S(2)}) collective-permute-start(bf16[64,1024]{1,0:T(8,128)(2,1)S(1)} %get-tuple-element.97), channel_id=1, source_target_pairs={{0,2},{1,3},{2,0},{3,1},{4,6},{5,7},{6,4},{7,5},{8,10},{9,11},{10,... | collective-permute-start | bytes 393224 | tf_op jit(solution)/shard_map/ppermute | solution.py:622
  130.3 8.8 %collective-permute-start.29 = (bf16[64,1024]{1,0:T(8,128)(2,1)S(1)}, bf16[64,1024]{1,0:T(8,128)(2,1)S(1)}, u32[]{:S(2)}, u32[]{:S(2)}) collective-permute-start(bf16[64,1024]{1,0:T(8,128)(2,1)S(1)} %get-tuple-element.99), channel_id=1, source_target_pairs={{0,3},{1,0},{2,1},{3,2},{4,7},{5,4},{6,5},{7,6},{8,11},{9,8},{10,9... | collective-permute-start | bytes 393224 | tf_op jit(solution)/shard_map/ppermute | solution.py:622
  140.0 1.6 collective-permute-start.20
  140.1 2.1 %collective-permute-start.21 = (bf16[2,256,256]{2,1,0:T(8,128)(2,1)}, bf16[2,256,256]{2,1,0:T(8,128)(2,1)S(1)}, u32[]{:S(2)}, u32[]{:S(2)}) collective-permute-start(bf16[2,256,256]{2,1,0:T(8,128)(2,1)} %collective-permute-done.19.refs_11_), channel_id=1, source_target_pairs={{0,4},{4,0},{8,12},{12,8},{1,5},{5,1},{9,13},{13,9},{2,6},{6,2},{1... | collective-permute-start | bytes 786440 | tf_op jit(solution)/shard_map/ppermute | solution.py:468
  140.6 8.3 %collective-permute-start.18 = (bf16[2,256,256]{2,1,0:T(8,128)(2,1)S(1)}, bf16[2,256,256]{2,1,0:T(8,128)(2,1)S(1)}, u32[]{:S(2)}, u32[]{:S(2)}) collective-permute-start(bf16[2,256,256]{2,1,0:T(8,128)(2,1)S(1)} %finish_kv.4.refs_10_), channel_id=1, source_target_pairs={{0,8},{4,12},{8,0},{12,4},{1,9},{5,13},{9,1},{13,5},{2,10},{6,14},... | collective-permute-start | bytes 786440 | tf_op jit(solution)/shard_map/ppermute | solution.py:461
  140.9 14.2 %collective-permute-start.22 = (bf16[2,256,256]{2,1,0:T(8,128)(2,1)S(1)}, bf16[2,256,256]{2,1,0:T(8,128)(2,1)S(1)}, u32[]{:S(2)}, u32[]{:S(2)}) collective-permute-start(bf16[2,256,256]{2,1,0:T(8,128)(2,1)S(1)} %finish_kv.4.refs_10_), channel_id=1, source_target_pairs={{0,4},{4,0},{8,12},{12,8},{1,5},{5,1},{9,13},{13,9},{2,6},{6,2},{1... | collective-permute-start | bytes 786440 | tf_op jit(solution)/shard_map/ppermute | solution.py:468
  148.9 6.2 %collective-permute-start.23 = (bf16[2,256,256]{2,1,0:T(8,128)(2,1)S(1)}, bf16[2,256,256]{2,1,0:T(8,128)(2,1)S(1)}, u32[]{:S(2)}, u32[]{:S(2)}) collective-permute-start(bf16[2,256,256]{2,1,0:T(8,128)(2,1)S(1)} %collective-permute-done.18.refs_11_), channel_id=1, source_target_pairs={{0,4},{4,0},{8,12},{12,8},{1,5},{5,1},{9,13},{13,9},{2,6},{6,2},{1... | collective-permute-start | bytes 786440 | tf_op jit(solution)/shard_map/ppermute | solution.py:468
  148.9 11.9 %collective-permute-start.30 = (bf16[256,256]{1,0:T(8,128)(2,1)S(1)}, bf16[256,256]{1,0:T(8,128)(2,1)S(1)}, u32[]{:S(2)}, u32[]{:S(2)}) collective-permute-start(bf16[256,256]{1,0:T(8,128)(2,1)S(1)} %attend_reverse.2.refs_0_), channel_id=1, source_target_pairs={{0,1},{1,2},{2,3},{3,0},{4,5},{5,6},{6,7},{7,4},{8,9},{9,10},{10,1... | collective-permute-start | bytes 393224 | tf_op jit(solution)/shard_map/ppermute | solution.py:622
  152.2 12.4 %collective-permute-start.31 = (bf16[256,256]{1,0:T(8,128)(2,1)S(1)}, bf16[256,256]{1,0:T(8,128)(2,1)S(1)}, u32[]{:S(2)}, u32[]{:S(2)}) collective-permute-start(bf16[256,256]{1,0:T(8,128)(2,1)S(1)} %attend_reverse.2.refs_0_), channel_id=1, source_target_pairs={{0,2},{1,3},{2,0},{3,1},{4,6},{5,7},{6,4},{7,5},{8,10},{9,11},{10,... | collective-permute-start | bytes 393224 | tf_op jit(solution)/shard_map/ppermute | solution.py:622
  155.0 9.5 %collective-permute-start.32 = (bf16[256,256]{1,0:T(8,128)(2,1)S(1)}, bf16[256,256]{1,0:T(8,128)(2,1)S(1)}, u32[]{:S(2)}, u32[]{:S(2)}) collective-permute-start(bf16[256,256]{1,0:T(8,128)(2,1)S(1)} %attend_reverse.2.refs_0_), channel_id=1, source_target_pairs={{0,3},{1,0},{2,1},{3,2},{4,7},{5,4},{6,5},{7,6},{8,11},{9,8},{10,9... | collective-permute-start | bytes 393224 | tf_op jit(solution)/shard_map/ppermute | solution.py:622
  158.7 24.9 %collective-permute-start.24 = (bf16[256,256]{1,0:T(8,128)(2,1)S(1)}, bf16[256,256]{1,0:T(8,128)(2,1)S(1)}, u32[]{:S(2)}, u32[]{:S(2)}) collective-permute-start(bf16[256,256]{1,0:T(8,128)(2,1)S(1)} %attend_reverse.3.refs_0_), channel_id=1, source_target_pairs={{0,1},{1,2},{2,3},{3,0},{4,5},{5,6},{6,7},{7,4},{8,9},{9,10},{10,1... | collective-permute-start | bytes 393224 | tf_op jit(solution)/shard_map/ppermute | solution.py:622
  160.8 22.8 %collective-permute-start.25 = (bf16[256,256]{1,0:T(8,128)(2,1)S(1)}, bf16[256,256]{1,0:T(8,128)(2,1)S(1)}, u32[]{:S(2)}, u32[]{:S(2)}) collective-permute-start(bf16[256,256]{1,0:T(8,128)(2,1)S(1)} %attend_reverse.3.refs_0_), channel_id=1, source_target_pairs={{0,2},{1,3},{2,0},{3,1},{4,6},{5,7},{6,4},{7,5},{8,10},{9,11},{10,... | collective-permute-start | bytes 393224 | tf_op jit(solution)/shard_map/ppermute | solution.py:622
  160.8 22.8 %collective-permute-start.26 = (bf16[256,256]{1,0:T(8,128)(2,1)S(1)}, bf16[256,256]{1,0:T(8,128)(2,1)S(1)}, u32[]{:S(2)}, u32[]{:S(2)}) collective-permute-start(bf16[256,256]{1,0:T(8,128)(2,1)S(1)} %attend_reverse.3.refs_0_), channel_id=1, source_target_pairs={{0,3},{1,0},{2,1},{3,2},{4,7},{5,4},{6,5},{7,6},{8,11},{9,8},{10,9... | collective-permute-start | bytes 393224 | tf_op jit(solution)/shard_map/ppermute | solution.py:622
  (44 other events, 130.1 us)
Sparse Core Ops, SparseCore 0:
  140.1 39.0 all-gather.1

commit v5 on v4

--- a/solution.py
+++ b/solution.py
@@ -17,12 +17,13 @@
 COST_CUT = 64
 SCORE_SCALE = math.log2(math.e) / math.sqrt(HEAD_DIM)
 VMEM_LIMIT = 24 * 1024 * 1024
+WEIGHT_VMEM_LIMIT = 50 * 1024 * 1024
 F32 = jnp.float32
 BF16 = jnp.bfloat16
 
 
-def params():
-    return pltpu.CompilerParams(vmem_limit_bytes=VMEM_LIMIT)
+def params(limit=VMEM_LIMIT):
+    return pltpu.CompilerParams(vmem_limit_bytes=limit)
 
 
 def cost(flops, moved, exps=0):
@@ -58,203 +59,209 @@
     return jnp.where(at < BASES, high.astype(F32), low.astype(F32)).astype(BF16)
 
 
-def read_rows(refs):
-    parts = [ref[...].reshape(ref.shape[-2:]) for ref in refs]
+def read_rows(refs, strand):
+    parts = [ref[strand] if len(ref.shape) == 3 else ref[...] for ref in refs]
     return parts[0] if len(parts) == 1 else jnp.concatenate(parts, axis=0)
 
 
-def x_spec(x, strand):
-    if x.ndim == 3:
-        return pl.BlockSpec((1, *x.shape[1:]), lambda j, s: (strand, 0, 0))
-    return pl.BlockSpec(x.shape, lambda j, s: (0, 0))
-
-
-def slab_kernel(slab_parts, with_embed, has_total, scalars, *refs):
-    del scalars
-    sums = [None] * (6 if with_embed else 3)
-
-    def add(index, item):
-        sums[index] = item if sums[index] is None else sums[index] + item
-
+def local_call(kernel, name, scalars, operands, far, out_shape, scratch, work):
+    vmem = pl.BlockSpec(memory_space=pltpu.VMEM)
+    hbm = pl.BlockSpec(memory_space=pltpu.HBM)
+    return pl.pallas_call(
+        kernel,
+        in_specs=[pl.BlockSpec(memory_space=pltpu.SMEM)]
+        + [hbm] * far
+        + [vmem] * (len(operands) - far),
+        out_specs=[vmem] * len(out_shape),
+        out_shape=out_shape,
+        scratch_shapes=scratch,
+        compiler_params=params(WEIGHT_VMEM_LIMIT),
+        cost_estimate=work,
+        name=name,
+    )(scalars, *operands)
+
+
+def fetch(weight_refs, slab, held, sems):
+    tile = held.shape[1]
+    copies = []
+    for index, weight in enumerate(weight_refs):
+        first = pl.multiple_of(slab * tile, tile)
+        copy = pltpu.make_async_copy(
+            weight.at[pl.ds(first, tile), :], held.at[index], sems.at[index]
+        )
+        copy.start()
+        copies.append(copy)
+    return copies
+
+
+def slab_kernel(strand, slab_parts, with_embed, has_total, slab_ref, *refs):
+    weights, refs = refs[:3], refs[3:]
+    count = len(slab_parts)
+    held, sems = refs[-2:]
+    refs = refs[:-2]
+    copies = [fetch(weights, slab_ref[at], held.at[at], sems.at[at]) for at in range(count)]
+    if with_embed:
+        embed_ref, refs = refs[0], refs[1:]
+    rows = []
     for parts in slab_parts:
-        x_refs, refs = refs[:parts], refs[parts:]
-        weights, refs = refs[:3], refs[3:]
-        rows = read_rows(x_refs)
-        if with_embed:
-            embed, refs = refs[0][...], refs[1:]
-        for index, weight in enumerate(weights):
-            add(index, dot(rows, weight[...]))
+        rows.append(read_rows(refs[:parts], strand))
+        refs = refs[parts:]
+    size = 6 if with_embed else 3
+    totals = refs[:size] if has_total else [None] * size
+    outs = refs[-size:]
+    tile = held.shape[2]
+    for at in range(count):
+        for index in range(3):
+            copies[at][index].wait()
+            weight = held[at, index]
+            pairs = [(index, rows[at])]
             if with_embed:
-                add(3 + index, dot(embed, weight[...]))
-    if has_total:
-        for index in range(len(sums)):
-            sums[index] = refs[index][...] + sums[index]
-        refs = refs[len(sums) :]
-    for ref, item in zip(refs, sums):
-        ref[...] = item
+                first = pl.multiple_of(slab_ref[at] * tile, tile)
+                pairs.append((3 + index, embed_ref[:, pl.ds(first, tile)]))
+            for slot, left in pairs:
+                item = dot(left, weight)
+                if at:
+                    item = outs[slot][...] + item
+                elif has_total:
+                    item = totals[slot][...] + item
+                outs[slot][...] = item
 
 
 def slab_sums(slabs, scalars, strand, weights, embed=None, total=None):
     width = weights[0].shape[1]
-    cols = min(2 * HEAD_DIM, width)
     tile = slabs[0][0].shape[-1]
     rows = sum(x.shape[-2] for x in slabs[0])
-    in_specs, operands = [], []
-    for index, parts in enumerate(slabs):
-        in_specs += [x_spec(x, strand) for x in parts]
-        in_specs += [pl.BlockSpec((tile, cols), lambda j, s, index=index: (s[index], j))] * 3
-        operands += [*parts, *weights]
-        if embed is not None:
-            in_specs.append(pl.BlockSpec((CODES, tile), lambda j, s, index=index: (0, s[index])))
-            operands.append(embed)
+    operands = [*weights] + ([embed] if embed is not None else [])
+    for parts in slabs:
+        operands += parts
+    if total is not None:
+        operands += total
     heights = [rows] * 3 + ([CODES] * 3 if embed is not None else [])
-    sum_specs = [pl.BlockSpec((height, cols), lambda j, s: (0, j)) for height in heights]
-    aliases = {}
-    if total is not None:
-        aliases = {1 + len(operands) + index: index for index in range(len(heights))}
-        in_specs += sum_specs
-        operands += total
-    return pl.pallas_call(
+    return local_call(
         functools.partial(
-            slab_kernel, [len(parts) for parts in slabs], embed is not None, total is not None
+            slab_kernel,
+            strand,
+            [len(parts) for parts in slabs],
+            embed is not None,
+            total is not None,
         ),
-        grid_spec=pltpu.PrefetchScalarGridSpec(
-            num_scalar_prefetch=1,
-            grid=(width // cols,),
-            in_specs=in_specs,
-            out_specs=sum_specs,
-        ),
-        out_shape=[jax.ShapeDtypeStruct((height, width), F32) for height in heights],
-        input_output_aliases=aliases,
-        compiler_params=params(),
-        cost_estimate=cost(
-            6 * rows * tile * width * len(slabs), 6 * tile * width * len(slabs) + 20 * rows * width
-        ),
-        name="slab_sums",
-    )(scalars, *operands)
-
-
-def finish_kv_kernel(parts, with_embed, scalars, *refs):
-    del scalars
-    x_refs, refs = refs[:parts], refs[parts:]
-    (wk_ref, wv_ref, ksum_ref, vsum_ref, cos_ref, sin_ref), refs = refs[:6], refs[6:]
+        "slab_sums",
+        scalars,
+        operands,
+        3,
+        [jax.ShapeDtypeStruct((height, width), F32) for height in heights],
+        [
+            pltpu.VMEM((len(slabs), 3, tile, width), BF16),
+            pltpu.SemaphoreType.DMA((len(slabs), 3)),
+        ],
+        cost(6 * rows * tile * width * len(slabs), 6 * tile * width * len(slabs)),
+    )
+
+
+def finish_kv_kernel(x_count, part_count, with_embed, scalars, *refs):
+    weights, refs = refs[:2], refs[2:]
+    held, sems = refs[-2:]
+    copies = fetch(weights, scalars[0], held, sems)
+    x_refs, refs = refs[:x_count], refs[x_count:]
+    (ksum_ref, vsum_ref, cos_ref, sin_ref), refs = refs[:4], refs[4:]
     if with_embed:
         (embed_ref, ek_ref, ev_ref), refs = refs[:3], refs[3:]
-    kv_ref = refs[0]
-    rows = read_rows(x_refs)
-    cos, sin = cos_ref[...], sin_ref[...]
-    key = ksum_ref[...] + dot(rows, wk_ref[...])
-    for start in range(0, key.shape[1], HEAD_DIM):
-        cols = slice(start, start + HEAD_DIM)
-        kv_ref[0, :, cols] = turned(key[:, cols], cos, sin).astype(BF16)
-    kv_ref[1] = (vsum_ref[...] + dot(rows, wv_ref[...])).astype(BF16)
+    kv_refs, refs = refs[:part_count], refs[part_count:]
+    tile = held.shape[1]
+    rows = read_rows(x_refs, 0)
+    height, width = ksum_ref.shape
+    part_cols = width // part_count
+    own = pl.ds(pl.multiple_of(scalars[1] * height, height), height)
+    cos, sin = cos_ref[own, :], sin_ref[own, :]
     if with_embed:
-        _, table_ref, swapped_ref, ev_out = refs
-        embed = embed_ref[...]
-        ek = ek_ref[...] + dot(embed, wk_ref[...])
+        embed = embed_ref[:, pl.ds(pl.multiple_of(scalars[0] * tile, tile), tile)]
+        table_ref, swapped_ref, ev_out = refs[:3]
+    copies[0].wait()
+    key = ksum_ref[...] + dot(rows, held[0])
+    for start in range(0, width, HEAD_DIM):
+        part, at = start // part_cols, start % part_cols
+        turned_key = turned(key[:, start : start + HEAD_DIM], cos, sin)
+        kv_refs[part][0, :, at : at + HEAD_DIM] = turned_key.astype(BF16)
+    if with_embed:
+        ek = ek_ref[...] + dot(embed, held[0])
         table_ref[...] = code_table(ek)
-        for start in range(0, key.shape[1], HEAD_DIM):
+        for start in range(0, width, HEAD_DIM):
             cols = slice(start, start + HEAD_DIM)
             swapped_ref[:, cols] = code_table(swapped(ek[:, cols]))
-        ev_out[...] = ev_ref[...] + dot(embed, wv_ref[...])
-
-
-def finish_kv(part, cols, x_parts, scalars, wk, wv, ksum, vsum, cos, sin, embed_parts):
+    copies[1].wait()
+    value = vsum_ref[...] + dot(rows, held[1])
+    for part in range(part_count):
+        kv_refs[part][1] = value[:, part * part_cols : (part + 1) * part_cols].astype(BF16)
+    if with_embed:
+        ev_out[...] = ev_ref[...] + dot(embed, held[1])
+
+
+def finish_kv(part_count, x_parts, scalars, wk, wv, ksum, vsum, cos, sin, embed_parts):
     tile = x_parts[0].shape[-1]
-    rows = ksum.shape[0]
-
-    def at(height):
-        return pl.BlockSpec((height, cols), lambda j, s: (0, part))
-
-    weight_spec = pl.BlockSpec((tile, cols), lambda j, s: (s[0], part))
-    table_spec = pl.BlockSpec((rows, HEAD_DIM), lambda j, s: (s[1], 0))
-    in_specs = [x_spec(x, 0) for x in x_parts]
-    in_specs += [weight_spec, weight_spec, at(rows), at(rows), table_spec, table_spec]
-    operands = [*x_parts, wk, wv, ksum, vsum, cos, sin]
-    out_specs = [pl.BlockSpec((2, rows, cols), lambda j, s: (0, 0, 0))]
-    out_shape = [jax.ShapeDtypeStruct((2, rows, cols), BF16)]
+    rows, width = ksum.shape
+    operands = [wk, wv, *x_parts, ksum, vsum, cos, sin]
+    out_shape = [jax.ShapeDtypeStruct((2, rows, width // part_count), BF16)] * part_count
     if embed_parts is not None:
-        in_specs += [
-            pl.BlockSpec((CODES, tile), lambda j, s: (0, s[0])),
-            at(CODES),
-            at(CODES),
-        ]
         operands += embed_parts
-        out_specs += [pl.BlockSpec((CODES, cols), lambda j, s: (0, 0))] * 3
-        out_shape += [jax.ShapeDtypeStruct((CODES, cols), kind) for kind in (BF16, BF16, F32)]
-    return pl.pallas_call(
-        functools.partial(finish_kv_kernel, len(x_parts), embed_parts is not None),
-        grid_spec=pltpu.PrefetchScalarGridSpec(
-            num_scalar_prefetch=1,
-            grid=(1,),
-            in_specs=in_specs,
-            out_specs=out_specs,
-        ),
-        out_shape=out_shape,
-        compiler_params=params(),
-        cost_estimate=cost(4 * rows * tile * cols, 4 * tile * cols + 14 * rows * cols),
-        name="finish_kv",
-    )(scalars, *operands)
-
-
-def finish_q_kernel(parts, with_embed, scalars, *refs):
-    del scalars
-    x_refs, refs = refs[:parts], refs[parts:]
-    (wq_ref, qsum_ref, cos_ref, sin_ref, codes_ref, eq_ref), refs = refs[:6], refs[6:]
+        out_shape += [jax.ShapeDtypeStruct((CODES, width), kind) for kind in (BF16, BF16, F32)]
+    return local_call(
+        functools.partial(finish_kv_kernel, len(x_parts), part_count, embed_parts is not None),
+        "finish_kv",
+        scalars,
+        operands,
+        2,
+        out_shape,
+        [pltpu.VMEM((2, tile, width), BF16), pltpu.SemaphoreType.DMA((2,))],
+        cost(4 * rows * tile * width, 4 * tile * width + 14 * rows * width),
+    )
+
+
+def finish_q_kernel(x_count, with_embed, scalars, *refs):
+    weights, refs = refs[:1], refs[1:]
+    held, sems = refs[-2:]
+    copies = fetch(weights, scalars[0], held, sems)
+    x_refs, refs = refs[:x_count], refs[x_count:]
+    (qsum_ref, cos_ref, sin_ref, codes_ref, eq_ref), refs = refs[:5], refs[5:]
+    tile = held.shape[1]
+    height, width = qsum_ref.shape
+    own = pl.ds(pl.multiple_of(scalars[1] * height, height), height)
+    cos, sin = cos_ref[own, :] * SCORE_SCALE, sin_ref[own, :] * SCORE_SCALE
+    rows = read_rows(x_refs, 0)
+    copies[0].wait()
     eq = eq_ref[...]
     if with_embed:
-        embed_ref, q_ref, qm_ref, eq_out = refs
-        eq = eq + dot(embed_ref[...], wq_ref[...])
+        embed_ref, q_ref, qm_ref, eq_out = refs[:4]
+        first = pl.multiple_of(scalars[0] * tile, tile)
+        eq = eq + dot(embed_ref[:, pl.ds(first, tile)], held[0])
         eq_out[...] = eq
     else:
-        q_ref, qm_ref = refs
-    cos, sin = cos_ref[...] * SCORE_SCALE, sin_ref[...] * SCORE_SCALE
-    query = qsum_ref[...] + dot(read_rows(x_refs), wq_ref[...])
+        q_ref, qm_ref = refs[:2]
+    query = qsum_ref[...] + dot(rows, held[0])
     mutant = query + dot(codes_ref[0], code_table(eq))
-    for start in range(0, query.shape[1], HEAD_DIM):
+    for start in range(0, width, HEAD_DIM):
         cols = slice(start, start + HEAD_DIM)
         q_ref[:, cols] = turned(query[:, cols], cos, sin).astype(BF16)
         qm_ref[:, cols] = turned(mutant[:, cols], cos, sin).astype(BF16)
 
 
-def finish_q(cols, x_parts, scalars, wq, qsum, cos, sin, codes, eq, embed):
+def finish_q(x_parts, scalars, wq, qsum, cos, sin, codes, eq, embed):
     tile = x_parts[0].shape[-1]
     rows, width = qsum.shape
-
-    def at(height):
-        return pl.BlockSpec((height, cols), lambda j, s: (0, j))
-
-    table_spec = pl.BlockSpec((rows, HEAD_DIM), lambda j, s: (s[1], 0))
-    in_specs = [x_spec(x, 0) for x in x_parts]
-    in_specs += [
-        pl.BlockSpec((tile, cols), lambda j, s: (s[0], j)),
-        at(rows),
-        table_spec,
-        table_spec,
-        pl.BlockSpec((1, rows, CODES), lambda j, s: (0, 0, 0)),
-        at(CODES),
-    ]
-    operands = [*x_parts, wq, qsum, cos, sin, codes, eq]
-    out_specs = [at(rows), at(rows)]
+    operands = [wq, *x_parts, qsum, cos, sin, codes, eq]
     out_shape = [jax.ShapeDtypeStruct((rows, width), BF16)] * 2
     if embed is not None:
-        in_specs.append(pl.BlockSpec((CODES, tile), lambda j, s: (0, s[0])))
         operands.append(embed)
-        out_specs.append(at(CODES))
         out_shape.append(jax.ShapeDtypeStruct((CODES, width), F32))
-    return pl.pallas_call(
+    return local_call(
         functools.partial(finish_q_kernel, len(x_parts), embed is not None),
-        grid_spec=pltpu.PrefetchScalarGridSpec(
-            num_scalar_prefetch=1,
-            grid=(width // cols,),
-            in_specs=in_specs,
-            out_specs=out_specs,
-        ),
-        out_shape=out_shape,
-        compiler_params=params(),
-        cost_estimate=cost(2 * rows * tile * width, 2 * tile * width + 8 * rows * width),
-        name="finish_q",
-    )(scalars, *operands)
+        "finish_q",
+        scalars,
+        operands,
+        1,
+        out_shape,
+        [pltpu.VMEM((1, tile, width), BF16), pltpu.SemaphoreType.DMA((1,))],
+        cost(2 * rows * tile * width, 2 * tile * width + 8 * rows * width),
+    )
 
 
 def attend_kernel(forward, block_count, has_before, q_start, table_start, before_start, *refs):
@@ -377,53 +384,42 @@
     )(ids, *operands)
 
 
-def out_kernel(slabs, has_before, *refs):
-    row_refs, weight_ref, refs = refs[:slabs], refs[slabs], refs[slabs + 1 :]
-    if has_before:
-        before_ref, out_ref, acc = refs
-    else:
-        out_ref, acc = refs
-    step = pl.program_id(0)
+def out_kernel(part, slabs, has_before, scalars, weight_ref, *refs):
+    del scalars
+    held, sems = refs[-2:]
+    out_ref = refs[-3]
+    row_refs = refs[:slabs]
+    cols = held.shape[1]
+    copies = []
     for index in range(slabs):
-
-        @pl.when(step == index)
-        def _(index=index):
-            item = dot(row_refs[index][...], weight_ref[0])
-            if index:
-                item = acc[...] + item
-            elif has_before:
-                item = before_ref[...] + item
-            if index < slabs - 1:
-                acc[...] = item
-            else:
-                out_ref[...] = item.astype(out_ref.dtype)
-
-
-def out_project(part, slab_rows, weight, last, before):
+        copy = pltpu.make_async_copy(
+            weight_ref.at[index, pl.ds(part * cols, cols), :], held.at[index], sems.at[index]
+        )
+        copy.start()
+        copies.append(copy)
+    total = refs[slabs][...] if has_before else None
+    for index in range(slabs):
+        copies[index].wait()
+        item = dot(row_refs[index][...], held[index])
+        total = item if total is None else total + item
+    out_ref[...] = total.astype(out_ref.dtype)
+
+
+def out_project(part, slab_rows, weight, last, before, scalars):
     slabs = len(slab_rows)
     rows, cols = slab_rows[0].shape
     width = weight.shape[2]
-
-    def whole(item):
-        return pl.BlockSpec(item.shape, lambda i: (0, 0))
-
-    in_specs = [whole(item) for item in slab_rows]
-    in_specs.append(pl.BlockSpec((1, cols, width), lambda i: (i, part, 0)))
-    operands = [*slab_rows, weight]
-    if before is not None:
-        in_specs.append(whole(before))
-        operands.append(before)
-    return pl.pallas_call(
-        functools.partial(out_kernel, slabs, before is not None),
-        grid=(slabs,),
-        in_specs=in_specs,
-        out_specs=pl.BlockSpec((rows, width), lambda i: (0, 0)),
-        out_shape=jax.ShapeDtypeStruct((rows, width), BF16 if last else F32),
-        scratch_shapes=[pltpu.VMEM((rows, width), F32)],
-        compiler_params=params(),
-        cost_estimate=cost(2 * slabs * rows * cols * width, 2 * slabs * cols * width),
-        name="out_project",
-    )(*operands)
+    operands = [weight, *slab_rows] + ([before] if before is not None else [])
+    return local_call(
+        functools.partial(out_kernel, part, slabs, before is not None),
+        "out_project",
+        scalars,
+        operands,
+        1,
+        [jax.ShapeDtypeStruct((rows, width), BF16 if last else F32)],
+        [pltpu.VMEM((slabs, cols, width), BF16), pltpu.SemaphoreType.DMA((slabs,))],
+        cost(2 * slabs * rows * cols * width, 2 * slabs * cols * width),
+    )[0]
 
 
 def shards(
@@ -541,28 +537,23 @@
             total = add_slabs(strand, waiting, total)
         return total
 
-    def finish(strand, last, total, eq, cols):
+    def finish(strand, last, total, eq, count):
         first = strand == 0
         cos, sin = rope[strand]
         scalars = jnp.stack([slab_at[-1], my_row])
-        made = [
-            finish_kv(
-                part,
-                cols,
-                last,
-                scalars,
-                key_weight,
-                value_weight,
-                total[1],
-                total[2],
-                cos,
-                sin,
-                [embed, total[4], total[5]] if first else None,
-            )
-            for part in range(width // cols)
-        ]
+        made = finish_kv(
+            count,
+            last,
+            scalars,
+            key_weight,
+            value_weight,
+            total[1],
+            total[2],
+            cos,
+            sin,
+            [embed, total[4], total[5]] if first else None,
+        )
         query = finish_q(
-            min(2 * HEAD_DIM, width),
             last,
             scalars,
             query_weight,
@@ -599,11 +590,11 @@
     total = run_ring(0, moving, [None, (code_sets, cut)])
     last = arrived[0][-1]
     moving = hop([tie(block, item, total) for block, item in zip(cut, last)])
-    made, query = finish(0, last, total, None, width)
-    own, tables, eq = made[0][0], made[0][1:], query[2]
+    made, query = finish(0, last, total, None, 1)
+    own, tables, eq = made[0], made[1:], query[2]
     far = ctx_far(own)
 
-    total = run_ring(1, moving, [])
+    total = run_ring(1, moving, [(own,)])
     blocks = spread_out(own, tie(far, partial[:1]))
     before = attend_part(0, 0, width, blocks, query, tables, None, tie(ids, total))
     last = tie(arrived[1][-1], before)
@@ -616,15 +607,14 @@
     for shift in range(slabs):
         target = (head + shift) % slabs
         pieces.append(lax.dynamic_slice_in_dim(piece, target * tile, tile, 1))
-    pieces = tie(pieces, arrived[1][max(0, slabs - 3)])
+    pieces = tie(pieces, partial)
 
     def around(item, shift):
         return lax.ppermute(item, "head", [(i, (i + shift) % slabs) for i in range(slabs)])
 
     pieces = [around(tie(item, last), shift) if shift else item for shift, item in enumerate(pieces)]
 
-    made, query_then = finish(1, last, total, eq, cols)
-    own_then = [item[0] for item in made]
+    own_then, query_then = finish(1, last, total, eq, parts)
     far_then = [ctx_far(item) for item in own_then]
     far_then[0] = tie(far_then[0], own_then, query_then)
     pieces = tie(jnp.stack(pieces), far_then[0])
@@ -636,7 +626,7 @@
         combined.append(item)
     for part, item in enumerate(combined):
         slab_rows = [around(item, shift) if shift else item for shift in range(slabs)]
-        result = out_project(part, slab_rows, out_slabs, part == parts - 1, result)
+        result = out_project(part, slab_rows, out_slabs, part == parts - 1, result, ids)
     return result
 
 

time: 195 us -> 181 us (0.928)
  local copies, waits for them, and re-layouts: 34.2 us -> 11.5 us
  waiting for transfers between devices: 53.3 us -> 66.2 us
  Pallas kernels: 38.3 us -> 45.4 us
  starting transfers between devices: 36.1 us -> 29.8 us
  other arithmetic: 17.4 us -> 13.7 us
    unnamed x116 -> x32, local copies, waits for them, and re-layouts: 30.8 us -> 8.04 us
    ppermute x12, waiting for transfers between devices: 31.9 us -> 40 us  [hop(): return [lax.ppermute(block, 'head', ring) for block in blocks]]
    pallas_call x11 -> x10, Pallas kernels: 27.4 us -> 34.9 us  [local_call(): pl.pallas_call(kernel, in_specs=[pl.BlockSpec(memory_space=pltpu.SMEM)] +...]
    ppermute x9, waiting for transfers between devices: 2.43 us -> 8.21 us  [around(): lax.ppermute(item, 'head', [(i, (i + shift) % slabs) for i in range(slabs)])]
    ppermute x9, starting transfers between devices: 18 us -> 13.9 us  [around(): lax.ppermute(item, 'head', [(i, (i + shift) % slabs) for i in range(slabs)])]
    ppermute x12, starting transfers between devices: 10.3 us -> 8 us  [hop(): return [lax.ppermute(block, 'head', ring) for block in blocks]]
  transfers between devices with their start and end apart: 34 -> 34, of which waited for: 13 -> 15; matrix products, arithmetic and copies ran while one was open for 11% -> 10% of each run, Pallas kernels for 17% -> 19%
where the time goes in v5:
time: 181 us; the launch traced here: 180 us
  waiting for transfers between devices  66.2 us (37%)
  Pallas kernels  45.4 us (25%)
  starting transfers between devices  29.8 us (16%)
  between operations  13.8 us (8%)
  other arithmetic  13.7 us (8%)
  local copies, waits for them, and re-layouts  11.5 us (6%)
    ppermute x12, waiting for transfers between devices, hop(): return [lax.ppermute(block, 'head', ring) for block in blocks]  40 us
    pallas_call x10, Pallas kernels, local_call(): pl.pallas_call(kernel, in_specs=[pl.BlockSpec(memory_space=pltpu.SMEM)] +...  34.9 us
    ppermute x9, starting transfers between devices, around(): lax.ppermute(item, 'head', [(i, (i + shift) % slabs) for i in range(slabs)])  13.9 us
    all_gather x1, waiting for transfers between devices, shards(): out_slabs = lax.all_gather(pieces, ('groups', 'ctx'), axis=1, tiled=True)  12.8 us
    pallas_call x3, Pallas kernels, attend(): pl.pallas_call(functools.partial(attend_kernel, forward, count, before is...  10.5 us
    ppermute x9, waiting for transfers between devices, around(): lax.ppermute(item, 'head', [(i, (i + shift) % slabs) for i in range(slabs)])  8.21 us
    unnamed x32, local copies, waits for them, and re-layouts  8.04 us
    ppermute x12, starting transfers between devices, hop(): return [lax.ppermute(block, 'head', ring) for block in blocks]  8 us
  transfers between devices with their start and end apart: 34, of which 15 were waited for; matrix products, arithmetic and copies ran while one was open for 10% of the time, Pallas kernels for 19%

profile of v5, /device:TPU:0, one launch (start us, length us, event | category | flops | bytes accessed | tf_op | source)
XLA Modules:
  0.0 180.4 jit_solution(14787168796426603054)
XLA Ops:
  6.5 3.0 %collective-permute-start.3 = (s32[256]{0:T(256)}, s32[256]{0:T(256)S(1)}, u32[]{:S(2)}, u32[]{:S(2)}) collective-permute-start(s32[256]{0:T(256)} %param.10), channel_id=1, source_target_pairs={{0,8},{4,12},{8,0},{12,4},{1,9},{5,13},{9,1},{13,5},{2,10},{6,14},... | collective-permute-start | bytes 3080 | tf_op jit(solution)/shard_map/ppermute | solution.py:457
  9.5 1.1 slice_bitcast_fusion.2
  10.6 1.6 collective-permute-start
  12.2 1.6 collective-permute-start.1
  14.1 0.9 maximum_maximum_fusion.refs_3_.refs_8_
  15.0 1.0 select_reduce_fusion
  16.2 1.0 collective-permute-done.5
  18.3 3.2 %collective-permute-done.refs_5_ = bf16[128,1024]{1,0:T(8,128)(2,1)S(1)} collective-permute-done((bf16[128,1024]{1,0:T(8,128)(2,1)S(1)}, bf16[128,1024]{1,0:T(8,128)(2,1)S(1)}, u32[]{:S(2)}, u32[]{:S(2)}) %collective-permute-start) | collective-permute-done | bytes 262176 | tf_op jit(solution)/shard_map/ppermute | solution.py:467
  21.5 5.6 %collective-permute-done.1.refs_6_ = bf16[128,1024]{1,0:T(8,128)(2,1)S(1)} collective-permute-done((bf16[128,1024]{1,0:T(8,128)(2,1)S(1)}, bf16[128,1024]{1,0:T(8,128)(2,1)S(1)}, u32[]{:S(2)}, u32[]{:S(2)}) %collective-permute-start.1) | collective-permute-done | bytes 262176 | tf_op jit(solution)/shard_map/ppermute | solution.py:467
  27.2 1.2 copy-done
  28.5 4.7 %slab_sums.4 = (f32[256,512]{1,0:T(8,128)S(1)}, f32[256,512]{1,0:T(8,128)S(1)}, f32[256,512]{1,0:T(8,128)S(1)}, f32[16,512]{1,0:T(8,128)S(1)}, f32[16,512]{1,0:T(8,128)S(1)}, /*index=5*/f32[16,512]{1,0:T(8,128)S(1)}) custom-call(s32[2]{0:T(128)S(1)} %pad_add_fusion.2.slab_ref, bf16[4096,512]{1,0:T(8,128)(2,1)} %refs_0_.15, bf16[4096,512]{1,0:T(8,128)(2,1)} %refs_0_.14, ...), custom_call_target="tpu_custom_call" | custom-call | flops 25165824 | bytes 98304 | tf_op jit(solution)/shard_map/slab_sums/pallas_call | solution.py:70
  33.2 0.9 slice_bitcast_fusion
  34.1 1.4 collective-permute-start.6
  35.5 2.7 %collective-permute-done.7.refs_5_ = bf16[128,1024]{1,0:T(8,128)(2,1)} collective-permute-done((bf16[128,1024]{1,0:T(8,128)(2,1)S(1)}, bf16[128,1024]{1,0:T(8,128)(2,1)}, u32[]{:S(2)}, u32[]{:S(2)}) %collective-permute-start.7) | collective-permute-done | bytes 262176 | tf_op jit(solution)/shard_map/ppermute | solution.py:467
  38.3 5.5 %fusion.1 = (f32[1024,64]{1,0:T(8,128)}, f32[1024,64]{1,0:T(8,128)}, f32[1024,64]{1,0:T(8,128)}, f32[1024,64]{1,0:T(8,128)}, f32[1024,64]{1,0:T(8,128)}, /*index=5*/f32[1024,64]{1,0:T(8,128)}) fusion(f32[64]{0:T(128)S(1)} %multiply_power_fusion, f32[1024]{0:T(1024)S(1)} %subtract_convert_fusion, f32[1024]{0:T(1024)S(1)} %iota_convert_fusion), kind=kLoop, calls=%fused_computation.17 | loop fusion | flops 262144 | bytes 1581312 | tf_op jit(solution)/shard_map/neg | solution.py:44
  43.8 2.0 %pad_maximum_fusion = (f32[1024,128]{1,0:T(8,128)S(1)}, f32[1024,128]{1,0:T(8,128)S(1)}) fusion(f32[1024,64]{1,0:T(8,128)} %get-tuple-element.131, f32[1024,64]{1,0:T(8,128)} %get-tuple-element.132, f32[1024,64]{1,0:T(8,128)} %get-tuple-element.133), kind=kLoop, calls=%fused_computation.4 | loop fusion | flops 262144 | bytes 1835008 | tf_op jit(solution)/shard_map/concatenate | solution.py:44
  45.8 1.0 copy-done.9
  46.8 3.9 %slab_sums.5 = (f32[256,512]{1,0:T(8,128)S(1)}, f32[256,512]{1,0:T(8,128)S(1)}, f32[256,512]{1,0:T(8,128)S(1)}, f32[16,512]{1,0:T(8,128)S(1)}, f32[16,512]{1,0:T(8,128)S(1)}, /*index=5*/f32[16,512]{1,0:T(8,128)S(1)}) custom-call(s32[1]{0:T(128)} %bitcast.14.slab_ref, bf16[4096,512]{1,0:T(8,128)(2,1)} %refs_0_.15, bf16[4096,512]{1,0:T(8,128)(2,1)} %refs_0_.14, ...), custom_call_target="tpu_custom_call" | custom-call | flops 12582912 | bytes 49152 | tf_op jit(solution)/shard_map/slab_sums/pallas_call | solution.py:70
  51.6 3.7 %finish_kv.2 = (bf16[2,256,512]{2,1,0:T(8,128)(2,1)}, bf16[16,512]{1,0:T(8,128)(2,1)S(1)}, bf16[16,512]{1,0:T(8,128)(2,1)S(1)}, f32[16,512]{1,0:T(8,128)S(1)}) custom-call(s32[2]{0:T(128)S(1)} %pad_add_fusion.3.scalars, bf16[4096,512]{1,0:T(8,128)(2,1)} %refs_0_.14, bf16[4096,512]{1,0:T(8,128)(2,1)} %refs_1_.11, ...), custom_call_target="tpu_custom_call" | custom-call | flops 8388608 | bytes 61440 | tf_op jit(solution)/shard_map/finish_kv/pallas_call | solution.py:70
  55.9 1.6 collective-permute-start.8
  57.4 1.2 collective-permute-start.10
  58.6 8.3 %collective-permute-done.8.refs_4_ = bf16[128,1024]{1,0:T(8,128)(2,1)S(1)} collective-permute-done((bf16[128,1024]{1,0:T(8,128)(2,1)S(1)}, bf16[128,1024]{1,0:T(8,128)(2,1)S(1)}, u32[]{:S(2)}, u32[]{:S(2)}) %collective-permute-start.8) | collective-permute-done | bytes 262176 | tf_op jit(solution)/shard_map/ppermute | solution.py:467
  66.9 4.2 %collective-permute-done.10.refs_5_ = bf16[128,1024]{1,0:T(8,128)(2,1)S(1)} collective-permute-done((bf16[128,1024]{1,0:T(8,128)(2,1)S(1)}, bf16[128,1024]{1,0:T(8,128)(2,1)S(1)}, u32[]{:S(2)}, u32[]{:S(2)}) %collective-permute-start.10) | collective-permute-done | bytes 262176 | tf_op jit(solution)/shard_map/ppermute | solution.py:467
  71.1 4.1 %slab_sums.6 = (f32[256,512]{1,0:T(8,128)S(1)}, f32[256,512]{1,0:T(8,128)S(1)}, f32[256,512]{1,0:T(8,128)S(1)}) custom-call(s32[2]{0:T(128)S(1)} %pad_add_fusion.2.slab_ref, bf16[4096,512]{1,0:T(8,128)(2,1)} %refs_0_.15, bf16[4096,512]{1,0:T(8,128)(2,1)} %refs_0_.14, bf16[4096,512]{1,0:T(8,128)(2,1)} %refs_1_.11, bf16[2,256,1024]{2,1,0:T(8,128)(2,1)S(1)} %copy-done.1, ...), custom_call_target="tpu_custom_call" | custom-call | flops 25165824 | bytes 98304 | tf_op jit(solution)/shard_map/slab_sums/pallas_call | solution.py:70
  78.1 10.4 %collective-permute-done.11.refs_3_ = bf16[128,1024]{1,0:T(8,128)(2,1)} collective-permute-done((bf16[128,1024]{1,0:T(8,128)(2,1)S(1)}, bf16[128,1024]{1,0:T(8,128)(2,1)}, u32[]{:S(2)}, u32[]{:S(2)}) %collective-permute-start.11) | collective-permute-done | bytes 262176 | tf_op jit(solution)/shard_map/ppermute | solution.py:467
  88.6 5.6 %collective-permute-done.12.refs_4_ = bf16[128,1024]{1,0:T(8,128)(2,1)} collective-permute-done((bf16[128,1024]{1,0:T(8,128)(2,1)S(1)}, bf16[128,1024]{1,0:T(8,128)(2,1)}, u32[]{:S(2)}, u32[]{:S(2)}) %collective-permute-start.12) | collective-permute-done | bytes 262176 | tf_op jit(solution)/shard_map/ppermute | solution.py:467
  94.2 2.0 %pad_maximum_fusion.3 = (f32[1024,128]{1,0:T(8,128)S(1)}, f32[1024,128]{1,0:T(8,128)S(1)}) fusion(f32[1024,64]{1,0:T(8,128)} %get-tuple-element.124, f32[1024,64]{1,0:T(8,128)} %get-tuple-element.125, f32[1024,64]{1,0:T(8,128)} %get-tuple-element.123), kind=kLoop, calls=%fused_computation.7 | loop fusion | flops 262144 | bytes 1835008 | tf_op jit(solution)/shard_map/concatenate | solution.py:44
  96.2 1.0 copy-done.11
  97.2 2.6 %finish_q.2 = (bf16[256,512]{1,0:T(8,128)(2,1)S(1)}, bf16[256,512]{1,0:T(8,128)(2,1)S(1)}, f32[16,512]{1,0:T(8,128)S(1)}) custom-call(s32[2]{0:T(128)S(1)} %pad_add_fusion.3.scalars, bf16[4096,512]{1,0:T(8,128)(2,1)} %refs_0_.15, bf16[128,1024]{1,0:T(8,128)(2,1)S(1)} %collective-permute-done.6.refs_2_.refs_1_, ...), custom_call_target="tpu_custom_call" | custom-call | flops 4194304 | bytes 32768 | tf_op jit(solution)/shard_map/finish_q/pallas_call | solution.py:70
  99.9 3.6 %slab_sums.7 = (f32[256,512]{1,0:T(8,128)S(1)}, f32[256,512]{1,0:T(8,128)S(1)}, f32[256,512]{1,0:T(8,128)S(1)}) custom-call(s32[1]{0:T(128)} %bitcast.14.slab_ref, bf16[4096,512]{1,0:T(8,128)(2,1)} %refs_0_.15, bf16[4096,512]{1,0:T(8,128)(2,1)} %refs_0_.14, bf16[4096,512]{1,0:T(8,128)(2,1)} %refs_1_.11, bf16[128,1024]{1,0:T(8,128)(2,1)} %collective-permute-done.11.refs_3_, ...), custom_call_target="tpu_custom_call" | custom-call | flops 12582912 | bytes 49152 | tf_op jit(solution)/shard_map/slab_sums/pallas_call | solution.py:70
  103.6 3.3 %attend_forward.1.refs_14_ = f32[256,512]{1,0:T(8,128)S(1)} custom-call(s32[4]{0:T(128)S(1)} %get-tuple-element.87.refs_0_.scalars, bf16[256,512]{1,0:T(8,128)(2,1)S(1)} %get-tuple-element.88.refs_1_, bf16[256,512]{1,0:T(8,128)(2,1)S(1)} %get-tuple-element.89.refs_2_, bf16[16,512]{1,0:T(8,128)(2,1)S(1)} %get-tuple-element.90.refs_3_, ...), custom_call_target="tpu_custom_call" | custom-call | flops 16777216 | bytes 32768 | tf_op jit(solution)/shard_map/attend_forward/pallas_call | solution.py:366
  106.8 3.3 %finish_kv.3 = (bf16[2,256,256]{2,1,0:T(8,128)(2,1)S(1)}, bf16[2,256,256]{2,1,0:T(8,128)(2,1)S(1)}) custom-call(s32[2]{0:T(128)S(1)} %pad_add_fusion.3.scalars, bf16[4096,512]{1,0:T(8,128)(2,1)} %refs_0_.14, bf16[4096,512]{1,0:T(8,128)(2,1)} %refs_1_.11, bf16[128,1024]{1,0:T(8,128)(2,1)} %collective-permute-done.13.refs_2_.refs_1_, ...), custom_call_target="tpu_custom_call" | custom-call | flops 8388608 | bytes 61440 | tf_op jit(solution)/shard_map/finish_kv/pallas_call | solution.py:70
  110.2 3.2 %collective-permute-start.21 = (bf16[2,256,256]{2,1,0:T(8,128)(2,1)S(1)}, bf16[2,256,256]{2,1,0:T(8,128)(2,1)S(1)}, u32[]{:S(2)}, u32[]{:S(2)}) collective-permute-start(bf16[2,256,256]{2,1,0:T(8,128)(2,1)S(1)} %get-tuple-element.101.refs_10_), channel_id=1, source_target_pairs={{0,8},{4,12},{8,0},{12,4},{1,9},{5,13},{9,1},{13,5},{2,10},{6,14},... | collective-permute-start | bytes 786440 | tf_op jit(solution)/shard_map/ppermute | solution.py:457
  113.4 1.4 fusion.3
  114.8 3.9 %collective-permute-start.20 = (bf16[64,1024]{1,0:T(8,128)(2,1)S(1)}, bf16[64,1024]{1,0:T(8,128)(2,1)S(1)}, u32[]{:S(2)}, u32[]{:S(2)}) collective-permute-start(bf16[64,1024]{1,0:T(8,128)(2,1)S(1)} %get-tuple-element.100), channel_id=1, source_target_pairs={{0,3},{1,0},{2,1},{3,2},{4,7},{5,4},{6,5},{7,6},{8,11},{9,8},{10,9... | collective-permute-start | bytes 393224 | tf_op jit(solution)/shard_map/ppermute | solution.py:613
  119.4 3.0 %finish_q.3 = (bf16[256,512]{1,0:T(8,128)(2,1)S(1)}, bf16[256,512]{1,0:T(8,128)(2,1)S(1)}) custom-call(s32[2]{0:T(128)S(1)} %pad_add_fusion.3.scalars, bf16[4096,512]{1,0:T(8,128)(2,1)} %refs_0_.15, bf16[128,1024]{1,0:T(8,128)(2,1)} %collective-permute-done.13.refs_2_.refs_1_, bf16[128,1024]{1,0:T(8,128)(2,1)} %collective-permute-done.14.refs_3_.refs_2_, ...), custom_call_target="tpu_custom_call" | custom-call | flops 4194304 | bytes 32768 | tf_op jit(solution)/shard_map/finish_q/pallas_call | solution.py:70
  122.6 7.1 %collective-permute-done.19 = bf16[64,1024]{1,0:T(8,128)(2,1)S(1)} collective-permute-done((bf16[64,1024]{1,0:T(8,128)(2,1)S(1)}, bf16[64,1024]{1,0:T(8,128)(2,1)S(1)}, u32[]{:S(2)}, u32[]{:S(2)}) %collective-permute-start.19) | collective-permute-done | bytes 131104 | tf_op jit(solution)/shard_map/ppermute | solution.py:613
  129.7 0.9 pad_maximum_fusion.2
  132.6 3.6 %attend_reverse.2.refs_0_ = bf16[256,256]{1,0:T(8,128)(2,1)S(1)} custom-call(s32[4]{0:T(128)S(1)} %get-tuple-element.87.refs_0_.scalars, bf16[256,512]{1,0:T(8,128)(2,1)S(1)} %get-tuple-element.104.refs_1_, bf16[256,512]{1,0:T(8,128)(2,1)S(1)} %get-tuple-element.105.refs_2_, bf16[16,512]{1,0:T(8,128)(2,1)S(1)} %get-tuple-element.90.refs_3_, ...), custom_call_target="tpu_custom_call" | custom-call | flops 8388608 | bytes 16384 | tf_op jit(solution)/shard_map/attend_reverse/pallas_call | solution.py:366
  136.2 3.3 %collective-permute-done.22.refs_11_ = bf16[2,256,256]{2,1,0:T(8,128)(2,1)S(1)} collective-permute-done((bf16[2,256,256]{2,1,0:T(8,128)(2,1)S(1)}, bf16[2,256,256]{2,1,0:T(8,128)(2,1)S(1)}, u32[]{:S(2)}, u32[]{:S(2)}) %collective-permute-start.22) | collective-permute-done | bytes 262176 | tf_op jit(solution)/shard_map/ppermute | solution.py:457
  140.1 1.9 %collective-permute-start.31 = (bf16[256,256]{1,0:T(8,128)(2,1)S(1)}, bf16[256,256]{1,0:T(8,128)(2,1)S(1)}, u32[]{:S(2)}, u32[]{:S(2)}) collective-permute-start(bf16[256,256]{1,0:T(8,128)(2,1)S(1)} %attend_reverse.2.refs_0_), channel_id=1, source_target_pairs={{0,2},{1,3},{2,0},{3,1},{4,6},{5,7},{6,4},{7,5},{8,10},{9,11},{10,... | collective-permute-start | bytes 393224 | tf_op jit(solution)/shard_map/ppermute | solution.py:613
  142.0 2.9 %collective-permute-start.32 = (bf16[256,256]{1,0:T(8,128)(2,1)S(1)}, bf16[256,256]{1,0:T(8,128)(2,1)S(1)}, u32[]{:S(2)}, u32[]{:S(2)}) collective-permute-start(bf16[256,256]{1,0:T(8,128)(2,1)S(1)} %attend_reverse.2.refs_0_), channel_id=1, source_target_pairs={{0,3},{1,0},{2,1},{3,2},{4,7},{5,4},{6,5},{7,6},{8,11},{9,8},{10,9... | collective-permute-start | bytes 393224 | tf_op jit(solution)/shard_map/ppermute | solution.py:613
  145.0 3.6 %attend_reverse.3.refs_0_ = bf16[256,256]{1,0:T(8,128)(2,1)S(1)} custom-call(s32[4]{0:T(128)S(1)} %get-tuple-element.87.refs_0_.scalars, bf16[256,512]{1,0:T(8,128)(2,1)S(1)} %get-tuple-element.104.refs_1_, bf16[256,512]{1,0:T(8,128)(2,1)S(1)} %get-tuple-element.105.refs_2_, bf16[16,512]{1,0:T(8,128)(2,1)S(1)} %get-tuple-element.90.refs_3_, ...), custom_call_target="tpu_custom_call" | custom-call | flops 8388608 | bytes 16384 | tf_op jit(solution)/shard_map/attend_reverse/pallas_call | solution.py:366
  149.2 3.3 %collective-permute-start.29 = (bf16[256,256]{1,0:T(8,128)(2,1)S(1)}, bf16[256,256]{1,0:T(8,128)(2,1)S(1)}, u32[]{:S(2)}, u32[]{:S(2)}) collective-permute-start(bf16[256,256]{1,0:T(8,128)(2,1)S(1)} %attend_reverse.3.refs_0_), channel_id=1, source_target_pairs={{0,3},{1,0},{2,1},{3,2},{4,7},{5,4},{6,5},{7,6},{8,11},{9,8},{10,9... | collective-permute-start | bytes 393224 | tf_op jit(solution)/shard_map/ppermute | solution.py:613
  154.0 12.8 %all-gather.2.cloned.1.call-done.weight_ref = bf16[4,512,1024]{2,1,0:T(8,128)(2,1)} async-done(((bf16[4,64,1024]{2,1,0:T(8,128)(2,1)}), bf16[4,512,1024]{2,1,0:T(8,128)(2,1)}) %all-gather.2.cloned.1.call-update) | async-done | bytes 4194320 | tf_op jit(solution)/shard_map/all_gather | solution.py:621
  166.7 0.9 copy-done.13
  167.6 2.6 %out_project.2.refs_4_ = f32[256,1024]{1,0:T(8,128)S(1)} custom-call(s32[4]{0:T(128)S(1)} %get-tuple-element.87.refs_0_.scalars, bf16[4,512,1024]{2,1,0:T(8,128)(2,1)} %all-gather.2.cloned.1.call-done.weight_ref, bf16[256,256]{1,0:T(8,128)(2,1)S(1)} %attend_reverse.2.refs_0_, bf16[256,256]{1,0:T(8,128)(2,1)S(1)} %collective-permute-done.30.refs_1_, ...), custom_call_target="tpu_custom_call" | custom-call | flops 8388608 | bytes 32768 | tf_op jit(solution)/shard_map/out_project/pallas_call | solution.py:70
  170.3 3.3 %out_project.3 = bf16[256,1024]{1,0:T(8,128)(2,1)} custom-call(s32[4]{0:T(128)S(1)} %get-tuple-element.87.refs_0_.scalars, bf16[4,512,1024]{2,1,0:T(8,128)(2,1)} %all-gather.2.cloned.1.call-done.weight_ref, bf16[256,256]{1,0:T(8,128)(2,1)S(1)} %attend_reverse.3.refs_0_, bf16[256,256]{1,0:T(8,128)(2,1)S(1)} %collective-permute-done.27.refs_1_, ...), custom_call_target="tpu_custom_call" | custom-call | flops 8388608 | bytes 32768 | tf_op jit(solution)/shard_map/out_project/pallas_call | solution.py:70
  (89 shorter events, 11.7 us)
Async XLA Ops:
  6.5 160.2 %all-gather.2.cloned.1.call-start = ((), (), s32[]{:S(2)}) async-start(), calls=%async_computation | async-start | bytes 4718592 | tf_op jit(solution)/shard_map/all_gather | solution.py:621
  6.5 9.5 %collective-permute-start.3 = (s32[256]{0:T(256)}, s32[256]{0:T(256)S(1)}, u32[]{:S(2)}, u32[]{:S(2)}) collective-permute-start(s32[256]{0:T(256)} %param.10), channel_id=1, source_target_pairs={{0,8},{4,12},{8,0},{12,4},{1,9},{5,13},{9,1},{13,5},{2,10},{6,14},... | collective-permute-start | bytes 3080 | tf_op jit(solution)/shard_map/ppermute | solution.py:457
  9.5 6.7 %collective-permute-start.4 = (s32[256]{0:T(256)}, s32[256]{0:T(256)S(1)}, u32[]{:S(2)}, u32[]{:S(2)}) collective-permute-start(s32[256]{0:T(256)} %param.10), channel_id=1, source_target_pairs={{0,4},{4,0},{8,12},{12,8},{1,5},{5,1},{9,13},{13,9},{2,6},{6,2},{1... | collective-permute-start | bytes 3080 | tf_op jit(solution)/shard_map/ppermute | solution.py:464
  10.6 10.9 %collective-permute-start = (bf16[128,1024]{1,0:T(8,128)(2,1)S(1)}, bf16[128,1024]{1,0:T(8,128)(2,1)S(1)}, u32[]{:S(2)}, u32[]{:S(2)}) collective-permute-start(bf16[128,1024]{1,0:T(8,128)(2,1)S(1)} %get-tuple-element.118), channel_id=1, source_target_pairs={{0,1},{1,2},{2,3},{3,0},{4,5},{5,6},{6,7},{7,4},{8,9},{9,10},{10,1... | collective-permute-start | bytes 786440 | tf_op jit(solution)/shard_map/ppermute | solution.py:467
  12.2 14.9 %collective-permute-start.1 = (bf16[128,1024]{1,0:T(8,128)(2,1)S(1)}, bf16[128,1024]{1,0:T(8,128)(2,1)S(1)}, u32[]{:S(2)}, u32[]{:S(2)}) collective-permute-start(bf16[128,1024]{1,0:T(8,128)(2,1)S(1)} %get-tuple-element.117), channel_id=1, source_target_pairs={{0,1},{1,2},{2,3},{3,0},{4,5},{5,6},{6,7},{7,4},{8,9},{9,10},{10,1... | collective-permute-start | bytes 786440 | tf_op jit(solution)/shard_map/ppermute | solution.py:467
  16.1 1.2 collective-permute-start.5
  21.5 12.6 %collective-permute-start.2 = (bf16[128,1024]{1,0:T(8,128)(2,1)S(1)}, bf16[128,1024]{1,0:T(8,128)(2,1)}, u32[]{:S(2)}, u32[]{:S(2)}) collective-permute-start(bf16[128,1024]{1,0:T(8,128)(2,1)S(1)} %collective-permute-done.refs_5_), channel_id=1, source_target_pairs={{0,1},{1,2},{2,3},{3,0},{4,5},{5,6},{6,7},{7,4},{8,9},{9,10},{10,1... | collective-permute-start | bytes 786440 | tf_op jit(solution)/shard_map/ppermute | solution.py:467
  27.1 11.0 %collective-permute-start.7 = (bf16[128,1024]{1,0:T(8,128)(2,1)S(1)}, bf16[128,1024]{1,0:T(8,128)(2,1)}, u32[]{:S(2)}, u32[]{:S(2)}) collective-permute-start(bf16[128,1024]{1,0:T(8,128)(2,1)S(1)} %collective-permute-done.1.refs_6_), channel_id=1, source_target_pairs={{0,1},{1,2},{2,3},{3,0},{4,5},{5,6},{6,7},{7,4},{8,9},{9,10},{10,1... | collective-permute-start | bytes 786440 | tf_op jit(solution)/shard_map/ppermute | solution.py:467
  27.2 1.2 copy-start
  33.2 10.6 %copy-start.8 = (f32[256,512]{1,0:T(8,128)}, f32[256,512]{1,0:T(8,128)S(1)}, u32[]{:S(2)}) copy-start(f32[256,512]{1,0:T(8,128)S(1)} %get-tuple-element.60.refs_8_) | copy-start | bytes 1572868
  34.1 17.4 %collective-permute-start.6 = (bf16[128,1024]{1,0:T(8,128)(2,1)}, bf16[128,1024]{1,0:T(8,128)(2,1)S(1)}, u32[]{:S(2)}, u32[]{:S(2)}) collective-permute-start(bf16[128,1024]{1,0:T(8,128)(2,1)} %collective-permute-done.2.refs_4_), channel_id=1, source_target_pairs={{0,1},{1,2},{2,3},{3,0},{4,5},{5,6},{6,7},{7,4},{8,9},{9,10},{10,1... | collective-permute-start | bytes 786440 | tf_op jit(solution)/shard_map/ppermute | solution.py:467
  38.2 13.4 %collective-permute-start.9 = (bf16[128,1024]{1,0:T(8,128)(2,1)}, bf16[128,1024]{1,0:T(8,128)(2,1)S(1)}, u32[]{:S(2)}, u32[]{:S(2)}) collective-permute-start(bf16[128,1024]{1,0:T(8,128)(2,1)} %collective-permute-done.7.refs_5_), channel_id=1, source_target_pairs={{0,1},{1,2},{2,3},{3,0},{4,5},{5,6},{6,7},{7,4},{8,9},{9,10},{10,1... | collective-permute-start | bytes 786440 | tf_op jit(solution)/shard_map/ppermute | solution.py:467
  45.8 1.0 copy-start.9
  50.8 0.8 copy-start.10
  51.6 4.3 %copy-start.15 = (bf16[128,1024]{1,0:T(8,128)(2,1)S(1)}, bf16[128,1024]{1,0:T(8,128)(2,1)}, u32[]{:S(2)}) copy-start(bf16[128,1024]{1,0:T(8,128)(2,1)} %get-tuple-element.71) | copy-start | bytes 786436
  51.6 5.9 %copy-start.14 = (bf16[128,1024]{1,0:T(8,128)(2,1)S(1)}, bf16[128,1024]{1,0:T(8,128)(2,1)}, u32[]{:S(2)}) copy-start(bf16[128,1024]{1,0:T(8,128)(2,1)} %get-tuple-element.73) | copy-start | bytes 786436
  51.6 19.5 %copy-start.1 = (bf16[2,256,1024]{2,1,0:T(8,128)(2,1)S(1)}, bf16[2,256,1024]{2,1,0:T(8,128)(2,1)}, u32[]{:S(2)}) copy-start(bf16[2,256,1024]{2,1,0:T(8,128)(2,1)} %refs_3_.1) | copy-start | bytes 3145732
  55.3 22.3 %collective-permute-start.15 = (bf16[2,256,512]{2,1,0:T(8,128)(2,1)}, bf16[2,256,512]{2,1,0:T(8,128)(2,1)}, u32[]{:S(2)}, u32[]{:S(2)}) collective-permute-start(bf16[2,256,512]{2,1,0:T(8,128)(2,1)} %get-tuple-element.77.refs_10_), channel_id=1, source_target_pairs={{0,8},{4,12},{8,0},{12,4},{1,9},{5,13},{9,1},{13,5},{2,10},{6,14},... | collective-permute-start | bytes 1572872 | tf_op jit(solution)/shard_map/ppermute | solution.py:457
  55.9 11.0 %collective-permute-start.8 = (bf16[128,1024]{1,0:T(8,128)(2,1)S(1)}, bf16[128,1024]{1,0:T(8,128)(2,1)S(1)}, u32[]{:S(2)}, u32[]{:S(2)}) collective-permute-start(bf16[128,1024]{1,0:T(8,128)(2,1)S(1)} %copy-done.15), channel_id=1, source_target_pairs={{0,1},{1,2},{2,3},{3,0},{4,5},{5,6},{6,7},{7,4},{8,9},{9,10},{10,1... | collective-permute-start | bytes 786440 | tf_op jit(solution)/shard_map/ppermute | solution.py:467
  57.4 13.6 %collective-permute-start.10 = (bf16[128,1024]{1,0:T(8,128)(2,1)S(1)}, bf16[128,1024]{1,0:T(8,128)(2,1)S(1)}, u32[]{:S(2)}, u32[]{:S(2)}) collective-permute-start(bf16[128,1024]{1,0:T(8,128)(2,1)S(1)} %copy-done.14), channel_id=1, source_target_pairs={{0,1},{1,2},{2,3},{3,0},{4,5},{5,6},{6,7},{7,4},{8,9},{9,10},{10,1... | collective-permute-start | bytes 786440 | tf_op jit(solution)/shard_map/ppermute | solution.py:467
  58.6 44.9 %collective-permute-start.16 = (bf16[2,256,512]{2,1,0:T(8,128)(2,1)}, bf16[2,256,512]{2,1,0:T(8,128)(2,1)}, u32[]{:S(2)}, u32[]{:S(2)}) collective-permute-start(bf16[2,256,512]{2,1,0:T(8,128)(2,1)} %get-tuple-element.77.refs_10_), channel_id=1, source_target_pairs={{0,4},{4,0},{8,12},{12,8},{1,5},{5,1},{9,13},{13,9},{2,6},{6,2},{1... | collective-permute-start | bytes 1572872 | tf_op jit(solution)/shard_map/ppermute | solution.py:464
  75.2 0.8 copy-start.2
  76.0 0.8 copy-start.4
  77.6 26.0 %collective-permute-start.17 = (bf16[2,256,512]{2,1,0:T(8,128)(2,1)}, bf16[2,256,512]{2,1,0:T(8,128)(2,1)}, u32[]{:S(2)}, u32[]{:S(2)}) collective-permute-start(bf16[2,256,512]{2,1,0:T(8,128)(2,1)} %collective-permute-done.15.refs_11_), channel_id=1, source_target_pairs={{0,4},{4,0},{8,12},{12,8},{1,5},{5,1},{9,13},{13,9},{2,6},{6,2},{1... | collective-permute-start | bytes 1572872 | tf_op jit(solution)/shard_map/ppermute | solution.py:464
  77.6 11.0 %collective-permute-start.11 = (bf16[128,1024]{1,0:T(8,128)(2,1)S(1)}, bf16[128,1024]{1,0:T(8,128)(2,1)}, u32[]{:S(2)}, u32[]{:S(2)}) collective-permute-start(bf16[128,1024]{1,0:T(8,128)(2,1)S(1)} %collective-permute-done.8.refs_4_), channel_id=1, source_target_pairs={{0,1},{1,2},{2,3},{3,0},{4,5},{5,6},{6,7},{7,4},{8,9},{9,10},{10,1... | collective-permute-start | bytes 786440 | tf_op jit(solution)/shard_map/ppermute | solution.py:467
  77.6 16.6 %collective-permute-start.12 = (bf16[128,1024]{1,0:T(8,128)(2,1)S(1)}, bf16[128,1024]{1,0:T(8,128)(2,1)}, u32[]{:S(2)}, u32[]{:S(2)}) collective-permute-start(bf16[128,1024]{1,0:T(8,128)(2,1)S(1)} %collective-permute-done.10.refs_5_), channel_id=1, source_target_pairs={{0,1},{1,2},{2,3},{3,0},{4,5},{5,6},{6,7},{7,4},{8,9},{9,10},{10,1... | collective-permute-start | bytes 786440 | tf_op jit(solution)/shard_map/ppermute | solution.py:467
  88.6 18.2 %collective-permute-start.13 = (bf16[128,1024]{1,0:T(8,128)(2,1)}, bf16[128,1024]{1,0:T(8,128)(2,1)}, u32[]{:S(2)}, u32[]{:S(2)}) collective-permute-start(bf16[128,1024]{1,0:T(8,128)(2,1)} %collective-permute-done.11.refs_3_), channel_id=1, source_target_pairs={{0,1},{1,2},{2,3},{3,0},{4,5},{5,6},{6,7},{7,4},{8,9},{9,10},{10,1... | collective-permute-start | bytes 786440 | tf_op jit(solution)/shard_map/ppermute | solution.py:467
  94.2 12.6 %collective-permute-start.14 = (bf16[128,1024]{1,0:T(8,128)(2,1)}, bf16[128,1024]{1,0:T(8,128)(2,1)}, u32[]{:S(2)}, u32[]{:S(2)}) collective-permute-start(bf16[128,1024]{1,0:T(8,128)(2,1)} %collective-permute-done.12.refs_4_), channel_id=1, source_target_pairs={{0,1},{1,2},{2,3},{3,0},{4,5},{5,6},{6,7},{7,4},{8,9},{9,10},{10,1... | collective-permute-start | bytes 786440 | tf_op jit(solution)/shard_map/ppermute | solution.py:467
  94.2 5.7 %copy-start.3 = (f32[256,512]{1,0:T(8,128)S(1)}, f32[256,512]{1,0:T(8,128)}, u32[]{:S(2)}) copy-start(f32[256,512]{1,0:T(8,128)} %copy-done.2) | copy-start | bytes 1572868
  94.2 5.7 %copy-start.5 = (f32[256,512]{1,0:T(8,128)S(1)}, f32[256,512]{1,0:T(8,128)}, u32[]{:S(2)}) copy-start(f32[256,512]{1,0:T(8,128)} %copy-done.4) | copy-start | bytes 1572868
  94.2 5.7 %copy-start.7 = (f32[256,512]{1,0:T(8,128)S(1)}, f32[256,512]{1,0:T(8,128)}, u32[]{:S(2)}) copy-start(f32[256,512]{1,0:T(8,128)} %copy-done.6) | copy-start | bytes 1572868
  96.2 1.0 copy-start.11
  110.2 20.4 %collective-permute-start.21 = (bf16[2,256,256]{2,1,0:T(8,128)(2,1)S(1)}, bf16[2,256,256]{2,1,0:T(8,128)(2,1)S(1)}, u32[]{:S(2)}, u32[]{:S(2)}) collective-permute-start(bf16[2,256,256]{2,1,0:T(8,128)(2,1)S(1)} %get-tuple-element.101.refs_10_), channel_id=1, source_target_pairs={{0,8},{4,12},{8,0},{12,4},{1,9},{5,13},{9,1},{13,5},{2,10},{6,14},... | collective-permute-start | bytes 786440 | tf_op jit(solution)/shard_map/ppermute | solution.py:457
  114.8 7.8 %collective-permute-start.20 = (bf16[64,1024]{1,0:T(8,128)(2,1)S(1)}, bf16[64,1024]{1,0:T(8,128)(2,1)S(1)}, u32[]{:S(2)}, u32[]{:S(2)}) collective-permute-start(bf16[64,1024]{1,0:T(8,128)(2,1)S(1)} %get-tuple-element.100), channel_id=1, source_target_pairs={{0,3},{1,0},{2,1},{3,2},{4,7},{5,4},{6,5},{7,6},{8,11},{9,8},{10,9... | collective-permute-start | bytes 393224 | tf_op jit(solution)/shard_map/ppermute | solution.py:613
  118.7 11.0 %collective-permute-start.19 = (bf16[64,1024]{1,0:T(8,128)(2,1)S(1)}, bf16[64,1024]{1,0:T(8,128)(2,1)S(1)}, u32[]{:S(2)}, u32[]{:S(2)}) collective-permute-start(bf16[64,1024]{1,0:T(8,128)(2,1)S(1)} %get-tuple-element.98), channel_id=1, source_target_pairs={{0,2},{1,3},{2,0},{3,1},{4,6},{5,7},{6,4},{7,5},{8,10},{9,11},{10,... | collective-permute-start | bytes 393224 | tf_op jit(solution)/shard_map/ppermute | solution.py:613
  118.7 11.0 %collective-permute-start.18 = (bf16[64,1024]{1,0:T(8,128)(2,1)S(1)}, bf16[64,1024]{1,0:T(8,128)(2,1)S(1)}, u32[]{:S(2)}, u32[]{:S(2)}) collective-permute-start(bf16[64,1024]{1,0:T(8,128)(2,1)S(1)} %get-tuple-element.96), channel_id=1, source_target_pairs={{0,1},{1,2},{2,3},{3,0},{4,5},{5,6},{6,7},{7,4},{8,9},{9,10},{10,1... | collective-permute-start | bytes 393224 | tf_op jit(solution)/shard_map/ppermute | solution.py:613
  130.6 1.6 collective-permute-start.23
  130.7 1.9 %collective-permute-start.24 = (bf16[2,256,256]{2,1,0:T(8,128)(2,1)S(1)}, bf16[2,256,256]{2,1,0:T(8,128)(2,1)S(1)}, u32[]{:S(2)}, u32[]{:S(2)}) collective-permute-start(bf16[2,256,256]{2,1,0:T(8,128)(2,1)S(1)} %collective-permute-done.21.refs_11_), channel_id=1, source_target_pairs={{0,4},{4,0},{8,12},{12,8},{1,5},{5,1},{9,13},{13,9},{2,6},{6,2},{1... | collective-permute-start | bytes 786440 | tf_op jit(solution)/shard_map/ppermute | solution.py:464
  131.2 8.3 %collective-permute-start.22 = (bf16[2,256,256]{2,1,0:T(8,128)(2,1)S(1)}, bf16[2,256,256]{2,1,0:T(8,128)(2,1)S(1)}, u32[]{:S(2)}, u32[]{:S(2)}) collective-permute-start(bf16[2,256,256]{2,1,0:T(8,128)(2,1)S(1)} %get-tuple-element.102.refs_10_), channel_id=1, source_target_pairs={{0,8},{4,12},{8,0},{12,4},{1,9},{5,13},{9,1},{13,5},{2,10},{6,14},... | collective-permute-start | bytes 786440 | tf_op jit(solution)/shard_map/ppermute | solution.py:457
  131.7 13.3 %collective-permute-start.25 = (bf16[2,256,256]{2,1,0:T(8,128)(2,1)S(1)}, bf16[2,256,256]{2,1,0:T(8,128)(2,1)S(1)}, u32[]{:S(2)}, u32[]{:S(2)}) collective-permute-start(bf16[2,256,256]{2,1,0:T(8,128)(2,1)S(1)} %get-tuple-element.102.refs_10_), channel_id=1, source_target_pairs={{0,4},{4,0},{8,12},{12,8},{1,5},{5,1},{9,13},{13,9},{2,6},{6,2},{1... | collective-permute-start | bytes 786440 | tf_op jit(solution)/shard_map/ppermute | solution.py:464
  139.5 5.5 %collective-permute-start.26 = (bf16[2,256,256]{2,1,0:T(8,128)(2,1)S(1)}, bf16[2,256,256]{2,1,0:T(8,128)(2,1)S(1)}, u32[]{:S(2)}, u32[]{:S(2)}) collective-permute-start(bf16[2,256,256]{2,1,0:T(8,128)(2,1)S(1)} %collective-permute-done.22.refs_11_), channel_id=1, source_target_pairs={{0,4},{4,0},{8,12},{12,8},{1,5},{5,1},{9,13},{13,9},{2,6},{6,2},{1... | collective-permute-start | bytes 786440 | tf_op jit(solution)/shard_map/ppermute | solution.py:464
  139.5 9.7 %collective-permute-start.30 = (bf16[256,256]{1,0:T(8,128)(2,1)S(1)}, bf16[256,256]{1,0:T(8,128)(2,1)S(1)}, u32[]{:S(2)}, u32[]{:S(2)}) collective-permute-start(bf16[256,256]{1,0:T(8,128)(2,1)S(1)} %attend_reverse.2.refs_0_), channel_id=1, source_target_pairs={{0,1},{1,2},{2,3},{3,0},{4,5},{5,6},{6,7},{7,4},{8,9},{9,10},{10,1... | collective-permute-start | bytes 393224 | tf_op jit(solution)/shard_map/ppermute | solution.py:613
  140.1 13.2 %collective-permute-start.31 = (bf16[256,256]{1,0:T(8,128)(2,1)S(1)}, bf16[256,256]{1,0:T(8,128)(2,1)S(1)}, u32[]{:S(2)}, u32[]{:S(2)}) collective-permute-start(bf16[256,256]{1,0:T(8,128)(2,1)S(1)} %attend_reverse.2.refs_0_), channel_id=1, source_target_pairs={{0,2},{1,3},{2,0},{3,1},{4,6},{5,7},{6,4},{7,5},{8,10},{9,11},{10,... | collective-permute-start | bytes 393224 | tf_op jit(solution)/shard_map/ppermute | solution.py:613
  142.0 11.3 %collective-permute-start.32 = (bf16[256,256]{1,0:T(8,128)(2,1)S(1)}, bf16[256,256]{1,0:T(8,128)(2,1)S(1)}, u32[]{:S(2)}, u32[]{:S(2)}) collective-permute-start(bf16[256,256]{1,0:T(8,128)(2,1)S(1)} %attend_reverse.2.refs_0_), channel_id=1, source_target_pairs={{0,3},{1,0},{2,1},{3,2},{4,7},{5,4},{6,5},{7,6},{8,11},{9,8},{10,9... | collective-permute-start | bytes 393224 | tf_op jit(solution)/shard_map/ppermute | solution.py:613
  148.6 21.6 %collective-permute-start.27 = (bf16[256,256]{1,0:T(8,128)(2,1)S(1)}, bf16[256,256]{1,0:T(8,128)(2,1)S(1)}, u32[]{:S(2)}, u32[]{:S(2)}) collective-permute-start(bf16[256,256]{1,0:T(8,128)(2,1)S(1)} %attend_reverse.3.refs_0_), channel_id=1, source_target_pairs={{0,1},{1,2},{2,3},{3,0},{4,5},{5,6},{6,7},{7,4},{8,9},{9,10},{10,1... | collective-permute-start | bytes 393224 | tf_op jit(solution)/shard_map/ppermute | solution.py:613
  148.7 21.6 %collective-permute-start.28 = (bf16[256,256]{1,0:T(8,128)(2,1)S(1)}, bf16[256,256]{1,0:T(8,128)(2,1)S(1)}, u32[]{:S(2)}, u32[]{:S(2)}) collective-permute-start(bf16[256,256]{1,0:T(8,128)(2,1)S(1)} %attend_reverse.3.refs_0_), channel_id=1, source_target_pairs={{0,2},{1,3},{2,0},{3,1},{4,6},{5,7},{6,4},{7,5},{8,10},{9,11},{10,... | collective-permute-start | bytes 393224 | tf_op jit(solution)/shard_map/ppermute | solution.py:613
  149.2 21.0 %collective-permute-start.29 = (bf16[256,256]{1,0:T(8,128)(2,1)S(1)}, bf16[256,256]{1,0:T(8,128)(2,1)S(1)}, u32[]{:S(2)}, u32[]{:S(2)}) collective-permute-start(bf16[256,256]{1,0:T(8,128)(2,1)S(1)} %attend_reverse.3.refs_0_), channel_id=1, source_target_pairs={{0,3},{1,0},{2,1},{3,2},{4,7},{5,4},{6,5},{7,6},{8,11},{9,8},{10,9... | collective-permute-start | bytes 393224 | tf_op jit(solution)/shard_map/ppermute | solution.py:613
  166.7 0.9 copy-start.13
  (2 other events, 1.4 us)
Sparse Core Ops, SparseCore 0:
  130.7 35.9 all-gather.1

commit v6 on v5

--- a/solution.py
+++ b/solution.py
@@ -528,7 +528,7 @@
             arrived[strand].append(moving)
             if step < slabs - 1:
                 first = (early.pop(0) if early else None, total)
-                moving = hop([tie(block, first) for block in moving])
+                moving = hop(moving[:-1] + [tie(moving[-1], first)])
                 waiting.append(step)
                 total = add_slabs(strand, waiting, total)
                 partial.append(total)
@@ -587,18 +587,6 @@
 
     arrived, partial = [[], []], []
     cut = own_chains(tie(hidden, moving), 1)
-    total = run_ring(0, moving, [None, (code_sets, cut)])
-    last = arrived[0][-1]
-    moving = hop([tie(block, item, total) for block, item in zip(cut, last)])
-    made, query = finish(0, last, total, None, 1)
-    own, tables, eq = made[0], made[1:], query[2]
-    far = ctx_far(own)
-
-    total = run_ring(1, moving, [(own,)])
-    blocks = spread_out(own, tie(far, partial[:1]))
-    before = attend_part(0, 0, width, blocks, query, tables, None, tie(ids, total))
-    last = tie(arrived[1][-1], before)
-
     lanes = lax.axis_size("groups") * ctx
     piece_rows = width // lanes
     lane = lax.axis_index("groups") * ctx + me
@@ -607,17 +595,27 @@
     for shift in range(slabs):
         target = (head + shift) % slabs
         pieces.append(lax.dynamic_slice_in_dim(piece, target * tile, tile, 1))
-    pieces = tie(pieces, partial)
-
     def around(item, shift):
         return lax.ppermute(item, "head", [(i, (i + shift) % slabs) for i in range(slabs)])
 
-    pieces = [around(tie(item, last), shift) if shift else item for shift, item in enumerate(pieces)]
+    pieces = [around(tie(item, moving), shift) if shift else item for shift, item in enumerate(pieces)]
+    total = run_ring(0, moving, [rope, (code_sets, cut, pieces)])
+    last = arrived[0][-1]
+    moving = [tie(block, item) for block, item in zip(cut, last)]
+    moving = hop(moving[:-1] + [tie(moving[-1], total)])
+    made, query = finish(0, last, total, None, 1)
+    own, tables, eq = made[0], made[1:], query[2]
+    far = ctx_far(own)
+
+    total = run_ring(1, moving, [(own,)])
+    blocks = spread_out(own, tie(far, arrived[1][0]))
+    before = attend_part(0, 0, width, blocks, query, tables, None, tie(ids, total))
+    last = tie(arrived[1][-1], before)
 
     own_then, query_then = finish(1, last, total, eq, parts)
     far_then = [ctx_far(item) for item in own_then]
     far_then[0] = tie(far_then[0], own_then, query_then)
-    pieces = tie(jnp.stack(pieces), far_then[0])
+    pieces = tie(jnp.stack(pieces), own)
     out_slabs = lax.all_gather(pieces, ("groups", "ctx"), axis=1, tiled=True)
     combined, result = [], None
     for part in range(parts):

time: 181 us -> 174 us (0.961)
  waiting for transfers between devices: 66.2 us -> 54.8 us
  local copies, waits for them, and re-layouts: 11.5 us -> 17.4 us
  other arithmetic: 13.7 us -> 11.5 us
  Pallas kernels: 45.4 us -> 43.3 us
  starting transfers between devices: 29.8 us -> 31.8 us
    all_gather x1, waiting for transfers between devices: 12.8 us -> 0.01 us  [shards(): out_slabs = lax.all_gather(pieces, ('groups', 'ctx'), axis=1, tiled=True)]
    ppermute x12, waiting for transfers between devices: 40 us -> 28.3 us  [hop(): return [lax.ppermute(block, 'head', ring) for block in blocks]]
    ppermute x4, waiting for transfers between devices: 3.28 us -> 10.1 us  [ctx_far(): lax.ppermute(block, 'ctx', [(i, (i + cores * shift) % ctx) for i in range...]
    ppermute x9, waiting for transfers between devices: 8.21 us -> 14.8 us  [around(): lax.ppermute(item, 'head', [(i, (i + shift) % slabs) for i in range(slabs)])]
    unnamed x32 -> x64, local copies, waits for them, and re-layouts: 8.04 us -> 12.3 us
    concatenate x2, other arithmetic: 3.95 us -> 0.68 us  [rope_tables(): jnp.concatenate([cos, cos], axis=1)]
    ppermute x12, starting transfers between devices: 8 us -> 11.1 us  [hop(): return [lax.ppermute(block, 'head', ring) for block in blocks]]
  transfers between devices with their start and end apart: 34 -> 34, of which waited for: 15 -> 17; matrix products, arithmetic and copies ran while one was open for 10% -> 10% of each run, Pallas kernels for 19% -> 21%
where the time goes in v6:
time: 174 us; the launch traced here: 173 us
  waiting for transfers between devices  54.8 us (31%)
  Pallas kernels  43.3 us (25%)
  starting transfers between devices  31.8 us (18%)
  local copies, waits for them, and re-layouts  17.4 us (10%)
  between operations  13.9 us (8%)
  other arithmetic  11.5 us (7%)
    pallas_call x10, Pallas kernels, local_call(): pl.pallas_call(kernel, in_specs=[pl.BlockSpec(memory_space=pltpu.SMEM)] +...  33.7 us
    ppermute x12, waiting for transfers between devices, hop(): return [lax.ppermute(block, 'head', ring) for block in blocks]  28.3 us
    ppermute x9, starting transfers between devices, around(): lax.ppermute(item, 'head', [(i, (i + shift) % slabs) for i in range(slabs)])  14.9 us
    ppermute x9, waiting for transfers between devices, around(): lax.ppermute(item, 'head', [(i, (i + shift) % slabs) for i in range(slabs)])  14.8 us
    unnamed x64, local copies, waits for them, and re-layouts  12.3 us
    ppermute x12, starting transfers between devices, hop(): return [lax.ppermute(block, 'head', ring) for block in blocks]  11.1 us
    ppermute x4, waiting for transfers between devices, ctx_far(): lax.ppermute(block, 'ctx', [(i, (i + cores * shift) % ctx) for i in range...  10.1 us
    pallas_call x3, Pallas kernels, attend(): pl.pallas_call(functools.partial(attend_kernel, forward, count, before is...  9.58 us
  transfers between devices with their start and end apart: 34, of which 17 were waited for; matrix products, arithmetic and copies ran while one was open for 10% of the time, Pallas kernels for 21%

profile of v6, /device:TPU:0, one launch (start us, length us, event | category | flops | bytes accessed | tf_op | source)
XLA Modules:
  0.0 172.6 jit_solution(10128304322322677034)
XLA Ops:
  6.5 3.0 %collective-permute-start.8 = (s32[256]{0:T(256)}, s32[256]{0:T(256)S(1)}, u32[]{:S(2)}, u32[]{:S(2)}) collective-permute-start(s32[256]{0:T(256)} %param.10), channel_id=1, source_target_pairs={{0,8},{4,12},{8,0},{12,4},{1,9},{5,13},{9,1},{13,5},{2,10},{6,14},... | collective-permute-start | bytes 3080 | tf_op jit(solution)/shard_map/ppermute | solution.py:457
  9.5 1.8 %slice_bitcast_fusion.2 = (bf16[128,1024]{1,0:T(8,128)(2,1)}, bf16[128,1024]{1,0:T(8,128)(2,1)}) fusion(bf16[2,256,1024]{2,1,0:T(8,128)(2,1)} %refs_3_.1), kind=kLoop, calls=%fused_computation.14 | loop fusion | bytes 1048576 | tf_op jit(solution)/shard_map/squeeze | solution.py:477
  11.4 1.6 collective-permute-start
  12.9 1.6 collective-permute-start.1
  16.3 1.0 select_reduce_fusion
  17.4 3.7 %fusion.1 = (f32[1024,64]{1,0:T(8,128)S(1)}, f32[1024,64]{1,0:T(8,128)S(1)}, f32[1024,64]{1,0:T(8,128)S(1)}, f32[1024,64]{1,0:T(8,128)S(1)}, f32[1024,64]{1,0:T(8,128)S(1)}, /*index=5*/f32[1024,64]{1,0:T(8,128)S(1)}) fusion(f32[64]{0:T(128)S(1)} %multiply_power_fusion, f32[1024]{0:T(1024)S(1)} %subtract_convert_fusion, f32[1024]{0:T(1024)S(1)} %iota_convert_fusion), kind=kLoop, calls=%fused_computation.17 | loop fusion | flops 262144 | bytes 1581312 | tf_op jit(solution)/shard_map/neg | solution.py:44
  21.8 2.3 %fusion.3 = (bf16[64,1024]{1,0:T(8,128)(2,1)}, bf16[64,1024]{1,0:T(8,128)(2,1)}, bf16[64,1024]{1,0:T(8,128)(2,1)}, bf16[64,1024]{1,0:T(8,128)(2,1)}) fusion(bf16[512,4096]{1,0:T(8,128)(2,1)} %param.17, s32[]{:T(128)S(6)} %select_n.137, s32[]{:T(128)S(6)} %select_n.140, s32[]{:T(128)S(6)} %select_n.143, s32[]{:T(128)S(6)} %select_n.149, s32[]{:T(128)S(6)} %select_n.146), kind=kLoop, calls=%fused_computation.38 | loop fusion | bytes 1048596 | tf_op jit(solution)/shard_map/dynamic_slice | solution.py:597
  24.2 1.0 collective-permute-done.10
  25.3 1.1 select_convert_fusion
  26.3 1.5 collective-permute-done.1.refs_6_
  27.9 1.2 collective-permute-start.5
  29.9 1.6 collective-permute-start.2
  31.4 1.6 collective-permute-start.3
  33.0 2.9 %collective-permute-start.4 = (bf16[64,1024]{1,0:T(8,128)(2,1)}, bf16[64,1024]{1,0:T(8,128)(2,1)}, u32[]{:S(2)}, u32[]{:S(2)}) collective-permute-start(bf16[64,1024]{1,0:T(8,128)(2,1)} %get-tuple-element.54), channel_id=1, source_target_pairs={{0,3},{1,0},{2,1},{3,2},{4,7},{5,4},{6,5},{7,6},{8,11},{9,8},{10,9... | collective-permute-start | bytes 393224 | tf_op jit(solution)/shard_map/ppermute | solution.py:599
  35.9 5.2 %slab_sums.4 = (f32[256,512]{1,0:T(8,128)S(1)}, f32[256,512]{1,0:T(8,128)S(1)}, f32[256,512]{1,0:T(8,128)S(1)}, f32[16,512]{1,0:T(8,128)S(1)}, f32[16,512]{1,0:T(8,128)S(1)}, /*index=5*/f32[16,512]{1,0:T(8,128)S(1)}) custom-call(s32[2]{0:T(128)S(1)} %pad_add_fusion.3.slab_ref, bf16[4096,512]{1,0:T(8,128)(2,1)} %refs_0_.14, bf16[4096,512]{1,0:T(8,128)(2,1)} %refs_0_.15, ...), custom_call_target="tpu_custom_call" | custom-call | flops 25165824 | bytes 98304 | tf_op jit(solution)/shard_map/slab_sums/pallas_call | solution.py:70
  46.2 1.5 collective-permute-done.2
  47.8 4.4 %collective-permute-done.3 = bf16[64,1024]{1,0:T(8,128)(2,1)} collective-permute-done((bf16[64,1024]{1,0:T(8,128)(2,1)}, bf16[64,1024]{1,0:T(8,128)(2,1)}, u32[]{:S(2)}, u32[]{:S(2)}) %collective-permute-start.3) | collective-permute-done | bytes 131104 | tf_op jit(solution)/shard_map/ppermute | solution.py:599
  52.2 3.3 %collective-permute-start.11 = (bf16[128,1024]{1,0:T(8,128)(2,1)}, bf16[128,1024]{1,0:T(8,128)(2,1)}, u32[]{:S(2)}, u32[]{:S(2)}) collective-permute-start(bf16[128,1024]{1,0:T(8,128)(2,1)} %collective-permute-done.7.refs_5_), channel_id=1, source_target_pairs={{0,1},{1,2},{2,3},{3,0},{4,5},{5,6},{6,7},{7,4},{8,9},{9,10},{10,1... | collective-permute-start | bytes 786440 | tf_op jit(solution)/shard_map/ppermute | solution.py:467
  56.2 2.0 %pad_maximum_fusion = bf16[4,64,1024]{2,1,0:T(8,128)(2,1)} fusion(bf16[1,64,1024]{2,1,0:T(8,128)(2,1)} %bitcast.9, bf16[1,64,1024]{2,1,0:T(8,128)(2,1)} %bitcast.8, bf16[1,64,1024]{2,1,0:T(8,128)(2,1)} %bitcast.7, bf16[1,64,1024]{2,1,0:T(8,128)(2,1)} %bitcast.25), kind=kLoop, calls=%fused_computation.4 | loop fusion | flops 786432 | bytes 1048576 | tf_op jit(solution)/shard_map/stack | solution.py:618
  58.1 1.0 copy-done.3
  63.5 4.0 %slab_sums.5 = (f32[256,512]{1,0:T(8,128)S(1)}, f32[256,512]{1,0:T(8,128)S(1)}, f32[256,512]{1,0:T(8,128)S(1)}, f32[16,512]{1,0:T(8,128)S(1)}, f32[16,512]{1,0:T(8,128)S(1)}, /*index=5*/f32[16,512]{1,0:T(8,128)S(1)}) custom-call(s32[1]{0:T(128)} %bitcast.20.slab_ref, bf16[4096,512]{1,0:T(8,128)(2,1)} %refs_0_.14, bf16[4096,512]{1,0:T(8,128)(2,1)} %refs_0_.15, ...), custom_call_target="tpu_custom_call" | custom-call | flops 12582912 | bytes 49152 | tf_op jit(solution)/shard_map/slab_sums/pallas_call | solution.py:70
  68.0 3.5 %finish_kv.2 = (bf16[2,256,512]{2,1,0:T(8,128)(2,1)S(1)}, bf16[16,512]{1,0:T(8,128)(2,1)S(1)}, bf16[16,512]{1,0:T(8,128)(2,1)S(1)}, f32[16,512]{1,0:T(8,128)S(1)}) custom-call(s32[2]{0:T(128)S(1)} %copy-done.27, bf16[4096,512]{1,0:T(8,128)(2,1)} %refs_0_.15, bf16[4096,512]{1,0:T(8,128)(2,1)} %refs_1_.11, ...), custom_call_target="tpu_custom_call" | custom-call | flops 8388608 | bytes 61440 | tf_op jit(solution)/shard_map/finish_kv/pallas_call | solution.py:70
  74.3 1.6 collective-permute-start.15
  76.2 9.4 %collective-permute-done.15.refs_5_ = bf16[128,1024]{1,0:T(8,128)(2,1)S(1)} collective-permute-done((bf16[128,1024]{1,0:T(8,128)(2,1)}, bf16[128,1024]{1,0:T(8,128)(2,1)S(1)}, u32[]{:S(2)}, u32[]{:S(2)}) %collective-permute-start.15) | collective-permute-done | bytes 262176 | tf_op jit(solution)/shard_map/ppermute | solution.py:467
  85.6 3.7 %collective-permute-done.12.refs_4_ = bf16[128,1024]{1,0:T(8,128)(2,1)S(1)} collective-permute-done((bf16[128,1024]{1,0:T(8,128)(2,1)}, bf16[128,1024]{1,0:T(8,128)(2,1)S(1)}, u32[]{:S(2)}, u32[]{:S(2)}) %collective-permute-start.12) | collective-permute-done | bytes 262176 | tf_op jit(solution)/shard_map/ppermute | solution.py:467
  89.3 2.0 %collective-permute-done.18.refs_11_ = bf16[2,256,512]{2,1,0:T(8,128)(2,1)S(1)} collective-permute-done((bf16[2,256,512]{2,1,0:T(8,128)(2,1)}, bf16[2,256,512]{2,1,0:T(8,128)(2,1)S(1)}, u32[]{:S(2)}, u32[]{:S(2)}) %collective-permute-start.18) | collective-permute-done | bytes 524320 | tf_op jit(solution)/shard_map/ppermute | solution.py:457
  91.3 1.4 collective-permute-start.16
  93.4 4.1 %slab_sums.6 = (f32[256,512]{1,0:T(8,128)S(1)}, f32[256,512]{1,0:T(8,128)S(1)}, f32[256,512]{1,0:T(8,128)S(1)}) custom-call(s32[2]{0:T(128)S(1)} %copy-done.30, bf16[4096,512]{1,0:T(8,128)(2,1)} %refs_0_.14, bf16[4096,512]{1,0:T(8,128)(2,1)} %refs_0_.15, bf16[4096,512]{1,0:T(8,128)(2,1)} %refs_1_.11, bf16[2,256,1024]{2,1,0:T(8,128)(2,1)S(1)} %copy-done, ...), custom_call_target="tpu_custom_call" | custom-call | flops 25165824 | bytes 98304 | tf_op jit(solution)/shard_map/slab_sums/pallas_call | solution.py:70
  97.5 4.7 %collective-permute-done.16.refs_4_ = bf16[128,1024]{1,0:T(8,128)(2,1)S(1)} collective-permute-done((bf16[128,1024]{1,0:T(8,128)(2,1)S(1)}, bf16[128,1024]{1,0:T(8,128)(2,1)S(1)}, u32[]{:S(2)}, u32[]{:S(2)}) %collective-permute-start.16) | collective-permute-done | bytes 262176 | tf_op jit(solution)/shard_map/ppermute | solution.py:467
  102.2 5.6 %collective-permute-done.13.refs_3_ = bf16[128,1024]{1,0:T(8,128)(2,1)S(1)} collective-permute-done((bf16[128,1024]{1,0:T(8,128)(2,1)S(1)}, bf16[128,1024]{1,0:T(8,128)(2,1)S(1)}, u32[]{:S(2)}, u32[]{:S(2)}) %collective-permute-start.13) | collective-permute-done | bytes 262176 | tf_op jit(solution)/shard_map/ppermute | solution.py:467
  107.9 3.2 %finish_q.2 = (bf16[256,512]{1,0:T(8,128)(2,1)S(1)}, bf16[256,512]{1,0:T(8,128)(2,1)S(1)}, f32[16,512]{1,0:T(8,128)S(1)}) custom-call(s32[2]{0:T(128)S(1)} %copy-done.28, bf16[4096,512]{1,0:T(8,128)(2,1)} %refs_0_.14, bf16[128,1024]{1,0:T(8,128)(2,1)} %collective-permute-done.6.refs_2_.refs_1_, bf16[128,1024]{1,0:T(8,128)(2,1)} %collective-permute-done.11.refs_3_.refs_2_, ...), custom_call_target="tpu_custom_call" | custom-call | flops 4194304 | bytes 32768 | tf_op jit(solution)/shard_map/finish_q/pallas_call | solution.py:70
  111.1 2.6 %slab_sums.7 = (f32[256,512]{1,0:T(8,128)S(1)}, f32[256,512]{1,0:T(8,128)S(1)}, f32[256,512]{1,0:T(8,128)S(1)}) custom-call(s32[1]{0:T(128)} %bitcast.20.slab_ref, bf16[4096,512]{1,0:T(8,128)(2,1)} %refs_0_.14, bf16[4096,512]{1,0:T(8,128)(2,1)} %refs_0_.15, bf16[4096,512]{1,0:T(8,128)(2,1)} %refs_1_.11, ...), custom_call_target="tpu_custom_call" | custom-call | flops 12582912 | bytes 49152 | tf_op jit(solution)/shard_map/slab_sums/pallas_call | solution.py:70
  113.8 2.1 %attend_forward.1.refs_14_ = f32[256,512]{1,0:T(8,128)S(1)} custom-call(s32[4]{0:T(128)S(1)} %copy-done.26, bf16[256,512]{1,0:T(8,128)(2,1)S(1)} %get-tuple-element.84.refs_1_, bf16[256,512]{1,0:T(8,128)(2,1)S(1)} %get-tuple-element.85.refs_2_, bf16[16,512]{1,0:T(8,128)(2,1)S(1)} %get-tuple-element.86.refs_3_, bf16[16,512]{1,0:T(8,128)(2,1)S(1)} %copy-done.16, ...), custom_call_target="tpu_custom_call" | custom-call | flops 16777216 | bytes 32768 | tf_op jit(solution)/shard_map/attend_forward/pallas_call | solution.py:366
  115.9 2.9 %collective-permute-done.14.refs_1_.refs_2_ = bf16[128,1024]{1,0:T(8,128)(2,1)S(1)} collective-permute-done((bf16[128,1024]{1,0:T(8,128)(2,1)S(1)}, bf16[128,1024]{1,0:T(8,128)(2,1)S(1)}, u32[]{:S(2)}, u32[]{:S(2)}) %collective-permute-start.14) | collective-permute-done | bytes 262176 | tf_op jit(solution)/shard_map/ppermute | solution.py:467
  118.8 2.8 %finish_kv.3 = (bf16[2,256,256]{2,1,0:T(8,128)(2,1)S(1)}, bf16[2,256,256]{2,1,0:T(8,128)(2,1)S(1)}) custom-call(s32[2]{0:T(128)S(1)} %copy-done.28, bf16[4096,512]{1,0:T(8,128)(2,1)} %refs_0_.15, bf16[4096,512]{1,0:T(8,128)(2,1)} %refs_1_.11, bf16[128,1024]{1,0:T(8,128)(2,1)S(1)} %collective-permute-done.14.refs_1_.refs_2_, ...), custom_call_target="tpu_custom_call" | custom-call | flops 8388608 | bytes 61440 | tf_op jit(solution)/shard_map/finish_kv/pallas_call | solution.py:70
  122.6 2.5 %finish_q.3 = (bf16[256,512]{1,0:T(8,128)(2,1)S(1)}, bf16[256,512]{1,0:T(8,128)(2,1)S(1)}) custom-call(s32[2]{0:T(128)S(1)} %copy-done.28, bf16[4096,512]{1,0:T(8,128)(2,1)} %refs_0_.14, bf16[128,1024]{1,0:T(8,128)(2,1)S(1)} %collective-permute-done.14.refs_1_.refs_2_, bf16[128,1024]{1,0:T(8,128)(2,1)S(1)} %collective-permute-done.17.refs_2_.refs_3_, ...), custom_call_target="tpu_custom_call" | custom-call | flops 4194304 | bytes 32768 | tf_op jit(solution)/shard_map/finish_q/pallas_call | solution.py:70
  125.1 4.6 %collective-permute-done.22.refs_11_ = bf16[2,256,256]{2,1,0:T(8,128)(2,1)S(1)} collective-permute-done((bf16[2,256,256]{2,1,0:T(8,128)(2,1)S(1)}, bf16[2,256,256]{2,1,0:T(8,128)(2,1)S(1)}, u32[]{:S(2)}, u32[]{:S(2)}) %collective-permute-start.22) | collective-permute-done | bytes 262176 | tf_op jit(solution)/shard_map/ppermute | solution.py:457
  131.2 3.6 %attend_reverse.2.refs_0_ = bf16[256,256]{1,0:T(8,128)(2,1)S(1)} custom-call(s32[4]{0:T(128)S(1)} %copy-done.26, bf16[256,512]{1,0:T(8,128)(2,1)S(1)} %get-tuple-element.93.refs_1_, bf16[256,512]{1,0:T(8,128)(2,1)S(1)} %get-tuple-element.94.refs_2_, bf16[16,512]{1,0:T(8,128)(2,1)S(1)} %get-tuple-element.86.refs_3_, bf16[16,512]{1,0:T(8,128)(2,1)S(1)} %copy-done.16, ...), custom_call_target="tpu_custom_call" | custom-call | flops 8388608 | bytes 16384 | tf_op jit(solution)/shard_map/attend_reverse/pallas_call | solution.py:366
  134.9 3.5 %collective-permute-done.21.refs_11_ = bf16[2,256,256]{2,1,0:T(8,128)(2,1)S(1)} collective-permute-done((bf16[2,256,256]{2,1,0:T(8,128)(2,1)S(1)}, bf16[2,256,256]{2,1,0:T(8,128)(2,1)S(1)}, u32[]{:S(2)}, u32[]{:S(2)}) %collective-permute-start.21) | collective-permute-done | bytes 262176 | tf_op jit(solution)/shard_map/ppermute | solution.py:457
  138.4 2.8 %collective-permute-start.31 = (bf16[256,256]{1,0:T(8,128)(2,1)S(1)}, bf16[256,256]{1,0:T(8,128)(2,1)S(1)}, u32[]{:S(2)}, u32[]{:S(2)}) collective-permute-start(bf16[256,256]{1,0:T(8,128)(2,1)S(1)} %attend_reverse.2.refs_0_), channel_id=1, source_target_pairs={{0,2},{1,3},{2,0},{3,1},{4,6},{5,7},{6,4},{7,5},{8,10},{9,11},{10,... | collective-permute-start | bytes 393224 | tf_op jit(solution)/shard_map/ppermute | solution.py:599
  142.2 3.8 %attend_reverse.3.refs_0_ = bf16[256,256]{1,0:T(8,128)(2,1)S(1)} custom-call(s32[4]{0:T(128)S(1)} %copy-done.26, bf16[256,512]{1,0:T(8,128)(2,1)S(1)} %get-tuple-element.93.refs_1_, bf16[256,512]{1,0:T(8,128)(2,1)S(1)} %get-tuple-element.94.refs_2_, bf16[16,512]{1,0:T(8,128)(2,1)S(1)} %get-tuple-element.86.refs_3_, bf16[16,512]{1,0:T(8,128)(2,1)S(1)} %copy-done.16, ...), custom_call_target="tpu_custom_call" | custom-call | flops 8388608 | bytes 16384 | tf_op jit(solution)/shard_map/attend_reverse/pallas_call | solution.py:366
  146.1 1.1 collective-permute-start.27
  147.1 1.1 collective-permute-start.28
  148.2 2.8 %collective-permute-start.29 = (bf16[256,256]{1,0:T(8,128)(2,1)S(1)}, bf16[256,256]{1,0:T(8,128)(2,1)S(1)}, u32[]{:S(2)}, u32[]{:S(2)}) collective-permute-start(bf16[256,256]{1,0:T(8,128)(2,1)S(1)} %attend_reverse.3.refs_0_), channel_id=1, source_target_pairs={{0,3},{1,0},{2,1},{3,2},{4,7},{5,4},{6,5},{7,6},{8,11},{9,8},{10,9... | collective-permute-start | bytes 393224 | tf_op jit(solution)/shard_map/ppermute | solution.py:599
  151.3 2.6 %out_project.2.refs_4_ = f32[256,1024]{1,0:T(8,128)S(1)} custom-call(s32[4]{0:T(128)S(1)} %copy-done.26, bf16[4,512,1024]{2,1,0:T(8,128)(2,1)} %all-gather.2.cloned.1.call-done.weight_ref, bf16[256,256]{1,0:T(8,128)(2,1)S(1)} %attend_reverse.2.refs_0_, bf16[256,256]{1,0:T(8,128)(2,1)S(1)} %collective-permute-done.30.refs_1_, ...), custom_call_target="tpu_custom_call" | custom-call | flops 8388608 | bytes 32768 | tf_op jit(solution)/shard_map/out_project/pallas_call | solution.py:70
  153.9 1.2 collective-permute-done.27.refs_1_
  155.1 7.4 %collective-permute-done.28.refs_2_ = bf16[256,256]{1,0:T(8,128)(2,1)S(1)} collective-permute-done((bf16[256,256]{1,0:T(8,128)(2,1)S(1)}, bf16[256,256]{1,0:T(8,128)(2,1)S(1)}, u32[]{:S(2)}, u32[]{:S(2)}) %collective-permute-start.28) | collective-permute-done | bytes 131104 | tf_op jit(solution)/shard_map/ppermute | solution.py:599
  162.5 3.3 %out_project.3 = bf16[256,1024]{1,0:T(8,128)(2,1)} custom-call(s32[4]{0:T(128)S(1)} %copy-done.26, bf16[4,512,1024]{2,1,0:T(8,128)(2,1)} %all-gather.2.cloned.1.call-done.weight_ref, bf16[256,256]{1,0:T(8,128)(2,1)S(1)} %attend_reverse.3.refs_0_, bf16[256,256]{1,0:T(8,128)(2,1)S(1)} %collective-permute-done.27.refs_1_, ...), custom_call_target="tpu_custom_call" | custom-call | flops 8388608 | bytes 32768 | tf_op jit(solution)/shard_map/out_project/pallas_call | solution.py:70
  (121 shorter events, 21.4 us)
Async XLA Ops:
  6.5 144.7 %all-gather.2.cloned.1.call-start = ((), (), s32[]{:S(2)}) async-start(), calls=%async_computation | async-start | bytes 4718592 | tf_op jit(solution)/shard_map/all_gather | solution.py:619
  6.5 17.5 %collective-permute-start.8 = (s32[256]{0:T(256)}, s32[256]{0:T(256)S(1)}, u32[]{:S(2)}, u32[]{:S(2)}) collective-permute-start(s32[256]{0:T(256)} %param.10), channel_id=1, source_target_pairs={{0,8},{4,12},{8,0},{12,4},{1,9},{5,13},{9,1},{13,5},{2,10},{6,14},... | collective-permute-start | bytes 3080 | tf_op jit(solution)/shard_map/ppermute | solution.py:457
  9.5 14.7 %collective-permute-start.9 = (s32[256]{0:T(256)}, s32[256]{0:T(256)S(1)}, u32[]{:S(2)}, u32[]{:S(2)}) collective-permute-start(s32[256]{0:T(256)} %param.10), channel_id=1, source_target_pairs={{0,4},{4,0},{8,12},{12,8},{1,5},{5,1},{9,13},{13,9},{2,6},{6,2},{1... | collective-permute-start | bytes 3080 | tf_op jit(solution)/shard_map/ppermute | solution.py:464
  11.4 16.6 %collective-permute-start = (bf16[128,1024]{1,0:T(8,128)(2,1)}, bf16[128,1024]{1,0:T(8,128)(2,1)}, u32[]{:S(2)}, u32[]{:S(2)}) collective-permute-start(bf16[128,1024]{1,0:T(8,128)(2,1)} %get-tuple-element.108), channel_id=1, source_target_pairs={{0,1},{1,2},{2,3},{3,0},{4,5},{5,6},{6,7},{7,4},{8,9},{9,10},{10,1... | collective-permute-start | bytes 786440 | tf_op jit(solution)/shard_map/ppermute | solution.py:467
  12.9 14.9 %collective-permute-start.1 = (bf16[128,1024]{1,0:T(8,128)(2,1)}, bf16[128,1024]{1,0:T(8,128)(2,1)}, u32[]{:S(2)}, u32[]{:S(2)}) collective-permute-start(bf16[128,1024]{1,0:T(8,128)(2,1)} %get-tuple-element.107), channel_id=1, source_target_pairs={{0,1},{1,2},{2,3},{3,0},{4,5},{5,6},{6,7},{7,4},{8,9},{9,10},{10,1... | collective-permute-start | bytes 786440 | tf_op jit(solution)/shard_map/ppermute | solution.py:467
  17.3 7.9 %copy-start.31 = (s32[256]{0:T(256)S(1)}, s32[256]{0:T(256)}, u32[]{:S(2)}) copy-start(s32[256]{0:T(256)} %param.10) | copy-start | bytes 3076
  21.1 14.8 %copy-start = (bf16[2,256,1024]{2,1,0:T(8,128)(2,1)S(1)}, bf16[2,256,1024]{2,1,0:T(8,128)(2,1)}, u32[]{:S(2)}) copy-start(bf16[2,256,1024]{2,1,0:T(8,128)(2,1)} %refs_3_.1) | copy-start | bytes 3145732
  24.1 1.2 collective-permute-start.10
  24.2 17.0 %copy-start.29 = (s32[2]{0:T(128)}, s32[2]{0:T(128)S(1)}, u32[]{:S(2)}) copy-start(s32[2]{0:T(128)S(1)} %pad_add_fusion.3.slab_ref) | copy-start | bytes 28
  27.9 24.3 %collective-permute-start.7 = (bf16[128,1024]{1,0:T(8,128)(2,1)}, bf16[128,1024]{1,0:T(8,128)(2,1)}, u32[]{:S(2)}, u32[]{:S(2)}) collective-permute-start(bf16[128,1024]{1,0:T(8,128)(2,1)} %collective-permute-done.1.refs_6_), channel_id=1, source_target_pairs={{0,1},{1,2},{2,3},{3,0},{4,5},{5,6},{6,7},{7,4},{8,9},{9,10},{10,1... | collective-permute-start | bytes 786440 | tf_op jit(solution)/shard_map/ppermute | solution.py:467
  27.9 27.5 %collective-permute-start.5 = (bf16[128,1024]{1,0:T(8,128)(2,1)}, bf16[128,1024]{1,0:T(8,128)(2,1)}, u32[]{:S(2)}, u32[]{:S(2)}) collective-permute-start(bf16[128,1024]{1,0:T(8,128)(2,1)} %collective-permute-done.refs_5_), channel_id=1, source_target_pairs={{0,1},{1,2},{2,3},{3,0},{4,5},{5,6},{6,7},{7,4},{8,9},{9,10},{10,1... | collective-permute-start | bytes 786440 | tf_op jit(solution)/shard_map/ppermute | solution.py:467
  29.9 17.9 %collective-permute-start.2 = (bf16[64,1024]{1,0:T(8,128)(2,1)}, bf16[64,1024]{1,0:T(8,128)(2,1)}, u32[]{:S(2)}, u32[]{:S(2)}) collective-permute-start(bf16[64,1024]{1,0:T(8,128)(2,1)} %get-tuple-element.52), channel_id=1, source_target_pairs={{0,1},{1,2},{2,3},{3,0},{4,5},{5,6},{6,7},{7,4},{8,9},{9,10},{10,1... | collective-permute-start | bytes 393224 | tf_op jit(solution)/shard_map/ppermute | solution.py:599
  31.4 20.7 %collective-permute-start.3 = (bf16[64,1024]{1,0:T(8,128)(2,1)}, bf16[64,1024]{1,0:T(8,128)(2,1)}, u32[]{:S(2)}, u32[]{:S(2)}) collective-permute-start(bf16[64,1024]{1,0:T(8,128)(2,1)} %get-tuple-element.53), channel_id=1, source_target_pairs={{0,2},{1,3},{2,0},{3,1},{4,6},{5,7},{6,4},{7,5},{8,10},{9,11},{10,... | collective-permute-start | bytes 393224 | tf_op jit(solution)/shard_map/ppermute | solution.py:599
  33.0 19.2 %collective-permute-start.4 = (bf16[64,1024]{1,0:T(8,128)(2,1)}, bf16[64,1024]{1,0:T(8,128)(2,1)}, u32[]{:S(2)}, u32[]{:S(2)}) collective-permute-start(bf16[64,1024]{1,0:T(8,128)(2,1)} %get-tuple-element.54), channel_id=1, source_target_pairs={{0,3},{1,0},{2,1},{3,2},{4,7},{5,4},{6,5},{7,6},{8,11},{9,8},{10,9... | collective-permute-start | bytes 393224 | tf_op jit(solution)/shard_map/ppermute | solution.py:599
  52.2 15.4 %collective-permute-start.11 = (bf16[128,1024]{1,0:T(8,128)(2,1)}, bf16[128,1024]{1,0:T(8,128)(2,1)}, u32[]{:S(2)}, u32[]{:S(2)}) collective-permute-start(bf16[128,1024]{1,0:T(8,128)(2,1)} %collective-permute-done.7.refs_5_), channel_id=1, source_target_pairs={{0,1},{1,2},{2,3},{3,0},{4,5},{5,6},{6,7},{7,4},{8,9},{9,10},{10,1... | collective-permute-start | bytes 786440 | tf_op jit(solution)/shard_map/ppermute | solution.py:467
  55.5 12.6 %collective-permute-start.6 = (bf16[128,1024]{1,0:T(8,128)(2,1)}, bf16[128,1024]{1,0:T(8,128)(2,1)}, u32[]{:S(2)}, u32[]{:S(2)}) collective-permute-start(bf16[128,1024]{1,0:T(8,128)(2,1)} %collective-permute-done.5.refs_4_), channel_id=1, source_target_pairs={{0,1},{1,2},{2,3},{3,0},{4,5},{5,6},{6,7},{7,4},{8,9},{9,10},{10,1... | collective-permute-start | bytes 786440 | tf_op jit(solution)/shard_map/ppermute | solution.py:467
  63.5 4.5 %copy-start.27 = (s32[2]{0:T(128)S(1)}, s32[2]{0:T(128)}, u32[]{:S(2)}) copy-start(s32[2]{0:T(128)} %pad_add_fusion.2.scalars) | copy-start | bytes 28
  67.5 4.0 %copy-start.10 = (f32[256,512]{1,0:T(8,128)}, f32[256,512]{1,0:T(8,128)S(1)}, u32[]{:S(2)}) copy-start(f32[256,512]{1,0:T(8,128)S(1)} %get-tuple-element.72.refs_3_) | copy-start | bytes 1572868
  67.5 4.0 %copy-start.24 = (f32[16,512]{1,0:T(8,128)}, f32[16,512]{1,0:T(8,128)S(1)}, u32[]{:S(2)}) copy-start(f32[16,512]{1,0:T(8,128)S(1)} %get-tuple-element.73.refs_7_) | copy-start | bytes 98308
  73.6 17.8 %collective-permute-start.18 = (bf16[2,256,512]{2,1,0:T(8,128)(2,1)}, bf16[2,256,512]{2,1,0:T(8,128)(2,1)S(1)}, u32[]{:S(2)}, u32[]{:S(2)}) collective-permute-start(bf16[2,256,512]{2,1,0:T(8,128)(2,1)} %copy-done.8), channel_id=1, source_target_pairs={{0,8},{4,12},{8,0},{12,4},{1,9},{5,13},{9,1},{13,5},{2,10},{6,14},... | collective-permute-start | bytes 1572872 | tf_op jit(solution)/shard_map/ppermute | solution.py:457
  74.3 33.6 %copy-start.1 = (bf16[4,256,16]{2,1,0:T(8,128)(2,1)S(1)}, bf16[4,256,16]{2,1,0:T(8,128)(2,1)}, u32[]{:S(2)}) copy-start(bf16[4,256,16]{2,1,0:T(8,128)(2,1)} %get-tuple-element.112.refs_6_) | copy-start | bytes 98308
  74.3 33.6 %copy-start.11 = (f32[256,512]{1,0:T(8,128)S(1)}, f32[256,512]{1,0:T(8,128)}, u32[]{:S(2)}) copy-start(f32[256,512]{1,0:T(8,128)} %copy-done.10) | copy-start | bytes 1572868
  74.3 33.6 %copy-start.25 = (f32[16,512]{1,0:T(8,128)S(1)}, f32[16,512]{1,0:T(8,128)}, u32[]{:S(2)}) copy-start(f32[16,512]{1,0:T(8,128)} %copy-done.24) | copy-start | bytes 98308
  74.3 33.6 %copy-start.28 = (s32[2]{0:T(128)S(1)}, s32[2]{0:T(128)}, u32[]{:S(2)}) copy-start(s32[2]{0:T(128)} %pad_add_fusion.2.scalars) | copy-start | bytes 28
  74.3 11.3 %collective-permute-start.15 = (bf16[128,1024]{1,0:T(8,128)(2,1)}, bf16[128,1024]{1,0:T(8,128)(2,1)S(1)}, u32[]{:S(2)}, u32[]{:S(2)}) collective-permute-start(bf16[128,1024]{1,0:T(8,128)(2,1)} %get-tuple-element.74), channel_id=1, source_target_pairs={{0,1},{1,2},{2,3},{3,0},{4,5},{5,6},{6,7},{7,4},{8,9},{9,10},{10,1... | collective-permute-start | bytes 786440 | tf_op jit(solution)/shard_map/ppermute | solution.py:467
  75.9 13.4 %collective-permute-start.12 = (bf16[128,1024]{1,0:T(8,128)(2,1)}, bf16[128,1024]{1,0:T(8,128)(2,1)S(1)}, u32[]{:S(2)}, u32[]{:S(2)}) collective-permute-start(bf16[128,1024]{1,0:T(8,128)(2,1)} %get-tuple-element.70), channel_id=1, source_target_pairs={{0,1},{1,2},{2,3},{3,0},{4,5},{5,6},{6,7},{7,4},{8,9},{9,10},{10,1... | collective-permute-start | bytes 786440 | tf_op jit(solution)/shard_map/ppermute | solution.py:467
  76.2 37.5 %collective-permute-start.19 = (bf16[2,256,512]{2,1,0:T(8,128)(2,1)}, bf16[2,256,512]{2,1,0:T(8,128)(2,1)S(1)}, u32[]{:S(2)}, u32[]{:S(2)}) collective-permute-start(bf16[2,256,512]{2,1,0:T(8,128)(2,1)} %copy-done.8), channel_id=1, source_target_pairs={{0,4},{4,0},{8,12},{12,8},{1,5},{5,1},{9,13},{13,9},{2,6},{6,2},{1... | collective-permute-start | bytes 1572872 | tf_op jit(solution)/shard_map/ppermute | solution.py:464
  91.3 22.4 %collective-permute-start.20 = (bf16[2,256,512]{2,1,0:T(8,128)(2,1)S(1)}, bf16[2,256,512]{2,1,0:T(8,128)(2,1)S(1)}, u32[]{:S(2)}, u32[]{:S(2)}) collective-permute-start(bf16[2,256,512]{2,1,0:T(8,128)(2,1)S(1)} %collective-permute-done.18.refs_11_), channel_id=1, source_target_pairs={{0,4},{4,0},{8,12},{12,8},{1,5},{5,1},{9,13},{13,9},{2,6},{6,2},{1... | collective-permute-start | bytes 1572872 | tf_op jit(solution)/shard_map/ppermute | solution.py:464
  91.3 10.9 %collective-permute-start.16 = (bf16[128,1024]{1,0:T(8,128)(2,1)S(1)}, bf16[128,1024]{1,0:T(8,128)(2,1)S(1)}, u32[]{:S(2)}, u32[]{:S(2)}) collective-permute-start(bf16[128,1024]{1,0:T(8,128)(2,1)S(1)} %collective-permute-done.15.refs_5_), channel_id=1, source_target_pairs={{0,1},{1,2},{2,3},{3,0},{4,5},{5,6},{6,7},{7,4},{8,9},{9,10},{10,1... | collective-permute-start | bytes 786440 | tf_op jit(solution)/shard_map/ppermute | solution.py:467
  92.7 15.1 %collective-permute-start.13 = (bf16[128,1024]{1,0:T(8,128)(2,1)S(1)}, bf16[128,1024]{1,0:T(8,128)(2,1)S(1)}, u32[]{:S(2)}, u32[]{:S(2)}) collective-permute-start(bf16[128,1024]{1,0:T(8,128)(2,1)S(1)} %collective-permute-done.12.refs_4_), channel_id=1, source_target_pairs={{0,1},{1,2},{2,3},{3,0},{4,5},{5,6},{6,7},{7,4},{8,9},{9,10},{10,1... | collective-permute-start | bytes 786440 | tf_op jit(solution)/shard_map/ppermute | solution.py:467
  102.2 13.7 %collective-permute-start.17 = (bf16[128,1024]{1,0:T(8,128)(2,1)S(1)}, bf16[128,1024]{1,0:T(8,128)(2,1)S(1)}, u32[]{:S(2)}, u32[]{:S(2)}) collective-permute-start(bf16[128,1024]{1,0:T(8,128)(2,1)S(1)} %collective-permute-done.16.refs_4_), channel_id=1, source_target_pairs={{0,1},{1,2},{2,3},{3,0},{4,5},{5,6},{6,7},{7,4},{8,9},{9,10},{10,1... | collective-permute-start | bytes 786440 | tf_op jit(solution)/shard_map/ppermute | solution.py:467
  107.8 10.9 %collective-permute-start.14 = (bf16[128,1024]{1,0:T(8,128)(2,1)S(1)}, bf16[128,1024]{1,0:T(8,128)(2,1)S(1)}, u32[]{:S(2)}, u32[]{:S(2)}) collective-permute-start(bf16[128,1024]{1,0:T(8,128)(2,1)S(1)} %collective-permute-done.13.refs_3_), channel_id=1, source_target_pairs={{0,1},{1,2},{2,3},{3,0},{4,5},{5,6},{6,7},{7,4},{8,9},{9,10},{10,1... | collective-permute-start | bytes 786440 | tf_op jit(solution)/shard_map/ppermute | solution.py:467
  111.0 2.7 %copy-start.9 = (bf16[2,256,512]{2,1,0:T(8,128)(2,1)S(1)}, bf16[2,256,512]{2,1,0:T(8,128)(2,1)}, u32[]{:S(2)}) copy-start(bf16[2,256,512]{2,1,0:T(8,128)(2,1)} %copy-done.8) | copy-start | bytes 1572868
  111.0 2.7 %copy-start.13 = (f32[16,512]{1,0:T(8,128)S(1)}, f32[16,512]{1,0:T(8,128)}, u32[]{:S(2)}) copy-start(f32[16,512]{1,0:T(8,128)} %copy-done.12) | copy-start | bytes 98308
  111.1 2.7 %copy-start.16 = (bf16[16,512]{1,0:T(8,128)(2,1)S(1)}, bf16[16,512]{1,0:T(8,128)(2,1)}, u32[]{:S(2)}) copy-start(bf16[16,512]{1,0:T(8,128)(2,1)} %copy-done.15) | copy-start | bytes 49156
  121.6 9.6 %copy-start.14 = (bf16[4,16,256]{2,1,0:T(8,128)(2,1)S(1)}, bf16[4,16,256]{2,1,0:T(8,128)(2,1)}, u32[]{:S(2)}) copy-start(bf16[4,16,256]{2,1,0:T(8,128)(2,1)} %get-tuple-element.109.refs_7_) | copy-start | bytes 98308
  121.6 8.1 %collective-permute-start.22 = (bf16[2,256,256]{2,1,0:T(8,128)(2,1)S(1)}, bf16[2,256,256]{2,1,0:T(8,128)(2,1)S(1)}, u32[]{:S(2)}, u32[]{:S(2)}) collective-permute-start(bf16[2,256,256]{2,1,0:T(8,128)(2,1)S(1)} %get-tuple-element.96.refs_10_), channel_id=1, source_target_pairs={{0,8},{4,12},{8,0},{12,4},{1,9},{5,13},{9,1},{13,5},{2,10},{6,14},... | collective-permute-start | bytes 786440 | tf_op jit(solution)/shard_map/ppermute | solution.py:457
  122.6 8.2 %collective-permute-start.23 = (bf16[2,256,256]{2,1,0:T(8,128)(2,1)S(1)}, bf16[2,256,256]{2,1,0:T(8,128)(2,1)S(1)}, u32[]{:S(2)}, u32[]{:S(2)}) collective-permute-start(bf16[2,256,256]{2,1,0:T(8,128)(2,1)S(1)} %get-tuple-element.96.refs_10_), channel_id=1, source_target_pairs={{0,4},{4,0},{8,12},{12,8},{1,5},{5,1},{9,13},{13,9},{2,6},{6,2},{1... | collective-permute-start | bytes 786440 | tf_op jit(solution)/shard_map/ppermute | solution.py:464
  129.7 1.5 collective-permute-start.24
  129.7 8.7 %collective-permute-start.21 = (bf16[2,256,256]{2,1,0:T(8,128)(2,1)S(1)}, bf16[2,256,256]{2,1,0:T(8,128)(2,1)S(1)}, u32[]{:S(2)}, u32[]{:S(2)}) collective-permute-start(bf16[2,256,256]{2,1,0:T(8,128)(2,1)S(1)} %get-tuple-element.95.refs_10_), channel_id=1, source_target_pairs={{0,8},{4,12},{8,0},{12,4},{1,9},{5,13},{9,1},{13,5},{2,10},{6,14},... | collective-permute-start | bytes 786440 | tf_op jit(solution)/shard_map/ppermute | solution.py:457
  130.5 11.7 %collective-permute-start.25 = (bf16[2,256,256]{2,1,0:T(8,128)(2,1)S(1)}, bf16[2,256,256]{2,1,0:T(8,128)(2,1)S(1)}, u32[]{:S(2)}, u32[]{:S(2)}) collective-permute-start(bf16[2,256,256]{2,1,0:T(8,128)(2,1)S(1)} %get-tuple-element.95.refs_10_), channel_id=1, source_target_pairs={{0,4},{4,0},{8,12},{12,8},{1,5},{5,1},{9,13},{13,9},{2,6},{6,2},{1... | collective-permute-start | bytes 786440 | tf_op jit(solution)/shard_map/ppermute | solution.py:464
  138.4 3.8 %collective-permute-start.26 = (bf16[2,256,256]{2,1,0:T(8,128)(2,1)S(1)}, bf16[2,256,256]{2,1,0:T(8,128)(2,1)S(1)}, u32[]{:S(2)}, u32[]{:S(2)}) collective-permute-start(bf16[2,256,256]{2,1,0:T(8,128)(2,1)S(1)} %collective-permute-done.21.refs_11_), channel_id=1, source_target_pairs={{0,4},{4,0},{8,12},{12,8},{1,5},{5,1},{9,13},{13,9},{2,6},{6,2},{1... | collective-permute-start | bytes 786440 | tf_op jit(solution)/shard_map/ppermute | solution.py:464
  138.4 9.8 %collective-permute-start.30 = (bf16[256,256]{1,0:T(8,128)(2,1)S(1)}, bf16[256,256]{1,0:T(8,128)(2,1)S(1)}, u32[]{:S(2)}, u32[]{:S(2)}) collective-permute-start(bf16[256,256]{1,0:T(8,128)(2,1)S(1)} %attend_reverse.2.refs_0_), channel_id=1, source_target_pairs={{0,1},{1,2},{2,3},{3,0},{4,5},{5,6},{6,7},{7,4},{8,9},{9,10},{10,1... | collective-permute-start | bytes 393224 | tf_op jit(solution)/shard_map/ppermute | solution.py:599
  138.4 12.9 %collective-permute-start.31 = (bf16[256,256]{1,0:T(8,128)(2,1)S(1)}, bf16[256,256]{1,0:T(8,128)(2,1)S(1)}, u32[]{:S(2)}, u32[]{:S(2)}) collective-permute-start(bf16[256,256]{1,0:T(8,128)(2,1)S(1)} %attend_reverse.2.refs_0_), channel_id=1, source_target_pairs={{0,2},{1,3},{2,0},{3,1},{4,6},{5,7},{6,4},{7,5},{8,10},{9,11},{10,... | collective-permute-start | bytes 393224 | tf_op jit(solution)/shard_map/ppermute | solution.py:599
  141.2 10.0 %collective-permute-start.32 = (bf16[256,256]{1,0:T(8,128)(2,1)S(1)}, bf16[256,256]{1,0:T(8,128)(2,1)S(1)}, u32[]{:S(2)}, u32[]{:S(2)}) collective-permute-start(bf16[256,256]{1,0:T(8,128)(2,1)S(1)} %attend_reverse.2.refs_0_), channel_id=1, source_target_pairs={{0,3},{1,0},{2,1},{3,2},{4,7},{5,4},{6,5},{7,6},{8,11},{9,8},{10,9... | collective-permute-start | bytes 393224 | tf_op jit(solution)/shard_map/ppermute | solution.py:599
  146.1 9.0 %collective-permute-start.27 = (bf16[256,256]{1,0:T(8,128)(2,1)S(1)}, bf16[256,256]{1,0:T(8,128)(2,1)S(1)}, u32[]{:S(2)}, u32[]{:S(2)}) collective-permute-start(bf16[256,256]{1,0:T(8,128)(2,1)S(1)} %attend_reverse.3.refs_0_), channel_id=1, source_target_pairs={{0,1},{1,2},{2,3},{3,0},{4,5},{5,6},{6,7},{7,4},{8,9},{9,10},{10,1... | collective-permute-start | bytes 393224 | tf_op jit(solution)/shard_map/ppermute | solution.py:599
  147.1 15.3 %collective-permute-start.28 = (bf16[256,256]{1,0:T(8,128)(2,1)S(1)}, bf16[256,256]{1,0:T(8,128)(2,1)S(1)}, u32[]{:S(2)}, u32[]{:S(2)}) collective-permute-start(bf16[256,256]{1,0:T(8,128)(2,1)S(1)} %attend_reverse.3.refs_0_), channel_id=1, source_target_pairs={{0,2},{1,3},{2,0},{3,1},{4,6},{5,7},{6,4},{7,5},{8,10},{9,11},{10,... | collective-permute-start | bytes 393224 | tf_op jit(solution)/shard_map/ppermute | solution.py:599
  148.2 14.3 %collective-permute-start.29 = (bf16[256,256]{1,0:T(8,128)(2,1)S(1)}, bf16[256,256]{1,0:T(8,128)(2,1)S(1)}, u32[]{:S(2)}, u32[]{:S(2)}) collective-permute-start(bf16[256,256]{1,0:T(8,128)(2,1)S(1)} %attend_reverse.3.refs_0_), channel_id=1, source_target_pairs={{0,3},{1,0},{2,1},{3,2},{4,7},{5,4},{6,5},{7,6},{8,11},{9,8},{10,9... | collective-permute-start | bytes 393224 | tf_op jit(solution)/shard_map/ppermute | solution.py:599
  (18 other events, 17.7 us)
Sparse Core Ops, SparseCore 0:
  73.7 39.8 all-gather.1

commit v7 on v6

--- a/solution.py
+++ b/solution.py
@@ -599,23 +599,22 @@
         return lax.ppermute(item, "head", [(i, (i + shift) % slabs) for i in range(slabs)])
 
     pieces = [around(tie(item, moving), shift) if shift else item for shift, item in enumerate(pieces)]
-    total = run_ring(0, moving, [rope, (code_sets, cut, pieces)])
+    total = run_ring(0, moving, [rope, (code_sets, cut)])
     last = arrived[0][-1]
     moving = [tie(block, item) for block, item in zip(cut, last)]
     moving = hop(moving[:-1] + [tie(moving[-1], total)])
     made, query = finish(0, last, total, None, 1)
     own, tables, eq = made[0], made[1:], query[2]
-    far = ctx_far(own)
-
-    total = run_ring(1, moving, [(own,)])
-    blocks = spread_out(own, tie(far, arrived[1][0]))
+    total = run_ring(1, moving, [])
+    far = ctx_far(tie(own, arrived[1][0]))
+    blocks = spread_out(own, tie(far, arrived[1][max(0, slabs - 3)]))
     before = attend_part(0, 0, width, blocks, query, tables, None, tie(ids, total))
     last = tie(arrived[1][-1], before)
 
     own_then, query_then = finish(1, last, total, eq, parts)
     far_then = [ctx_far(item) for item in own_then]
     far_then[0] = tie(far_then[0], own_then, query_then)
-    pieces = tie(jnp.stack(pieces), own)
+    pieces = tie(jnp.stack(pieces), partial[:1])
     out_slabs = lax.all_gather(pieces, ("groups", "ctx"), axis=1, tiled=True)
     combined, result = [], None
     for part in range(parts):

time: 174 us -> 187 us (1.075)
  local copies, waits for them, and re-layouts: 17.4 us -> 24.2 us
  waiting for transfers between devices: 54.8 us -> 59.3 us
  starting transfers between devices: 31.8 us -> 34.8 us
    ppermute x9, waiting for transfers between devices: 14.8 us -> 23.7 us  [around(): lax.ppermute(item, 'head', [(i, (i + shift) % slabs) for i in range(slabs)])]
    unnamed x64 -> x74, local copies, waits for them, and re-layouts: 12.3 us -> 20 us
    ppermute x12, waiting for transfers between devices: 28.3 us -> 22.2 us  [hop(): return [lax.ppermute(block, 'head', ring) for block in blocks]]
    ppermute x12, starting transfers between devices: 11.1 us -> 14.6 us  [hop(): return [lax.ppermute(block, 'head', ring) for block in blocks]]
    dynamic_slice x1 -> x0, local copies, waits for them, and re-layouts: 2.26 us -> none  [shards(): pieces.append(lax.dynamic_slice_in_dim(piece, target * tile, tile, 1))]
  transfers between devices with their start and end apart: 34 -> 34, of which waited for: 17 -> 15; matrix products, arithmetic and copies ran while one was open for 10% -> 8% of each run, Pallas kernels for 21% -> 19%
where the time goes in v7:
time: 187 us; the launch traced here: 186 us
  waiting for transfers between devices  59.3 us (32%)
  Pallas kernels  43.6 us (23%)
  starting transfers between devices  34.8 us (19%)
  local copies, waits for them, and re-layouts  24.2 us (13%)
  between operations  13.8 us (7%)
  other arithmetic  10.6 us (6%)
    pallas_call x10, Pallas kernels, local_call(): pl.pallas_call(kernel, in_specs=[pl.BlockSpec(memory_space=pltpu.SMEM)] +...  34.2 us
    ppermute x9, waiting for transfers between devices, around(): lax.ppermute(item, 'head', [(i, (i + shift) % slabs) for i in range(slabs)])  23.7 us
    ppermute x12, waiting for transfers between devices, hop(): return [lax.ppermute(block, 'head', ring) for block in blocks]  22.2 us
    unnamed x74, local copies, waits for them, and re-layouts  20 us
    ppermute x9, starting transfers between devices, around(): lax.ppermute(item, 'head', [(i, (i + shift) % slabs) for i in range(slabs)])  14.9 us
    ppermute x12, starting transfers between devices, hop(): return [lax.ppermute(block, 'head', ring) for block in blocks]  14.6 us
    ppermute x4, waiting for transfers between devices, ctx_far(): lax.ppermute(block, 'ctx', [(i, (i + cores * shift) % ctx) for i in range...  11.6 us
    pallas_call x3, Pallas kernels, attend(): pl.pallas_call(functools.partial(attend_kernel, forward, count, before is...  9.39 us
  transfers between devices with their start and end apart: 34, of which 15 were waited for; matrix products, arithmetic and copies ran while one was open for 8% of the time, Pallas kernels for 19%

profile of v7, /device:TPU:0, one launch (start us, length us, event | category | flops | bytes accessed | tf_op | source)
XLA Modules:
  0.0 186.4 jit_solution(2914009553536272709)
XLA Ops:
  6.5 3.0 %collective-permute-start.9 = (s32[256]{0:T(256)}, s32[256]{0:T(256)S(1)}, u32[]{:S(2)}, u32[]{:S(2)}) collective-permute-start(s32[256]{0:T(256)} %param.10), channel_id=1, source_target_pairs={{0,8},{4,12},{8,0},{12,4},{1,9},{5,13},{9,1},{13,5},{2,10},{6,14},... | collective-permute-start | bytes 3080 | tf_op jit(solution)/shard_map/ppermute | solution.py:457
  9.5 1.9 slice_bitcast_fusion.2
  11.4 1.6 collective-permute-start
  12.9 1.6 collective-permute-start.1
  16.4 3.7 %fusion.1 = (f32[1024,64]{1,0:T(8,128)S(1)}, f32[1024,64]{1,0:T(8,128)S(1)}, f32[1024,64]{1,0:T(8,128)S(1)}, f32[1024,64]{1,0:T(8,128)S(1)}, f32[1024,64]{1,0:T(8,128)S(1)}, /*index=5*/f32[1024,64]{1,0:T(8,128)S(1)}) fusion(f32[64]{0:T(128)S(1)} %multiply_power_fusion, f32[1024]{0:T(1024)S(1)} %subtract_convert_fusion, f32[1024]{0:T(1024)S(1)} %iota_convert_fusion), kind=kLoop, calls=%fused_computation.17 | loop fusion | flops 262144 | bytes 1581312 | tf_op jit(solution)/shard_map/neg | solution.py:44
  21.4 1.0 collective-permute-done.11
  22.4 1.7 select_convert_fusion
  24.2 3.7 %collective-permute-done.1.refs_6_ = bf16[128,1024]{1,0:T(8,128)(2,1)} collective-permute-done((bf16[128,1024]{1,0:T(8,128)(2,1)}, bf16[128,1024]{1,0:T(8,128)(2,1)}, u32[]{:S(2)}, u32[]{:S(2)}) %collective-permute-start.1) | collective-permute-done | bytes 262176 | tf_op jit(solution)/shard_map/ppermute | solution.py:467
  27.9 1.3 collective-permute-start.5
  29.2 1.4 select_convert_fusion.2
  30.6 5.2 %slab_sums.4 = (f32[256,512]{1,0:T(8,128)S(1)}, f32[256,512]{1,0:T(8,128)S(1)}, f32[256,512]{1,0:T(8,128)S(1)}, f32[16,512]{1,0:T(8,128)S(1)}, f32[16,512]{1,0:T(8,128)S(1)}, /*index=5*/f32[16,512]{1,0:T(8,128)S(1)}) custom-call(s32[2]{0:T(128)S(1)} %pad_add_fusion.2.slab_ref, bf16[4096,512]{1,0:T(8,128)(2,1)} %refs_0_.14, bf16[4096,512]{1,0:T(8,128)(2,1)} %refs_0_.15, ...), custom_call_target="tpu_custom_call" | custom-call | flops 25165824 | bytes 98304 | tf_op jit(solution)/shard_map/slab_sums/pallas_call | solution.py:70
  41.0 1.6 collective-permute-start.12
  42.5 1.1 collective-permute-done.5.refs_4_
  44.6 1.0 copy-done.3
  46.7 1.0 copy-done.7
  50.0 4.0 %slab_sums.5 = (f32[256,512]{1,0:T(8,128)S(1)}, f32[256,512]{1,0:T(8,128)S(1)}, f32[256,512]{1,0:T(8,128)S(1)}, f32[16,512]{1,0:T(8,128)S(1)}, f32[16,512]{1,0:T(8,128)S(1)}, /*index=5*/f32[16,512]{1,0:T(8,128)S(1)}) custom-call(s32[1]{0:T(128)} %bitcast.18.slab_ref, bf16[4096,512]{1,0:T(8,128)(2,1)} %refs_0_.14, bf16[4096,512]{1,0:T(8,128)(2,1)} %refs_0_.15, ...), custom_call_target="tpu_custom_call" | custom-call | flops 12582912 | bytes 49152 | tf_op jit(solution)/shard_map/slab_sums/pallas_call | solution.py:70
  58.3 1.2 collective-permute-start.7
  59.5 1.4 dynamic-slice_bitcast_fusion
  61.0 2.7 %collective-permute-start.2 = (bf16[64,1024]{1,0:T(8,128)(2,1)S(1)}, bf16[64,1024]{1,0:T(8,128)(2,1)S(1)}, u32[]{:S(2)}, u32[]{:S(2)}) collective-permute-start(bf16[64,1024]{1,0:T(8,128)(2,1)S(1)} %get-tuple-element.52), channel_id=1, source_target_pairs={{0,1},{1,2},{2,3},{3,0},{4,5},{5,6},{6,7},{7,4},{8,9},{9,10},{10,1... | collective-permute-start | bytes 393224 | tf_op jit(solution)/shard_map/ppermute | solution.py:599
  64.2 2.8 %collective-permute-start.4 = (bf16[64,1024]{1,0:T(8,128)(2,1)S(1)}, bf16[64,1024]{1,0:T(8,128)(2,1)S(1)}, u32[]{:S(2)}, u32[]{:S(2)}) collective-permute-start(bf16[64,1024]{1,0:T(8,128)(2,1)S(1)} %get-tuple-element.54), channel_id=1, source_target_pairs={{0,3},{1,0},{2,1},{3,2},{4,7},{5,4},{6,5},{7,6},{8,11},{9,8},{10,9... | collective-permute-start | bytes 393224 | tf_op jit(solution)/shard_map/ppermute | solution.py:599
  67.1 11.0 %collective-permute-done.2 = bf16[64,1024]{1,0:T(8,128)(2,1)S(1)} collective-permute-done((bf16[64,1024]{1,0:T(8,128)(2,1)S(1)}, bf16[64,1024]{1,0:T(8,128)(2,1)S(1)}, u32[]{:S(2)}, u32[]{:S(2)}) %collective-permute-start.2) | collective-permute-done | bytes 131104 | tf_op jit(solution)/shard_map/ppermute | solution.py:599
  78.1 3.3 %collective-permute-done.3 = bf16[64,1024]{1,0:T(8,128)(2,1)S(1)} collective-permute-done((bf16[64,1024]{1,0:T(8,128)(2,1)S(1)}, bf16[64,1024]{1,0:T(8,128)(2,1)S(1)}, u32[]{:S(2)}, u32[]{:S(2)}) %collective-permute-start.3) | collective-permute-done | bytes 131104 | tf_op jit(solution)/shard_map/ppermute | solution.py:599
  82.2 4.6 %slab_sums.6 = (f32[256,512]{1,0:T(8,128)S(1)}, f32[256,512]{1,0:T(8,128)S(1)}, f32[256,512]{1,0:T(8,128)S(1)}) custom-call(s32[2]{0:T(128)S(1)} %pad_add_fusion.2.slab_ref, bf16[4096,512]{1,0:T(8,128)(2,1)} %refs_0_.14, bf16[4096,512]{1,0:T(8,128)(2,1)} %refs_0_.15, bf16[4096,512]{1,0:T(8,128)(2,1)} %refs_1_.11, bf16[2,256,1024]{2,1,0:T(8,128)(2,1)S(1)} %copy-done, ...), custom_call_target="tpu_custom_call" | custom-call | flops 25165824 | bytes 98304 | tf_op jit(solution)/shard_map/slab_sums/pallas_call | solution.py:70
  89.4 1.0 copy-done.9
  90.4 1.0 copy-done.11
  93.0 3.5 %finish_kv.2 = (bf16[2,256,512]{2,1,0:T(8,128)(2,1)S(1)}, bf16[16,512]{1,0:T(8,128)(2,1)S(1)}, bf16[16,512]{1,0:T(8,128)(2,1)S(1)}, f32[16,512]{1,0:T(8,128)S(1)}) custom-call(s32[2]{0:T(128)S(1)} %pad_add_fusion.3.scalars, bf16[4096,512]{1,0:T(8,128)(2,1)} %refs_0_.15, bf16[4096,512]{1,0:T(8,128)(2,1)} %refs_1_.11, ...), custom_call_target="tpu_custom_call" | custom-call | flops 8388608 | bytes 61440 | tf_op jit(solution)/shard_map/finish_kv/pallas_call | solution.py:70
  97.3 3.3 %collective-permute-start.16 = (bf16[128,1024]{1,0:T(8,128)(2,1)}, bf16[128,1024]{1,0:T(8,128)(2,1)S(1)}, u32[]{:S(2)}, u32[]{:S(2)}) collective-permute-start(bf16[128,1024]{1,0:T(8,128)(2,1)} %collective-permute-done.13.refs_5_), channel_id=1, source_target_pairs={{0,1},{1,2},{2,3},{3,0},{4,5},{5,6},{6,7},{7,4},{8,9},{9,10},{10,1... | collective-permute-start | bytes 786440 | tf_op jit(solution)/shard_map/ppermute | solution.py:467
  100.6 7.9 %collective-permute-done.16.refs_4_ = bf16[128,1024]{1,0:T(8,128)(2,1)S(1)} collective-permute-done((bf16[128,1024]{1,0:T(8,128)(2,1)}, bf16[128,1024]{1,0:T(8,128)(2,1)S(1)}, u32[]{:S(2)}, u32[]{:S(2)}) %collective-permute-start.16) | collective-permute-done | bytes 262176 | tf_op jit(solution)/shard_map/ppermute | solution.py:467
  108.5 4.3 %collective-permute-done.14.refs_3_ = bf16[128,1024]{1,0:T(8,128)(2,1)S(1)} collective-permute-done((bf16[128,1024]{1,0:T(8,128)(2,1)}, bf16[128,1024]{1,0:T(8,128)(2,1)S(1)}, u32[]{:S(2)}, u32[]{:S(2)}) %collective-permute-start.14) | collective-permute-done | bytes 262176 | tf_op jit(solution)/shard_map/ppermute | solution.py:467
  112.8 3.2 %collective-permute-done.18.refs_11_ = bf16[2,256,512]{2,1,0:T(8,128)(2,1)S(1)} collective-permute-done((bf16[2,256,512]{2,1,0:T(8,128)(2,1)S(1)}, bf16[2,256,512]{2,1,0:T(8,128)(2,1)S(1)}, u32[]{:S(2)}, u32[]{:S(2)}) %collective-permute-start.18) | collective-permute-done | bytes 524320 | tf_op jit(solution)/shard_map/ppermute | solution.py:457
  116.0 2.2 %collective-permute-start.17 = (bf16[128,1024]{1,0:T(8,128)(2,1)S(1)}, bf16[128,1024]{1,0:T(8,128)(2,1)S(1)}, u32[]{:S(2)}, u32[]{:S(2)}) collective-permute-start(bf16[128,1024]{1,0:T(8,128)(2,1)S(1)} %collective-permute-done.16.refs_4_), channel_id=1, source_target_pairs={{0,1},{1,2},{2,3},{3,0},{4,5},{5,6},{6,7},{7,4},{8,9},{9,10},{10,1... | collective-permute-start | bytes 786440 | tf_op jit(solution)/shard_map/ppermute | solution.py:467
  118.9 3.1 %finish_q.2 = (bf16[256,512]{1,0:T(8,128)(2,1)S(1)}, bf16[256,512]{1,0:T(8,128)(2,1)S(1)}, f32[16,512]{1,0:T(8,128)S(1)}) custom-call(s32[2]{0:T(128)S(1)} %pad_add_fusion.3.scalars, bf16[4096,512]{1,0:T(8,128)(2,1)} %refs_0_.14, bf16[128,1024]{1,0:T(8,128)(2,1)} %collective-permute-done.6.refs_1_.refs_2_, ...), custom_call_target="tpu_custom_call" | custom-call | flops 4194304 | bytes 32768 | tf_op jit(solution)/shard_map/finish_q/pallas_call | solution.py:70
  122.1 2.6 %slab_sums.7 = (f32[256,512]{1,0:T(8,128)S(1)}, f32[256,512]{1,0:T(8,128)S(1)}, f32[256,512]{1,0:T(8,128)S(1)}) custom-call(s32[1]{0:T(128)} %bitcast.18.slab_ref, bf16[4096,512]{1,0:T(8,128)(2,1)} %refs_0_.14, bf16[4096,512]{1,0:T(8,128)(2,1)} %refs_0_.15, bf16[4096,512]{1,0:T(8,128)(2,1)} %refs_1_.11, ...), custom_call_target="tpu_custom_call" | custom-call | flops 12582912 | bytes 49152 | tf_op jit(solution)/shard_map/slab_sums/pallas_call | solution.py:70
  124.7 2.1 %attend_forward.1.refs_14_ = f32[256,512]{1,0:T(8,128)S(1)} custom-call(s32[4]{0:T(128)S(1)} %get-tuple-element.81.refs_0_.scalars, bf16[256,512]{1,0:T(8,128)(2,1)S(1)} %get-tuple-element.82.refs_1_, bf16[256,512]{1,0:T(8,128)(2,1)S(1)} %get-tuple-element.83.refs_2_, bf16[16,512]{1,0:T(8,128)(2,1)S(1)} %get-tuple-element.84.refs_3_, ...), custom_call_target="tpu_custom_call" | custom-call | flops 16777216 | bytes 32768 | tf_op jit(solution)/shard_map/attend_forward/pallas_call | solution.py:366
  126.9 5.2 %collective-permute-done.15.refs_1_.refs_2_ = bf16[128,1024]{1,0:T(8,128)(2,1)S(1)} collective-permute-done((bf16[128,1024]{1,0:T(8,128)(2,1)S(1)}, bf16[128,1024]{1,0:T(8,128)(2,1)S(1)}, u32[]{:S(2)}, u32[]{:S(2)}) %collective-permute-start.15) | collective-permute-done | bytes 262176 | tf_op jit(solution)/shard_map/ppermute | solution.py:467
  132.1 2.8 %finish_kv.3 = (bf16[2,256,256]{2,1,0:T(8,128)(2,1)S(1)}, bf16[2,256,256]{2,1,0:T(8,128)(2,1)S(1)}) custom-call(s32[2]{0:T(128)S(1)} %pad_add_fusion.3.scalars, bf16[4096,512]{1,0:T(8,128)(2,1)} %refs_0_.15, bf16[4096,512]{1,0:T(8,128)(2,1)} %refs_1_.11, bf16[128,1024]{1,0:T(8,128)(2,1)S(1)} %collective-permute-done.15.refs_1_.refs_2_, ...), custom_call_target="tpu_custom_call" | custom-call | flops 8388608 | bytes 61440 | tf_op jit(solution)/shard_map/finish_kv/pallas_call | solution.py:70
  135.7 2.5 %finish_q.3 = (bf16[256,512]{1,0:T(8,128)(2,1)S(1)}, bf16[256,512]{1,0:T(8,128)(2,1)S(1)}) custom-call(s32[2]{0:T(128)S(1)} %pad_add_fusion.3.scalars, bf16[4096,512]{1,0:T(8,128)(2,1)} %refs_0_.14, bf16[128,1024]{1,0:T(8,128)(2,1)S(1)} %collective-permute-done.15.refs_1_.refs_2_, bf16[128,1024]{1,0:T(8,128)(2,1)S(1)} %collective-permute-done.17.refs_2_.refs_3_, ...), custom_call_target="tpu_custom_call" | custom-call | flops 4194304 | bytes 32768 | tf_op jit(solution)/shard_map/finish_q/pallas_call | solution.py:70
  138.2 4.8 %collective-permute-done.22.refs_11_ = bf16[2,256,256]{2,1,0:T(8,128)(2,1)S(1)} collective-permute-done((bf16[2,256,256]{2,1,0:T(8,128)(2,1)S(1)}, bf16[2,256,256]{2,1,0:T(8,128)(2,1)S(1)}, u32[]{:S(2)}, u32[]{:S(2)}) %collective-permute-start.22) | collective-permute-done | bytes 262176 | tf_op jit(solution)/shard_map/ppermute | solution.py:457
  144.5 3.6 %attend_reverse.2.refs_0_ = bf16[256,256]{1,0:T(8,128)(2,1)S(1)} custom-call(s32[4]{0:T(128)S(1)} %get-tuple-element.81.refs_0_.scalars, bf16[256,512]{1,0:T(8,128)(2,1)S(1)} %get-tuple-element.93.refs_1_, bf16[256,512]{1,0:T(8,128)(2,1)S(1)} %get-tuple-element.94.refs_2_, bf16[16,512]{1,0:T(8,128)(2,1)S(1)} %get-tuple-element.84.refs_3_, ...), custom_call_target="tpu_custom_call" | custom-call | flops 8388608 | bytes 16384 | tf_op jit(solution)/shard_map/attend_reverse/pallas_call | solution.py:366
  148.2 3.5 %collective-permute-done.21.refs_11_ = bf16[2,256,256]{2,1,0:T(8,128)(2,1)S(1)} collective-permute-done((bf16[2,256,256]{2,1,0:T(8,128)(2,1)S(1)}, bf16[2,256,256]{2,1,0:T(8,128)(2,1)S(1)}, u32[]{:S(2)}, u32[]{:S(2)}) %collective-permute-start.21) | collective-permute-done | bytes 262176 | tf_op jit(solution)/shard_map/ppermute | solution.py:457
  152.8 2.7 %collective-permute-start.32 = (bf16[256,256]{1,0:T(8,128)(2,1)S(1)}, bf16[256,256]{1,0:T(8,128)(2,1)S(1)}, u32[]{:S(2)}, u32[]{:S(2)}) collective-permute-start(bf16[256,256]{1,0:T(8,128)(2,1)S(1)} %attend_reverse.2.refs_0_), channel_id=1, source_target_pairs={{0,3},{1,0},{2,1},{3,2},{4,7},{5,4},{6,5},{7,6},{8,11},{9,8},{10,9... | collective-permute-start | bytes 393224 | tf_op jit(solution)/shard_map/ppermute | solution.py:599
  155.5 3.6 %attend_reverse.3.refs_0_ = bf16[256,256]{1,0:T(8,128)(2,1)S(1)} custom-call(s32[4]{0:T(128)S(1)} %get-tuple-element.81.refs_0_.scalars, bf16[256,512]{1,0:T(8,128)(2,1)S(1)} %get-tuple-element.93.refs_1_, bf16[256,512]{1,0:T(8,128)(2,1)S(1)} %get-tuple-element.94.refs_2_, bf16[16,512]{1,0:T(8,128)(2,1)S(1)} %get-tuple-element.84.refs_3_, ...), custom_call_target="tpu_custom_call" | custom-call | flops 8388608 | bytes 16384 | tf_op jit(solution)/shard_map/attend_reverse/pallas_call | solution.py:366
  159.8 1.5 collective-permute-start.28
  161.3 2.8 %collective-permute-start.29 = (bf16[256,256]{1,0:T(8,128)(2,1)S(1)}, bf16[256,256]{1,0:T(8,128)(2,1)S(1)}, u32[]{:S(2)}, u32[]{:S(2)}) collective-permute-start(bf16[256,256]{1,0:T(8,128)(2,1)S(1)} %attend_reverse.3.refs_0_), channel_id=1, source_target_pairs={{0,3},{1,0},{2,1},{3,2},{4,7},{5,4},{6,5},{7,6},{8,11},{9,8},{10,9... | collective-permute-start | bytes 393224 | tf_op jit(solution)/shard_map/ppermute | solution.py:599
  164.2 1.1 collective-permute-done.31.refs_2_
  165.3 2.6 %out_project.2.refs_4_ = f32[256,1024]{1,0:T(8,128)S(1)} custom-call(s32[4]{0:T(128)S(1)} %get-tuple-element.81.refs_0_.scalars, bf16[4,512,1024]{2,1,0:T(8,128)(2,1)} %all-gather.2.cloned.1.call-done.weight_ref, bf16[256,256]{1,0:T(8,128)(2,1)S(1)} %attend_reverse.2.refs_0_, bf16[256,256]{1,0:T(8,128)(2,1)S(1)} %collective-permute-done.30.refs_1_, ...), custom_call_target="tpu_custom_call" | custom-call | flops 8388608 | bytes 32768 | tf_op jit(solution)/shard_map/out_project/pallas_call | solution.py:70
  168.4 7.8 %collective-permute-done.28.refs_2_ = bf16[256,256]{1,0:T(8,128)(2,1)S(1)} collective-permute-done((bf16[256,256]{1,0:T(8,128)(2,1)S(1)}, bf16[256,256]{1,0:T(8,128)(2,1)S(1)}, u32[]{:S(2)}, u32[]{:S(2)}) %collective-permute-start.28) | collective-permute-done | bytes 131104 | tf_op jit(solution)/shard_map/ppermute | solution.py:599
  176.3 3.3 %out_project.3 = bf16[256,1024]{1,0:T(8,128)(2,1)} custom-call(s32[4]{0:T(128)S(1)} %get-tuple-element.81.refs_0_.scalars, bf16[4,512,1024]{2,1,0:T(8,128)(2,1)} %all-gather.2.cloned.1.call-done.weight_ref, bf16[256,256]{1,0:T(8,128)(2,1)S(1)} %attend_reverse.3.refs_0_, bf16[256,256]{1,0:T(8,128)(2,1)S(1)} %collective-permute-done.27.refs_1_, ...), custom_call_target="tpu_custom_call" | custom-call | flops 8388608 | bytes 32768 | tf_op jit(solution)/shard_map/out_project/pallas_call | solution.py:70
  (131 shorter events, 28.3 us)
Async XLA Ops:
  6.5 158.8 %all-gather.2.cloned.1.call-start = ((), (), s32[]{:S(2)}) async-start(), calls=%async_computation | async-start | bytes 4718592 | tf_op jit(solution)/shard_map/all_gather | solution.py:618
  6.5 14.7 %collective-permute-start.9 = (s32[256]{0:T(256)}, s32[256]{0:T(256)S(1)}, u32[]{:S(2)}, u32[]{:S(2)}) collective-permute-start(s32[256]{0:T(256)} %param.10), channel_id=1, source_target_pairs={{0,8},{4,12},{8,0},{12,4},{1,9},{5,13},{9,1},{13,5},{2,10},{6,14},... | collective-permute-start | bytes 3080 | tf_op jit(solution)/shard_map/ppermute | solution.py:457
  9.5 11.9 %collective-permute-start.10 = (s32[256]{0:T(256)}, s32[256]{0:T(256)S(1)}, u32[]{:S(2)}, u32[]{:S(2)}) collective-permute-start(s32[256]{0:T(256)} %param.10), channel_id=1, source_target_pairs={{0,4},{4,0},{8,12},{12,8},{1,5},{5,1},{9,13},{13,9},{2,6},{6,2},{1... | collective-permute-start | bytes 3080 | tf_op jit(solution)/shard_map/ppermute | solution.py:464
  11.4 16.5 %collective-permute-start = (bf16[128,1024]{1,0:T(8,128)(2,1)}, bf16[128,1024]{1,0:T(8,128)(2,1)}, u32[]{:S(2)}, u32[]{:S(2)}) collective-permute-start(bf16[128,1024]{1,0:T(8,128)(2,1)} %get-tuple-element.108), channel_id=1, source_target_pairs={{0,1},{1,2},{2,3},{3,0},{4,5},{5,6},{6,7},{7,4},{8,9},{9,10},{10,1... | collective-permute-start | bytes 786440 | tf_op jit(solution)/shard_map/ppermute | solution.py:467
  12.9 14.9 %collective-permute-start.1 = (bf16[128,1024]{1,0:T(8,128)(2,1)}, bf16[128,1024]{1,0:T(8,128)(2,1)}, u32[]{:S(2)}, u32[]{:S(2)}) collective-permute-start(bf16[128,1024]{1,0:T(8,128)(2,1)} %get-tuple-element.107), channel_id=1, source_target_pairs={{0,1},{1,2},{2,3},{3,0},{4,5},{5,6},{6,7},{7,4},{8,9},{9,10},{10,1... | collective-permute-start | bytes 786440 | tf_op jit(solution)/shard_map/ppermute | solution.py:467
  16.3 4.5 %copy-start.35 = (s32[128]{0:T(128)S(1)}, s32[128]{0:T(128)}, u32[]{:S(2)}) copy-start(s32[128]{0:T(128)} %param.12) | copy-start | bytes 1540
  16.3 4.5 %copy-start.36 = (s32[128]{0:T(128)S(1)}, s32[128]{0:T(128)}, u32[]{:S(2)}) copy-start(s32[128]{0:T(128)} %param.11) | copy-start | bytes 1540
  16.3 6.1 %copy-start.34 = (s32[256]{0:T(256)S(1)}, s32[256]{0:T(256)}, u32[]{:S(2)}) copy-start(s32[256]{0:T(256)} %param.10) | copy-start | bytes 3076
  16.3 14.2 %copy-start = (bf16[2,256,1024]{2,1,0:T(8,128)(2,1)S(1)}, bf16[2,256,1024]{2,1,0:T(8,128)(2,1)}, u32[]{:S(2)}) copy-start(bf16[2,256,1024]{2,1,0:T(8,128)(2,1)} %refs_3_.1) | copy-start | bytes 3145732
  21.2 1.2 collective-permute-start.11
  27.9 13.1 %collective-permute-start.8 = (bf16[128,1024]{1,0:T(8,128)(2,1)}, bf16[128,1024]{1,0:T(8,128)(2,1)}, u32[]{:S(2)}, u32[]{:S(2)}) collective-permute-start(bf16[128,1024]{1,0:T(8,128)(2,1)} %collective-permute-done.1.refs_6_), channel_id=1, source_target_pairs={{0,1},{1,2},{2,3},{3,0},{4,5},{5,6},{6,7},{7,4},{8,9},{9,10},{10,1... | collective-permute-start | bytes 786440 | tf_op jit(solution)/shard_map/ppermute | solution.py:467
  27.9 15.7 %collective-permute-start.5 = (bf16[128,1024]{1,0:T(8,128)(2,1)}, bf16[128,1024]{1,0:T(8,128)(2,1)}, u32[]{:S(2)}, u32[]{:S(2)}) collective-permute-start(bf16[128,1024]{1,0:T(8,128)(2,1)} %collective-permute-done.refs_5_), channel_id=1, source_target_pairs={{0,1},{1,2},{2,3},{3,0},{4,5},{5,6},{6,7},{7,4},{8,9},{9,10},{10,1... | collective-permute-start | bytes 786440 | tf_op jit(solution)/shard_map/ppermute | solution.py:467
  41.0 17.3 %collective-permute-start.12 = (bf16[128,1024]{1,0:T(8,128)(2,1)}, bf16[128,1024]{1,0:T(8,128)(2,1)}, u32[]{:S(2)}, u32[]{:S(2)}) collective-permute-start(bf16[128,1024]{1,0:T(8,128)(2,1)} %collective-permute-done.8.refs_5_), channel_id=1, source_target_pairs={{0,1},{1,2},{2,3},{3,0},{4,5},{5,6},{6,7},{7,4},{8,9},{9,10},{10,1... | collective-permute-start | bytes 786440 | tf_op jit(solution)/shard_map/ppermute | solution.py:467
  43.6 14.7 %collective-permute-start.6 = (bf16[128,1024]{1,0:T(8,128)(2,1)}, bf16[128,1024]{1,0:T(8,128)(2,1)}, u32[]{:S(2)}, u32[]{:S(2)}) collective-permute-start(bf16[128,1024]{1,0:T(8,128)(2,1)} %collective-permute-done.5.refs_4_), channel_id=1, source_target_pairs={{0,1},{1,2},{2,3},{3,0},{4,5},{5,6},{6,7},{7,4},{8,9},{9,10},{10,1... | collective-permute-start | bytes 786440 | tf_op jit(solution)/shard_map/ppermute | solution.py:467
  44.6 1.0 copy-start.3
  58.2 23.9 %collective-permute-start.13 = (bf16[128,1024]{1,0:T(8,128)(2,1)}, bf16[128,1024]{1,0:T(8,128)(2,1)}, u32[]{:S(2)}, u32[]{:S(2)}) collective-permute-start(bf16[128,1024]{1,0:T(8,128)(2,1)} %get-tuple-element.72), channel_id=1, source_target_pairs={{0,1},{1,2},{2,3},{3,0},{4,5},{5,6},{6,7},{7,4},{8,9},{9,10},{10,1... | collective-permute-start | bytes 786440 | tf_op jit(solution)/shard_map/ppermute | solution.py:467
  58.3 23.9 %collective-permute-start.7 = (bf16[128,1024]{1,0:T(8,128)(2,1)}, bf16[128,1024]{1,0:T(8,128)(2,1)}, u32[]{:S(2)}, u32[]{:S(2)}) collective-permute-start(bf16[128,1024]{1,0:T(8,128)(2,1)} %get-tuple-element.56), channel_id=1, source_target_pairs={{0,1},{1,2},{2,3},{3,0},{4,5},{5,6},{6,7},{7,4},{8,9},{9,10},{10,1... | collective-permute-start | bytes 786440 | tf_op jit(solution)/shard_map/ppermute | solution.py:467
  61.0 17.1 %collective-permute-start.2 = (bf16[64,1024]{1,0:T(8,128)(2,1)S(1)}, bf16[64,1024]{1,0:T(8,128)(2,1)S(1)}, u32[]{:S(2)}, u32[]{:S(2)}) collective-permute-start(bf16[64,1024]{1,0:T(8,128)(2,1)S(1)} %get-tuple-element.52), channel_id=1, source_target_pairs={{0,1},{1,2},{2,3},{3,0},{4,5},{5,6},{6,7},{7,4},{8,9},{9,10},{10,1... | collective-permute-start | bytes 393224 | tf_op jit(solution)/shard_map/ppermute | solution.py:599
  63.7 17.6 %collective-permute-start.3 = (bf16[64,1024]{1,0:T(8,128)(2,1)S(1)}, bf16[64,1024]{1,0:T(8,128)(2,1)S(1)}, u32[]{:S(2)}, u32[]{:S(2)}) collective-permute-start(bf16[64,1024]{1,0:T(8,128)(2,1)S(1)} %get-tuple-element.53), channel_id=1, source_target_pairs={{0,2},{1,3},{2,0},{3,1},{4,6},{5,7},{6,4},{7,5},{8,10},{9,11},{10,... | collective-permute-start | bytes 393224 | tf_op jit(solution)/shard_map/ppermute | solution.py:599
  64.2 17.1 %collective-permute-start.4 = (bf16[64,1024]{1,0:T(8,128)(2,1)S(1)}, bf16[64,1024]{1,0:T(8,128)(2,1)S(1)}, u32[]{:S(2)}, u32[]{:S(2)}) collective-permute-start(bf16[64,1024]{1,0:T(8,128)(2,1)S(1)} %get-tuple-element.54), channel_id=1, source_target_pairs={{0,3},{1,0},{2,1},{3,2},{4,7},{5,4},{6,5},{7,6},{8,11},{9,8},{10,9... | collective-permute-start | bytes 393224 | tf_op jit(solution)/shard_map/ppermute | solution.py:599
  89.4 1.0 copy-start.9
  93.0 25.9 %copy-start.1 = (bf16[4,256,16]{2,1,0:T(8,128)(2,1)S(1)}, bf16[4,256,16]{2,1,0:T(8,128)(2,1)}, u32[]{:S(2)}) copy-start(bf16[4,256,16]{2,1,0:T(8,128)(2,1)} %get-tuple-element.112.refs_6_) | copy-start | bytes 98308
  93.0 25.9 %copy-start.19 = (f32[256,512]{1,0:T(8,128)S(1)}, f32[256,512]{1,0:T(8,128)}, u32[]{:S(2)}) copy-start(f32[256,512]{1,0:T(8,128)} %copy-done.18) | copy-start | bytes 1572868
  93.0 25.9 %copy-start.29 = (f32[16,512]{1,0:T(8,128)S(1)}, f32[16,512]{1,0:T(8,128)}, u32[]{:S(2)}) copy-start(f32[16,512]{1,0:T(8,128)} %copy-done.28) | copy-start | bytes 98308
  96.5 25.5 %copy-start.13 = (f32[256,512]{1,0:T(8,128)S(1)}, f32[256,512]{1,0:T(8,128)}, u32[]{:S(2)}) copy-start(f32[256,512]{1,0:T(8,128)} %copy-done.12) | copy-start | bytes 1572868
  96.6 25.5 %copy-start.15 = (f32[256,512]{1,0:T(8,128)S(1)}, f32[256,512]{1,0:T(8,128)}, u32[]{:S(2)}) copy-start(f32[256,512]{1,0:T(8,128)} %copy-done.14) | copy-start | bytes 1572868
  96.6 25.5 %copy-start.17 = (f32[256,512]{1,0:T(8,128)S(1)}, f32[256,512]{1,0:T(8,128)}, u32[]{:S(2)}) copy-start(f32[256,512]{1,0:T(8,128)} %copy-done.16) | copy-start | bytes 1572868
  96.6 19.4 %collective-permute-start.18 = (bf16[2,256,512]{2,1,0:T(8,128)(2,1)S(1)}, bf16[2,256,512]{2,1,0:T(8,128)(2,1)S(1)}, u32[]{:S(2)}, u32[]{:S(2)}) collective-permute-start(bf16[2,256,512]{2,1,0:T(8,128)(2,1)S(1)} %get-tuple-element.88.refs_10_), channel_id=1, source_target_pairs={{0,8},{4,12},{8,0},{12,4},{1,9},{5,13},{9,1},{13,5},{2,10},{6,14},... | collective-permute-start | bytes 1572872 | tf_op jit(solution)/shard_map/ppermute | solution.py:457
  97.3 11.2 %collective-permute-start.16 = (bf16[128,1024]{1,0:T(8,128)(2,1)}, bf16[128,1024]{1,0:T(8,128)(2,1)S(1)}, u32[]{:S(2)}, u32[]{:S(2)}) collective-permute-start(bf16[128,1024]{1,0:T(8,128)(2,1)} %collective-permute-done.13.refs_5_), channel_id=1, source_target_pairs={{0,1},{1,2},{2,3},{3,0},{4,5},{5,6},{6,7},{7,4},{8,9},{9,10},{10,1... | collective-permute-start | bytes 786440 | tf_op jit(solution)/shard_map/ppermute | solution.py:467
  100.6 12.2 %collective-permute-start.14 = (bf16[128,1024]{1,0:T(8,128)(2,1)}, bf16[128,1024]{1,0:T(8,128)(2,1)S(1)}, u32[]{:S(2)}, u32[]{:S(2)}) collective-permute-start(bf16[128,1024]{1,0:T(8,128)(2,1)} %collective-permute-done.7.refs_4_), channel_id=1, source_target_pairs={{0,1},{1,2},{2,3},{3,0},{4,5},{5,6},{6,7},{7,4},{8,9},{9,10},{10,1... | collective-permute-start | bytes 786440 | tf_op jit(solution)/shard_map/ppermute | solution.py:467
  100.6 24.1 %collective-permute-start.19 = (bf16[2,256,512]{2,1,0:T(8,128)(2,1)S(1)}, bf16[2,256,512]{2,1,0:T(8,128)(2,1)S(1)}, u32[]{:S(2)}, u32[]{:S(2)}) collective-permute-start(bf16[2,256,512]{2,1,0:T(8,128)(2,1)S(1)} %get-tuple-element.88.refs_10_), channel_id=1, source_target_pairs={{0,4},{4,0},{8,12},{12,8},{1,5},{5,1},{9,13},{13,9},{2,6},{6,2},{1... | collective-permute-start | bytes 1572872 | tf_op jit(solution)/shard_map/ppermute | solution.py:464
  116.0 8.7 %collective-permute-start.20 = (bf16[2,256,512]{2,1,0:T(8,128)(2,1)S(1)}, bf16[2,256,512]{2,1,0:T(8,128)(2,1)S(1)}, u32[]{:S(2)}, u32[]{:S(2)}) collective-permute-start(bf16[2,256,512]{2,1,0:T(8,128)(2,1)S(1)} %collective-permute-done.18.refs_11_), channel_id=1, source_target_pairs={{0,4},{4,0},{8,12},{12,8},{1,5},{5,1},{9,13},{13,9},{2,6},{6,2},{1... | collective-permute-start | bytes 1572872 | tf_op jit(solution)/shard_map/ppermute | solution.py:464
  116.0 10.9 %collective-permute-start.17 = (bf16[128,1024]{1,0:T(8,128)(2,1)S(1)}, bf16[128,1024]{1,0:T(8,128)(2,1)S(1)}, u32[]{:S(2)}, u32[]{:S(2)}) collective-permute-start(bf16[128,1024]{1,0:T(8,128)(2,1)S(1)} %collective-permute-done.16.refs_4_), channel_id=1, source_target_pairs={{0,1},{1,2},{2,3},{3,0},{4,5},{5,6},{6,7},{7,4},{8,9},{9,10},{10,1... | collective-permute-start | bytes 786440 | tf_op jit(solution)/shard_map/ppermute | solution.py:467
  118.2 13.9 %collective-permute-start.15 = (bf16[128,1024]{1,0:T(8,128)(2,1)S(1)}, bf16[128,1024]{1,0:T(8,128)(2,1)S(1)}, u32[]{:S(2)}, u32[]{:S(2)}) collective-permute-start(bf16[128,1024]{1,0:T(8,128)(2,1)S(1)} %collective-permute-done.14.refs_3_), channel_id=1, source_target_pairs={{0,1},{1,2},{2,3},{3,0},{4,5},{5,6},{6,7},{7,4},{8,9},{9,10},{10,1... | collective-permute-start | bytes 786440 | tf_op jit(solution)/shard_map/ppermute | solution.py:467
  122.1 2.6 %copy-start.21 = (bf16[4,16,256]{2,1,0:T(8,128)(2,1)S(1)}, bf16[4,16,256]{2,1,0:T(8,128)(2,1)}, u32[]{:S(2)}) copy-start(bf16[4,16,256]{2,1,0:T(8,128)(2,1)} %get-tuple-element.110.refs_7_) | copy-start | bytes 98308
  135.0 9.6 %copy-start.20 = (bf16[4,16,256]{2,1,0:T(8,128)(2,1)S(1)}, bf16[4,16,256]{2,1,0:T(8,128)(2,1)}, u32[]{:S(2)}) copy-start(bf16[4,16,256]{2,1,0:T(8,128)(2,1)} %get-tuple-element.109.refs_7_) | copy-start | bytes 98308
  135.0 8.0 %collective-permute-start.22 = (bf16[2,256,256]{2,1,0:T(8,128)(2,1)S(1)}, bf16[2,256,256]{2,1,0:T(8,128)(2,1)S(1)}, u32[]{:S(2)}, u32[]{:S(2)}) collective-permute-start(bf16[2,256,256]{2,1,0:T(8,128)(2,1)S(1)} %get-tuple-element.96.refs_10_), channel_id=1, source_target_pairs={{0,8},{4,12},{8,0},{12,4},{1,9},{5,13},{9,1},{13,5},{2,10},{6,14},... | collective-permute-start | bytes 786440 | tf_op jit(solution)/shard_map/ppermute | solution.py:457
  135.7 8.2 %collective-permute-start.23 = (bf16[2,256,256]{2,1,0:T(8,128)(2,1)S(1)}, bf16[2,256,256]{2,1,0:T(8,128)(2,1)S(1)}, u32[]{:S(2)}, u32[]{:S(2)}) collective-permute-start(bf16[2,256,256]{2,1,0:T(8,128)(2,1)S(1)} %get-tuple-element.96.refs_10_), channel_id=1, source_target_pairs={{0,4},{4,0},{8,12},{12,8},{1,5},{5,1},{9,13},{13,9},{2,6},{6,2},{1... | collective-permute-start | bytes 786440 | tf_op jit(solution)/shard_map/ppermute | solution.py:464
  143.0 1.5 collective-permute-start.24
  143.0 8.7 %collective-permute-start.21 = (bf16[2,256,256]{2,1,0:T(8,128)(2,1)S(1)}, bf16[2,256,256]{2,1,0:T(8,128)(2,1)S(1)}, u32[]{:S(2)}, u32[]{:S(2)}) collective-permute-start(bf16[2,256,256]{2,1,0:T(8,128)(2,1)S(1)} %get-tuple-element.95.refs_10_), channel_id=1, source_target_pairs={{0,8},{4,12},{8,0},{12,4},{1,9},{5,13},{9,1},{13,5},{2,10},{6,14},... | collective-permute-start | bytes 786440 | tf_op jit(solution)/shard_map/ppermute | solution.py:457
  143.6 11.9 %collective-permute-start.25 = (bf16[2,256,256]{2,1,0:T(8,128)(2,1)S(1)}, bf16[2,256,256]{2,1,0:T(8,128)(2,1)S(1)}, u32[]{:S(2)}, u32[]{:S(2)}) collective-permute-start(bf16[2,256,256]{2,1,0:T(8,128)(2,1)S(1)} %get-tuple-element.95.refs_10_), channel_id=1, source_target_pairs={{0,4},{4,0},{8,12},{12,8},{1,5},{5,1},{9,13},{13,9},{2,6},{6,2},{1... | collective-permute-start | bytes 786440 | tf_op jit(solution)/shard_map/ppermute | solution.py:464
  151.7 3.8 %collective-permute-start.26 = (bf16[2,256,256]{2,1,0:T(8,128)(2,1)S(1)}, bf16[2,256,256]{2,1,0:T(8,128)(2,1)S(1)}, u32[]{:S(2)}, u32[]{:S(2)}) collective-permute-start(bf16[2,256,256]{2,1,0:T(8,128)(2,1)S(1)} %collective-permute-done.21.refs_11_), channel_id=1, source_target_pairs={{0,4},{4,0},{8,12},{12,8},{1,5},{5,1},{9,13},{13,9},{2,6},{6,2},{1... | collective-permute-start | bytes 786440 | tf_op jit(solution)/shard_map/ppermute | solution.py:464
  151.7 9.6 %collective-permute-start.30 = (bf16[256,256]{1,0:T(8,128)(2,1)S(1)}, bf16[256,256]{1,0:T(8,128)(2,1)S(1)}, u32[]{:S(2)}, u32[]{:S(2)}) collective-permute-start(bf16[256,256]{1,0:T(8,128)(2,1)S(1)} %attend_reverse.2.refs_0_), channel_id=1, source_target_pairs={{0,1},{1,2},{2,3},{3,0},{4,5},{5,6},{6,7},{7,4},{8,9},{9,10},{10,1... | collective-permute-start | bytes 393224 | tf_op jit(solution)/shard_map/ppermute | solution.py:599
  152.1 13.2 %collective-permute-start.31 = (bf16[256,256]{1,0:T(8,128)(2,1)S(1)}, bf16[256,256]{1,0:T(8,128)(2,1)S(1)}, u32[]{:S(2)}, u32[]{:S(2)}) collective-permute-start(bf16[256,256]{1,0:T(8,128)(2,1)S(1)} %attend_reverse.2.refs_0_), channel_id=1, source_target_pairs={{0,2},{1,3},{2,0},{3,1},{4,6},{5,7},{6,4},{7,5},{8,10},{9,11},{10,... | collective-permute-start | bytes 393224 | tf_op jit(solution)/shard_map/ppermute | solution.py:599
  152.8 12.5 %collective-permute-start.32 = (bf16[256,256]{1,0:T(8,128)(2,1)S(1)}, bf16[256,256]{1,0:T(8,128)(2,1)S(1)}, u32[]{:S(2)}, u32[]{:S(2)}) collective-permute-start(bf16[256,256]{1,0:T(8,128)(2,1)S(1)} %attend_reverse.2.refs_0_), channel_id=1, source_target_pairs={{0,3},{1,0},{2,1},{3,2},{4,7},{5,4},{6,5},{7,6},{8,11},{9,8},{10,9... | collective-permute-start | bytes 393224 | tf_op jit(solution)/shard_map/ppermute | solution.py:599
  159.2 9.2 %collective-permute-start.27 = (bf16[256,256]{1,0:T(8,128)(2,1)S(1)}, bf16[256,256]{1,0:T(8,128)(2,1)S(1)}, u32[]{:S(2)}, u32[]{:S(2)}) collective-permute-start(bf16[256,256]{1,0:T(8,128)(2,1)S(1)} %attend_reverse.3.refs_0_), channel_id=1, source_target_pairs={{0,1},{1,2},{2,3},{3,0},{4,5},{5,6},{6,7},{7,4},{8,9},{9,10},{10,1... | collective-permute-start | bytes 393224 | tf_op jit(solution)/shard_map/ppermute | solution.py:599
  159.8 16.5 %collective-permute-start.28 = (bf16[256,256]{1,0:T(8,128)(2,1)S(1)}, bf16[256,256]{1,0:T(8,128)(2,1)S(1)}, u32[]{:S(2)}, u32[]{:S(2)}) collective-permute-start(bf16[256,256]{1,0:T(8,128)(2,1)S(1)} %attend_reverse.3.refs_0_), channel_id=1, source_target_pairs={{0,2},{1,3},{2,0},{3,1},{4,6},{5,7},{6,4},{7,5},{8,10},{9,11},{10,... | collective-permute-start | bytes 393224 | tf_op jit(solution)/shard_map/ppermute | solution.py:599
  161.3 14.9 %collective-permute-start.29 = (bf16[256,256]{1,0:T(8,128)(2,1)S(1)}, bf16[256,256]{1,0:T(8,128)(2,1)S(1)}, u32[]{:S(2)}, u32[]{:S(2)}) collective-permute-start(bf16[256,256]{1,0:T(8,128)(2,1)S(1)} %attend_reverse.3.refs_0_), channel_id=1, source_target_pairs={{0,3},{1,0},{2,1},{3,2},{4,7},{5,4},{6,5},{7,6},{8,11},{9,8},{10,9... | collective-permute-start | bytes 393224 | tf_op jit(solution)/shard_map/ppermute | solution.py:599
  (23 other events, 17.9 us)
Sparse Core Ops, SparseCore 0:
  89.4 41.3 all-gather.1

commit v8 on v6

--- a/solution.py
+++ b/solution.py
@@ -17,7 +17,7 @@
 COST_CUT = 64
 SCORE_SCALE = math.log2(math.e) / math.sqrt(HEAD_DIM)
 VMEM_LIMIT = 24 * 1024 * 1024
-WEIGHT_VMEM_LIMIT = 50 * 1024 * 1024
+WEIGHT_VMEM_LIMIT = 53 * 1024 * 1024
 F32 = jnp.float32
 BF16 = jnp.bfloat16
 

time: 174 us -> 177 us (1.017)
  local copies, waits for them, and re-layouts: 17.4 us -> 3.37 us
  Pallas kernels: 43.3 us -> 55.3 us
  starting transfers between devices: 31.8 us -> 34.6 us
  waiting for transfers between devices: 54.8 us -> 57.4 us
    pallas_call x10, Pallas kernels: 33.7 us -> 45.7 us  [local_call(): pl.pallas_call(kernel, in_specs=[pl.BlockSpec(memory_space=pltpu.SMEM)] +...]
    unnamed x64 -> x24, local copies, waits for them, and re-layouts: 12.3 us -> 0.74 us
    ppermute x9, waiting for transfers between devices: 14.8 us -> 18.6 us  [around(): lax.ppermute(item, 'head', [(i, (i + shift) % slabs) for i in range(slabs)])]
    ppermute x4, starting transfers between devices: 5.45 us -> 7.95 us  [ctx_far(): lax.ppermute(block, 'ctx', [(i, (i + cores * shift) % ctx) for i in range...]
    concatenate x2, other arithmetic: 0.68 us -> 2.69 us  [rope_tables(): jnp.concatenate([cos, cos], axis=1)]
  transfers between devices with their start and end apart: 34 -> 34, of which waited for: 17 -> 15; matrix products, arithmetic and copies ran while one was open for 10% -> 8% of each run, Pallas kernels for 21% -> 27%
where the time goes in v8:
time: 177 us; the launch traced here: 175 us
  waiting for transfers between devices  57.4 us (32%)
  Pallas kernels  55.3 us (31%)
  starting transfers between devices  34.6 us (20%)
  between operations  13.9 us (8%)
  other arithmetic  10.8 us (6%)
  local copies, waits for them, and re-layouts  3.37 us (2%)
    pallas_call x10, Pallas kernels, local_call(): pl.pallas_call(kernel, in_specs=[pl.BlockSpec(memory_space=pltpu.SMEM)] +...  45.7 us
    ppermute x12, waiting for transfers between devices, hop(): return [lax.ppermute(block, 'head', ring) for block in blocks]  27.7 us
    ppermute x9, waiting for transfers between devices, around(): lax.ppermute(item, 'head', [(i, (i + shift) % slabs) for i in range(slabs)])  18.6 us
    ppermute x9, starting transfers between devices, around(): lax.ppermute(item, 'head', [(i, (i + shift) % slabs) for i in range(slabs)])  14.8 us
    ppermute x12, starting transfers between devices, hop(): return [lax.ppermute(block, 'head', ring) for block in blocks]  11.5 us
    ppermute x4, waiting for transfers between devices, ctx_far(): lax.ppermute(block, 'ctx', [(i, (i + cores * shift) % ctx) for i in range...  10 us
    pallas_call x3, Pallas kernels, attend(): pl.pallas_call(functools.partial(attend_kernel, forward, count, before is...  9.62 us
    ppermute x4, starting transfers between devices, ctx_far(): lax.ppermute(block, 'ctx', [(i, (i + cores * shift) % ctx) for i in range...  7.95 us
  transfers between devices with their start and end apart: 34, of which 15 were waited for; matrix products, arithmetic and copies ran while one was open for 8% of the time, Pallas kernels for 27%

profile of v8, /device:TPU:0, one launch (start us, length us, event | category | flops | bytes accessed | tf_op | source)
XLA Modules:
  0.0 175.4 jit_solution(6660725154540013430)
XLA Ops:
  6.5 3.0 %collective-permute-start.8 = (s32[256]{0:T(256)}, s32[256]{0:T(256)S(1)}, u32[]{:S(2)}, u32[]{:S(2)}) collective-permute-start(s32[256]{0:T(256)} %param.10), channel_id=1, source_target_pairs={{0,8},{4,12},{8,0},{12,4},{1,9},{5,13},{9,1},{13,5},{2,10},{6,14},... | collective-permute-start | bytes 3080 | tf_op jit(solution)/shard_map/ppermute | solution.py:457
  9.5 1.1 slice_bitcast_fusion.2
  10.6 1.6 collective-permute-start
  12.2 1.6 collective-permute-start.1
  15.0 1.0 select_reduce_fusion
  16.1 3.7 %fusion.1 = (f32[1024,64]{1,0:T(8,128)S(1)}, f32[1024,64]{1,0:T(8,128)S(1)}, f32[1024,64]{1,0:T(8,128)S(1)}, f32[1024,64]{1,0:T(8,128)S(1)}, f32[1024,64]{1,0:T(8,128)S(1)}, /*index=5*/f32[1024,64]{1,0:T(8,128)S(1)}) fusion(f32[64]{0:T(128)S(1)} %multiply_power_fusion, f32[1024]{0:T(1024)S(1)} %subtract_convert_fusion, f32[1024]{0:T(1024)S(1)} %iota_convert_fusion), kind=kLoop, calls=%fused_computation.17 | loop fusion | flops 262144 | bytes 1581312 | tf_op jit(solution)/shard_map/neg | solution.py:44
  19.8 1.4 pad_maximum_fusion.3
  21.2 1.3 pad_maximum_fusion.1
  22.5 1.4 fusion.3
  25.2 1.1 select_convert_fusion
  26.8 1.1 collective-permute-start.7
  28.3 1.6 collective-permute-start.2
  29.9 2.6 %collective-permute-start.3 = (bf16[64,1024]{1,0:T(8,128)(2,1)S(1)}, bf16[64,1024]{1,0:T(8,128)(2,1)S(1)}, u32[]{:S(2)}, u32[]{:S(2)}) collective-permute-start(bf16[64,1024]{1,0:T(8,128)(2,1)S(1)} %get-tuple-element.53), channel_id=1, source_target_pairs={{0,2},{1,3},{2,0},{3,1},{4,6},{5,7},{6,4},{7,5},{8,10},{9,11},{10,... | collective-permute-start | bytes 393224 | tf_op jit(solution)/shard_map/ppermute | solution.py:599
  32.5 1.8 %collective-permute-start.4 = (bf16[64,1024]{1,0:T(8,128)(2,1)S(1)}, bf16[64,1024]{1,0:T(8,128)(2,1)S(1)}, u32[]{:S(2)}, u32[]{:S(2)}) collective-permute-start(bf16[64,1024]{1,0:T(8,128)(2,1)S(1)} %get-tuple-element.54), channel_id=1, source_target_pairs={{0,3},{1,0},{2,1},{3,2},{4,7},{5,4},{6,5},{7,6},{8,11},{9,8},{10,9... | collective-permute-start | bytes 393224 | tf_op jit(solution)/shard_map/ppermute | solution.py:599
  34.3 6.1 %slab_sums.4 = (f32[256,512]{1,0:T(8,128)}, f32[256,512]{1,0:T(8,128)}, f32[256,512]{1,0:T(8,128)}, f32[16,512]{1,0:T(8,128)S(1)}, f32[16,512]{1,0:T(8,128)S(1)}, /*index=5*/f32[16,512]{1,0:T(8,128)S(1)}) custom-call(s32[2]{0:T(128)S(1)} %pad_add_fusion.3.slab_ref, bf16[4096,512]{1,0:T(8,128)(2,1)} %refs_0_.14, bf16[4096,512]{1,0:T(8,128)(2,1)} %refs_0_.15, ...), custom_call_target="tpu_custom_call" | custom-call | flops 25165824 | bytes 98304 | tf_op jit(solution)/shard_map/slab_sums/pallas_call | solution.py:70
  40.5 5.9 %collective-permute-done.2 = bf16[64,1024]{1,0:T(8,128)(2,1)S(1)} collective-permute-done((bf16[64,1024]{1,0:T(8,128)(2,1)S(1)}, bf16[64,1024]{1,0:T(8,128)(2,1)S(1)}, u32[]{:S(2)}, u32[]{:S(2)}) %collective-permute-start.2) | collective-permute-done | bytes 131104 | tf_op jit(solution)/shard_map/ppermute | solution.py:599
  46.4 4.4 %collective-permute-done.3 = bf16[64,1024]{1,0:T(8,128)(2,1)S(1)} collective-permute-done((bf16[64,1024]{1,0:T(8,128)(2,1)S(1)}, bf16[64,1024]{1,0:T(8,128)(2,1)S(1)}, u32[]{:S(2)}, u32[]{:S(2)}) %collective-permute-start.3) | collective-permute-done | bytes 131104 | tf_op jit(solution)/shard_map/ppermute | solution.py:599
  50.8 3.3 %collective-permute-start.11 = (bf16[128,1024]{1,0:T(8,128)(2,1)S(1)}, bf16[128,1024]{1,0:T(8,128)(2,1)S(1)}, u32[]{:S(2)}, u32[]{:S(2)}) collective-permute-start(bf16[128,1024]{1,0:T(8,128)(2,1)S(1)} %collective-permute-done.7.refs_5_), channel_id=1, source_target_pairs={{0,1},{1,2},{2,3},{3,0},{4,5},{5,6},{6,7},{7,4},{8,9},{9,10},{10,1... | collective-permute-start | bytes 786440 | tf_op jit(solution)/shard_map/ppermute | solution.py:467
  55.1 5.1 %slab_sums.5 = (f32[256,512]{1,0:T(8,128)}, f32[256,512]{1,0:T(8,128)}, f32[256,512]{1,0:T(8,128)}, f32[16,512]{1,0:T(8,128)S(1)}, f32[16,512]{1,0:T(8,128)S(1)}, /*index=5*/f32[16,512]{1,0:T(8,128)S(1)}) custom-call(s32[1]{0:T(128)} %bitcast.20.slab_ref, bf16[4096,512]{1,0:T(8,128)(2,1)} %refs_0_.14, bf16[4096,512]{1,0:T(8,128)(2,1)} %refs_0_.15, ...), custom_call_target="tpu_custom_call" | custom-call | flops 12582912 | bytes 49152 | tf_op jit(solution)/shard_map/slab_sums/pallas_call | solution.py:70
  60.2 1.6 collective-permute-done.11.refs_3_.refs_2_
  61.8 4.6 %collective-permute-done.6.refs_2_.refs_1_ = bf16[128,1024]{1,0:T(8,128)(2,1)S(1)} collective-permute-done((bf16[128,1024]{1,0:T(8,128)(2,1)S(1)}, bf16[128,1024]{1,0:T(8,128)(2,1)S(1)}, u32[]{:S(2)}, u32[]{:S(2)}) %collective-permute-start.6) | collective-permute-done | bytes 262176 | tf_op jit(solution)/shard_map/ppermute | solution.py:467
  66.4 4.7 %finish_kv.2 = (bf16[2,256,512]{2,1,0:T(8,128)(2,1)}, bf16[16,512]{1,0:T(8,128)(2,1)S(1)}, bf16[16,512]{1,0:T(8,128)(2,1)S(1)}, f32[16,512]{1,0:T(8,128)S(1)}) custom-call(s32[2]{0:T(128)S(1)} %pad_add_fusion.2.scalars, bf16[4096,512]{1,0:T(8,128)(2,1)} %refs_0_.15, bf16[4096,512]{1,0:T(8,128)(2,1)} %refs_1_.11, ...), custom_call_target="tpu_custom_call" | custom-call | flops 8388608 | bytes 61440 | tf_op jit(solution)/shard_map/finish_kv/pallas_call | solution.py:70
  71.8 1.6 collective-permute-start.15
  73.7 9.2 %collective-permute-done.15.refs_5_ = bf16[128,1024]{1,0:T(8,128)(2,1)S(1)} collective-permute-done((bf16[128,1024]{1,0:T(8,128)(2,1)S(1)}, bf16[128,1024]{1,0:T(8,128)(2,1)S(1)}, u32[]{:S(2)}, u32[]{:S(2)}) %collective-permute-start.15) | collective-permute-done | bytes 262176 | tf_op jit(solution)/shard_map/ppermute | solution.py:467
  82.9 3.4 %collective-permute-done.12.refs_4_ = bf16[128,1024]{1,0:T(8,128)(2,1)S(1)} collective-permute-done((bf16[128,1024]{1,0:T(8,128)(2,1)S(1)}, bf16[128,1024]{1,0:T(8,128)(2,1)S(1)}, u32[]{:S(2)}, u32[]{:S(2)}) %collective-permute-start.12) | collective-permute-done | bytes 262176 | tf_op jit(solution)/shard_map/ppermute | solution.py:467
  86.2 3.7 %collective-permute-done.18.refs_11_ = bf16[2,256,512]{2,1,0:T(8,128)(2,1)S(1)} collective-permute-done((bf16[2,256,512]{2,1,0:T(8,128)(2,1)}, bf16[2,256,512]{2,1,0:T(8,128)(2,1)S(1)}, u32[]{:S(2)}, u32[]{:S(2)}) %collective-permute-start.18) | collective-permute-done | bytes 524320 | tf_op jit(solution)/shard_map/ppermute | solution.py:457
  89.9 1.7 collective-permute-start.16
  91.6 6.3 %slab_sums.6 = (f32[256,512]{1,0:T(8,128)}, f32[256,512]{1,0:T(8,128)}, f32[256,512]{1,0:T(8,128)}) custom-call(s32[2]{0:T(128)S(1)} %pad_add_fusion.3.slab_ref, bf16[4096,512]{1,0:T(8,128)(2,1)} %refs_0_.14, bf16[4096,512]{1,0:T(8,128)(2,1)} %refs_0_.15, bf16[4096,512]{1,0:T(8,128)(2,1)} %refs_1_.11, bf16[2,256,1024]{2,1,0:T(8,128)(2,1)} %refs_3_.1, ...), custom_call_target="tpu_custom_call" | custom-call | flops 25165824 | bytes 98304 | tf_op jit(solution)/shard_map/slab_sums/pallas_call | solution.py:70
  97.9 2.9 %collective-permute-done.16.refs_4_ = bf16[128,1024]{1,0:T(8,128)(2,1)S(1)} collective-permute-done((bf16[128,1024]{1,0:T(8,128)(2,1)S(1)}, bf16[128,1024]{1,0:T(8,128)(2,1)S(1)}, u32[]{:S(2)}, u32[]{:S(2)}) %collective-permute-start.16) | collective-permute-done | bytes 262176 | tf_op jit(solution)/shard_map/ppermute | solution.py:467
  100.8 5.6 %collective-permute-done.13.refs_3_ = bf16[128,1024]{1,0:T(8,128)(2,1)S(1)} collective-permute-done((bf16[128,1024]{1,0:T(8,128)(2,1)S(1)}, bf16[128,1024]{1,0:T(8,128)(2,1)S(1)}, u32[]{:S(2)}, u32[]{:S(2)}) %collective-permute-start.13) | collective-permute-done | bytes 262176 | tf_op jit(solution)/shard_map/ppermute | solution.py:467
  106.4 3.7 %finish_q.2 = (bf16[256,512]{1,0:T(8,128)(2,1)S(1)}, bf16[256,512]{1,0:T(8,128)(2,1)S(1)}, f32[16,512]{1,0:T(8,128)S(1)}) custom-call(s32[2]{0:T(128)S(1)} %pad_add_fusion.2.scalars, bf16[4096,512]{1,0:T(8,128)(2,1)} %refs_0_.14, bf16[128,1024]{1,0:T(8,128)(2,1)} %copy-done.7, bf16[128,1024]{1,0:T(8,128)(2,1)} %copy-done.6, ...), custom_call_target="tpu_custom_call" | custom-call | flops 4194304 | bytes 32768 | tf_op jit(solution)/shard_map/finish_q/pallas_call | solution.py:70
  110.2 4.9 %slab_sums.7 = (f32[256,512]{1,0:T(8,128)}, f32[256,512]{1,0:T(8,128)}, f32[256,512]{1,0:T(8,128)}) custom-call(s32[1]{0:T(128)} %bitcast.20.slab_ref, bf16[4096,512]{1,0:T(8,128)(2,1)} %refs_0_.14, bf16[4096,512]{1,0:T(8,128)(2,1)} %refs_0_.15, bf16[4096,512]{1,0:T(8,128)(2,1)} %refs_1_.11, bf16[128,1024]{1,0:T(8,128)(2,1)S(1)} %collective-permute-done.13.refs_3_, ...), custom_call_target="tpu_custom_call" | custom-call | flops 12582912 | bytes 49152 | tf_op jit(solution)/shard_map/slab_sums/pallas_call | solution.py:70
  115.2 2.1 %attend_forward.1.refs_14_ = f32[256,512]{1,0:T(8,128)S(1)} custom-call(s32[4]{0:T(128)S(1)} %get-tuple-element.83.refs_0_.scalars, bf16[256,512]{1,0:T(8,128)(2,1)S(1)} %get-tuple-element.84.refs_1_, bf16[256,512]{1,0:T(8,128)(2,1)S(1)} %get-tuple-element.85.refs_2_, bf16[16,512]{1,0:T(8,128)(2,1)S(1)} %get-tuple-element.86.refs_3_, ...), custom_call_target="tpu_custom_call" | custom-call | flops 16777216 | bytes 32768 | tf_op jit(solution)/shard_map/attend_forward/pallas_call | solution.py:366
  118.0 3.9 %finish_kv.3 = (bf16[2,256,256]{2,1,0:T(8,128)(2,1)S(1)}, bf16[2,256,256]{2,1,0:T(8,128)(2,1)S(1)}) custom-call(s32[2]{0:T(128)S(1)} %pad_add_fusion.2.scalars, bf16[4096,512]{1,0:T(8,128)(2,1)} %refs_0_.15, bf16[4096,512]{1,0:T(8,128)(2,1)} %refs_1_.11, bf16[128,1024]{1,0:T(8,128)(2,1)S(1)} %collective-permute-done.14.refs_1_.refs_2_, ...), custom_call_target="tpu_custom_call" | custom-call | flops 8388608 | bytes 61440 | tf_op jit(solution)/shard_map/finish_kv/pallas_call | solution.py:70
  121.9 2.5 %collective-permute-start.22 = (bf16[2,256,256]{2,1,0:T(8,128)(2,1)S(1)}, bf16[2,256,256]{2,1,0:T(8,128)(2,1)S(1)}, u32[]{:S(2)}, u32[]{:S(2)}) collective-permute-start(bf16[2,256,256]{2,1,0:T(8,128)(2,1)S(1)} %get-tuple-element.96.refs_10_), channel_id=1, source_target_pairs={{0,8},{4,12},{8,0},{12,4},{1,9},{5,13},{9,1},{13,5},{2,10},{6,14},... | collective-permute-start | bytes 786440 | tf_op jit(solution)/shard_map/ppermute | solution.py:457
  124.5 3.5 %finish_q.3 = (bf16[256,512]{1,0:T(8,128)(2,1)S(1)}, bf16[256,512]{1,0:T(8,128)(2,1)S(1)}) custom-call(s32[2]{0:T(128)S(1)} %pad_add_fusion.2.scalars, bf16[4096,512]{1,0:T(8,128)(2,1)} %refs_0_.14, bf16[128,1024]{1,0:T(8,128)(2,1)S(1)} %collective-permute-done.14.refs_1_.refs_2_, bf16[128,1024]{1,0:T(8,128)(2,1)} %copy-done.10, ...), custom_call_target="tpu_custom_call" | custom-call | flops 4194304 | bytes 32768 | tf_op jit(solution)/shard_map/finish_q/pallas_call | solution.py:70
  128.0 3.3 %collective-permute-done.22.refs_11_ = bf16[2,256,256]{2,1,0:T(8,128)(2,1)S(1)} collective-permute-done((bf16[2,256,256]{2,1,0:T(8,128)(2,1)S(1)}, bf16[2,256,256]{2,1,0:T(8,128)(2,1)S(1)}, u32[]{:S(2)}, u32[]{:S(2)}) %collective-permute-start.22) | collective-permute-done | bytes 262176 | tf_op jit(solution)/shard_map/ppermute | solution.py:457
  131.2 1.7 collective-permute-start.21
  133.2 3.6 %attend_reverse.2.refs_0_ = bf16[256,256]{1,0:T(8,128)(2,1)S(1)} custom-call(s32[4]{0:T(128)S(1)} %get-tuple-element.83.refs_0_.scalars, bf16[256,512]{1,0:T(8,128)(2,1)S(1)} %get-tuple-element.93.refs_1_, bf16[256,512]{1,0:T(8,128)(2,1)S(1)} %get-tuple-element.94.refs_2_, bf16[16,512]{1,0:T(8,128)(2,1)S(1)} %get-tuple-element.86.refs_3_, ...), custom_call_target="tpu_custom_call" | custom-call | flops 8388608 | bytes 16384 | tf_op jit(solution)/shard_map/attend_reverse/pallas_call | solution.py:366
  136.9 3.1 %collective-permute-done.21.refs_11_ = bf16[2,256,256]{2,1,0:T(8,128)(2,1)S(1)} collective-permute-done((bf16[2,256,256]{2,1,0:T(8,128)(2,1)S(1)}, bf16[2,256,256]{2,1,0:T(8,128)(2,1)S(1)}, u32[]{:S(2)}, u32[]{:S(2)}) %collective-permute-start.21) | collective-permute-done | bytes 262176 | tf_op jit(solution)/shard_map/ppermute | solution.py:457
  140.2 3.9 %collective-permute-start.31 = (bf16[256,256]{1,0:T(8,128)(2,1)S(1)}, bf16[256,256]{1,0:T(8,128)(2,1)S(1)}, u32[]{:S(2)}, u32[]{:S(2)}) collective-permute-start(bf16[256,256]{1,0:T(8,128)(2,1)S(1)} %attend_reverse.2.refs_0_), channel_id=1, source_target_pairs={{0,2},{1,3},{2,0},{3,1},{4,6},{5,7},{6,4},{7,5},{8,10},{9,11},{10,... | collective-permute-start | bytes 393224 | tf_op jit(solution)/shard_map/ppermute | solution.py:599
  144.1 3.9 %attend_reverse.3.refs_0_ = bf16[256,256]{1,0:T(8,128)(2,1)S(1)} custom-call(s32[4]{0:T(128)S(1)} %get-tuple-element.83.refs_0_.scalars, bf16[256,512]{1,0:T(8,128)(2,1)S(1)} %get-tuple-element.93.refs_1_, bf16[256,512]{1,0:T(8,128)(2,1)S(1)} %get-tuple-element.94.refs_2_, bf16[16,512]{1,0:T(8,128)(2,1)S(1)} %get-tuple-element.86.refs_3_, ...), custom_call_target="tpu_custom_call" | custom-call | flops 8388608 | bytes 16384 | tf_op jit(solution)/shard_map/attend_reverse/pallas_call | solution.py:366
  147.9 2.1 %collective-permute-start.27 = (bf16[256,256]{1,0:T(8,128)(2,1)S(1)}, bf16[256,256]{1,0:T(8,128)(2,1)S(1)}, u32[]{:S(2)}, u32[]{:S(2)}) collective-permute-start(bf16[256,256]{1,0:T(8,128)(2,1)S(1)} %attend_reverse.3.refs_0_), channel_id=1, source_target_pairs={{0,1},{1,2},{2,3},{3,0},{4,5},{5,6},{6,7},{7,4},{8,9},{9,10},{10,1... | collective-permute-start | bytes 393224 | tf_op jit(solution)/shard_map/ppermute | solution.py:599
  150.0 2.7 %collective-permute-start.29 = (bf16[256,256]{1,0:T(8,128)(2,1)S(1)}, bf16[256,256]{1,0:T(8,128)(2,1)S(1)}, u32[]{:S(2)}, u32[]{:S(2)}) collective-permute-start(bf16[256,256]{1,0:T(8,128)(2,1)S(1)} %attend_reverse.3.refs_0_), channel_id=1, source_target_pairs={{0,3},{1,0},{2,1},{3,2},{4,7},{5,4},{6,5},{7,6},{8,11},{9,8},{10,9... | collective-permute-start | bytes 393224 | tf_op jit(solution)/shard_map/ppermute | solution.py:599
  152.7 1.1 collective-permute-done.31.refs_2_
  153.8 3.6 %out_project.2.refs_4_ = f32[256,1024]{1,0:T(8,128)} custom-call(s32[4]{0:T(128)S(1)} %get-tuple-element.83.refs_0_.scalars, bf16[4,512,1024]{2,1,0:T(8,128)(2,1)} %all-gather.2.cloned.1.call-done.weight_ref, bf16[256,256]{1,0:T(8,128)(2,1)S(1)} %attend_reverse.2.refs_0_, bf16[256,256]{1,0:T(8,128)(2,1)S(1)} %collective-permute-done.30.refs_1_, ...), custom_call_target="tpu_custom_call" | custom-call | flops 8388608 | bytes 32768 | tf_op jit(solution)/shard_map/out_project/pallas_call | solution.py:70
  157.4 7.2 %collective-permute-done.28.refs_2_ = bf16[256,256]{1,0:T(8,128)(2,1)S(1)} collective-permute-done((bf16[256,256]{1,0:T(8,128)(2,1)S(1)}, bf16[256,256]{1,0:T(8,128)(2,1)S(1)}, u32[]{:S(2)}, u32[]{:S(2)}) %collective-permute-start.28) | collective-permute-done | bytes 131104 | tf_op jit(solution)/shard_map/ppermute | solution.py:599
  164.6 4.0 %out_project.3 = bf16[256,1024]{1,0:T(8,128)(2,1)} custom-call(s32[4]{0:T(128)S(1)} %get-tuple-element.83.refs_0_.scalars, bf16[4,512,1024]{2,1,0:T(8,128)(2,1)} %all-gather.2.cloned.1.call-done.weight_ref, bf16[256,256]{1,0:T(8,128)(2,1)S(1)} %attend_reverse.3.refs_0_, bf16[256,256]{1,0:T(8,128)(2,1)S(1)} %collective-permute-done.27.refs_1_, ...), custom_call_target="tpu_custom_call" | custom-call | flops 8388608 | bytes 32768 | tf_op jit(solution)/shard_map/out_project/pallas_call | solution.py:70
  (81 shorter events, 6.5 us)
Async XLA Ops:
  6.5 147.2 %all-gather.2.cloned.1.call-start = ((), (), s32[]{:S(2)}) async-start(), calls=%async_computation | async-start | bytes 4718592 | tf_op jit(solution)/shard_map/all_gather | solution.py:619
  6.5 17.5 %collective-permute-start.8 = (s32[256]{0:T(256)}, s32[256]{0:T(256)S(1)}, u32[]{:S(2)}, u32[]{:S(2)}) collective-permute-start(s32[256]{0:T(256)} %param.10), channel_id=1, source_target_pairs={{0,8},{4,12},{8,0},{12,4},{1,9},{5,13},{9,1},{13,5},{2,10},{6,14},... | collective-permute-start | bytes 3080 | tf_op jit(solution)/shard_map/ppermute | solution.py:457
  9.5 14.7 %collective-permute-start.9 = (s32[256]{0:T(256)}, s32[256]{0:T(256)S(1)}, u32[]{:S(2)}, u32[]{:S(2)}) collective-permute-start(s32[256]{0:T(256)} %param.10), channel_id=1, source_target_pairs={{0,4},{4,0},{8,12},{12,8},{1,5},{5,1},{9,13},{13,9},{2,6},{6,2},{1... | collective-permute-start | bytes 3080 | tf_op jit(solution)/shard_map/ppermute | solution.py:464
  10.6 17.4 %collective-permute-start = (bf16[128,1024]{1,0:T(8,128)(2,1)S(1)}, bf16[128,1024]{1,0:T(8,128)(2,1)S(1)}, u32[]{:S(2)}, u32[]{:S(2)}) collective-permute-start(bf16[128,1024]{1,0:T(8,128)(2,1)S(1)} %get-tuple-element.108), channel_id=1, source_target_pairs={{0,1},{1,2},{2,3},{3,0},{4,5},{5,6},{6,7},{7,4},{8,9},{9,10},{10,1... | collective-permute-start | bytes 786440 | tf_op jit(solution)/shard_map/ppermute | solution.py:467
  12.2 14.6 %collective-permute-start.1 = (bf16[128,1024]{1,0:T(8,128)(2,1)S(1)}, bf16[128,1024]{1,0:T(8,128)(2,1)S(1)}, u32[]{:S(2)}, u32[]{:S(2)}) collective-permute-start(bf16[128,1024]{1,0:T(8,128)(2,1)S(1)} %get-tuple-element.107), channel_id=1, source_target_pairs={{0,1},{1,2},{2,3},{3,0},{4,5},{5,6},{6,7},{7,4},{8,9},{9,10},{10,1... | collective-permute-start | bytes 786440 | tf_op jit(solution)/shard_map/ppermute | solution.py:467
  16.1 9.1 %copy-start.11 = (s32[256]{0:T(256)S(1)}, s32[256]{0:T(256)}, u32[]{:S(2)}) copy-start(s32[256]{0:T(256)} %param.10) | copy-start | bytes 3076
  24.0 1.2 collective-permute-start.10
  26.8 24.0 %collective-permute-start.7 = (bf16[128,1024]{1,0:T(8,128)(2,1)S(1)}, bf16[128,1024]{1,0:T(8,128)(2,1)S(1)}, u32[]{:S(2)}, u32[]{:S(2)}) collective-permute-start(bf16[128,1024]{1,0:T(8,128)(2,1)S(1)} %collective-permute-done.1.refs_6_), channel_id=1, source_target_pairs={{0,1},{1,2},{2,3},{3,0},{4,5},{5,6},{6,7},{7,4},{8,9},{9,10},{10,1... | collective-permute-start | bytes 786440 | tf_op jit(solution)/shard_map/ppermute | solution.py:467
  28.0 26.1 %collective-permute-start.5 = (bf16[128,1024]{1,0:T(8,128)(2,1)S(1)}, bf16[128,1024]{1,0:T(8,128)(2,1)S(1)}, u32[]{:S(2)}, u32[]{:S(2)}) collective-permute-start(bf16[128,1024]{1,0:T(8,128)(2,1)S(1)} %collective-permute-done.refs_5_), channel_id=1, source_target_pairs={{0,1},{1,2},{2,3},{3,0},{4,5},{5,6},{6,7},{7,4},{8,9},{9,10},{10,1... | collective-permute-start | bytes 786440 | tf_op jit(solution)/shard_map/ppermute | solution.py:467
  28.3 18.1 %collective-permute-start.2 = (bf16[64,1024]{1,0:T(8,128)(2,1)S(1)}, bf16[64,1024]{1,0:T(8,128)(2,1)S(1)}, u32[]{:S(2)}, u32[]{:S(2)}) collective-permute-start(bf16[64,1024]{1,0:T(8,128)(2,1)S(1)} %get-tuple-element.52), channel_id=1, source_target_pairs={{0,1},{1,2},{2,3},{3,0},{4,5},{5,6},{6,7},{7,4},{8,9},{9,10},{10,1... | collective-permute-start | bytes 393224 | tf_op jit(solution)/shard_map/ppermute | solution.py:599
  29.9 20.9 %collective-permute-start.3 = (bf16[64,1024]{1,0:T(8,128)(2,1)S(1)}, bf16[64,1024]{1,0:T(8,128)(2,1)S(1)}, u32[]{:S(2)}, u32[]{:S(2)}) collective-permute-start(bf16[64,1024]{1,0:T(8,128)(2,1)S(1)} %get-tuple-element.53), channel_id=1, source_target_pairs={{0,2},{1,3},{2,0},{3,1},{4,6},{5,7},{6,4},{7,5},{8,10},{9,11},{10,... | collective-permute-start | bytes 393224 | tf_op jit(solution)/shard_map/ppermute | solution.py:599
  32.5 7.9 %copy-start.9 = (bf16[2,256,1024]{2,1,0:T(8,128)(2,1)S(1)}, bf16[2,256,1024]{2,1,0:T(8,128)(2,1)}, u32[]{:S(2)}) copy-start(bf16[2,256,1024]{2,1,0:T(8,128)(2,1)} %refs_3_.1) | copy-start | bytes 3145732
  32.5 18.3 %collective-permute-start.4 = (bf16[64,1024]{1,0:T(8,128)(2,1)S(1)}, bf16[64,1024]{1,0:T(8,128)(2,1)S(1)}, u32[]{:S(2)}, u32[]{:S(2)}) collective-permute-start(bf16[64,1024]{1,0:T(8,128)(2,1)S(1)} %get-tuple-element.54), channel_id=1, source_target_pairs={{0,3},{1,0},{2,1},{3,2},{4,7},{5,4},{6,5},{7,6},{8,11},{9,8},{10,9... | collective-permute-start | bytes 393224 | tf_op jit(solution)/shard_map/ppermute | solution.py:599
  50.8 11.0 %collective-permute-start.11 = (bf16[128,1024]{1,0:T(8,128)(2,1)S(1)}, bf16[128,1024]{1,0:T(8,128)(2,1)S(1)}, u32[]{:S(2)}, u32[]{:S(2)}) collective-permute-start(bf16[128,1024]{1,0:T(8,128)(2,1)S(1)} %collective-permute-done.7.refs_5_), channel_id=1, source_target_pairs={{0,1},{1,2},{2,3},{3,0},{4,5},{5,6},{6,7},{7,4},{8,9},{9,10},{10,1... | collective-permute-start | bytes 786440 | tf_op jit(solution)/shard_map/ppermute | solution.py:467
  54.1 12.3 %collective-permute-start.6 = (bf16[128,1024]{1,0:T(8,128)(2,1)S(1)}, bf16[128,1024]{1,0:T(8,128)(2,1)S(1)}, u32[]{:S(2)}, u32[]{:S(2)}) collective-permute-start(bf16[128,1024]{1,0:T(8,128)(2,1)S(1)} %collective-permute-done.5.refs_4_), channel_id=1, source_target_pairs={{0,1},{1,2},{2,3},{3,0},{4,5},{5,6},{6,7},{7,4},{8,9},{9,10},{10,1... | collective-permute-start | bytes 786440 | tf_op jit(solution)/shard_map/ppermute | solution.py:467
  61.8 9.3 %copy-start.6 = (bf16[128,1024]{1,0:T(8,128)(2,1)}, bf16[128,1024]{1,0:T(8,128)(2,1)S(1)}, u32[]{:S(2)}) copy-start(bf16[128,1024]{1,0:T(8,128)(2,1)S(1)} %collective-permute-done.11.refs_3_.refs_2_) | copy-start | bytes 786436
  66.4 4.7 %copy-start.7 = (bf16[128,1024]{1,0:T(8,128)(2,1)}, bf16[128,1024]{1,0:T(8,128)(2,1)S(1)}, u32[]{:S(2)}) copy-start(bf16[128,1024]{1,0:T(8,128)(2,1)S(1)} %collective-permute-done.6.refs_2_.refs_1_) | copy-start | bytes 786436
  71.1 18.8 %collective-permute-start.18 = (bf16[2,256,512]{2,1,0:T(8,128)(2,1)}, bf16[2,256,512]{2,1,0:T(8,128)(2,1)S(1)}, u32[]{:S(2)}, u32[]{:S(2)}) collective-permute-start(bf16[2,256,512]{2,1,0:T(8,128)(2,1)} %get-tuple-element.68.refs_10_), channel_id=1, source_target_pairs={{0,8},{4,12},{8,0},{12,4},{1,9},{5,13},{9,1},{13,5},{2,10},{6,14},... | collective-permute-start | bytes 1572872 | tf_op jit(solution)/shard_map/ppermute | solution.py:457
  71.8 11.0 %collective-permute-start.15 = (bf16[128,1024]{1,0:T(8,128)(2,1)S(1)}, bf16[128,1024]{1,0:T(8,128)(2,1)S(1)}, u32[]{:S(2)}, u32[]{:S(2)}) collective-permute-start(bf16[128,1024]{1,0:T(8,128)(2,1)S(1)} %get-tuple-element.74), channel_id=1, source_target_pairs={{0,1},{1,2},{2,3},{3,0},{4,5},{5,6},{6,7},{7,4},{8,9},{9,10},{10,1... | collective-permute-start | bytes 786440 | tf_op jit(solution)/shard_map/ppermute | solution.py:467
  73.4 12.8 %collective-permute-start.12 = (bf16[128,1024]{1,0:T(8,128)(2,1)S(1)}, bf16[128,1024]{1,0:T(8,128)(2,1)S(1)}, u32[]{:S(2)}, u32[]{:S(2)}) collective-permute-start(bf16[128,1024]{1,0:T(8,128)(2,1)S(1)} %get-tuple-element.70), channel_id=1, source_target_pairs={{0,1},{1,2},{2,3},{3,0},{4,5},{5,6},{6,7},{7,4},{8,9},{9,10},{10,1... | collective-permute-start | bytes 786440 | tf_op jit(solution)/shard_map/ppermute | solution.py:467
  73.7 41.4 %collective-permute-start.19 = (bf16[2,256,512]{2,1,0:T(8,128)(2,1)}, bf16[2,256,512]{2,1,0:T(8,128)(2,1)S(1)}, u32[]{:S(2)}, u32[]{:S(2)}) collective-permute-start(bf16[2,256,512]{2,1,0:T(8,128)(2,1)} %get-tuple-element.68.refs_10_), channel_id=1, source_target_pairs={{0,4},{4,0},{8,12},{12,8},{1,5},{5,1},{9,13},{13,9},{2,6},{6,2},{1... | collective-permute-start | bytes 1572872 | tf_op jit(solution)/shard_map/ppermute | solution.py:464
  89.9 25.2 %collective-permute-start.20 = (bf16[2,256,512]{2,1,0:T(8,128)(2,1)S(1)}, bf16[2,256,512]{2,1,0:T(8,128)(2,1)S(1)}, u32[]{:S(2)}, u32[]{:S(2)}) collective-permute-start(bf16[2,256,512]{2,1,0:T(8,128)(2,1)S(1)} %collective-permute-done.18.refs_11_), channel_id=1, source_target_pairs={{0,4},{4,0},{8,12},{12,8},{1,5},{5,1},{9,13},{13,9},{2,6},{6,2},{1... | collective-permute-start | bytes 1572872 | tf_op jit(solution)/shard_map/ppermute | solution.py:464
  89.9 10.9 %collective-permute-start.16 = (bf16[128,1024]{1,0:T(8,128)(2,1)S(1)}, bf16[128,1024]{1,0:T(8,128)(2,1)S(1)}, u32[]{:S(2)}, u32[]{:S(2)}) collective-permute-start(bf16[128,1024]{1,0:T(8,128)(2,1)S(1)} %collective-permute-done.15.refs_5_), channel_id=1, source_target_pairs={{0,1},{1,2},{2,3},{3,0},{4,5},{5,6},{6,7},{7,4},{8,9},{9,10},{10,1... | collective-permute-start | bytes 786440 | tf_op jit(solution)/shard_map/ppermute | solution.py:467
  91.6 14.8 %collective-permute-start.13 = (bf16[128,1024]{1,0:T(8,128)(2,1)S(1)}, bf16[128,1024]{1,0:T(8,128)(2,1)S(1)}, u32[]{:S(2)}, u32[]{:S(2)}) collective-permute-start(bf16[128,1024]{1,0:T(8,128)(2,1)S(1)} %collective-permute-done.12.refs_4_), channel_id=1, source_target_pairs={{0,1},{1,2},{2,3},{3,0},{4,5},{5,6},{6,7},{7,4},{8,9},{9,10},{10,1... | collective-permute-start | bytes 786440 | tf_op jit(solution)/shard_map/ppermute | solution.py:467
  100.8 16.5 %collective-permute-start.17 = (bf16[128,1024]{1,0:T(8,128)(2,1)S(1)}, bf16[128,1024]{1,0:T(8,128)(2,1)S(1)}, u32[]{:S(2)}, u32[]{:S(2)}) collective-permute-start(bf16[128,1024]{1,0:T(8,128)(2,1)S(1)} %collective-permute-done.16.refs_4_), channel_id=1, source_target_pairs={{0,1},{1,2},{2,3},{3,0},{4,5},{5,6},{6,7},{7,4},{8,9},{9,10},{10,1... | collective-permute-start | bytes 786440 | tf_op jit(solution)/shard_map/ppermute | solution.py:467
  106.4 10.9 %collective-permute-start.14 = (bf16[128,1024]{1,0:T(8,128)(2,1)S(1)}, bf16[128,1024]{1,0:T(8,128)(2,1)S(1)}, u32[]{:S(2)}, u32[]{:S(2)}) collective-permute-start(bf16[128,1024]{1,0:T(8,128)(2,1)S(1)} %collective-permute-done.13.refs_3_), channel_id=1, source_target_pairs={{0,1},{1,2},{2,3},{3,0},{4,5},{5,6},{6,7},{7,4},{8,9},{9,10},{10,1... | collective-permute-start | bytes 786440 | tf_op jit(solution)/shard_map/ppermute | solution.py:467
  110.2 5.0 %copy-start.2 = (f32[1024,128]{1,0:T(8,128)S(1)}, f32[1024,128]{1,0:T(8,128)}, u32[]{:S(2)}) copy-start(f32[1024,128]{1,0:T(8,128)} %get-tuple-element.124.refs_6_.refs_4_.refs_8_) | copy-start | bytes 1572868
  110.2 5.0 %copy-start.3 = (f32[1024,128]{1,0:T(8,128)S(1)}, f32[1024,128]{1,0:T(8,128)}, u32[]{:S(2)}) copy-start(f32[1024,128]{1,0:T(8,128)} %get-tuple-element.125.refs_7_.refs_5_.refs_9_) | copy-start | bytes 1572868
  110.2 5.0 %copy-start.5 = (bf16[4,256,16]{2,1,0:T(8,128)(2,1)S(1)}, bf16[4,256,16]{2,1,0:T(8,128)(2,1)}, u32[]{:S(2)}) copy-start(bf16[4,256,16]{2,1,0:T(8,128)(2,1)} %get-tuple-element.112.refs_6_) | copy-start | bytes 98308
  110.2 5.0 %copy-start.8 = (bf16[2,256,512]{2,1,0:T(8,128)(2,1)S(1)}, bf16[2,256,512]{2,1,0:T(8,128)(2,1)}, u32[]{:S(2)}) copy-start(bf16[2,256,512]{2,1,0:T(8,128)(2,1)} %get-tuple-element.68.refs_10_) | copy-start | bytes 1572868
  117.3 0.7 copy-start.10
  121.9 11.3 %copy-start = (f32[1024,128]{1,0:T(8,128)S(1)}, f32[1024,128]{1,0:T(8,128)}, u32[]{:S(2)}) copy-start(f32[1024,128]{1,0:T(8,128)} %get-tuple-element.126.refs_4_.refs_6_.refs_8_) | copy-start | bytes 1572868
  121.9 11.3 %copy-start.1 = (f32[1024,128]{1,0:T(8,128)S(1)}, f32[1024,128]{1,0:T(8,128)}, u32[]{:S(2)}) copy-start(f32[1024,128]{1,0:T(8,128)} %get-tuple-element.127.refs_5_.refs_7_.refs_9_) | copy-start | bytes 1572868
  121.9 11.3 %copy-start.4 = (bf16[4,256,16]{2,1,0:T(8,128)(2,1)S(1)}, bf16[4,256,16]{2,1,0:T(8,128)(2,1)}, u32[]{:S(2)}) copy-start(bf16[4,256,16]{2,1,0:T(8,128)(2,1)} %get-tuple-element.111.refs_6_) | copy-start | bytes 98308
  121.9 9.3 %collective-permute-start.22 = (bf16[2,256,256]{2,1,0:T(8,128)(2,1)S(1)}, bf16[2,256,256]{2,1,0:T(8,128)(2,1)S(1)}, u32[]{:S(2)}, u32[]{:S(2)}) collective-permute-start(bf16[2,256,256]{2,1,0:T(8,128)(2,1)S(1)} %get-tuple-element.96.refs_10_), channel_id=1, source_target_pairs={{0,8},{4,12},{8,0},{12,4},{1,9},{5,13},{9,1},{13,5},{2,10},{6,14},... | collective-permute-start | bytes 786440 | tf_op jit(solution)/shard_map/ppermute | solution.py:457
  124.5 8.7 %collective-permute-start.23 = (bf16[2,256,256]{2,1,0:T(8,128)(2,1)S(1)}, bf16[2,256,256]{2,1,0:T(8,128)(2,1)S(1)}, u32[]{:S(2)}, u32[]{:S(2)}) collective-permute-start(bf16[2,256,256]{2,1,0:T(8,128)(2,1)S(1)} %get-tuple-element.96.refs_10_), channel_id=1, source_target_pairs={{0,4},{4,0},{8,12},{12,8},{1,5},{5,1},{9,13},{13,9},{2,6},{6,2},{1... | collective-permute-start | bytes 786440 | tf_op jit(solution)/shard_map/ppermute | solution.py:464
  131.2 2.0 %collective-permute-start.24 = (bf16[2,256,256]{2,1,0:T(8,128)(2,1)S(1)}, bf16[2,256,256]{2,1,0:T(8,128)(2,1)S(1)}, u32[]{:S(2)}, u32[]{:S(2)}) collective-permute-start(bf16[2,256,256]{2,1,0:T(8,128)(2,1)S(1)} %collective-permute-done.22.refs_11_), channel_id=1, source_target_pairs={{0,4},{4,0},{8,12},{12,8},{1,5},{5,1},{9,13},{13,9},{2,6},{6,2},{1... | collective-permute-start | bytes 786440 | tf_op jit(solution)/shard_map/ppermute | solution.py:464
  131.2 8.7 %collective-permute-start.21 = (bf16[2,256,256]{2,1,0:T(8,128)(2,1)S(1)}, bf16[2,256,256]{2,1,0:T(8,128)(2,1)S(1)}, u32[]{:S(2)}, u32[]{:S(2)}) collective-permute-start(bf16[2,256,256]{2,1,0:T(8,128)(2,1)S(1)} %get-tuple-element.95.refs_10_), channel_id=1, source_target_pairs={{0,8},{4,12},{8,0},{12,4},{1,9},{5,13},{9,1},{13,5},{2,10},{6,14},... | collective-permute-start | bytes 786440 | tf_op jit(solution)/shard_map/ppermute | solution.py:457
  133.0 11.1 %collective-permute-start.25 = (bf16[2,256,256]{2,1,0:T(8,128)(2,1)S(1)}, bf16[2,256,256]{2,1,0:T(8,128)(2,1)S(1)}, u32[]{:S(2)}, u32[]{:S(2)}) collective-permute-start(bf16[2,256,256]{2,1,0:T(8,128)(2,1)S(1)} %get-tuple-element.95.refs_10_), channel_id=1, source_target_pairs={{0,4},{4,0},{8,12},{12,8},{1,5},{5,1},{9,13},{13,9},{2,6},{6,2},{1... | collective-permute-start | bytes 786440 | tf_op jit(solution)/shard_map/ppermute | solution.py:464
  140.0 4.1 %collective-permute-start.26 = (bf16[2,256,256]{2,1,0:T(8,128)(2,1)S(1)}, bf16[2,256,256]{2,1,0:T(8,128)(2,1)S(1)}, u32[]{:S(2)}, u32[]{:S(2)}) collective-permute-start(bf16[2,256,256]{2,1,0:T(8,128)(2,1)S(1)} %collective-permute-done.21.refs_11_), channel_id=1, source_target_pairs={{0,4},{4,0},{8,12},{12,8},{1,5},{5,1},{9,13},{13,9},{2,6},{6,2},{1... | collective-permute-start | bytes 786440 | tf_op jit(solution)/shard_map/ppermute | solution.py:464
  140.0 10.0 %collective-permute-start.30 = (bf16[256,256]{1,0:T(8,128)(2,1)S(1)}, bf16[256,256]{1,0:T(8,128)(2,1)S(1)}, u32[]{:S(2)}, u32[]{:S(2)}) collective-permute-start(bf16[256,256]{1,0:T(8,128)(2,1)S(1)} %attend_reverse.2.refs_0_), channel_id=1, source_target_pairs={{0,1},{1,2},{2,3},{3,0},{4,5},{5,6},{6,7},{7,4},{8,9},{9,10},{10,1... | collective-permute-start | bytes 393224 | tf_op jit(solution)/shard_map/ppermute | solution.py:599
  140.2 13.6 %collective-permute-start.31 = (bf16[256,256]{1,0:T(8,128)(2,1)S(1)}, bf16[256,256]{1,0:T(8,128)(2,1)S(1)}, u32[]{:S(2)}, u32[]{:S(2)}) collective-permute-start(bf16[256,256]{1,0:T(8,128)(2,1)S(1)} %attend_reverse.2.refs_0_), channel_id=1, source_target_pairs={{0,2},{1,3},{2,0},{3,1},{4,6},{5,7},{6,4},{7,5},{8,10},{9,11},{10,... | collective-permute-start | bytes 393224 | tf_op jit(solution)/shard_map/ppermute | solution.py:599
  144.1 9.7 %collective-permute-start.32 = (bf16[256,256]{1,0:T(8,128)(2,1)S(1)}, bf16[256,256]{1,0:T(8,128)(2,1)S(1)}, u32[]{:S(2)}, u32[]{:S(2)}) collective-permute-start(bf16[256,256]{1,0:T(8,128)(2,1)S(1)} %attend_reverse.2.refs_0_), channel_id=1, source_target_pairs={{0,3},{1,0},{2,1},{3,2},{4,7},{5,4},{6,5},{7,6},{8,11},{9,8},{10,9... | collective-permute-start | bytes 393224 | tf_op jit(solution)/shard_map/ppermute | solution.py:599
  147.9 9.5 %collective-permute-start.27 = (bf16[256,256]{1,0:T(8,128)(2,1)S(1)}, bf16[256,256]{1,0:T(8,128)(2,1)S(1)}, u32[]{:S(2)}, u32[]{:S(2)}) collective-permute-start(bf16[256,256]{1,0:T(8,128)(2,1)S(1)} %attend_reverse.3.refs_0_), channel_id=1, source_target_pairs={{0,1},{1,2},{2,3},{3,0},{4,5},{5,6},{6,7},{7,4},{8,9},{9,10},{10,1... | collective-permute-start | bytes 393224 | tf_op jit(solution)/shard_map/ppermute | solution.py:599
  150.0 14.6 %collective-permute-start.28 = (bf16[256,256]{1,0:T(8,128)(2,1)S(1)}, bf16[256,256]{1,0:T(8,128)(2,1)S(1)}, u32[]{:S(2)}, u32[]{:S(2)}) collective-permute-start(bf16[256,256]{1,0:T(8,128)(2,1)S(1)} %attend_reverse.3.refs_0_), channel_id=1, source_target_pairs={{0,2},{1,3},{2,0},{3,1},{4,6},{5,7},{6,4},{7,5},{8,10},{9,11},{10,... | collective-permute-start | bytes 393224 | tf_op jit(solution)/shard_map/ppermute | solution.py:599
  150.0 14.6 %collective-permute-start.29 = (bf16[256,256]{1,0:T(8,128)(2,1)S(1)}, bf16[256,256]{1,0:T(8,128)(2,1)S(1)}, u32[]{:S(2)}, u32[]{:S(2)}) collective-permute-start(bf16[256,256]{1,0:T(8,128)(2,1)S(1)} %attend_reverse.3.refs_0_), channel_id=1, source_target_pairs={{0,3},{1,0},{2,1},{3,2},{4,7},{5,4},{6,5},{7,6},{8,11},{9,8},{10,9... | collective-permute-start | bytes 393224 | tf_op jit(solution)/shard_map/ppermute | solution.py:599
Sparse Core Ops, SparseCore 0:
  71.3 37.6 all-gather.1
